TPU v7x, 128 devices: a whole 4x4x4 slice. The times are simulated.
128 devices in a mesh: chan: 4 (over y), pix: 32 (over x, z, core).
Axes of the slice: x: 4, y: 4, z: 4, core: 2. Of those that a mesh axis runs over, the one named last changes fastest.
Arguments:
- pixels: bfloat16 [16384, 2048], P('pix', 'chan'), may hold values from -6 to 6
- tile_number: int32 [256], replicated, may hold values from 0 to 6, never falling along the last dimension, each value on 1 to 64 neighbouring positions
- task_draws: int32 [3], replicated, may hold values from 0 to 8, as said below
- reduce_weight: bfloat16 [2048, 512], P(None, 'chan'), may hold values from -0.125 to 0.125
- reduce_gain: float32 [512], P('chan'), may hold values from 0.1 to 1.9
- reduce_bias: float32 [512], P('chan'), may hold values from -3 to 3
- dilate_weight: bfloat16 [9, 512, 512], P(None, None, 'chan'), may hold values from -0.09375 to 0.09375
- dilate_gain: float32 [512], P('chan'), may hold values from 0.1 to 1.9
- dilate_bias: float32 [512], P('chan'), may hold values from -3 to 3
- expand_weight: bfloat16 [512, 2048], P(None, 'chan'), may hold values from -0.25 to 0.25
- expand_gain: float32 [2048], P('chan'), may hold values from 0.1 to 1.9
- expand_bias: float32 [2048], P('chan'), may hold values from -3 to 3
- point_weight: bfloat16 [3, 256, 2048], P(None, 'chan'), may hold values from -0.125 to 0.125
- atrous_weight: bfloat16 [3, 3, 9, 256, 2048], P(None, None, None, 'chan'), may hold values from -0.046875 to 0.046875
- pooled_weight: bfloat16 [3, 256, 2048], P(None, 'chan'), may hold values from -0.125 to 0.125
- project_weight: bfloat16 [3, 256, 1280], P(None, 'chan'), may hold values from -0.15625 to 0.15625
- cotangent: bfloat16 [3, 16384, 256], P(None, 'pix', 'chan'), may hold values from -6 to 6
Outputs:
- task_maps: bfloat16 [3, 16384, 256], P(None, 'pix', 'chan')
- grad_pixels: bfloat16 [16384, 2048], P('pix', 'chan')
- grad_reduce_weight: float32 [2048, 512], P('pix', 'chan')
- grad_reduce_gain: float32 [512], P('chan')
- grad_reduce_bias: float32 [512], P('chan')
- grad_dilate_weight: float32 [9, 512, 512], P(None, 'pix', 'chan')
- grad_dilate_gain: float32 [512], P('chan')
- grad_dilate_bias: float32 [512], P('chan')
- grad_expand_weight: float32 [512, 2048], P('pix', 'chan')
- grad_expand_gain: float32 [2048], P('chan')
- grad_expand_bias: float32 [2048], P('chan')
- grad_point_weight: float32 [3, 2048, 256], P(None, 'pix', 'chan')
- grad_atrous_weight: float32 [3, 3, 9, 2048, 256], P(None, None, None, 'pix', 'chan')
- grad_pooled_weight: float32 [3, 2048, 256], P(None, None, 'chan')
- grad_project_weight: float32 [3, 1280, 256], P(None, 'pix', 'chan')
Inputs may be any that keep to these rules, and one draw needn't show every extreme that they name: `task_draws`: the three draws are distinct and one of them is 8.
All inputs are finite; a program needn't handle non-finite values.
Results may differ from a plain program's by a relative error of at most 0.03.
Values may be sent and summed in bfloat16 or wider, within the bound.
A program may use at most 832 MiB of HBM per device.

v0:
```python
import jax
import jax.numpy as jnp
from jax import lax
from jax.sharding import PartitionSpec as P

TASKS = 3
TILE_W = 64


eps = 1e-05
section_rate = 4
head_rates = (6, 12, 18)
tap_offsets = tuple(((row_step, col_step) for row_step in (-1, 0, 1) for col_step in (-1, 0, 1)))


def cut_along(x, dim, count):
    dims = x.shape
    tiles = x.reshape(*dims[:dim], count, dims[dim] // count, *dims[dim + 1 :])
    return jnp.moveaxis(tiles, dim, 0)


def sum_at_owner(x, axis, dim):
    count = lax.axis_size(axis)
    tiles = lax.all_to_all(cut_along(x, dim, count), axis, 0, 0, tiled=True)
    return jnp.sum(tiles.astype(jnp.float32), axis=0)


def for_sending(x):
    return jax.tree.map(lambda a: a.astype(jnp.bfloat16) if a.dtype == jnp.float32 else a, x)


def from_behind(block, axis, distance):
    devices = range(lax.axis_size(axis))
    route = [(i - distance, i) for i in devices if i - distance in devices]
    return lax.ppermute(block, axis, route)


def sent_to_all(x, axis):
    copies = jnp.broadcast_to(x, (lax.axis_size(axis), *x.shape))
    return lax.all_to_all(copies, axis, split_axis=0, concat_axis=0, tiled=True)


def of_everyone(x, axis):
    everything = sent_to_all(x, axis)
    return jnp.sum(everything, axis=0)


def in_one(arrays, axis):
    ravelled, at, finished = (jnp.concatenate([a.reshape(-1) for a in arrays]), 0, [])
    total = of_everyone(ravelled, axis)
    for a in arrays:
        finished.append(total[at : at + a.size].reshape(a.shape))
        at += a.size
    return tuple(finished)


def of_everyone_2(x, axis):
    return sent_to_all(x, axis).astype(jnp.float32).sum(axis=0)


def sent_together(arrays, axis, dim, along):
    both = jnp.concatenate(arrays, axis=along)
    result, at, finished = (lax.psum_scatter(both, axis, scatter_dimension=dim, tiled=True), 0, [])
    for a in arrays:
        finished.append(lax.slice_in_dim(result, at, at + a.shape[along], axis=along))
        at += a.shape[along]
    return tuple(finished)


def widen(tensor):
    return lax.all_gather(tensor, "chan", axis=2, tiled=True)


def collect(tensors):
    return jax.tree.map(lambda part: sum_at_owner(part, "chan", 2), for_sending(tensors))


def move_forward(slab_rows, distance):
    return from_behind(slab_rows, "pix", distance)


def move_backward(slab_rows, distance):
    return from_behind(slab_rows, "pix", distance)


def extend_rows(source, reach_rows, mover):
    row_count = source.shape[0]
    upper_rows = []
    lower_rows = []
    for distance in range(1, -(-reach_rows // row_count) + 1):
        wanted = min(row_count, reach_rows - (distance - 1) * row_count)
        upper_rows = [mover(source[row_count - wanted :], distance)] + upper_rows
        lower_rows = lower_rows + [mover(source[:wanted], -distance)]
    return jnp.concatenate(upper_rows + [source] + lower_rows, axis=0)


def tap_read(extended, row_start, col_shift, row_count):
    window = lax.slice_in_dim(extended, row_start, row_start + row_count, axis=0)
    col_count = window.shape[1]
    if col_shift > 0:
        window = jnp.pad(window[:, col_shift:], ((0, 0), (0, col_shift), (0, 0)))
    elif col_shift < 0:
        window = jnp.pad(window[:, : col_count + col_shift], ((0, 0), (-col_shift, 0), (0, 0)))
    return window


def seam_masks(tile_pad, first_row, margin, dilation, row_count):
    own_tiles = lax.dynamic_slice_in_dim(tile_pad, first_row + margin, row_count)
    return [
        (
            lax.dynamic_slice_in_dim(tile_pad, first_row + margin + row_step * dilation, row_count)
            == own_tiles
        ).astype(jnp.float32)
        for row_step in (-1, 0, 1)
    ]


def dilated_apply(extended, kernel, dilation, reach_rows, seam_rows, row_count, form):
    result = None
    for tap_index, (row_step, col_step) in enumerate(tap_offsets):
        window = tap_read(
            extended, reach_rows + row_step * dilation, col_step * dilation, row_count
        )
        product = jnp.einsum(form, window, kernel[tap_index], preferred_element_type=jnp.float32)
        product = product * seam_rows[row_step + 1][:, None, None]
        result = product if result is None else result + product
    return result


def dilated_transpose(extended, kernel, dilation, reach_rows, seam_rows, row_count, form):
    result = None
    for tap_index, (row_step, col_step) in enumerate(tap_offsets):
        window = tap_read(
            extended, reach_rows - row_step * dilation, -col_step * dilation, row_count
        )
        product = jnp.einsum(form, window, kernel[tap_index], preferred_element_type=jnp.float32)
        product = product * seam_rows[1 - row_step][:, None, None]
        result = product if result is None else result + product
    return result


def dilated_weight_grad(extended, grad_pre, dilation, reach_rows, seam_rows, row_count):
    products = []
    for tap_index, (row_step, col_step) in enumerate(tap_offsets):
        window = tap_read(
            extended, reach_rows + row_step * dilation, col_step * dilation, row_count
        )
        masked = grad_pre * seam_rows[row_step + 1].astype(jnp.bfloat16)[:, None, None]
        products.append(
            jnp.einsum("rwc,rwd->cd", window, masked, preferred_element_type=jnp.float32)
        )
    return jnp.stack(products)


def norm_forward(pre_act, scale_gain, shift_bias, pixel_total):
    first_sum, second_sum = in_one(
        (jnp.sum(pre_act, axis=(0, 1)), jnp.sum(pre_act * pre_act, axis=(0, 1))), "pix"
    )
    center = first_sum / pixel_total
    variance = second_sum / pixel_total - center * center
    inv_std = lax.rsqrt(variance + eps)
    unit_act = (pre_act - center) * inv_std
    return (unit_act * scale_gain + shift_bias, unit_act, inv_std)


def norm_backward(grad_out, unit_act, inv_std, scale_gain, pixel_total):
    grad_bias, grad_gain = in_one(
        (jnp.sum(grad_out, axis=(0, 1)), jnp.sum(grad_out * unit_act, axis=(0, 1))), "pix"
    )
    grad_pre = (
        scale_gain
        * inv_std
        * (grad_out - grad_bias / pixel_total - unit_act * grad_gain / pixel_total)
    )
    return (grad_pre, grad_gain, grad_bias)


def silu_slope(pre_act):
    logistic = jax.nn.sigmoid(pre_act)
    return logistic * (1.0 + pre_act * (1.0 - logistic))


def shards(
    pixels,
    tile_number,
    task_draws,
    reduce_weight,
    reduce_gain,
    reduce_bias,
    dilate_weight,
    dilate_gain,
    dilate_bias,
    expand_weight,
    expand_gain,
    expand_bias,
    point_weight,
    atrous_weight,
    pooled_weight,
    project_weight,
    cotangent,
):
    highest = lax.Precision.HIGHEST
    pixel_count = pixels.shape[0]
    row_count = pixel_count // TILE_W
    pixel_total = pixel_count * lax.axis_size("pix")
    tile_count = tile_number.shape[0] // 40 + 1
    margin = max(head_rates)
    first_row = lax.axis_index("pix") * row_count
    tile_pad = jnp.pad(tile_number, (margin, margin), constant_values=-1)
    own_tiles = lax.dynamic_slice_in_dim(tile_pad, first_row + margin, row_count)
    row_onehot = (own_tiles[:, None] == jnp.arange(tile_count)[None, :]).astype(jnp.float32)
    every_tile = (tile_number[:, None] == jnp.arange(tile_count)[None, :]).astype(jnp.float32)
    tile_sizes = jnp.sum(every_tile, axis=0) * TILE_W
    local_in = pixels.reshape(row_count, TILE_W, -1)
    full_in = widen(local_in)
    pre_reduce = jnp.einsum(
        "rwc,cd->rwd", full_in, reduce_weight, preferred_element_type=jnp.float32
    )
    norm_reduce, unit_reduce, scale_reduce = norm_forward(
        pre_reduce, reduce_gain, reduce_bias, pixel_total
    )
    act_reduce = jax.nn.silu(norm_reduce).astype(jnp.bfloat16)
    section_seams = seam_masks(tile_pad, first_row, margin, section_rate, row_count)
    reduce_ext = extend_rows(widen(act_reduce), section_rate, move_forward)
    pre_dilate = dilated_apply(
        reduce_ext,
        dilate_weight,
        section_rate,
        section_rate,
        section_seams,
        row_count,
        "rwc,cd->rwd",
    )
    norm_dilate, unit_dilate, scale_dilate = norm_forward(
        pre_dilate, dilate_gain, dilate_bias, pixel_total
    )
    act_dilate = jax.nn.silu(norm_dilate).astype(jnp.bfloat16)
    full_dilate = widen(act_dilate)
    pre_expand = jnp.einsum(
        "rwc,cd->rwd", full_dilate, expand_weight, preferred_element_type=jnp.float32
    )
    norm_expand, unit_expand, scale_expand = norm_forward(
        pre_expand, expand_gain, expand_bias, pixel_total
    )
    summed = norm_expand + local_in.astype(jnp.float32)
    trunk_out = jax.nn.silu(summed).astype(jnp.bfloat16)
    trunk_full = widen(trunk_out)
    trunk_ext = extend_rows(trunk_full, margin, move_forward)
    row_sums = jnp.sum(trunk_full, axis=1, dtype=jnp.float32)
    tile_sums = of_everyone_2(
        jnp.dot(row_onehot.T, row_sums, precision=highest).astype(jnp.bfloat16), "pix"
    ).astype(jnp.float32)
    tile_mean = (tile_sums / tile_sizes[:, None]).astype(jnp.bfloat16)
    head_seams = [
        seam_masks(tile_pad, first_row, margin, dilation, row_count) for dilation in head_rates
    ]
    pre_point = []
    pre_atrous = []
    pre_pooled = []
    branches = []
    for task_index in range(TASKS):
        point_pre = jnp.einsum(
            "rwc,dc->rwd", trunk_full, point_weight[task_index], preferred_element_type=jnp.float32
        )
        pre_point.append(point_pre)
        branches.append(jax.nn.silu(point_pre).astype(jnp.bfloat16))
        for rate_index in range(3):
            atrous_pre = dilated_apply(
                trunk_ext,
                atrous_weight[task_index, rate_index],
                head_rates[rate_index],
                margin,
                head_seams[rate_index],
                row_count,
                "rwc,dc->rwd",
            )
            pre_atrous.append(atrous_pre)
            branches.append(jax.nn.silu(atrous_pre).astype(jnp.bfloat16))
        pooled_pre = jnp.einsum(
            "kc,dc->kd", tile_mean, pooled_weight[task_index], preferred_element_type=jnp.float32
        )
        pooled_act = jax.nn.silu(pooled_pre).astype(jnp.bfloat16)
        pooled_rows = jnp.dot(
            row_onehot.astype(jnp.bfloat16), pooled_act, preferred_element_type=jnp.float32
        ).astype(jnp.bfloat16)
        pre_pooled.append(pooled_pre)
        branches.append(jnp.broadcast_to(pooled_rows[:, None, :], point_pre.shape))
    joined_local = jnp.stack(branches, axis=2).reshape(pixel_count, 5 * TASKS, -1)
    joined_heads = widen(joined_local).reshape(pixel_count, TASKS, 5, -1)
    project_parts = project_weight.reshape(TASKS, project_weight.shape[1], 5, -1)
    task_maps = jnp.einsum(
        "ptbc,tdbc->tpd", joined_heads, project_parts, preferred_element_type=jnp.float32
    ).astype(jnp.bfloat16)
    task_weight = jax.nn.softmax(task_draws.astype(jnp.float32) / 3.0)
    grad_maps = (task_weight[:, None, None] * cotangent.astype(jnp.float32)).astype(jnp.bfloat16)
    grad_project = jnp.einsum(
        "ptbc,tpd->tbcd", joined_heads, grad_maps, preferred_element_type=jnp.float32
    ).reshape(TASKS, -1, grad_maps.shape[2])
    joined_part = jnp.einsum(
        "tpd,tdbc->ptbc", grad_maps, project_parts, preferred_element_type=jnp.float32
    ).reshape(pixel_count, 5 * TASKS, -1)
    (grad_joined,) = collect((joined_part,))
    grad_joined = grad_joined.reshape(row_count, TILE_W, TASKS, 5, -1)
    grad_point_pre = []
    grad_atrous_pre = []
    pooled_terms = []
    for task_index in range(TASKS):
        grad_point_pre.append(
            (grad_joined[:, :, task_index, 0] * silu_slope(pre_point[task_index])).astype(
                jnp.bfloat16
            )
        )
        for rate_index in range(3):
            grad_atrous_pre.append(
                (
                    grad_joined[:, :, task_index, 1 + rate_index]
                    * silu_slope(pre_atrous[task_index * 3 + rate_index])
                ).astype(jnp.bfloat16)
            )
        pooled_terms.append(
            jnp.dot(
                row_onehot.T, jnp.sum(grad_joined[:, :, task_index, 4], axis=1), precision=highest
            )
        )
    pooled_total = of_everyone(jnp.stack(pooled_terms, axis=1), "pix")
    atrous_ext = extend_rows(jnp.concatenate(grad_atrous_pre, axis=2), margin, move_backward)
    head_width = point_weight.shape[1]
    trunk_part = None
    mean_part = None
    point_grads = []
    atrous_grads = []
    pooled_grads = []
    for task_index in range(TASKS):
        grad_pooled_pre = (pooled_total[:, task_index] * silu_slope(pre_pooled[task_index])).astype(
            jnp.bfloat16
        )
        trunk_term = jnp.einsum(
            "rwd,dc->rwc",
            grad_point_pre[task_index],
            point_weight[task_index],
            preferred_element_type=jnp.float32,
        )
        rate_grads = []
        for rate_index in range(3):
            branch_index = task_index * 3 + rate_index
            dilation = head_rates[rate_index]
            head_ext = atrous_ext[:, :, branch_index * head_width : (branch_index + 1) * head_width]
            trunk_term = trunk_term + dilated_transpose(
                head_ext,
                atrous_weight[task_index, rate_index],
                dilation,
                margin,
                head_seams[rate_index],
                row_count,
                "rwd,dc->rwc",
            )
            rate_grads.append(
                dilated_weight_grad(
                    trunk_ext,
                    grad_atrous_pre[branch_index],
                    dilation,
                    margin,
                    head_seams[rate_index],
                    row_count,
                )
            )
        mean_term = jnp.dot(
            grad_pooled_pre, pooled_weight[task_index], preferred_element_type=jnp.float32
        )
        trunk_part = trunk_term if trunk_part is None else trunk_part + trunk_term
        mean_part = mean_term if mean_part is None else mean_part + mean_term
        point_grads.append(
            jnp.einsum(
                "rwc,rwd->cd",
                trunk_full,
                grad_point_pre[task_index],
                preferred_element_type=jnp.float32,
            )
        )
        atrous_grads.append(jnp.stack(rate_grads))
        pooled_grads.append(
            jnp.dot(tile_mean.T, grad_pooled_pre, preferred_element_type=jnp.float32)
        )
    trunk_grad, mean_grad = collect((trunk_part, mean_part.reshape(tile_count, 1, -1)))
    mean_rows = jnp.dot(row_onehot, mean_grad[:, 0] / tile_sizes[:, None], precision=highest)
    grad_trunk = trunk_grad + mean_rows[:, None, :]
    grad_summed = grad_trunk * silu_slope(summed)
    grad_expand_pre, grad_expand_gain, grad_expand_bias = norm_backward(
        grad_summed, unit_expand, scale_expand, expand_gain, pixel_total
    )
    grad_expand_pre = grad_expand_pre.astype(jnp.bfloat16)
    expand_grad = jnp.einsum(
        "rwc,rwd->cd", full_dilate, grad_expand_pre, preferred_element_type=jnp.float32
    )
    (grad_dilate_act,) = collect(
        (
            jnp.einsum(
                "rwd,cd->rwc", grad_expand_pre, expand_weight, preferred_element_type=jnp.float32
            ),
        )
    )
    grad_dilate_pre, grad_dilate_gain, grad_dilate_bias = norm_backward(
        grad_dilate_act * silu_slope(norm_dilate),
        unit_dilate,
        scale_dilate,
        dilate_gain,
        pixel_total,
    )
    grad_dilate_pre = grad_dilate_pre.astype(jnp.bfloat16)
    dilate_grad = dilated_weight_grad(
        reduce_ext, grad_dilate_pre, section_rate, section_rate, section_seams, row_count
    )
    dilate_ext = extend_rows(grad_dilate_pre, section_rate, move_backward)
    (grad_reduce_act,) = collect(
        (
            dilated_transpose(
                dilate_ext,
                dilate_weight,
                section_rate,
                section_rate,
                section_seams,
                row_count,
                "rwd,cd->rwc",
            ),
        )
    )
    grad_reduce_pre, grad_reduce_gain, grad_reduce_bias = norm_backward(
        grad_reduce_act * silu_slope(norm_reduce),
        unit_reduce,
        scale_reduce,
        reduce_gain,
        pixel_total,
    )
    grad_reduce_pre = grad_reduce_pre.astype(jnp.bfloat16)
    reduce_grad = jnp.einsum(
        "rwc,rwd->cd", full_in, grad_reduce_pre, preferred_element_type=jnp.float32
    )
    (grad_input,) = collect(
        (
            jnp.einsum(
                "rwd,cd->rwc", grad_reduce_pre, reduce_weight, preferred_element_type=jnp.float32
            ),
        )
    )
    grad_pixels = (grad_input + grad_summed).astype(jnp.bfloat16).reshape(pixel_count, -1)
    atrous_stack = jnp.stack(atrous_grads)
    summed_grads = (
        lax.psum_scatter(
            reduce_grad[None].astype(jnp.bfloat16), "pix", scatter_dimension=1, tiled=True
        ).astype(jnp.float32),
        lax.psum_scatter(
            dilate_grad.astype(jnp.bfloat16), "pix", scatter_dimension=1, tiled=True
        ).astype(jnp.float32),
        lax.psum_scatter(
            expand_grad[None].astype(jnp.bfloat16), "pix", scatter_dimension=1, tiled=True
        ).astype(jnp.float32),
        *tuple(
            (
                part.astype(jnp.float32)
                for part in sent_together(
                    (
                        jnp.stack(point_grads).astype(jnp.bfloat16),
                        atrous_stack.reshape(
                            -1, atrous_stack.shape[3], atrous_stack.shape[4]
                        ).astype(jnp.bfloat16),
                    ),
                    "pix",
                    1,
                    0,
                )
            )
        ),
        lax.psum_scatter(
            grad_project.astype(jnp.bfloat16), "pix", scatter_dimension=1, tiled=True
        ).astype(jnp.float32),
    )
    grad_atrous_weight = summed_grads[4].reshape(TASKS, 3, 9, -1, atrous_stack.shape[4])
    return (
        task_maps,
        grad_pixels,
        summed_grads[0][0],
        grad_reduce_gain,
        grad_reduce_bias,
        summed_grads[1],
        grad_dilate_gain,
        grad_dilate_bias,
        summed_grads[2][0],
        grad_expand_gain,
        grad_expand_bias,
        summed_grads[3],
        grad_atrous_weight,
        jnp.stack(pooled_grads),
        summed_grads[5],
    )


def solution(mesh):
    placed = (
        P("pix", "chan"),
        P(),
        P(),
        P(None, "chan"),
        P("chan"),
        P("chan"),
        P(None, None, "chan"),
        P("chan"),
        P("chan"),
        P(None, "chan"),
        P("chan"),
        P("chan"),
        P(None, "chan", None),
        P(None, None, None, "chan", None),
        P(None, "chan", None),
        P(None, "chan", None),
        P(None, "pix", "chan"),
    )
    return jax.shard_map(
        shards,
        mesh=mesh,
        in_specs=placed,
        out_specs=(
            P(None, "pix", "chan"),
            P("pix", "chan"),
            P("pix", "chan"),
            P("chan"),
            P("chan"),
            P(None, "pix", "chan"),
            P("chan"),
            P("chan"),
            P("pix", "chan"),
            P("chan"),
            P("chan"),
            P(None, "pix", "chan"),
            P(None, None, None, "pix", "chan"),
            P(None, None, "chan"),
            P(None, "pix", "chan"),
        ),
        check_vma=False,
    )
```

profile of v0, /device:TPU:7, one launch (start us, length us, event | category | flops | bytes accessed | tf_op | source)
XLA Modules:
  0.0 1678.8 jit_solution(12020316364603350845)
XLA Ops:
  11.7 31.2 %all-gather.4.cloned.1.call-done = bf16[8,64,2048]{2,1,0:T(8,128)(2,1)} async-done(((bf16[8,64,512]{2,1,0:T(8,128)(2,1)}), bf16[8,64,2048]{2,1,0:T(8,128)(2,1)}) %all-gather.4.cloned.1.call-update) | async-done | bytes 2097168 | tf_op jit(solution)/shard_map/all_gather | solution.py:71
  46.0 7.9 all-to-all-start
  60.1 11.9 all_gather.16
  86.3 9.6 all-to-all-start.1
  102.1 11.3 all_gather.17
  115.0 8.7 all-to-all-start.2
  129.6 4.9 all-to-all-start.4
  136.7 60.5 %all-to-all-done.4 = bf16[4,512,15,64]{1,3,2,0:T(8,128)(2,1)} async-done(((bf16[4,512,15,64]{1,3,2,0:T(8,128)(2,1)}), bf16[4,512,15,64]{1,3,2,0:T(8,128)(2,1)}, u32[]{:S(2)}, u32[]{:S(2)}) %all-to-all-start.4) | async-done | bytes 3932192 | tf_op jit(solution)/shard_map/all_to_all | solution.py:24
  205.8 7.1 all-to-all-start.6
  212.9 6.2 all-to-all-done.6
  242.6 4.7 collective-permute-start.7
  249.2 5.6 all-to-all-start.3
  293.4 49.3 %all-to-all-done.3 = bf16[32,7,2048]{2,1,0:T(8,128)(2,1)} async-done(((bf16[32,7,2048]{2,1,0:T(8,128)(2,1)}), bf16[32,7,2048]{2,1,0:T(8,128)(2,1)}, u32[]{:S(2)}, u32[]{:S(2)}) %all-to-all-start.3) | async-done | bytes 917536 | tf_op jit(solution)/shard_map/all_to_all | solution.py:40
  349.7 8.8 all-gather.8.cloned.1.call-start
  544.0 6.1 collective-permute-start.10
  763.9 5.7 collective-permute-start.12
  942.9 103.8 %fusion.7 = bf16[8,64,2048]{2,1,0:T(8,128)(2,1)S(1)} fusion(f32[8,64,2048]{2,1,0:T(8,128)} %fusion.783, f32[8,64,2048]{2,1,0:T(8,128)} %fusion.786, f32[8,64,2048]{2,1,0:T(8,128)} %fusion.790, f32[8,64,2048]{2,1,0:T(8,128)} %fusion.800, f32[8,64,2048]{2,1,0:T(8,128)} %fusion.796, f32[8,64,2048]{2,1,0:T(8,128)} %fusion.812, f32[8,64,2048]{2,1,0:T(8,128)} %fusion.815, ...), kind=kOutput, calls=%fused_computation.14 | convolution fusion | flops 260046848 | bytes 350533824 | tf_op jit(solution)/shard_map/rwd,dc->rwc/dot_general | solution.py:136
  1048.3 4.6 all-to-all-start.5
  1058.3 9.6 maximum_bitcast_fusion
  1068.1 8.8 all-to-all-done.5
  1080.5 8.5 all-to-all-start.8
  1101.9 6.5 maximum_bitcast_fusion.2
  1112.0 7.3 all-to-all-start.10
  1153.9 10.6 all-to-all-start.12
  1165.6 4.5 all-to-all-done.12
  1180.6 15.3 pad_maximum_fusion.1
  1195.9 38.3 %copy.699 = bf16[81,2048,64]{2,1,0:T(8,128)(2,1)} copy(bf16[81,2048,64]{1,2,0:T(8,128)(2,1)} %bitcast.2162) | data formatting | bytes 42467328 | tf_op jit(solution)/shard_map/convert_element_type | solution.py:465
  1243.9 36.6 %pad_maximum_fusion = bf16[84,2048,64]{2,1,0:T(8,128)(2,1)} fusion(bf16[81,2048,64]{2,1,0:T(8,128)(2,1)} %copy.699, bf16[1,2048,64]{2,1,0:T(8,128)(2,1)S(1)} %copy.698, bf16[1,2048,64]{2,1,0:T(8,128)(2,1)S(1)} %copy-done.90, bf16[1,2048,64]{2,1,0:T(8,128)(2,1)S(1)} %copy.696), kind=kLoop, calls=%fused_computation | loop fusion | flops 33030144 | bytes 44040192 | tf_op jit(solution)/shard_map/concatenate | solution.py:62
  1283.7 4.6 all-to-all-start.13
  1294.7 61.1 %reduce-scatter.7.cloned.1.call-done = bf16[9,16,128]{2,1,0:T(8,128)(2,1)} async-done(((bf16[9,512,128]{2,1,0:T(8,128)(2,1)}), bf16[9,16,128]{2,1,0:T(8,128)(2,1)}) %reduce-scatter.7.cloned.1.call-update) | async-done | bytes 36880 | tf_op jit(solution)/shard_map/reduce_scatter | solution.py:451
  1361.8 103.0 %all-reduce.88.cloned.1.call-done = bf16[3,1280,64]{2,0,1:T(4,128)(2,1)} async-done(((bf16[3,1280,64]{2,0,1:T(4,128)(2,1)}), bf16[3,1280,64]{2,0,1:T(4,128)(2,1)}) %all-reduce.88.cloned.1.call-update) | async-done | bytes 491536
  1466.2 201.4 %reduce-scatter.11.cloned.1.call-done = bf16[84,64,64]{2,1,0:T(8,128)(2,1)} async-done(((bf16[84,2048,64]{2,1,0:T(8,128)(2,1)}), bf16[84,64,64]{2,1,0:T(8,128)(2,1)}) %reduce-scatter.11.cloned.1.call-update) | async-done | bytes 688144 | tf_op jit(solution)/shard_map/reduce_scatter | solution.py:63
  (1048 shorter events, 795.5 us)
Async XLA Ops:
  7.2 35.7 %all-gather.4.cloned.1.call-start = ((), (), s32[]{:S(2)}) async-start(), calls=%async_computation.18 | async-start | bytes 2621440 | tf_op jit(solution)/shard_map/all_gather | solution.py:71
  46.0 13.4 all-to-all-start
  86.3 15.1 all-to-all-start.1
  115.0 14.6 all-to-all-start.2
  129.6 67.6 %all-to-all-start.4 = ((bf16[4,512,15,64]{1,3,2,0:T(8,128)(2,1)}), bf16[4,512,15,64]{1,3,2,0:T(8,128)(2,1)}, u32[]{:S(2)}, u32[]{:S(2)}) async-start(bf16[4,512,15,64]{1,3,2,0:T(8,128)(2,1)} %bitcast.2167), calls=%async_computation.4 | async-start | bytes 7864320 | tf_op jit(solution)/shard_map/all_to_all | solution.py:24
  134.6 86.3 %all-gather.6.cloned.1.call-start = ((), (), s32[]{:S(2)}) async-start(), calls=%async_computation.19 | async-start | bytes 2621440 | tf_op jit(solution)/shard_map/all_gather | solution.py:71
  205.8 13.3 all-to-all-start.6
  239.7 47.6 %collective-permute-start.6 = (bf16[2,64,2048]{2,1,0:T(8,128)(2,1)}, bf16[2,64,2048]{2,1,0:T(8,128)(2,1)}, u32[]{:S(2)}, u32[]{:S(2)}) collective-permute-start(bf16[2,64,2048]{2,1,0:T(8,128)(2,1)} %get-tuple-element.174), channel_id=1, source_target_pairs={{0,3},{1,4},{2,5},{3,6},{4,7},{5,8},{6,9},{7,10},{8,11},{9,12},{10... | collective-permute-start | bytes 1572872 | tf_op jit(solution)/shard_map/ppermute | solution.py:35
  242.6 151.1 %collective-permute-start.7 = (bf16[2,64,2048]{2,1,0:T(8,128)(2,1)}, bf16[2,64,2048]{2,1,0:T(8,128)(2,1)}, u32[]{:S(2)}, u32[]{:S(2)}) collective-permute-start(bf16[2,64,2048]{2,1,0:T(8,128)(2,1)} %get-tuple-element.175), channel_id=1, source_target_pairs={{3,0},{4,1},{5,2},{6,3},{7,4},{8,5},{9,6},{10,7},{11,8},{12,9},{13... | collective-permute-start | bytes 1572872 | tf_op jit(solution)/shard_map/ppermute | solution.py:35
  249.2 93.5 %all-to-all-start.3 = ((bf16[32,7,2048]{2,1,0:T(8,128)(2,1)}), bf16[32,7,2048]{2,1,0:T(8,128)(2,1)}, u32[]{:S(2)}, u32[]{:S(2)}) async-start(bf16[32,7,2048]{2,1,0:T(8,128)(2,1)} %broadcast_in_dim.19), calls=%async_computation.3 | async-start | bytes 2097152 | tf_op jit(solution)/shard_map/all_to_all | solution.py:40
  254.8 108.0 %collective-permute-start.4 = (bf16[8,64,2048]{2,1,0:T(8,128)(2,1)S(1)}, bf16[8,64,2048]{2,1,0:T(8,128)(2,1)}, u32[]{:S(2)}, u32[]{:S(2)}) collective-permute-start(bf16[8,64,2048]{2,1,0:T(8,128)(2,1)S(1)} %copy-done.1), channel_id=1, source_target_pairs={{0,2},{1,3},{2,4},{3,5},{4,6},{5,7},{6,8},{7,9},{8,10},{9,11},{10,... | collective-permute-start | bytes 6291464 | tf_op jit(solution)/shard_map/ppermute | solution.py:35
  260.3 115.3 %collective-permute-start.2 = (bf16[8,64,2048]{2,1,0:T(8,128)(2,1)S(1)}, bf16[8,64,2048]{2,1,0:T(8,128)(2,1)}, u32[]{:S(2)}, u32[]{:S(2)}) collective-permute-start(bf16[8,64,2048]{2,1,0:T(8,128)(2,1)S(1)} %copy-done.1), channel_id=1, source_target_pairs={{0,1},{1,2},{2,3},{3,4},{4,5},{5,6},{6,7},{7,8},{8,9},{9,10},{10,1... | collective-permute-start | bytes 6291464 | tf_op jit(solution)/shard_map/ppermute | solution.py:35
  264.0 120.4 %collective-permute-start.3 = (bf16[8,64,2048]{2,1,0:T(8,128)(2,1)S(1)}, bf16[8,64,2048]{2,1,0:T(8,128)(2,1)}, u32[]{:S(2)}, u32[]{:S(2)}) collective-permute-start(bf16[8,64,2048]{2,1,0:T(8,128)(2,1)S(1)} %copy-done.1), channel_id=1, source_target_pairs={{1,0},{2,1},{3,2},{4,3},{5,4},{6,5},{7,6},{8,7},{9,8},{10,9},{11,1... | collective-permute-start | bytes 6291464 | tf_op jit(solution)/shard_map/ppermute | solution.py:35
  287.3 100.3 %collective-permute-start.5 = (bf16[8,64,2048]{2,1,0:T(8,128)(2,1)S(1)}, bf16[8,64,2048]{2,1,0:T(8,128)(2,1)}, u32[]{:S(2)}, u32[]{:S(2)}) collective-permute-start(bf16[8,64,2048]{2,1,0:T(8,128)(2,1)S(1)} %copy-done.1), channel_id=1, source_target_pairs={{2,0},{3,1},{4,2},{5,3},{6,4},{7,5},{8,6},{9,7},{10,8},{11,9},{12,... | collective-permute-start | bytes 6291464 | tf_op jit(solution)/shard_map/ppermute | solution.py:35
  346.4 15.6 all-to-all-start.7
  349.7 888.7 %all-gather.8.cloned.1.call-start = ((), (), s32[]{:S(2)}) async-start(), calls=%async_computation.20 | async-start | bytes 4915200 | tf_op jit(solution)/shard_map/all_gather | solution.py:71
  534.1 236.5 %collective-permute-start.11 = (bf16[8,64,576]{2,1,0:T(8,128)(2,1)S(1)}, bf16[8,64,576]{2,1,0:T(8,128)(2,1)}, u32[]{:S(2)}, u32[]{:S(2)}) collective-permute-start(bf16[8,64,576]{2,1,0:T(8,128)(2,1)S(1)} %concatenate.119), channel_id=1, source_target_pairs={{0,2},{1,3},{2,4},{3,5},{4,6},{5,7},{6,8},{7,9},{8,10},{9,11},{10,... | collective-permute-start | bytes 1769480 | tf_op jit(solution)/shard_map/ppermute | solution.py:35
  536.0 235.9 %collective-permute-start.9 = (bf16[8,64,576]{2,1,0:T(8,128)(2,1)S(1)}, bf16[8,64,576]{2,1,0:T(8,128)(2,1)}, u32[]{:S(2)}, u32[]{:S(2)}) collective-permute-start(bf16[8,64,576]{2,1,0:T(8,128)(2,1)S(1)} %concatenate.119), channel_id=1, source_target_pairs={{0,1},{1,2},{2,3},{3,4},{4,5},{5,6},{6,7},{7,8},{8,9},{9,10},{10,1... | collective-permute-start | bytes 1769480 | tf_op jit(solution)/shard_map/ppermute | solution.py:35
  537.9 257.8 %collective-permute-start.8 = (bf16[8,64,576]{2,1,0:T(8,128)(2,1)S(1)}, bf16[8,64,576]{2,1,0:T(8,128)(2,1)}, u32[]{:S(2)}, u32[]{:S(2)}) collective-permute-start(bf16[8,64,576]{2,1,0:T(8,128)(2,1)S(1)} %concatenate.119), channel_id=1, source_target_pairs={{1,0},{2,1},{3,2},{4,3},{5,4},{6,5},{7,6},{8,7},{9,8},{10,9},{11,1... | collective-permute-start | bytes 1769480 | tf_op jit(solution)/shard_map/ppermute | solution.py:35
  544.0 252.9 %collective-permute-start.10 = (bf16[8,64,576]{2,1,0:T(8,128)(2,1)S(1)}, bf16[8,64,576]{2,1,0:T(8,128)(2,1)}, u32[]{:S(2)}, u32[]{:S(2)}) collective-permute-start(bf16[8,64,576]{2,1,0:T(8,128)(2,1)S(1)} %concatenate.119), channel_id=1, source_target_pairs={{2,0},{3,1},{4,2},{5,3},{6,4},{7,5},{8,6},{9,7},{10,8},{11,9},{12,... | collective-permute-start | bytes 1769480 | tf_op jit(solution)/shard_map/ppermute | solution.py:35
  647.7 116.2 %collective-permute-start.13 = (bf16[2,64,576]{2,1,0:T(8,128)(2,1)}, bf16[2,64,576]{2,1,0:T(8,128)(2,1)}, u32[]{:S(2)}, u32[]{:S(2)}) collective-permute-start(bf16[2,64,576]{2,1,0:T(8,128)(2,1)} %get-tuple-element.218), channel_id=1, source_target_pairs={{0,3},{1,4},{2,5},{3,6},{4,7},{5,8},{6,9},{7,10},{8,11},{9,12},{10... | collective-permute-start | bytes 442376 | tf_op jit(solution)/shard_map/ppermute | solution.py:35
  763.9 34.4 %collective-permute-start.12 = (bf16[2,64,576]{2,1,0:T(8,128)(2,1)S(1)}, bf16[2,64,576]{2,1,0:T(8,128)(2,1)S(1)}, u32[]{:S(2)}, u32[]{:S(2)}) collective-permute-start(bf16[2,64,576]{2,1,0:T(8,128)(2,1)S(1)} %copy-done.180), channel_id=1, source_target_pairs={{3,0},{4,1},{5,2},{6,3},{7,4},{8,5},{9,6},{10,7},{11,8},{12,9},{13... | collective-permute-start | bytes 442376 | tf_op jit(solution)/shard_map/ppermute | solution.py:35
  1048.3 28.5 %all-to-all-start.5 = ((bf16[4,8,64,512]{3,2,1,0:T(8,128)(2,1)}), bf16[4,8,64,512]{3,2,1,0:T(8,128)(2,1)}, u32[]{:S(2)}, u32[]{:S(2)}) async-start(bf16[4,8,64,512]{3,2,1,0:T(8,128)(2,1)} %bitcast.2170), calls=%async_computation.5 | async-start | bytes 4194304 | tf_op jit(solution)/shard_map/all_to_all | solution.py:24
  1080.5 14.4 all-to-all-start.8
  1112.0 12.8 all-to-all-start.10
  1119.3 172.4 %reduce-scatter.9.cloned.1.call-start = ((), (), s32[]{:S(2)}) async-start(), calls=%async_computation.22 | async-start | bytes 540672 | tf_op jit(solution)/shard_map/reduce_scatter | solution.py:454
  1153.9 16.1 all-to-all-start.12
  1164.5 128.6 %reduce-scatter.13.cloned.1.call-start = ((), (), s32[]{:S(2)}) async-start(), calls=%async_computation.24 | async-start | bytes 540672
  1175.3 180.5 %reduce-scatter.7.cloned.1.call-start = ((), (), s32[]{:S(2)}) async-start(), calls=%async_computation.21 | async-start | bytes 1216512 | tf_op jit(solution)/shard_map/reduce_scatter | solution.py:451
  1180.5 284.2 %all-reduce.88.cloned.1.call-start = ((), (), s32[]{:S(2)}) async-start(), calls=%async_computation.25 | async-start | bytes 2621440
  1243.6 424.1 %reduce-scatter.11.cloned.1.call-start = ((), (), s32[]{:S(2)}) async-start(), calls=%async_computation.23 | async-start | bytes 45416448 | tf_op jit(solution)/shard_map/reduce_scatter | solution.py:63
  1283.7 73.5 %all-to-all-start.13 = ((bf16[4,8,64,512]{3,2,1,0:T(8,128)(2,1)}), bf16[4,8,64,512]{3,2,1,0:T(8,128)(2,1)}, u32[]{:S(2)}, u32[]{:S(2)}) async-start(bf16[4,8,64,512]{3,2,1,0:T(8,128)(2,1)} %bitcast.2154), calls=%async_computation.13 | async-start | bytes 4194304 | tf_op jit(solution)/shard_map/all_to_all | solution.py:24
  (266 other events, 5926.1 us)
Sparse Core Ops, SparseCore 0:
  9.7 33.1 all-gather.3
  137.6 47.1 all-gather.5
  761.0 49.5 all-gather.7
  1123.2 73.5 reduce-scatter.8
  1200.7 76.3 reduce-scatter.12
  1280.5 75.2 reduce-scatter.6
  1359.1 105.6 all-reduce.87
  1468.8 198.7 reduce-scatter.10
where the time goes:
time: 1700 us; the launch traced here: 1680 us
  matrix products  655 us (39%)
  waiting for transfers between devices  553 us (33%)
  local copies, waits for them, and re-layouts  170 us (10%)
  starting transfers between devices  153 us (9%)
  other arithmetic  106 us (6%)
  blocking collectives  23.2 us (1%)
  between operations  19.3 us (1%)
    dot_general x90, matrix products, dilated_transpose(): jnp.einsum(form, window, kernel[tap_index], preferred_element_type=jnp.fl...  372 us
    reduce_scatter x1, waiting for transfers between devices, sent_together(): lax.psum_scatter(both, axis, scatter_dimension=dim, tiled=True)  201 us
    dot_general x90, matrix products, dilated_apply(): jnp.einsum(form, window, kernel[tap_index], preferred_element_type=jnp.fl...  162 us
    unnamed x10, waiting for transfers between devices  104 us
    dot_general x90, matrix products, dilated_weight_grad(): jnp.einsum('rwc,rwd->cd', window, masked, preferred_element_type=jnp.floa...  87.9 us
    all_to_all x8, waiting for transfers between devices, sent_to_all(): return lax.all_to_all(copies, axis, split_axis=0, concat_axis=0, tiled=True)  76.8 us
    all_to_all x6, waiting for transfers between devices, sum_at_owner(): tiles = lax.all_to_all(cut_along(x, dim, count), axis, 0, 0, tiled=True)  74.6 us
    all_to_all x8, starting transfers between devices, sent_to_all(): return lax.all_to_all(copies, axis, split_axis=0, concat_axis=0, tiled=True)  65.3 us
  transfers between devices with their start and end apart: 38, of which 19 were waited for; matrix products, arithmetic and copies ran while one was open for 44% of the time, Pallas kernels for 0%

commit v1 on v0

--- a/solution.py
+++ b/solution.py
@@ -1,16 +1,665 @@
+import functools
+
 import jax
 import jax.numpy as jnp
 from jax import lax
+from jax.experimental import pallas as pl
+from jax.experimental.pallas import tpu as pltpu
 from jax.sharding import PartitionSpec as P
 
 TASKS = 3
 TILE_W = 64
-
-
+NROWS = 256
+PIX = 32
+CHAN = 4
+OWN_ROWS = NROWS // PIX
+REACH = 3
+EXT_ROWS = OWN_ROWS + 2 * REACH
+HEAD = 64
+BRANCH = TASKS * HEAD
+TILES = 7
+BRANCH_ORDER = (1, 2, 3, 0, 4)
+BRANCH_PLACE = (3, 0, 1, 2, 4)
+
+F32 = jnp.float32
+BF16 = jnp.bfloat16
+MESH = pl.DeviceIdType.MESH
 eps = 1e-05
 section_rate = 4
 head_rates = (6, 12, 18)
 tap_offsets = tuple(((row_step, col_step) for row_step in (-1, 0, 1) for col_step in (-1, 0, 1)))
+VMEM_LIMIT = 60 * 2**20
+
+
+def place_of_row(row):
+    kind = row % 6
+    return 43 * kind - kind // 5 + row // 6
+
+
+def row_at_place(place):
+    kind = (place + place // 214) // 43
+    return 6 * (place - 43 * kind + kind // 5) + kind
+
+
+PLACED_ROWS = tuple(row_at_place(place) for place in range(NROWS))
+
+
+def int_div(a, b):
+    return lax.div(a, jnp.int32(b))
+
+
+def int_rem(a, b):
+    return lax.rem(a, jnp.int32(b))
+
+
+def place_of(row):
+    kind = int_rem(row, 6)
+    return 43 * kind - int_div(kind, 5) + int_div(row, 6)
+
+
+def row_of(place):
+    kind = int_div(place + int_div(place, 214), 43)
+    return 6 * (place - 43 * kind + int_div(kind, 5)) + kind
+
+
+def signal(sem, **where):
+    pl.semaphore_signal(sem, inc=1, device_id=where, device_id_type=MESH)
+
+
+def remote(src, dst, send_sem, recv_sem, **where):
+    return pltpu.make_async_remote_copy(
+        src_ref=src,
+        dst_ref=dst,
+        send_sem=send_sem,
+        recv_sem=recv_sem,
+        device_id=where,
+        device_id_type=MESH,
+    )
+
+
+def gather_rows_kernel(
+    reach, src, out, ss_row, rs_row, ss_side, rs_side, ss_far, rs_far, ss_halo, rs_halo
+):
+    i, j = lax.axis_index("pix"), lax.axis_index("chan")
+    right, left = int_rem(j + 1, CHAN), int_rem(j + CHAN - 1, CHAN)
+    far = int_rem(j + 2, CHAN)
+    after, before = int_rem(i + 1, PIX), int_rem(i + PIX - 1, PIX)
+    barrier = pltpu.get_barrier_semaphore()
+    expected = 2 + (2 if reach else 0)
+    for s in range(OWN_ROWS):
+        origin = int_div(row_of(OWN_ROWS * i + s), OWN_ROWS)
+
+        @pl.when(origin != i)
+        def _():
+            signal(barrier, pix=origin)
+
+        target = int_div(place_of(OWN_ROWS * i + s), OWN_ROWS)
+        expected = expected + (target != i).astype(jnp.int32)
+    signal(barrier, chan=right)
+    signal(barrier, chan=left)
+    if reach:
+        signal(barrier, pix=after)
+        signal(barrier, pix=before)
+    pl.semaphore_wait(barrier, expected)
+
+    def row_send(s):
+        place = place_of(OWN_ROWS * i + s)
+        target, slot = int_div(place, OWN_ROWS), int_rem(place, OWN_ROWS)
+        landing = out.at[j, reach + slot]
+        return target, (
+            lambda: remote(src.at[s], landing, ss_row.at[s], rs_row.at[slot], pix=target),
+            lambda: pltpu.make_async_copy(src.at[s], landing, rs_row.at[slot]),
+        )
+
+    for s in range(OWN_ROWS):
+        target, (away, here) = row_send(s)
+        pl.when(target != i)(lambda: away().start())
+        pl.when(target == i)(lambda: here().start())
+
+    def block(chan, s):
+        return out.at[chan, reach + s]
+
+    def side_send(way, s):
+        return remote(
+            block(j, s),
+            block(j, s),
+            ss_side.at[way, s],
+            rs_side.at[way, s],
+            chan=(right, left)[way],
+        )
+
+    def side_arrival(way, s):
+        chan = (left, right)[way]
+        return remote(
+            block(chan, s), block(chan, s), ss_side.at[way, s], rs_side.at[way, s], chan=chan
+        )
+
+    def far_send(s):
+        way = 0 if s < OWN_ROWS // 2 else 1
+        chan = (left, right)[way]
+        return remote(
+            block(chan, s), block(chan, s), ss_far.at[s], rs_far.at[s], chan=(right, left)[way]
+        )
+
+    def far_arrival(s):
+        return remote(block(far, s), block(far, s), ss_far.at[s], rs_far.at[s], chan=left)
+
+    def halo_send(turn, chan, s):
+        if s < reach:
+            return remote(
+                block(chan, s),
+                out.at[chan, reach + OWN_ROWS + s],
+                ss_halo.at[turn, s],
+                rs_halo.at[chan, s],
+                pix=before,
+            )
+        lane = s - OWN_ROWS + 2 * reach
+        return remote(
+            block(chan, s),
+            out.at[chan, s - OWN_ROWS + reach],
+            ss_halo.at[turn, lane],
+            rs_halo.at[chan, lane],
+            pix=after,
+        )
+
+    def halo_arrival(chan, lane):
+        slot = reach + OWN_ROWS + lane if lane < reach else lane - reach
+        return remote(
+            out.at[chan, slot],
+            out.at[chan, slot],
+            ss_halo.at[0, lane],
+            rs_halo.at[chan, lane],
+            pix=after,
+        )
+
+    order = (0, 7, 1, 6, 2, 5, 3, 4)
+    edge = [s for s in order if s < reach or s >= OWN_ROWS - reach]
+    for s in order:
+        pltpu.make_async_copy(src.at[s], block(j, s), rs_row.at[s]).wait()
+        side_send(0, s).start()
+        side_send(1, s).start()
+        if s in edge:
+            halo_send(0, j, s).start()
+    for s in order:
+        for way in range(2):
+            side_arrival(way, s).wait_recv()
+            if way == (0 if s < OWN_ROWS // 2 else 1):
+                far_send(s).start()
+            if s in edge:
+                halo_send(1 + way, (left, right)[way], s).start()
+    for s in order:
+        far_arrival(s).wait_recv()
+        if s in edge:
+            halo_send(3, far, s).start()
+    if reach:
+        for chan in range(CHAN):
+            for lane in range(2 * reach):
+                halo_arrival(chan, lane).wait_recv()
+    for s in range(OWN_ROWS):
+        target, (away, here) = row_send(s)
+        pl.when(target != i)(lambda: away().wait_send())
+        side_send(0, s).wait_send()
+        side_send(1, s).wait_send()
+        far_send(s).wait_send()
+    for turn, chan in enumerate((j, left, right, far)):
+        for s in edge:
+            halo_send(turn, chan, s).wait_send()
+
+
+def gather_rows(rows, reach, collective_id, name):
+    width = rows.shape[2]
+    dma = pltpu.SemaphoreType.DMA
+    return pl.pallas_call(
+        functools.partial(gather_rows_kernel, reach),
+        out_shape=jax.ShapeDtypeStruct((CHAN, OWN_ROWS + 2 * reach, TILE_W, width), rows.dtype),
+        in_specs=[pl.BlockSpec(memory_space=pl.ANY)],
+        out_specs=pl.BlockSpec(memory_space=pl.ANY),
+        scratch_shapes=[
+            dma((OWN_ROWS,)),
+            dma((OWN_ROWS,)),
+            dma((2, OWN_ROWS)),
+            dma((2, OWN_ROWS)),
+            dma((OWN_ROWS,)),
+            dma((OWN_ROWS,)),
+            dma((CHAN, max(2 * reach, 1))),
+            dma((CHAN, max(2 * reach, 1))),
+        ],
+        compiler_params=pltpu.CompilerParams(collective_id=collective_id, has_side_effects=True),
+        cost_estimate=pl.CostEstimate(flops=0, bytes_accessed=60_000_000, transcendentals=0),
+        name=name,
+    )(rows)
+
+
+def return_rows_kernel(src, out, own, arrived, total, ls, ss_side, rs_side, ss_row, rs_row):
+    i, j = lax.axis_index("pix"), lax.axis_index("chan")
+    barrier = pltpu.get_barrier_semaphore()
+    expected = 3
+    for s in range(OWN_ROWS):
+        origin = int_div(place_of(OWN_ROWS * i + s), OWN_ROWS)
+
+        @pl.when(origin != i)
+        def _():
+            signal(barrier, pix=origin)
+
+        target = int_div(row_of(OWN_ROWS * i + s), OWN_ROWS)
+        expected = expected + (target != i).astype(jnp.int32)
+    for distance in (1, 2, 3):
+        signal(barrier, chan=int_rem(j + distance, CHAN))
+    pl.semaphore_wait(barrier, expected)
+
+    def side_send(distance, s):
+        chan = int_rem(j + distance, CHAN)
+        return remote(
+            src.at[chan, s],
+            arrived.at[distance - 1, s],
+            ss_side.at[distance - 1, s],
+            rs_side.at[distance - 1, s],
+            chan=chan,
+        )
+
+    for s in range(OWN_ROWS):
+        for distance in (2, 1, 3):
+            side_send(distance, s).start()
+    load = pltpu.make_async_copy(src.at[j], own, ls)
+    load.start()
+    load.wait()
+
+    def row_send(s):
+        row = row_of(OWN_ROWS * i + s)
+        target, slot = int_div(row, OWN_ROWS), int_rem(row, OWN_ROWS)
+        return target, (
+            lambda: remote(total.at[s], out.at[slot], ss_row.at[s], rs_row.at[slot], pix=target),
+            lambda: pltpu.make_async_copy(total.at[s], out.at[slot], rs_row.at[slot]),
+        )
+
+    for s in range(OWN_ROWS):
+        held = own[s].astype(F32)
+        for distance in (1, 3, 2):
+            side_send(distance, s).wait_recv()
+            held = held + arrived[distance - 1, s].astype(F32)
+        total[s] = held.astype(BF16)
+        target, (away, here) = row_send(s)
+        pl.when(target != i)(lambda: away().start())
+        pl.when(target == i)(lambda: here().start())
+    for s in range(OWN_ROWS):
+        pltpu.make_async_copy(total.at[s], out.at[s], rs_row.at[s]).wait()
+        target, (away, here) = row_send(s)
+        pl.when(target != i)(lambda: away().wait_send())
+        for distance in (1, 2, 3):
+            side_send(distance, s).wait_send()
+
+
+def return_rows(parts, collective_id, name):
+    width = parts.shape[3]
+    dma = pltpu.SemaphoreType.DMA
+    rows = (OWN_ROWS, TILE_W, width)
+    return pl.pallas_call(
+        return_rows_kernel,
+        out_shape=jax.ShapeDtypeStruct(rows, BF16),
+        in_specs=[pl.BlockSpec(memory_space=pl.ANY)],
+        out_specs=pl.BlockSpec(memory_space=pl.ANY),
+        scratch_shapes=[
+            pltpu.VMEM(rows, BF16),
+            pltpu.VMEM((CHAN - 1, *rows), BF16),
+            pltpu.VMEM(rows, BF16),
+            dma,
+            dma((CHAN - 1, OWN_ROWS)),
+            dma((CHAN - 1, OWN_ROWS)),
+            dma((OWN_ROWS,)),
+            dma((OWN_ROWS,)),
+        ],
+        compiler_params=pltpu.CompilerParams(collective_id=collective_id, has_side_effects=True),
+        cost_estimate=pl.CostEstimate(flops=0, bytes_accessed=60_000_000, transcendentals=0),
+        name=name,
+    )(parts)
+
+
+def dot_nt(a, b):
+    return lax.dot_general(a, b, (((1,), (1,)), ((), ())), preferred_element_type=F32)
+
+
+def dot_tn(a, b):
+    return lax.dot_general(a, b, (((0,), (0,)), ((), ())), preferred_element_type=F32)
+
+
+def dot_nn(a, b):
+    return jnp.dot(a, b, preferred_element_type=F32)
+
+
+def slope(v):
+    s = jax.nn.sigmoid(v)
+    return s * (1.0 + v * (1.0 - s))
+
+
+def silu(v):
+    return v * jax.nn.sigmoid(v)
+
+
+def heads_forward_kernel(
+    keep, x_hbm, kernel, point, spread, maps, pooled, grad_pre, head_part, grad_project, pool_rows,
+    x, acc, pre, sems,
+):
+    step = pl.program_id(0)
+    rate, row_tap = step // 3, step % 3
+    first = REACH + (row_tap - 1) * (rate + 1)
+
+    @pl.when(step == 0)
+    def _():
+        width = x_hbm.shape[3]
+        copies = [
+            pltpu.make_async_copy(
+                x_hbm.at[chan], x.at[:, :, width * chan : width * (chan + 1)], sems.at[chan]
+            )
+            for chan in range(CHAN)
+        ]
+        for copy in copies:
+            copy.start()
+        for copy in copies:
+            copy.wait()
+
+    def rows_from(start):
+        return x[pl.ds(start, OWN_ROWS)].reshape(OWN_ROWS * TILE_W, -1)
+
+    window = rows_from(first)
+    for b in range(3):
+        product = dot_nt(window, kernel[:, 0, 0, b].reshape(BRANCH, -1))
+        for r in range(OWN_ROWS):
+            part = slice(TILE_W * r, TILE_W * (r + 1))
+            term = jnp.where(keep[step, r] > 0, product[part], 0.0)
+            acc[b, part] = jnp.where(row_tap > 0, acc[b, part], 0.0) + term
+
+    for which, dilation in enumerate(head_rates):
+
+        @pl.when(step == 3 * which + 2)
+        def _():
+            col = lax.broadcasted_iota(jnp.int32, (OWN_ROWS * TILE_W, BRANCH), 0) % TILE_W
+            total = acc[1]
+            behind = pltpu.roll(acc[0], dilation, 0)
+            ahead = pltpu.roll(acc[2], OWN_ROWS * TILE_W - dilation, 0)
+            total = total + jnp.where(col >= dilation, behind, 0.0)
+            pre[which] = total + jnp.where(col < TILE_W - dilation, ahead, 0.0)
+
+    @pl.when(step == 0)
+    def _():
+        pre[3] = dot_nt(rows_from(REACH), point[...].reshape(BRANCH, -1))
+
+    @pl.when(step == 8)
+    def _():
+        cot = maps[...]
+        head = None
+        for which in range(5):
+            if which < 4:
+                before = pre[which]
+                logistic = jax.nn.sigmoid(before)
+                joined = (before * logistic).astype(BF16)
+            else:
+                joined = pooled[...]
+            weight = spread[which]
+            term = dot_nn(joined, weight)
+            head = term if head is None else head + term
+            grads = dot_tn(joined, cot)
+            for t in range(TASKS):
+                grad_project[which, t] = grads[
+                    HEAD * t : HEAD * (t + 1), 256 * t : 256 * (t + 1)
+                ].astype(BF16)
+            back = dot_nt(cot, weight)
+            if which < 4:
+                grad = back * (logistic * (1.0 + before * (1.0 - logistic)))
+                grad_pre[:, BRANCH * which : BRANCH * (which + 1)] = grad.astype(BF16)
+            else:
+                pool_rows[...] = jnp.sum(back.reshape(OWN_ROWS, TILE_W, BRANCH), axis=1)
+        head_part[...] = head.astype(BF16)
+
+
+def heads_forward(keep, x_ext, kernels, point, spread, maps, pooled):
+    pixels = OWN_ROWS * TILE_W
+    feat = point.shape[2]
+    whole = pl.BlockSpec(memory_space=pltpu.VMEM)
+    return pl.pallas_call(
+        heads_forward_kernel,
+        grid=(9,),
+        in_specs=[
+            pl.BlockSpec(memory_space=pltpu.SMEM),
+            pl.BlockSpec(memory_space=pl.ANY),
+            pl.BlockSpec((TASKS, 1, 1, 3, HEAD, feat), lambda s: (0, s // 3, s % 3, 0, 0, 0)),
+            whole,
+            whole,
+            whole,
+            whole,
+        ],
+        out_specs=[whole] * 4,
+        out_shape=[
+            jax.ShapeDtypeStruct((pixels, 4 * BRANCH), BF16),
+            jax.ShapeDtypeStruct((pixels, 256 * TASKS), BF16),
+            jax.ShapeDtypeStruct((5, TASKS, HEAD, 256), BF16),
+            jax.ShapeDtypeStruct((OWN_ROWS, BRANCH), F32),
+        ],
+        scratch_shapes=[
+            pltpu.VMEM((EXT_ROWS, TILE_W, feat), BF16),
+            pltpu.VMEM((3, pixels, BRANCH), F32),
+            pltpu.VMEM((4, pixels, BRANCH), F32),
+            pltpu.SemaphoreType.DMA((CHAN,)),
+        ],
+        compiler_params=pltpu.CompilerParams(vmem_limit_bytes=VMEM_LIMIT),
+        cost_estimate=pl.CostEstimate(
+            flops=12_000_000_000, bytes_accessed=28_000_000, transcendentals=0
+        ),
+        name="heads_forward",
+    )(keep, x_ext, kernels, point, spread, maps, pooled)
+
+
+PAD = 24
+PADDED = PAD + TILE_W + PAD
+
+
+def heads_input_grad_kernel(keep, mid, low, high, kernel, point, out, wide, taps, acc):
+    n, rate = pl.program_id(0), pl.program_id(1)
+
+    @pl.when((n == 0) & (rate == 0))
+    def _():
+        wide[...] = jnp.zeros_like(wide)
+        for start, part in ((0, low), (REACH, mid), (REACH + OWN_ROWS, high)):
+            held = part[...].astype(F32)
+            for which in range(3):
+                for t in range(TASKS):
+                    lane = BRANCH * which + HEAD * t
+                    one = held[:, :, lane : lane + HEAD]
+                    wide[3 * t + which, start : start + held.shape[0], PAD : PAD + TILE_W] = (
+                        jnp.concatenate([one, one], axis=2)
+                    )
+
+        def one_row(r, carry):
+            is_low = lax.broadcasted_iota(jnp.int32, (TILE_W, 2 * HEAD), 1) < HEAD
+            out_rows = pl.ds(pl.multiple_of(r * TILE_W, TILE_W), TILE_W)
+            for which, dilation in enumerate(head_rates):
+
+                def shifted(tap):
+                    t, a, b = tap // 9, tap // 3 % 3 - 1, tap % 3 - 1
+                    piece = wide[
+                        3 * t + which,
+                        r + REACH - a * (which + 1),
+                        PAD - b * dilation : PAD - b * dilation + TILE_W,
+                    ]
+                    return jnp.where(keep[3 * which + 1 - a, r] > 0, piece, 0.0)
+
+                for pair in range(14):
+                    first = shifted(2 * pair)
+                    second = shifted(2 * pair + 1) if pair < 13 else jnp.zeros_like(first)
+                    taps[which, out_rows, 2 * HEAD * pair : 2 * HEAD * (pair + 1)] = jnp.where(
+                        is_low, first, second
+                    ).astype(BF16)
+            return carry
+
+        lax.fori_loop(0, OWN_ROWS, one_row, 0)
+
+    product = dot_nn(taps[rate, :, : 27 * HEAD], kernel[...].reshape(27 * HEAD, -1))
+
+    @pl.when(rate == 0)
+    def _():
+        grads = mid[...].reshape(OWN_ROWS * TILE_W, -1)[:, 3 * BRANCH :]
+        acc[...] = product + dot_nn(grads, point[...].reshape(BRANCH, -1))
+
+    @pl.when(rate == 1)
+    def _():
+        acc[...] += product
+
+    @pl.when(rate == 2)
+    def _():
+        total = acc[...] + product
+        for c in range(out.shape[0]):
+            out[c] = total[:, 512 * c : 512 * (c + 1)].astype(BF16)
+
+
+def heads_input_grad(keep, grad_mid, grad_low, grad_high, kernels, point):
+    pixels = OWN_ROWS * TILE_W
+    block = 1024
+    whole = pl.BlockSpec(memory_space=pltpu.VMEM)
+    return pl.pallas_call(
+        heads_input_grad_kernel,
+        grid=(2, 3),
+        in_specs=[
+            pl.BlockSpec(memory_space=pltpu.SMEM),
+            whole,
+            whole,
+            whole,
+            pl.BlockSpec((TASKS, 1, 3, 3, HEAD, block), lambda n, r: (0, r, 0, 0, 0, n)),
+            pl.BlockSpec((TASKS, HEAD, block), lambda n, r: (0, 0, n)),
+        ],
+        out_specs=pl.BlockSpec((block // 512, pixels, 512), lambda n, r: (n, 0, 0)),
+        out_shape=jax.ShapeDtypeStruct((CHAN, pixels, 512), BF16),
+        scratch_shapes=[
+            pltpu.VMEM((9, EXT_ROWS, PADDED, 2 * HEAD), F32),
+            pltpu.VMEM((3, pixels, 28 * HEAD), BF16),
+            pltpu.VMEM((pixels, block), F32),
+        ],
+        compiler_params=pltpu.CompilerParams(vmem_limit_bytes=VMEM_LIMIT),
+        cost_estimate=pl.CostEstimate(
+            flops=12_000_000_000, bytes_accessed=28_000_000, transcendentals=0
+        ),
+        name="heads_input_grad",
+    )(keep, grad_mid, grad_low, grad_high, kernels, point)
+
+
+GROUP = 8
+GROUP_ROWS = GROUP * OWN_ROWS
+
+
+def heads_weight_grad_kernel(keep, *refs):
+    x_parts, g_parts, (g_low, g_high) = refs[:8], refs[8:16], refs[16:18]
+    out, out_point, x_all, x_wide, x_now, g_all, g_now, sems = refs[18:]
+    step = pl.program_id(0)
+    device = lax.axis_index("pix")
+    spot, core = int_div(int_rem(device, GROUP), 2), int_rem(device, 2)
+
+    @pl.when(step == 0)
+    def _():
+        copies = []
+        rows = lambda z, c: pl.ds(OWN_ROWS * (2 * z + c), OWN_ROWS)
+        for m in range(4):
+            z = spot ^ m
+            for src, c in ((x_parts[m], core), (x_parts[4 + m], 1 - core)):
+                for chan in range(CHAN):
+                    copies.append((src.at[chan], x_all.at[chan, rows(z, c)]))
+            for src, c in ((g_parts[m], core), (g_parts[4 + m], 1 - core)):
+                copies.append((src, g_all.at[pl.ds(REACH + OWN_ROWS * (2 * z + c), OWN_ROWS)]))
+        copies.append((g_low, g_all.at[0:REACH]))
+        copies.append((g_high, g_all.at[REACH + GROUP_ROWS : 2 * REACH + GROUP_ROWS]))
+        started = [
+            pltpu.make_async_copy(src, dst, sems.at[n]) for n, (src, dst) in enumerate(copies)
+        ]
+        for copy in started:
+            copy.start()
+        x_wide[:, 0:PAD] = jnp.zeros((GROUP_ROWS, PAD, 256), F32)
+        x_wide[:, PAD + TILE_W :] = jnp.zeros((GROUP_ROWS, PAD, 256), F32)
+        for copy in started:
+            copy.wait()
+
+        def widen_row(r, carry):
+            is_low = lax.broadcasted_iota(jnp.int32, (TILE_W, 128), 1) < HEAD
+            for pair in range(2):
+                first = x_all[2 * pair, r].astype(F32)
+                second = x_all[2 * pair + 1, r].astype(F32)
+                lower = jnp.where(is_low, first, pltpu.roll(second, HEAD, 1))
+                upper = jnp.where(is_low, pltpu.roll(first, HEAD, 1), second)
+                x_wide[r, PAD : PAD + TILE_W, 128 * pair : 128 * (pair + 1)] = jnp.where(
+                    core == 0, lower, upper
+                )
+            return carry
+
+        lax.fori_loop(0, GROUP_ROWS, widen_row, 0)
+
+    for which in range(3):
+
+        @pl.when(step == 3 * which)
+        def _():
+            def pick(r, carry):
+                for a in range(3):
+                    piece = g_all[
+                        r + REACH - (a - 1) * (which + 1), :, BRANCH * which : BRANCH * (which + 1)
+                    ]
+                    g_now[a, pl.ds(pl.multiple_of(r * TILE_W, TILE_W), TILE_W)] = jnp.where(
+                        keep[3 * which + 2 - a, r] > 0, piece, jnp.zeros_like(piece)
+                    )
+                return carry
+
+            lax.fori_loop(0, GROUP_ROWS, pick, 0)
+
+    for which, dilation in enumerate(head_rates):
+        for b in range(3):
+
+            @pl.when(step == 3 * which + b)
+            def _():
+                start = PAD + (b - 1) * dilation
+
+                def move(r, carry):
+                    x_now[pl.ds(pl.multiple_of(r * TILE_W, TILE_W), TILE_W)] = x_wide[
+                        r, start : start + TILE_W
+                    ].astype(BF16)
+                    return carry
+
+                lax.fori_loop(0, GROUP_ROWS, move, 0)
+
+    for a in range(3):
+        product = dot_tn(x_now[...], g_now[a]).astype(BF16)
+        for c in range(CHAN):
+            out[c, 0, :, BRANCH * a : BRANCH * (a + 1)] = product[HEAD * c : HEAD * (c + 1)]
+
+    @pl.when(step == 1)
+    def _():
+        grads = g_all[REACH : REACH + GROUP_ROWS, :, 3 * BRANCH :].reshape(-1, BRANCH)
+        product = dot_tn(x_now[...], grads).astype(BF16)
+        for c in range(CHAN):
+            out_point[c] = product[HEAD * c : HEAD * (c + 1)]
+
+
+def heads_weight_grad(keep, x_parts, g_parts, g_low, g_high):
+    pixels = GROUP_ROWS * TILE_W
+    whole = pl.BlockSpec(memory_space=pltpu.VMEM)
+    smem = pl.BlockSpec(memory_space=pltpu.SMEM)
+    hbm = pl.BlockSpec(memory_space=pl.ANY)
+    return pl.pallas_call(
+        heads_weight_grad_kernel,
+        grid=(9,),
+        in_specs=[smem] + [hbm] * 18,
+        out_specs=[pl.BlockSpec((CHAN, 1, HEAD, 3 * BRANCH), lambda s: (0, s, 0, 0)), whole],
+        out_shape=[
+            jax.ShapeDtypeStruct((CHAN, 9, HEAD, 3 * BRANCH), BF16),
+            jax.ShapeDtypeStruct((CHAN, HEAD, BRANCH), BF16),
+        ],
+        scratch_shapes=[
+            pltpu.VMEM((CHAN, GROUP_ROWS, TILE_W, 128), BF16),
+            pltpu.VMEM((GROUP_ROWS, PADDED, 256), F32),
+            pltpu.VMEM((pixels, 256), BF16),
+            pltpu.VMEM((GROUP_ROWS + 2 * REACH, TILE_W, 4 * BRANCH), BF16),
+            pltpu.VMEM((3, pixels, BRANCH), BF16),
+            pltpu.SemaphoreType.DMA((42,)),
+        ],
+        compiler_params=pltpu.CompilerParams(vmem_limit_bytes=VMEM_LIMIT),
+        cost_estimate=pl.CostEstimate(
+            flops=12_000_000_000, bytes_accessed=28_000_000, transcendentals=0
+        ),
+        name="heads_weight_grad",
+    )(keep, *x_parts, *g_parts, g_low, g_high)
 
 
 def cut_along(x, dim, count):
@@ -56,15 +705,6 @@
 
 def of_everyone_2(x, axis):
     return sent_to_all(x, axis).astype(jnp.float32).sum(axis=0)
-
-
-def sent_together(arrays, axis, dim, along):
-    both = jnp.concatenate(arrays, axis=along)
-    result, at, finished = (lax.psum_scatter(both, axis, scatter_dimension=dim, tiled=True), 0, [])
-    for a in arrays:
-        finished.append(lax.slice_in_dim(result, at, at + a.shape[along], axis=along))
-        at += a.shape[along]
-    return tuple(finished)
 
 
 def widen(tensor):
@@ -204,7 +844,8 @@
     row_count = pixel_count // TILE_W
     pixel_total = pixel_count * lax.axis_size("pix")
     tile_count = tile_number.shape[0] // 40 + 1
-    margin = max(head_rates)
+    margin = section_rate
+    device = lax.axis_index("pix")
     first_row = lax.axis_index("pix") * row_count
     tile_pad = jnp.pad(tile_number, (margin, margin), constant_values=-1)
     own_tiles = lax.dynamic_slice_in_dim(tile_pad, first_row + margin, row_count)
@@ -244,145 +885,137 @@
     )
     summed = norm_expand + local_in.astype(jnp.float32)
     trunk_out = jax.nn.silu(summed).astype(jnp.bfloat16)
-    trunk_full = widen(trunk_out)
-    trunk_ext = extend_rows(trunk_full, margin, move_forward)
-    row_sums = jnp.sum(trunk_full, axis=1, dtype=jnp.float32)
+    group_x, group_z, core = device // GROUP, device % GROUP // 2, device % 2
+    placed = jnp.array(PLACED_ROWS, jnp.int32)
+    place_key = tile_number[placed] + 8 * (placed % 6)
+    key_pad = jnp.pad(place_key, (REACH, REACH), constant_values=-1)
+    keep_all = jnp.stack(
+        [
+            key_pad[REACH + a * k : REACH + a * k + NROWS] == place_key
+            for k in (1, 2, 3)
+            for a in (-1, 0, 1)
+        ]
+    ).astype(jnp.int32)
+    keep_own = lax.dynamic_slice_in_dim(keep_all, device * OWN_ROWS, OWN_ROWS, axis=1)
+    keep_group = lax.dynamic_slice_in_dim(keep_all, group_x * GROUP_ROWS, GROUP_ROWS, axis=1)
+    place_tiles = lax.dynamic_slice_in_dim(tile_number[placed], device * OWN_ROWS, OWN_ROWS)
+    place_onehot = (place_tiles[:, None] == jnp.arange(tile_count)[None, :]).astype(jnp.float32)
+    x_ext = gather_rows(trunk_out, REACH, 1, "gather_trunk")
+    row_sums = jnp.sum(trunk_out, axis=1, dtype=jnp.float32)
     tile_sums = of_everyone_2(
         jnp.dot(row_onehot.T, row_sums, precision=highest).astype(jnp.bfloat16), "pix"
-    ).astype(jnp.float32)
-    tile_mean = (tile_sums / tile_sizes[:, None]).astype(jnp.bfloat16)
-    head_seams = [
-        seam_masks(tile_pad, first_row, margin, dilation, row_count) for dilation in head_rates
-    ]
-    pre_point = []
-    pre_atrous = []
-    pre_pooled = []
-    branches = []
-    for task_index in range(TASKS):
-        point_pre = jnp.einsum(
-            "rwc,dc->rwd", trunk_full, point_weight[task_index], preferred_element_type=jnp.float32
-        )
-        pre_point.append(point_pre)
-        branches.append(jax.nn.silu(point_pre).astype(jnp.bfloat16))
-        for rate_index in range(3):
-            atrous_pre = dilated_apply(
-                trunk_ext,
-                atrous_weight[task_index, rate_index],
-                head_rates[rate_index],
-                margin,
-                head_seams[rate_index],
-                row_count,
-                "rwc,dc->rwd",
-            )
-            pre_atrous.append(atrous_pre)
-            branches.append(jax.nn.silu(atrous_pre).astype(jnp.bfloat16))
-        pooled_pre = jnp.einsum(
-            "kc,dc->kd", tile_mean, pooled_weight[task_index], preferred_element_type=jnp.float32
-        )
-        pooled_act = jax.nn.silu(pooled_pre).astype(jnp.bfloat16)
-        pooled_rows = jnp.dot(
-            row_onehot.astype(jnp.bfloat16), pooled_act, preferred_element_type=jnp.float32
-        ).astype(jnp.bfloat16)
-        pre_pooled.append(pooled_pre)
-        branches.append(jnp.broadcast_to(pooled_rows[:, None, :], point_pre.shape))
-    joined_local = jnp.stack(branches, axis=2).reshape(pixel_count, 5 * TASKS, -1)
-    joined_heads = widen(joined_local).reshape(pixel_count, TASKS, 5, -1)
-    project_parts = project_weight.reshape(TASKS, project_weight.shape[1], 5, -1)
-    task_maps = jnp.einsum(
-        "ptbc,tdbc->tpd", joined_heads, project_parts, preferred_element_type=jnp.float32
+    )
+    tile_mean = lax.all_gather(
+        (tile_sums / tile_sizes[:, None]).astype(jnp.bfloat16), "chan", axis=1, tiled=True
+    )
+    pre_pooled = jnp.einsum("kc,tdc->ktd", tile_mean, pooled_weight, preferred_element_type=F32)
+    pooled_act = jax.nn.silu(pre_pooled).astype(jnp.bfloat16).reshape(tile_count, BRANCH)
+    pooled_rows = jnp.dot(
+        place_onehot.astype(jnp.bfloat16), pooled_act, preferred_element_type=F32
     ).astype(jnp.bfloat16)
+    pooled_pixels = jnp.broadcast_to(
+        pooled_rows[:, None, :], (OWN_ROWS, TILE_W, BRANCH)
+    ).reshape(pixel_count, BRANCH)
     task_weight = jax.nn.softmax(task_draws.astype(jnp.float32) / 3.0)
     grad_maps = (task_weight[:, None, None] * cotangent.astype(jnp.float32)).astype(jnp.bfloat16)
-    grad_project = jnp.einsum(
-        "ptbc,tpd->tbcd", joined_heads, grad_maps, preferred_element_type=jnp.float32
-    ).reshape(TASKS, -1, grad_maps.shape[2])
-    joined_part = jnp.einsum(
-        "tpd,tdbc->ptbc", grad_maps, project_parts, preferred_element_type=jnp.float32
-    ).reshape(pixel_count, 5 * TASKS, -1)
-    (grad_joined,) = collect((joined_part,))
-    grad_joined = grad_joined.reshape(row_count, TILE_W, TASKS, 5, -1)
-    grad_point_pre = []
-    grad_atrous_pre = []
-    pooled_terms = []
-    for task_index in range(TASKS):
-        grad_point_pre.append(
-            (grad_joined[:, :, task_index, 0] * silu_slope(pre_point[task_index])).astype(
-                jnp.bfloat16
-            )
-        )
-        for rate_index in range(3):
-            grad_atrous_pre.append(
-                (
-                    grad_joined[:, :, task_index, 1 + rate_index]
-                    * silu_slope(pre_atrous[task_index * 3 + rate_index])
-                ).astype(jnp.bfloat16)
-            )
-        pooled_terms.append(
-            jnp.dot(
-                row_onehot.T, jnp.sum(grad_joined[:, :, task_index, 4], axis=1), precision=highest
-            )
-        )
-    pooled_total = of_everyone(jnp.stack(pooled_terms, axis=1), "pix")
-    atrous_ext = extend_rows(jnp.concatenate(grad_atrous_pre, axis=2), margin, move_backward)
-    head_width = point_weight.shape[1]
-    trunk_part = None
-    mean_part = None
-    point_grads = []
-    atrous_grads = []
-    pooled_grads = []
-    for task_index in range(TASKS):
-        grad_pooled_pre = (pooled_total[:, task_index] * silu_slope(pre_pooled[task_index])).astype(
-            jnp.bfloat16
-        )
-        trunk_term = jnp.einsum(
-            "rwd,dc->rwc",
-            grad_point_pre[task_index],
-            point_weight[task_index],
-            preferred_element_type=jnp.float32,
-        )
-        rate_grads = []
-        for rate_index in range(3):
-            branch_index = task_index * 3 + rate_index
-            dilation = head_rates[rate_index]
-            head_ext = atrous_ext[:, :, branch_index * head_width : (branch_index + 1) * head_width]
-            trunk_term = trunk_term + dilated_transpose(
-                head_ext,
-                atrous_weight[task_index, rate_index],
-                dilation,
-                margin,
-                head_seams[rate_index],
-                row_count,
-                "rwd,dc->rwc",
-            )
-            rate_grads.append(
-                dilated_weight_grad(
-                    trunk_ext,
-                    grad_atrous_pre[branch_index],
-                    dilation,
-                    margin,
-                    head_seams[rate_index],
-                    row_count,
-                )
-            )
-        mean_term = jnp.dot(
-            grad_pooled_pre, pooled_weight[task_index], preferred_element_type=jnp.float32
-        )
-        trunk_part = trunk_term if trunk_part is None else trunk_part + trunk_term
-        mean_part = mean_term if mean_part is None else mean_part + mean_term
-        point_grads.append(
-            jnp.einsum(
-                "rwc,rwd->cd",
-                trunk_full,
-                grad_point_pre[task_index],
-                preferred_element_type=jnp.float32,
-            )
-        )
-        atrous_grads.append(jnp.stack(rate_grads))
-        pooled_grads.append(
-            jnp.dot(tile_mean.T, grad_pooled_pre, preferred_element_type=jnp.float32)
-        )
-    trunk_grad, mean_grad = collect((trunk_part, mean_part.reshape(tile_count, 1, -1)))
+    maps_own = jnp.moveaxis(grad_maps, 0, 1).reshape(OWN_ROWS, TILE_W, BRANCH)
+    maps_all = gather_rows(maps_own, 0, 2, "gather_maps")
+    maps_all = jnp.moveaxis(
+        maps_all.reshape(CHAN, pixel_count, TASKS, HEAD), 0, 2
+    ).reshape(pixel_count, 256 * TASKS)
+    project_cut = jnp.moveaxis(project_weight.reshape(TASKS, HEAD, 5, CHAN, HEAD), 3, 0)
+    project_own = lax.all_to_all(project_cut, "chan", 0, 0, tiled=True)
+    project_own = jnp.transpose(project_own, (3, 1, 4, 0, 2)).reshape(5, TASKS, HEAD, 256)
+    project_own = project_own[jnp.array(BRANCH_ORDER)]
+    spread = (
+        project_own[:, :, :, None, :] * jnp.eye(TASKS, dtype=jnp.bfloat16)[None, :, None, :, None]
+    ).reshape(5, BRANCH, 256 * TASKS)
+    grad_pre, head_part, grad_project, pool_rows = heads_forward(
+        keep_own, x_ext, atrous_weight.reshape(TASKS, 3, 3, 3, HEAD, -1), point_weight, spread,
+        maps_all, pooled_pixels,
+    )
+    g_own = grad_pre.reshape(OWN_ROWS, TILE_W, 4 * BRANCH)
+    ring = range(PIX)
+    g_low = lax.ppermute(g_own[OWN_ROWS - REACH :], "pix", [(p, (p + 1) % PIX) for p in ring])
+    g_high = lax.ppermute(g_own[:REACH], "pix", [(p, (p - 1) % PIX) for p in ring])
+    mate_route = [(p, p ^ 1) for p in ring]
+    x_parts, g_parts = [], []
+    for m in range(4):
+        block = lax.dynamic_slice(
+            x_ext, (0, REACH, 0, 128 * (group_z ^ m)), (CHAN, OWN_ROWS, TILE_W, 128)
+        )
+        route = [(p, p ^ (2 * m)) for p in ring]
+        x_parts.append(lax.ppermute(block, "pix", route) if m else block)
+        g_parts.append(lax.ppermute(g_own, "pix", route) if m else g_own)
+    x_parts = x_parts + [lax.ppermute(part, "pix", mate_route) for part in x_parts]
+    g_parts = g_parts + [lax.ppermute(part, "pix", mate_route) for part in g_parts]
+
+    def group_edge(spot, rows):
+        picked = g_parts[0][rows]
+        for m in range(4):
+            for other in range(2):
+                here = (group_z ^ m == spot // 2) & (core ^ other == spot % 2)
+                picked = jnp.where(here, g_parts[4 * other + m][rows], picked)
+        return picked
+
+    group_low = lax.ppermute(
+        group_edge(GROUP - 1, slice(OWN_ROWS - REACH, OWN_ROWS)),
+        "pix",
+        [(p, (p + GROUP) % PIX) for p in ring],
+    )
+    group_high = lax.ppermute(
+        group_edge(0, slice(0, REACH)), "pix", [(p, (p - GROUP) % PIX) for p in ring]
+    )
+    trunk_parts = heads_input_grad(
+        keep_own, g_own, g_low, g_high, atrous_weight.reshape(TASKS, 3, 3, 3, HEAD, -1), point_weight
+    )
+    trunk_grad = return_rows(
+        trunk_parts.reshape(CHAN, OWN_ROWS, TILE_W, -1), 3, "return_trunk"
+    ).astype(jnp.float32)
+    maps_parts = jnp.moveaxis(
+        head_part.reshape(OWN_ROWS, TILE_W, TASKS, CHAN, HEAD), 3, 0
+    ).reshape(CHAN, OWN_ROWS, TILE_W, BRANCH)
+    task_maps = jnp.moveaxis(
+        return_rows(maps_parts, 4, "return_maps").reshape(pixel_count, TASKS, HEAD), 1, 0
+    )
+    weight_parts, point_parts = heads_weight_grad(keep_group, x_parts, g_parts, group_low, group_high)
+
+    def sum_over_groups(parts):
+        total = lax.dynamic_index_in_dim(parts, group_x, 0, False).astype(jnp.float32)
+        for step in range(1, 4):
+            sent = lax.dynamic_index_in_dim(parts, (group_x + step) % 4, 0, False)
+            route = [(p, (p + GROUP * step) % PIX) for p in ring]
+            total = total + lax.ppermute(sent, "pix", route).astype(jnp.float32)
+        return total
+
+    grad_atrous_weight = jnp.transpose(
+        sum_over_groups(weight_parts).reshape(3, 3, HEAD, 3, TASKS, HEAD), (4, 0, 3, 1, 2, 5)
+    ).reshape(TASKS, 3, 9, HEAD, HEAD)
+    grad_point_weight = jnp.transpose(
+        sum_over_groups(point_parts).reshape(HEAD, TASKS, HEAD), (1, 0, 2)
+    )
+    pooled_total = of_everyone(jnp.dot(place_onehot.T, pool_rows, precision=highest), "pix")
+    grad_pooled_pre = (
+        pooled_total.reshape(tile_count, TASKS, HEAD) * silu_slope(pre_pooled)
+    ).astype(jnp.bfloat16)
+    grad_pooled_weight = jnp.einsum(
+        "kc,ktd->tcd", tile_mean, grad_pooled_pre, preferred_element_type=jnp.float32
+    )
+    mean_part = jnp.einsum(
+        "ktd,tdc->kc", grad_pooled_pre, pooled_weight, preferred_element_type=jnp.float32
+    )
+    (mean_grad,) = collect((mean_part.reshape(tile_count, 1, -1),))
     mean_rows = jnp.dot(row_onehot, mean_grad[:, 0] / tile_sizes[:, None], precision=highest)
+    project_sides = lax.all_to_all(
+        jnp.moveaxis(
+            grad_project[jnp.array(BRANCH_PLACE)].reshape(5, TASKS, HEAD, CHAN, HEAD), 3, 0
+        ),
+        "chan",
+        0,
+        0,
+        tiled=True,
+    )
+    grad_project = jnp.transpose(project_sides, (2, 1, 0, 3, 4)).reshape(TASKS, -1, HEAD)
     grad_trunk = trunk_grad + mean_rows[:, None, :]
     grad_summed = grad_trunk * silu_slope(summed)
     grad_expand_pre, grad_expand_gain, grad_expand_bias = norm_backward(
@@ -443,7 +1076,6 @@
         )
     )
     grad_pixels = (grad_input + grad_summed).astype(jnp.bfloat16).reshape(pixel_count, -1)
-    atrous_stack = jnp.stack(atrous_grads)
     summed_grads = (
         lax.psum_scatter(
             reduce_grad[None].astype(jnp.bfloat16), "pix", scatter_dimension=1, tiled=True
@@ -454,27 +1086,10 @@
         lax.psum_scatter(
             expand_grad[None].astype(jnp.bfloat16), "pix", scatter_dimension=1, tiled=True
         ).astype(jnp.float32),
-        *tuple(
-            (
-                part.astype(jnp.float32)
-                for part in sent_together(
-                    (
-                        jnp.stack(point_grads).astype(jnp.bfloat16),
-                        atrous_stack.reshape(
-                            -1, atrous_stack.shape[3], atrous_stack.shape[4]
-                        ).astype(jnp.bfloat16),
-                    ),
-                    "pix",
-                    1,
-                    0,
-                )
-            )
-        ),
         lax.psum_scatter(
             grad_project.astype(jnp.bfloat16), "pix", scatter_dimension=1, tiled=True
         ).astype(jnp.float32),
     )
-    grad_atrous_weight = summed_grads[4].reshape(TASKS, 3, 9, -1, atrous_stack.shape[4])
     return (
         task_maps,
         grad_pixels,
@@ -487,10 +1102,10 @@
         summed_grads[2][0],
         grad_expand_gain,
         grad_expand_bias,
+        grad_point_weight,
+        grad_atrous_weight,
+        grad_pooled_weight,
         summed_grads[3],
-        grad_atrous_weight,
-        jnp.stack(pooled_grads),
-        summed_grads[5],
     )
 
 

time: 1700 us -> 781 us (0.46)
  matrix products: 655 us -> 26.6 us
  waiting for transfers between devices: 553 us -> 215 us
  Pallas kernels: 0 us -> 209 us
  local copies, waits for them, and re-layouts: 170 us -> 90 us
  other arithmetic: 106 us -> 31.7 us
  blocking collectives: 23.2 us -> 54.5 us
  starting transfers between devices: 153 us -> 124 us
    dot_general x90 -> x9, matrix products: 372 us -> 2.71 us  [dilated_transpose(): jnp.einsum(form, window, kernel[tap_index], preferred_element_type=jnp.fl...]
    pallas_call x0 -> x7, Pallas kernels: none -> 209 us  [the longest x2 67 us: return_rows(): pl.pallas_call(return_rows_kernel, out_shape=jax.ShapeDtypeStruct(rows, B...]
    reduce_scatter x1 -> x0, waiting for transfers between devices: 201 us -> none  [sent_together(): lax.psum_scatter(both, axis, scatter_dimension=dim, tiled=True)]
    dot_general x90 -> x9, matrix products: 162 us -> 2.71 us  [dilated_apply(): jnp.einsum(form, window, kernel[tap_index], preferred_element_type=jnp.fl...]
    dot_general x90 -> x9, matrix products: 87.9 us -> 9.23 us  [dilated_weight_grad(): jnp.einsum('rwc,rwd->cd', window, masked, preferred_element_type=jnp.floa...]
    all_to_all x6 -> x4, waiting for transfers between devices: 74.6 us -> 7.81 us  [sum_at_owner(): tiles = lax.all_to_all(cut_along(x, dim, count), axis, 0, 0, tiled=True)]
    all_to_all x8 -> x7, waiting for transfers between devices: 76.8 us -> 11.8 us  [sent_to_all(): return lax.all_to_all(copies, axis, split_axis=0, concat_axis=0, tiled=True)]
    convert_element_type x6 -> x1, local copies, waits for them, and re-layouts: 42.6 us -> 0.01 us  [shards(): jax.nn.silu(pre_pooled).astype(jnp.bfloat16).reshape(tile_count, BRANCH)]
  transfers between devices with their start and end apart: 38 -> 46, of which waited for: 19 -> 15; matrix products, arithmetic and copies ran while one was open for 44% -> 16% of each run, Pallas kernels for 0% -> 16%
where the time goes in v1:
time: 781 us; the launch traced here: 768 us
  waiting for transfers between devices  215 us (28%)
  Pallas kernels  209 us (27%)
  starting transfers between devices  124 us (16%)
  local copies, waits for them, and re-layouts  90 us (12%)
  blocking collectives  54.5 us (7%)
  other arithmetic  31.7 us (4%)
  matrix products  26.6 us (3%)
  between operations  16.1 us (2%)
    unnamed x7, waiting for transfers between devices  75.1 us
    all_to_all x7, starting transfers between devices, sent_to_all(): return lax.all_to_all(copies, axis, split_axis=0, concat_axis=0, tiled=True)  70.3 us
    reduce_scatter x1, waiting for transfers between devices, shards(): lax.psum_scatter(dilate_grad.astype(jnp.bfloat16), 'pix', scatter_dimensi...  69.2 us
    pallas_call x2, Pallas kernels, return_rows(): pl.pallas_call(return_rows_kernel, out_shape=jax.ShapeDtypeStruct(rows, B...  67 us
    pallas_call x2, Pallas kernels, gather_rows(): pl.pallas_call(functools.partial(gather_rows_kernel, reach), out_shape=ja...  49.4 us
    pallas_call x1, Pallas kernels, heads_weight_grad(): pl.pallas_call(heads_weight_grad_kernel, grid=(9,), in_specs=[smem] + [hb...  45.2 us
    pallas_call x1, Pallas kernels, heads_forward(): pl.pallas_call(heads_forward_kernel, grid=(9,), in_specs=[pl.BlockSpec(me...  27.4 us
    all_gather x2, blocking collectives, widen(): return lax.all_gather(tensor, 'chan', axis=2, tiled=True)  26.5 us
  transfers between devices with their start and end apart: 46, of which 15 were waited for; matrix products, arithmetic and copies ran while one was open for 16% of the time, Pallas kernels for 16%

profile of v1, /device:TPU:7, one launch (start us, length us, event | category | flops | bytes accessed | tf_op | source)
XLA Modules:
  0.0 767.9 jit_solution(1173290528786547545)
XLA Ops:
  16.7 26.3 %all-gather.2.cloned.1.call-done = bf16[8,64,2048]{2,1,0:T(8,128)(2,1)} async-done(((bf16[8,64,512]{2,1,0:T(8,128)(2,1)}), bf16[8,64,2048]{2,1,0:T(8,128)(2,1)}) %all-gather.2.cloned.1.call-update) | async-done | bytes 2097168 | tf_op jit(solution)/shard_map/all_gather | solution.py:711
  46.0 7.9 %all-to-all-start = ((f32[32,1,256]{2,1,0:T(1,128)}), f32[32,1,256]{2,1,0:T(1,128)S(1)}, u32[]{:S(2)}, u32[]{:S(2)}) async-start(f32[32,1,256]{2,1,0:T(1,128)} %broadcast_in_dim.25), calls=%async_computation | async-start | bytes 65536 | tf_op jit(solution)/shard_map/all_to_all | solution.py:689
  63.6 15.9 %all_gather.13 = bf16[8,64,512]{2,1,0:T(8,128)(2,1)S(1)} all-gather(bf16[8,64,128]{2,1,0:T(8,128)(2,1)S(1)} %multiply_convert_fusion.6), channel_id=1, replica_groups=mesh['chan'=4,'pix'=32] {'chan'}, dimensions={2}, use_global_device_ids=true | all-gather | bytes 655360 | tf_op jit(solution)/shard_map/all_gather | solution.py:711
  79.5 4.8 collective-permute-start
  87.7 4.3 collective-permute-done.1
  97.6 9.3 %all-to-all-start.1 = ((f32[32,1,256]{2,1,0:T(1,128)}), f32[32,1,256]{2,1,0:T(1,128)S(1)}, u32[]{:S(2)}, u32[]{:S(2)}) async-start(f32[32,1,256]{2,1,0:T(1,128)} %broadcast_in_dim.26), calls=%async_computation.1 | async-start | bytes 65536 | tf_op jit(solution)/shard_map/all_to_all | solution.py:689
  109.6 17.3 %gather_maps.1 = bf16[4,8,64,192]{3,2,1,0:T(8,128)(2,1)} custom-call(bf16[8,64,192]{2,1,0:T(8,128)(2,1)} %copy.176.src), custom_call_target="tpu_custom_call" | custom-call | bytes 60000000 | tf_op jit(solution)/shard_map/gather_maps/pallas_call | solution.py:212
  134.7 10.6 %all_gather.14 = bf16[8,64,512]{2,1,0:T(8,128)(2,1)S(1)} all-gather(bf16[8,64,128]{2,1,0:T(8,128)(2,1)S(1)} %multiply_convert_fusion.5), channel_id=1, replica_groups=mesh['chan'=4,'pix'=32] {'chan'}, dimensions={2}, use_global_device_ids=true | all-gather | bytes 655360 | tf_op jit(solution)/shard_map/all_gather | solution.py:711
  148.4 14.6 %all-to-all-start.2 = ((f32[32,1,1024]{2,1,0:T(1,128)}), f32[32,1,1024]{2,1,0:T(1,128)S(1)}, u32[]{:S(2)}, u32[]{:S(2)}) async-start(f32[32,1,1024]{2,1,0:T(1,128)} %broadcast_in_dim.27), calls=%async_computation.2 | async-start | bytes 262144 | tf_op jit(solution)/shard_map/all_to_all | solution.py:689
  169.1 5.0 mul.425
  176.5 7.4 all-to-all-start.4
  186.5 32.1 %gather_trunk.1.x_hbm = bf16[4,14,64,512]{3,2,1,0:T(8,128)(2,1)} custom-call(bf16[8,64,512]{2,1,0:T(8,128)(2,1)} %get-tuple-element.174.src), custom_call_target="tpu_custom_call" | custom-call | bytes 60000000 | tf_op jit(solution)/shard_map/gather_trunk/pallas_call | solution.py:212
  218.8 9.0 %all_gather.15 = bf16[7,2048]{1,0:T(8,128)(2,1)S(1)} all-gather(bf16[7,512]{1,0:T(8,128)(2,1)S(1)} %divide_convert_fusion), channel_id=1, replica_groups=mesh['chan'=4,'pix'=32] {'chan'}, dimensions={1}, use_global_device_ids=true | all-gather | bytes 35840 | tf_op jit(solution)/shard_map/all_gather | solution.py:908
  229.3 27.4 %heads_forward.1 = (bf16[512,768]{1,0:T(8,128)(2,1)}, bf16[512,768]{1,0:T(8,128)(2,1)}, bf16[5,3,64,256]{3,2,1,0:T(8,128)(2,1)}, f32[8,192]{1,0:T(8,128)}) custom-call(s32[9,8]{1,0:T(8,128)} %constant_dynamic-slice_fusion.5.keep, bf16[4,14,64,512]{3,2,1,0:T(8,128)(2,1)} %gather_trunk.1.x_hbm, bf16[3,3,3,3,64,2048]{5,4,3,2,1,0:T(8,128)(2,1)} %bitcast.371, ...), custom_call_target="tpu_custom_call" | custom-call | flops 12000000000 | bytes 28000000 | tf_op jit(solution)/shard_map/heads_forward/pallas_call | solution.py:418
  257.6 18.9 %all_to_all.76 = f32[32,7,192]{2,1,0:T(8,128)S(1)} all-to-all(f32[32,7,192]{2,1,0:T(8,128)S(1)} %broadcast_in_dim.31), channel_id=1, replica_groups=mesh['chan'=4,'pix'=32] {'pix'}, dimensions={0} | all-to-all | bytes 344064 | tf_op jit(solution)/shard_map/all_to_all | solution.py:689
  289.7 20.5 %heads_input_grad.1 = bf16[4,512,512]{2,1,0:T(8,128)(2,1)} custom-call(s32[9,8]{1,0:T(8,128)} %constant_dynamic-slice_fusion.5.keep, bf16[8,64,768]{2,1,0:T(8,128)(2,1)} %bitcast.32.mid.refs_8_, bf16[3,64,768]{2,1,0:T(8,128)(2,1)} %copy-done.90, bf16[3,64,768]{2,1,0:T(8,128)(2,1)} %copy-done.91, bf16[3,3,3,3,64,2048]{5,4,3,2,1,0:T(8,128)(2,1)} %bitcast.372, ...), custom_call_target="tpu_custom_call" | custom-call | flops 12000000000 | bytes 28000000 | tf_op jit(solution)/shard_map/heads_input_grad/pallas_call | solution.py:517
  310.3 36.3 %return_trunk.1 = bf16[8,64,512]{2,1,0:T(8,128)(2,1)} custom-call(bf16[4,8,64,512]{3,2,1,0:T(8,128)(2,1)} %bitcast.358), custom_call_target="tpu_custom_call" | custom-call | bytes 60000000 | tf_op jit(solution)/shard_map/return_trunk/pallas_call | solution.py:296
  349.2 8.5 %all-to-all-start.7 = ((f32[32,1,1024]{2,1,0:T(1,128)}), f32[32,1,1024]{2,1,0:T(1,128)S(1)}, u32[]{:S(2)}, u32[]{:S(2)}) async-start(f32[32,1,1024]{2,1,0:T(1,128)} %broadcast_in_dim.32), calls=%async_computation.7 | async-start | bytes 262144 | tf_op jit(solution)/shard_map/all_to_all | solution.py:689
  373.9 5.3 all-to-all-done.13
  397.3 30.7 %return_maps.1 = bf16[8,64,192]{2,1,0:T(8,128)(2,1)} custom-call(bf16[4,8,64,192]{3,2,1,0:T(8,128)(2,1)} %copy.183.src), custom_call_target="tpu_custom_call" | custom-call | bytes 60000000 | tf_op jit(solution)/shard_map/return_maps/pallas_call | solution.py:296
  430.9 6.1 copy.244
  441.1 11.2 %all-to-all-start.9 = ((f32[32,1,256]{2,1,0:T(1,128)}), f32[32,1,256]{2,1,0:T(1,128)S(1)}, u32[]{:S(2)}, u32[]{:S(2)}) async-start(f32[32,1,256]{2,1,0:T(1,128)} %broadcast_in_dim.33), calls=%async_computation.9 | async-start | bytes 65536 | tf_op jit(solution)/shard_map/all_to_all | solution.py:689
  453.7 4.1 all-to-all-done.9
  471.8 4.5 all-to-all-start.10
  478.3 5.2 all-to-all-done.10
  485.2 11.5 %all-to-all-start.11 = ((f32[32,1,256]{2,1,0:T(1,128)}), f32[32,1,256]{2,1,0:T(1,128)S(1)}, u32[]{:S(2)}, u32[]{:S(2)}) async-start(f32[32,1,256]{2,1,0:T(1,128)} %broadcast_in_dim.34), calls=%async_computation.11 | async-start | bytes 65536 | tf_op jit(solution)/shard_map/all_to_all | solution.py:689
  497.7 7.1 all-to-all-done.11
  518.1 9.6 %collective-permute-done.8.refs_3_ = bf16[4,8,64,128]{3,2,1,0:T(8,128)(2,1)S(1)} collective-permute-done((bf16[4,8,64,128]{3,2,1,0:T(8,128)(2,1)S(1)}, bf16[4,8,64,128]{3,2,1,0:T(8,128)(2,1)S(1)}, u32[]{:S(2)}, u32[]{:S(2)}) %collective-permute-start.8) | collective-permute-done | bytes 524320 | tf_op jit(solution)/shard_map/ppermute | solution.py:948
  537.5 4.5 all-to-all-start.12
  544.2 45.2 %heads_weight_grad.1 = (bf16[4,9,64,576]{3,2,1,0:T(8,128)(2,1)}, bf16[4,64,192]{2,1,0:T(8,128)(2,1)}) custom-call(s32[9,64]{1,0:T(8,128)} %constant_dynamic-slice_fusion.4.keep, bf16[4,8,64,128]{3,2,1,0:T(8,128)(2,1)} %get-tuple-element.178.refs_0_, bf16[4,8,64,128]{3,2,1,0:T(8,128)(2,1)} %collective-permute-done.6.refs_1_, ...), custom_call_target="tpu_custom_call" | custom-call | flops 12000000000 | bytes 28000000 | tf_op jit(solution)/shard_map/heads_weight_grad/pallas_call | solution.py:640
  603.3 74.3 %reduce-scatter.13.cloned.1.call-done = bf16[64,128]{1,0:T(8,128)(2,1)} async-done(((bf16[2048,128]{1,0:T(8,128)(2,1)}), bf16[64,128]{1,0:T(8,128)(2,1)}) %reduce-scatter.13.cloned.1.call-update) | async-done | bytes 16400
  687.2 69.2 %reduce-scatter.9.cloned.1.call-done = bf16[9,16,128]{2,1,0:T(8,128)(2,1)} async-done(((bf16[9,512,128]{2,1,0:T(8,128)(2,1)}), bf16[9,16,128]{2,1,0:T(8,128)(2,1)}) %reduce-scatter.9.cloned.1.call-update) | async-done | bytes 36880 | tf_op jit(solution)/shard_map/reduce_scatter | solution.py:1083
  (442 shorter events, 187.2 us)
Async XLA Ops:
  7.3 35.7 %all-gather.2.cloned.1.call-start = ((), (), s32[]{:S(2)}) async-start(), calls=%async_computation.18 | async-start | bytes 2621440 | tf_op jit(solution)/shard_map/all_gather | solution.py:711
  46.0 13.4 %all-to-all-start = ((f32[32,1,256]{2,1,0:T(1,128)}), f32[32,1,256]{2,1,0:T(1,128)S(1)}, u32[]{:S(2)}, u32[]{:S(2)}) async-start(f32[32,1,256]{2,1,0:T(1,128)} %broadcast_in_dim.25), calls=%async_computation | async-start | bytes 65536 | tf_op jit(solution)/shard_map/all_to_all | solution.py:689
  59.4 37.4 %all-to-all-start.3 = ((bf16[4,2,30720]{2,1,0:T(2,128)(2,1)}), bf16[4,2,30720]{2,1,0:T(2,128)(2,1)S(1)}, u32[]{:S(2)}, u32[]{:S(2)}) async-start(bf16[4,2,30720]{2,1,0:T(2,128)(2,1)} %reshape.273), calls=%async_computation.3 | async-start | bytes 983040 | tf_op jit(solution)/shard_map/all_to_all | solution.py:927
  97.6 36.0 %all-to-all-start.1 = ((f32[32,1,256]{2,1,0:T(1,128)}), f32[32,1,256]{2,1,0:T(1,128)S(1)}, u32[]{:S(2)}, u32[]{:S(2)}) async-start(f32[32,1,256]{2,1,0:T(1,128)} %broadcast_in_dim.26), calls=%async_computation.1 | async-start | bytes 65536 | tf_op jit(solution)/shard_map/all_to_all | solution.py:689
  148.4 25.7 %all-to-all-start.2 = ((f32[32,1,1024]{2,1,0:T(1,128)}), f32[32,1,1024]{2,1,0:T(1,128)S(1)}, u32[]{:S(2)}, u32[]{:S(2)}) async-start(f32[32,1,1024]{2,1,0:T(1,128)} %broadcast_in_dim.27), calls=%async_computation.2 | async-start | bytes 262144 | tf_op jit(solution)/shard_map/all_to_all | solution.py:689
  176.5 42.1 %all-to-all-start.4 = ((bf16[32,7,512]{2,1,0:T(8,128)(2,1)}), bf16[32,7,512]{2,1,0:T(8,128)(2,1)S(1)}, u32[]{:S(2)}, u32[]{:S(2)}) async-start(bf16[32,7,512]{2,1,0:T(8,128)(2,1)} %broadcast_in_dim.29), calls=%async_computation.4 | async-start | bytes 524288 | tf_op jit(solution)/shard_map/all_to_all | solution.py:689
  349.2 17.7 %all-to-all-start.7 = ((f32[32,1,1024]{2,1,0:T(1,128)}), f32[32,1,1024]{2,1,0:T(1,128)S(1)}, u32[]{:S(2)}, u32[]{:S(2)}) async-start(f32[32,1,1024]{2,1,0:T(1,128)} %broadcast_in_dim.32), calls=%async_computation.7 | async-start | bytes 262144 | tf_op jit(solution)/shard_map/all_to_all | solution.py:689
  366.9 12.3 %all-to-all-start.13 = ((bf16[4,2,30720]{2,1,0:T(2,128)(2,1)}), bf16[4,2,30720]{2,1,0:T(2,128)(2,1)S(1)}, u32[]{:S(2)}, u32[]{:S(2)}) async-start(bf16[4,2,30720]{2,1,0:T(2,128)(2,1)} %reshape.275), calls=%async_computation.15 | async-start | bytes 983040 | tf_op jit(solution)/shard_map/all_to_all | solution.py:1009
  379.2 60.9 %all-to-all-start.8 = ((bf16[4,8,64,128]{3,2,1,0:T(8,128)(2,1)}), bf16[4,8,64,128]{3,2,1,0:T(8,128)(2,1)S(1)}, u32[]{:S(2)}, u32[]{:S(2)}) async-start(bf16[4,8,64,128]{3,2,1,0:T(8,128)(2,1)} %bitcast.342), calls=%async_computation.8 | async-start | bytes 1048576 | tf_op jit(solution)/shard_map/all_to_all | solution.py:673
  382.7 134.6 %reduce-scatter.15.cloned.1.call-start = ((), (), s32[]{:S(2)}) async-start(), calls=%async_computation.22 | async-start | bytes 675840
  385.8 125.3 %collective-permute-start.6 = (bf16[4,8,64,128]{3,2,1,0:T(8,128)(2,1)}, bf16[4,8,64,128]{3,2,1,0:T(8,128)(2,1)}, u32[]{:S(2)}, u32[]{:S(2)}) collective-permute-start(bf16[4,8,64,128]{3,2,1,0:T(8,128)(2,1)} %get-tuple-element.177), channel_id=1, source_target_pairs={{0,2},{1,3},{2,0},{3,1},{4,6},{5,7},{6,4},{7,5},{8,10},{9,11},{10,... | collective-permute-start | bytes 1572872 | tf_op jit(solution)/shard_map/ppermute | solution.py:948
  387.0 126.2 %collective-permute-start.7 = (bf16[4,8,64,128]{3,2,1,0:T(8,128)(2,1)}, bf16[4,8,64,128]{3,2,1,0:T(8,128)(2,1)}, u32[]{:S(2)}, u32[]{:S(2)}) collective-permute-start(bf16[4,8,64,128]{3,2,1,0:T(8,128)(2,1)} %get-tuple-element.176), channel_id=1, source_target_pairs={{0,4},{1,5},{2,6},{3,7},{4,0},{5,1},{6,2},{7,3},{8,12},{9,13},{10,... | collective-permute-start | bytes 1572872 | tf_op jit(solution)/shard_map/ppermute | solution.py:948
  389.4 122.1 %collective-permute-start.13 = (bf16[8,64,768]{2,1,0:T(8,128)(2,1)}, bf16[8,64,768]{2,1,0:T(8,128)(2,1)}, u32[]{:S(2)}, u32[]{:S(2)}) collective-permute-start(bf16[8,64,768]{2,1,0:T(8,128)(2,1)} %bitcast.32.mid.refs_8_), channel_id=1, source_target_pairs={{0,2},{1,3},{2,0},{3,1},{4,6},{5,7},{6,4},{7,5},{8,10},{9,11},{10,... | collective-permute-start | bytes 2359304 | tf_op jit(solution)/shard_map/ppermute | solution.py:949
  441.1 16.7 %all-to-all-start.9 = ((f32[32,1,256]{2,1,0:T(1,128)}), f32[32,1,256]{2,1,0:T(1,128)S(1)}, u32[]{:S(2)}, u32[]{:S(2)}) async-start(f32[32,1,256]{2,1,0:T(1,128)} %broadcast_in_dim.33), calls=%async_computation.9 | async-start | bytes 65536 | tf_op jit(solution)/shard_map/all_to_all | solution.py:689
  452.3 148.0 %reduce-scatter.11.cloned.1.call-start = ((), (), s32[]{:S(2)}) async-start(), calls=%async_computation.20 | async-start | bytes 540672 | tf_op jit(solution)/shard_map/reduce_scatter | solution.py:1086
  465.0 46.7 %collective-permute-start.14 = (bf16[8,64,768]{2,1,0:T(8,128)(2,1)}, bf16[8,64,768]{2,1,0:T(8,128)(2,1)}, u32[]{:S(2)}, u32[]{:S(2)}) collective-permute-start(bf16[8,64,768]{2,1,0:T(8,128)(2,1)} %bitcast.32.mid.refs_8_), channel_id=1, source_target_pairs={{0,4},{1,5},{2,6},{3,7},{4,0},{5,1},{6,2},{7,3},{8,12},{9,13},{10,... | collective-permute-start | bytes 2359304 | tf_op jit(solution)/shard_map/ppermute | solution.py:949
  466.8 45.3 %collective-permute-start.15 = (bf16[8,64,768]{2,1,0:T(8,128)(2,1)}, bf16[8,64,768]{2,1,0:T(8,128)(2,1)}, u32[]{:S(2)}, u32[]{:S(2)}) collective-permute-start(bf16[8,64,768]{2,1,0:T(8,128)(2,1)} %bitcast.32.mid.refs_8_), channel_id=1, source_target_pairs={{0,6},{1,7},{2,4},{3,5},{4,2},{5,3},{6,0},{7,1},{8,14},{9,15},{10,... | collective-permute-start | bytes 2359304 | tf_op jit(solution)/shard_map/ppermute | solution.py:949
  485.2 19.7 %all-to-all-start.11 = ((f32[32,1,256]{2,1,0:T(1,128)}), f32[32,1,256]{2,1,0:T(1,128)S(1)}, u32[]{:S(2)}, u32[]{:S(2)}) async-start(f32[32,1,256]{2,1,0:T(1,128)} %broadcast_in_dim.34), calls=%async_computation.11 | async-start | bytes 65536 | tf_op jit(solution)/shard_map/all_to_all | solution.py:689
  496.7 180.9 %reduce-scatter.13.cloned.1.call-start = ((), (), s32[]{:S(2)}) async-start(), calls=%async_computation.21 | async-start | bytes 540672
  511.0 245.3 %reduce-scatter.9.cloned.1.call-start = ((), (), s32[]{:S(2)}) async-start(), calls=%async_computation.19 | async-start | bytes 1216512 | tf_op jit(solution)/shard_map/reduce_scatter | solution.py:1083
  511.1 17.8 %collective-permute-start.16 = (bf16[8,64,768]{2,1,0:T(8,128)(2,1)}, bf16[8,64,768]{2,1,0:T(8,128)(2,1)}, u32[]{:S(2)}, u32[]{:S(2)}) collective-permute-start(bf16[8,64,768]{2,1,0:T(8,128)(2,1)} %bitcast.32.mid.refs_8_), channel_id=1, source_target_pairs={{0,1},{1,0},{2,3},{3,2},{4,5},{5,4},{6,7},{7,6},{8,9},{9,8},{10,11... | collective-permute-start | bytes 2359304 | tf_op jit(solution)/shard_map/ppermute | solution.py:951
  511.6 17.4 %collective-permute-start.17 = (bf16[8,64,768]{2,1,0:T(8,128)(2,1)}, bf16[8,64,768]{2,1,0:T(8,128)(2,1)}, u32[]{:S(2)}, u32[]{:S(2)}) collective-permute-start(bf16[8,64,768]{2,1,0:T(8,128)(2,1)} %collective-permute-done.13.refs_9_), channel_id=1, source_target_pairs={{0,1},{1,0},{2,3},{3,2},{4,5},{5,4},{6,7},{7,6},{8,9},{9,8},{10,11... | collective-permute-start | bytes 2359304 | tf_op jit(solution)/shard_map/ppermute | solution.py:951
  511.7 17.7 %collective-permute-start.18 = (bf16[8,64,768]{2,1,0:T(8,128)(2,1)}, bf16[8,64,768]{2,1,0:T(8,128)(2,1)}, u32[]{:S(2)}, u32[]{:S(2)}) collective-permute-start(bf16[8,64,768]{2,1,0:T(8,128)(2,1)} %collective-permute-done.14.refs_10_), channel_id=1, source_target_pairs={{0,1},{1,0},{2,3},{3,2},{4,5},{5,4},{6,7},{7,6},{8,9},{9,8},{10,11... | collective-permute-start | bytes 2359304 | tf_op jit(solution)/shard_map/ppermute | solution.py:951
  512.1 17.4 %collective-permute-start.19 = (bf16[8,64,768]{2,1,0:T(8,128)(2,1)}, bf16[8,64,768]{2,1,0:T(8,128)(2,1)}, u32[]{:S(2)}, u32[]{:S(2)}) collective-permute-start(bf16[8,64,768]{2,1,0:T(8,128)(2,1)} %collective-permute-done.15.refs_11_), channel_id=1, source_target_pairs={{0,1},{1,0},{2,3},{3,2},{4,5},{5,4},{6,7},{7,6},{8,9},{9,8},{10,11... | collective-permute-start | bytes 2359304 | tf_op jit(solution)/shard_map/ppermute | solution.py:951
  513.2 14.5 %collective-permute-start.8 = (bf16[4,8,64,128]{3,2,1,0:T(8,128)(2,1)S(1)}, bf16[4,8,64,128]{3,2,1,0:T(8,128)(2,1)S(1)}, u32[]{:S(2)}, u32[]{:S(2)}) collective-permute-start(bf16[4,8,64,128]{3,2,1,0:T(8,128)(2,1)S(1)} %copy-done.45), channel_id=1, source_target_pairs={{0,6},{1,7},{2,4},{3,5},{4,2},{5,3},{6,0},{7,1},{8,14},{9,15},{10,... | collective-permute-start | bytes 1572872 | tf_op jit(solution)/shard_map/ppermute | solution.py:948
  528.9 13.1 %collective-permute-start.10 = (bf16[4,8,64,128]{3,2,1,0:T(8,128)(2,1)}, bf16[4,8,64,128]{3,2,1,0:T(8,128)(2,1)S(1)}, u32[]{:S(2)}, u32[]{:S(2)}) collective-permute-start(bf16[4,8,64,128]{3,2,1,0:T(8,128)(2,1)} %collective-permute-done.6.refs_1_), channel_id=1, source_target_pairs={{0,1},{1,0},{2,3},{3,2},{4,5},{5,4},{6,7},{7,6},{8,9},{9,8},{10,11... | collective-permute-start | bytes 1572872 | tf_op jit(solution)/shard_map/ppermute | solution.py:950
  529.0 13.0 %collective-permute-start.11 = (bf16[4,8,64,128]{3,2,1,0:T(8,128)(2,1)}, bf16[4,8,64,128]{3,2,1,0:T(8,128)(2,1)}, u32[]{:S(2)}, u32[]{:S(2)}) collective-permute-start(bf16[4,8,64,128]{3,2,1,0:T(8,128)(2,1)} %collective-permute-done.7.refs_2_), channel_id=1, source_target_pairs={{0,1},{1,0},{2,3},{3,2},{4,5},{5,4},{6,7},{7,6},{8,9},{9,8},{10,11... | collective-permute-start | bytes 1572872 | tf_op jit(solution)/shard_map/ppermute | solution.py:950
  529.4 12.6 %collective-permute-start.12 = (bf16[4,8,64,128]{3,2,1,0:T(8,128)(2,1)S(1)}, bf16[4,8,64,128]{3,2,1,0:T(8,128)(2,1)}, u32[]{:S(2)}, u32[]{:S(2)}) collective-permute-start(bf16[4,8,64,128]{3,2,1,0:T(8,128)(2,1)S(1)} %collective-permute-done.8.refs_3_), channel_id=1, source_target_pairs={{0,1},{1,0},{2,3},{3,2},{4,5},{5,4},{6,7},{7,6},{8,9},{9,8},{10,11... | collective-permute-start | bytes 1572872 | tf_op jit(solution)/shard_map/ppermute | solution.py:950
  537.5 220.2 %all-to-all-start.12 = ((bf16[4,8,64,512]{3,2,1,0:T(8,128)(2,1)}), bf16[4,8,64,512]{3,2,1,0:T(8,128)(2,1)}, u32[]{:S(2)}, u32[]{:S(2)}) async-start(bf16[4,8,64,512]{3,2,1,0:T(8,128)(2,1)} %bitcast.336), calls=%async_computation.12 | async-start | bytes 4194304 | tf_op jit(solution)/shard_map/all_to_all | solution.py:673
  596.4 82.8 %collective-permute-start.27 = (bf16[9,64,576]{2,1,0:T(8,128)(2,1)}, bf16[9,64,576]{2,1,0:T(8,128)(2,1)S(1)}, u32[]{:S(2)}, u32[]{:S(2)}) collective-permute-start(bf16[9,64,576]{2,1,0:T(8,128)(2,1)} %get-tuple-element.180), channel_id=1, source_target_pairs={{0,24},{1,25},{2,26},{3,27},{4,28},{5,29},{6,30},{7,31},{8,0},{9,1... | collective-permute-start | bytes 1990664 | tf_op jit(solution)/shard_map/ppermute | solution.py:988
  597.8 81.3 %collective-permute-start.26 = (bf16[9,64,576]{2,1,0:T(8,128)(2,1)S(1)}, bf16[9,64,576]{2,1,0:T(8,128)(2,1)S(1)}, u32[]{:S(2)}, u32[]{:S(2)}) collective-permute-start(bf16[9,64,576]{2,1,0:T(8,128)(2,1)S(1)} %get-tuple-element.181), channel_id=1, source_target_pairs={{0,16},{1,17},{2,18},{3,19},{4,20},{5,21},{6,22},{7,23},{8,24},{9,... | collective-permute-start | bytes 1990664 | tf_op jit(solution)/shard_map/ppermute | solution.py:988
  598.2 80.9 %collective-permute-start.25 = (bf16[9,64,576]{2,1,0:T(8,128)(2,1)S(1)}, bf16[9,64,576]{2,1,0:T(8,128)(2,1)}, u32[]{:S(2)}, u32[]{:S(2)}) collective-permute-start(bf16[9,64,576]{2,1,0:T(8,128)(2,1)S(1)} %get-tuple-element.179), channel_id=1, source_target_pairs={{0,8},{1,9},{2,10},{3,11},{4,12},{5,13},{6,14},{7,15},{8,16},{9,17... | collective-permute-start | bytes 1990664 | tf_op jit(solution)/shard_map/ppermute | solution.py:988
  (107 other events, 1342.2 us)
Sparse Core Ops, SparseCore 0:
  9.7 33.1 all-gather.1
  438.6 77.5 reduce-scatter.14
  519.7 77.8 reduce-scatter.10
  601.5 76.0 reduce-scatter.12
  681.0 75.3 reduce-scatter.8

commit v2 on v1

--- a/solution.py
+++ b/solution.py
@@ -27,7 +27,6 @@
 eps = 1e-05
 section_rate = 4
 head_rates = (6, 12, 18)
-tap_offsets = tuple(((row_step, col_step) for row_step in (-1, 0, 1) for col_step in (-1, 0, 1)))
 VMEM_LIMIT = 60 * 2**20
 
 
@@ -399,15 +398,19 @@
             head = term if head is None else head + term
             grads = dot_tn(joined, cot)
             for t in range(TASKS):
-                grad_project[which, t] = grads[
-                    HEAD * t : HEAD * (t + 1), 256 * t : 256 * (t + 1)
-                ].astype(BF16)
+                for c in range(CHAN):
+                    lane = 256 * t + HEAD * c
+                    grad_project[c, which, t] = grads[
+                        HEAD * t : HEAD * (t + 1), lane : lane + HEAD
+                    ].astype(BF16)
             back = dot_nt(cot, weight)
             if which < 4:
                 grad = back * (logistic * (1.0 + before * (1.0 - logistic)))
                 grad_pre[:, BRANCH * which : BRANCH * (which + 1)] = grad.astype(BF16)
             else:
-                pool_rows[...] = jnp.sum(back.reshape(OWN_ROWS, TILE_W, BRANCH), axis=1)
+                sums = jnp.sum(back.reshape(OWN_ROWS, TILE_W, BRANCH), axis=1)
+                pool_rows[:, :BRANCH] = sums
+                pool_rows[:, BRANCH:] = jnp.zeros((OWN_ROWS, 256 - BRANCH), F32)
         head_part[...] = head.astype(BF16)
 
 
@@ -431,8 +434,8 @@
         out_shape=[
             jax.ShapeDtypeStruct((pixels, 4 * BRANCH), BF16),
             jax.ShapeDtypeStruct((pixels, 256 * TASKS), BF16),
-            jax.ShapeDtypeStruct((5, TASKS, HEAD, 256), BF16),
-            jax.ShapeDtypeStruct((OWN_ROWS, BRANCH), F32),
+            jax.ShapeDtypeStruct((CHAN, 5, TASKS, HEAD, HEAD), BF16),
+            jax.ShapeDtypeStruct((OWN_ROWS, 256), F32),
         ],
         scratch_shapes=[
             pltpu.VMEM((EXT_ROWS, TILE_W, feat), BF16),
@@ -662,162 +665,555 @@
     )(keep, *x_parts, *g_parts, g_low, g_high)
 
 
-def cut_along(x, dim, count):
-    dims = x.shape
-    tiles = x.reshape(*dims[:dim], count, dims[dim] // count, *dims[dim + 1 :])
-    return jnp.moveaxis(tiles, dim, 0)
-
-
-def sum_at_owner(x, axis, dim):
-    count = lax.axis_size(axis)
-    tiles = lax.all_to_all(cut_along(x, dim, count), axis, 0, 0, tiled=True)
-    return jnp.sum(tiles.astype(jnp.float32), axis=0)
-
-
-def for_sending(x):
-    return jax.tree.map(lambda a: a.astype(jnp.bfloat16) if a.dtype == jnp.float32 else a, x)
-
-
-def from_behind(block, axis, distance):
-    devices = range(lax.axis_size(axis))
-    route = [(i - distance, i) for i in devices if i - distance in devices]
-    return lax.ppermute(block, axis, route)
-
-
-def sent_to_all(x, axis):
-    copies = jnp.broadcast_to(x, (lax.axis_size(axis), *x.shape))
-    return lax.all_to_all(copies, axis, split_axis=0, concat_axis=0, tiled=True)
-
-
-def of_everyone(x, axis):
-    everything = sent_to_all(x, axis)
-    return jnp.sum(everything, axis=0)
-
-
-def in_one(arrays, axis):
-    ravelled, at, finished = (jnp.concatenate([a.reshape(-1) for a in arrays]), 0, [])
-    total = of_everyone(ravelled, axis)
-    for a in arrays:
-        finished.append(total[at : at + a.size].reshape(a.shape))
-        at += a.size
-    return tuple(finished)
-
-
-def of_everyone_2(x, axis):
-    return sent_to_all(x, axis).astype(jnp.float32).sum(axis=0)
-
-
-def widen(tensor):
-    return lax.all_gather(tensor, "chan", axis=2, tiled=True)
-
-
-def collect(tensors):
-    return jax.tree.map(lambda part: sum_at_owner(part, "chan", 2), for_sending(tensors))
-
-
-def move_forward(slab_rows, distance):
-    return from_behind(slab_rows, "pix", distance)
-
-
-def move_backward(slab_rows, distance):
-    return from_behind(slab_rows, "pix", distance)
-
-
-def extend_rows(source, reach_rows, mover):
-    row_count = source.shape[0]
-    upper_rows = []
-    lower_rows = []
-    for distance in range(1, -(-reach_rows // row_count) + 1):
-        wanted = min(row_count, reach_rows - (distance - 1) * row_count)
-        upper_rows = [mover(source[row_count - wanted :], distance)] + upper_rows
-        lower_rows = lower_rows + [mover(source[:wanted], -distance)]
-    return jnp.concatenate(upper_rows + [source] + lower_rows, axis=0)
-
-
-def tap_read(extended, row_start, col_shift, row_count):
-    window = lax.slice_in_dim(extended, row_start, row_start + row_count, axis=0)
-    col_count = window.shape[1]
-    if col_shift > 0:
-        window = jnp.pad(window[:, col_shift:], ((0, 0), (0, col_shift), (0, 0)))
-    elif col_shift < 0:
-        window = jnp.pad(window[:, : col_count + col_shift], ((0, 0), (-col_shift, 0), (0, 0)))
-    return window
-
-
-def seam_masks(tile_pad, first_row, margin, dilation, row_count):
-    own_tiles = lax.dynamic_slice_in_dim(tile_pad, first_row + margin, row_count)
+class Links:
+    def __init__(self, send_sems, recv_sems):
+        self.send_sems, self.recv_sems, self.count, self.sent = send_sems, recv_sems, 0, []
+
+    def send(self, src, dst, **where):
+        n = self.count
+        self.count += 1
+        copy = remote(src, dst, self.send_sems.at[n], self.recv_sems.at[n], **where)
+        copy.start()
+        self.sent.append(copy)
+        return n
+
+    def arrive(self, n, dst):
+        beside = {"chan": int_rem(lax.axis_index("chan") + 1, CHAN)}
+        remote(dst, dst, self.send_sems.at[n], self.recv_sems.at[n], **beside).wait_recv()
+
+    def finish(self):
+        for copy in self.sent:
+            copy.wait_send()
+
+
+def greet(peers, more=0):
+    barrier = pltpu.get_barrier_semaphore()
+    for where in peers:
+        signal(barrier, **where)
+    pl.semaphore_wait(barrier, len(peers) + more)
+
+
+class Spot:
+    def __init__(self):
+        self.i, self.j = lax.axis_index("pix"), lax.axis_index("chan")
+        self.group, self.k = int_div(self.i, GROUP), int_rem(self.i, GROUP)
+        self.z, self.core = int_div(self.k, 2), int_rem(self.k, 2)
+        self.before, self.after = int_rem(self.i + PIX - 1, PIX), int_rem(self.i + 1, PIX)
+        self.mate = self.i + 1 - 2 * self.core
+
+    def chan(self, distance):
+        return int_rem(self.j + CHAN + distance, CHAN)
+
+    def in_group(self, distance):
+        return int_rem(self.k + GROUP + distance, GROUP)
+
+    def pix_in_group(self, distance):
+        return GROUP * self.group + self.in_group(distance)
+
+    def x_of(self, distance):
+        return int_rem(self.group + 4 + distance, 4)
+
+    def pix_in_x(self, distance):
+        return GROUP * self.x_of(distance) + self.k
+
+    def z_of(self, distance):
+        return int_rem(self.z + 4 + distance, 4)
+
+    def pix_in_z(self, distance):
+        return GROUP * self.group + 2 * self.z_of(distance) + self.core
+
+    def sum_peers(self):
+        return [{"pix": self.pix_in_group(d)} for d in range(1, GROUP)] + [
+            {"pix": self.pix_in_x(d)} for d in range(1, 4)
+        ]
+
+
+def sum_over_pix(value, near, across, spot, links):
+    near[spot.k] = value
+    sent = [
+        links.send(near.at[spot.k], near.at[spot.k], pix=spot.pix_in_group(d))
+        for d in range(1, GROUP)
+    ]
+    for d, n in zip(range(1, GROUP), sent):
+        links.arrive(n, near.at[spot.in_group(-d)])
+    total = near[0]
+    for k in range(1, GROUP):
+        total = total + near[k]
+    across[spot.group] = total
+    sent = [
+        links.send(across.at[spot.group], across.at[spot.group], pix=spot.pix_in_x(d))
+        for d in range(1, 4)
+    ]
+    for d, n in zip(range(1, 4), sent):
+        links.arrive(n, across.at[spot.x_of(-d)])
+    return across[0] + across[1] + across[2] + across[3]
+
+
+def two_sums(first, second):
+    width = first.shape[1]
+    rows = [jnp.sum(first, axis=0, keepdims=True), jnp.sum(second, axis=0, keepdims=True)]
+    return jnp.concatenate(rows + [jnp.zeros((6, width), F32)], axis=0)
+
+
+PIXELS = NROWS * TILE_W
+OWN = OWN_ROWS * TILE_W
+MID_OWN = 128
+FEAT_OWN = 512
+ROW_COLS = OWN_ROWS * TILE_W
+
+
+def col_shift(value, distance):
+    col = lax.broadcasted_iota(jnp.int32, value.shape, 0) % TILE_W
+    rows = value.shape[0]
+    moved = pltpu.roll(value, (rows - distance) % rows, 0)
+    inside = (col < TILE_W - distance) if distance > 0 else (col >= -distance)
+    return jnp.where(inside, moved, 0.0)
+
+
+def section_forward_kernel(
+    pixels, wr, wd, we, vec_mid, vec_feat, keep, tile_rows, sizes,
+    trunk, unit_r, unit_d, unit_e, act_r, act_d, wr_all, inv_mid, inv_feat, mean_all,
+    part_out, part_in, near_m, across_m, near_f, across_f, near_t, across_t, send_sems, recv_sems,
+):
+    spot = Spot()
+    links = Links(send_sems, recv_sems)
+    j = spot.j
+    peers = [{"chan": spot.chan(d)} for d in (1, 2, 3)] + spot.sum_peers()
+    for d in range(CHAN):
+        peers += [{"pix": p, "chan": spot.chan(d)} for p in (spot.before, spot.after)]
+    greet(peers)
+
+    def block(chan):
+        return pl.ds(pl.multiple_of(FEAT_OWN * chan, FEAT_OWN), FEAT_OWN)
+
+    sent = {
+        d: links.send(wr.at[block(spot.chan(d))], wr_all.at[j], chan=spot.chan(d)) for d in (2, 1, 3)
+    }
+    wr_all[j] = wr[block(j)]
+    pre = dot_nn(pixels[...], wr_all[j])
+    back = {}
+    for d in (1, 3, 2):
+        source = spot.chan(-d)
+        links.arrive(sent[d], wr_all.at[source])
+        part_out[d - 1] = dot_nn(pixels[...], wr_all[source]).astype(BF16)
+        back[d] = links.send(part_out.at[d - 1], part_in.at[d - 1], chan=source)
+    for d in (1, 3, 2):
+        links.arrive(back[d], part_in.at[d - 1])
+        pre = pre + part_in[d - 1].astype(F32)
+
+    def norm(value, near, across, gain, bias):
+        sums = sum_over_pix(two_sums(value, value * value), near, across, spot, links)
+        center = sums[0:1] / PIXELS
+        inv = lax.rsqrt(sums[1:2] / PIXELS - center * center + eps)
+        unit = (value - center) * inv
+        return unit, unit * gain + bias, inv
+
+    unit, normed, inv_r = norm(pre, near_m.at[0], across_m.at[0], vec_mid[0:1], vec_mid[1:2])
+    unit_r[...] = unit
+    own = slice(section_rate, section_rate + OWN_ROWS)
+    act_r[j, own] = silu(normed).astype(BF16).reshape(OWN_ROWS, TILE_W, MID_OWN)
+    low, high = slice(0, section_rate), slice(section_rate + OWN_ROWS, 2 * section_rate + OWN_ROWS)
+    first, last = slice(section_rate, 2 * section_rate), slice(OWN_ROWS, section_rate + OWN_ROWS)
+    arrivals = []
+    for d in (2, 1, 3, 0):
+        to, source = spot.chan(d), spot.chan(-d)
+        if d:
+            n = links.send(act_r.at[j, own], act_r.at[j, own], chan=to)
+            arrivals.append((n, act_r.at[source, own]))
+        n = links.send(act_r.at[j, first], act_r.at[j, high], pix=spot.before, chan=to)
+        arrivals.append((n, act_r.at[source, high]))
+        n = links.send(act_r.at[j, last], act_r.at[j, low], pix=spot.after, chan=to)
+        arrivals.append((n, act_r.at[source, low]))
+    for n, dst in arrivals:
+        links.arrive(n, dst)
+    pre = jnp.zeros((OWN, MID_OWN), F32)
+    for a in range(3):
+        rows = slice(section_rate * a, section_rate * a + OWN_ROWS)
+        window = jnp.concatenate(
+            [act_r[c, rows].reshape(OWN, MID_OWN) for c in range(CHAN)], axis=1
+        )
+        terms = [dot_nn(window, wd[3 * a + b]) for b in range(3)]
+        term = terms[1] + col_shift(terms[0], -section_rate) + col_shift(terms[2], section_rate)
+        pre = pre + (term if a == 1 else term * keep[a // 2])
+
+    unit, normed, inv_d = norm(pre, near_m.at[1], across_m.at[1], vec_mid[2:3], vec_mid[3:4])
+    unit_d[...] = unit
+    inv_mid[...] = jnp.concatenate([inv_r, inv_d, jnp.zeros((6, MID_OWN), F32)], axis=0)
+    act_d[j] = silu(normed).astype(BF16)
+    sent = {d: links.send(act_d.at[j], act_d.at[j], chan=spot.chan(d)) for d in (2, 1, 3)}
+    for d in (1, 3, 2):
+        links.arrive(sent[d], act_d.at[spot.chan(-d)])
+    full = jnp.concatenate([act_d[c] for c in range(CHAN)], axis=1)
+    unit, normed, inv_e = norm(
+        dot_nn(full, we[...]), near_f, across_f, vec_feat[0:1], vec_feat[1:2]
+    )
+    unit_e[...] = unit
+    inv_feat[...] = jnp.concatenate([inv_e, jnp.zeros((7, FEAT_OWN), F32)], axis=0)
+    out = silu(normed + pixels[...].astype(F32)).astype(BF16)
+    trunk[...] = out.reshape(OWN_ROWS, TILE_W, FEAT_OWN)
+    row_sums = jnp.sum(out.astype(F32).reshape(OWN_ROWS, TILE_W, FEAT_OWN), axis=1)
+    sums = jnp.zeros((8, FEAT_OWN), F32)
+    for r in range(OWN_ROWS):
+        sums = sums + tile_rows[:, r : r + 1] * row_sums[r : r + 1]
+    sums = sum_over_pix(sums, near_t, across_t, spot, links)
+    mean = jnp.concatenate([sums / sizes[:, 0:1], jnp.zeros((8, FEAT_OWN), F32)], axis=0)
+    mean_all[j] = mean.astype(BF16)
+    sent = {d: links.send(mean_all.at[j], mean_all.at[j], chan=spot.chan(d)) for d in (2, 1, 3)}
+    for d in (1, 3, 2):
+        links.arrive(sent[d], mean_all.at[spot.chan(-d)])
+    links.finish()
+
+
+def section_forward(pixels, wr, wd, we, vec_mid, vec_feat, keep, tile_rows, sizes):
+    whole = pl.BlockSpec(memory_space=pltpu.VMEM)
+    shape = jax.ShapeDtypeStruct
+    mid, feat = (OWN, MID_OWN), (OWN, FEAT_OWN)
+    dma = pltpu.SemaphoreType.DMA
+    return pl.pallas_call(
+        section_forward_kernel,
+        in_specs=[whole] * 9,
+        out_specs=[whole] * 10,
+        out_shape=[
+            shape((OWN_ROWS, TILE_W, FEAT_OWN), BF16),
+            shape(mid, F32),
+            shape(mid, F32),
+            shape(feat, F32),
+            shape((CHAN, OWN_ROWS + 2 * section_rate, TILE_W, MID_OWN), BF16),
+            shape((CHAN, *mid), BF16),
+            shape((CHAN, FEAT_OWN, MID_OWN), BF16),
+            shape((8, MID_OWN), F32),
+            shape((8, FEAT_OWN), F32),
+            shape((CHAN, 16, FEAT_OWN), BF16),
+        ],
+        scratch_shapes=[
+            pltpu.VMEM((3, *mid), BF16),
+            pltpu.VMEM((3, *mid), BF16),
+            pltpu.VMEM((2, GROUP, 8, MID_OWN), F32),
+            pltpu.VMEM((2, 4, 8, MID_OWN), F32),
+            pltpu.VMEM((GROUP, 8, FEAT_OWN), F32),
+            pltpu.VMEM((4, 8, FEAT_OWN), F32),
+            pltpu.VMEM((GROUP, 8, FEAT_OWN), F32),
+            pltpu.VMEM((4, 8, FEAT_OWN), F32),
+            dma((64,)),
+            dma((64,)),
+        ],
+        compiler_params=pltpu.CompilerParams(
+            collective_id=5, has_side_effects=True, vmem_limit_bytes=VMEM_LIMIT
+        ),
+        cost_estimate=pl.CostEstimate(
+            flops=2_000_000_000, bytes_accessed=120_000_000, transcendentals=0
+        ),
+        name="section_forward",
+    )(pixels, wr, wd, we, vec_mid, vec_feat, keep, tile_rows, sizes)
+
+
+class Scatter:
+    def __init__(self, parts, mate_in, near, near_in, far, far_in, spot, links):
+        self.parts, self.mate_in, self.near, self.near_in = parts, mate_in, near, near_in
+        self.far, self.far_in, self.spot, self.links = far, far_in, spot, links
+
+    def start(self):
+        spot = self.spot
+        self.sent = self.links.send(self.parts.at[1 - spot.core], self.mate_in, pix=spot.mate)
+
+    def along_z(self):
+        spot, links = self.spot, self.links
+        links.arrive(self.sent, self.mate_in)
+        for z in range(4):
+            self.near[z] = (
+                self.parts[spot.core, z].astype(F32) + self.mate_in[z].astype(F32)
+            ).astype(BF16)
+        self.sent = {
+            d: links.send(
+                self.near.at[spot.z_of(d)], self.near_in.at[d - 1], pix=spot.pix_in_z(d)
+            )
+            for d in (2, 1, 3)
+        }
+
+    def along_x(self):
+        spot, links = self.spot, self.links
+        total = self.near[spot.z].astype(F32)
+        for d in (1, 3, 2):
+            links.arrive(self.sent[d], self.near_in.at[d - 1])
+            total = total + self.near_in[d - 1].astype(F32)
+        self.far[...] = total.astype(BF16)
+        self.sent = {
+            d: links.send(self.far.at[spot.x_of(d)], self.far_in.at[d - 1], pix=spot.pix_in_x(d))
+            for d in (2, 1, 3)
+        }
+
+    def finish(self):
+        spot, links = self.spot, self.links
+        total = self.far[spot.group].astype(F32)
+        for d in (1, 3, 2):
+            links.arrive(self.sent[d], self.far_in.at[d - 1])
+            total = total + self.far_in[d - 1].astype(F32)
+        return total
+
+
+def scatter_scratch(*shape):
     return [
-        (
-            lax.dynamic_slice_in_dim(tile_pad, first_row + margin + row_step * dilation, row_count)
-            == own_tiles
-        ).astype(jnp.float32)
-        for row_step in (-1, 0, 1)
+        pltpu.VMEM((2, 4, 4, *shape), BF16),
+        pltpu.VMEM((4, 4, *shape), BF16),
+        pltpu.VMEM((4, 4, *shape), BF16),
+        pltpu.VMEM((3, 4, *shape), BF16),
+        pltpu.VMEM((4, *shape), BF16),
+        pltpu.VMEM((3, *shape), BF16),
     ]
 
 
-def dilated_apply(extended, kernel, dilation, reach_rows, seam_rows, row_count, form):
-    result = None
-    for tap_index, (row_step, col_step) in enumerate(tap_offsets):
-        window = tap_read(
-            extended, reach_rows + row_step * dilation, col_step * dilation, row_count
+def spot_of(device):
+    return device % 2, device % GROUP // 2, device // GROUP
+
+
+def section_backward_kernel(
+    trunk_grad, pixels, unit_r, unit_d, unit_e, act_r, act_d, wr_all, wd_cat, we, vec_mid, vec_feat,
+    inv_mid, inv_feat, keep, pool_rows, place_rows, tile_cols, sizes, pre_pooled, pooled, projects,
+    grad_pixels, mid_grads, feat_grads, grad_reduce, grad_dilate, grad_expand, grad_project, grad_pooled,
+    *scratch,
+):
+    (
+        side_out, side_in, halo, taps, full, mean_out, mean_in, project_in, project_wide, reduce_out,
+        near_m, across_m, near_f, across_f, near_p, across_p,
+    ) = scratch[:16]
+    send_sems, recv_sems, last_sems = scratch[-3:]
+    buffers = scratch[16:-3]
+    spot = Spot()
+    links = Links(send_sems, recv_sems)
+    i, j = spot.i, spot.j
+    by_expand, by_dilate, by_project, by_reduce = [
+        Scatter(*buffers[6 * n : 6 * n + 6], spot, links) for n in range(4)
+    ]
+    owner_i, owner_j = GROUP * j + int_div(i, 4), int_rem(i, 4)
+    maker_i, maker_j = 4 * int_rem(i, GROUP) + j, spot.group
+    stays = (owner_i == i) & (owner_j == j)
+    barrier = pltpu.get_barrier_semaphore()
+
+    @pl.when(jnp.logical_not(stays))
+    def _():
+        signal(barrier, pix=maker_i, chan=maker_j)
+
+    peers = [{"chan": spot.chan(d)} for d in (1, 2, 3)] + spot.sum_peers()
+    peers += [{"pix": spot.before}, {"pix": spot.after}]
+    greet(peers, 1 - stays.astype(jnp.int32))
+
+    project_sent = {
+        d: links.send(projects.at[spot.chan(d)], project_in.at[d - 1], chan=spot.chan(d))
+        for d in (2, 1, 3)
+    }
+
+    sums = jnp.zeros((8, 2 * MID_OWN), F32)
+    for r in range(OWN_ROWS):
+        sums = sums + place_rows[:, r : r + 1] * pool_rows[r : r + 1]
+    sums = sum_over_pix(sums, near_p, across_p, spot, links)
+    pooled_pre = (sums[:, :BRANCH] * slope(pre_pooled[...])).astype(BF16)
+    grad_pooled[...] = pooled_pre.astype(F32)
+    wide = jnp.concatenate([pooled_pre.astype(F32), jnp.zeros((8, BRANCH), F32)], axis=0).astype(BF16)
+    for c in range(CHAN):
+        mean_out[c] = dot_nn(wide, pooled[:, FEAT_OWN * c : FEAT_OWN * (c + 1)]).astype(BF16)
+    sent = {
+        d: links.send(mean_out.at[spot.chan(d)], mean_in.at[d - 1], chan=spot.chan(d))
+        for d in (2, 1, 3)
+    }
+    mean = mean_out[j].astype(F32)
+    for d in (1, 3, 2):
+        links.arrive(sent[d], mean_in.at[d - 1])
+        mean = mean + mean_in[d - 1].astype(F32)
+    mean = mean[0:8] / sizes[:, 0:1]
+    mean_rows = jnp.zeros((OWN_ROWS, FEAT_OWN), F32)
+    for k in range(8):
+        mean_rows = mean_rows + tile_cols[:, k : k + 1] * mean[k : k + 1]
+
+    def norm_back(grad, unit, near, across, scale):
+        sums = sum_over_pix(two_sums(grad, grad * unit), near, across, spot, links)
+        pre = scale * (grad - sums[0:1] / PIXELS - unit * (sums[1:2] / PIXELS))
+        return pre.astype(BF16), sums
+
+    grad_trunk = trunk_grad[...].astype(F32) + mean_rows[:, None, :]
+    grad_trunk = grad_trunk.reshape(OWN, FEAT_OWN)
+    unit = unit_e[...]
+    summed = unit * vec_feat[0:1] + vec_feat[1:2] + pixels[...].astype(F32)
+    grad_summed = grad_trunk * slope(summed)
+    g_expand, sums = norm_back(grad_summed, unit, near_f, across_f, vec_feat[0:1] * inv_feat[0:1])
+    feat_grads[...] = sums
+
+    def sides(turn, make):
+        sent = {}
+        for d in (2, 1, 3):
+            side_out[turn, d - 1] = make(spot.chan(d)).astype(BF16)
+            sent[d] = links.send(
+                side_out.at[turn, d - 1], side_in.at[turn, d - 1], chan=spot.chan(d)
+            )
+        return sent
+
+    def side_sum(turn, own, sent):
+        for d in (1, 3, 2):
+            links.arrive(sent[d], side_in.at[turn, d - 1])
+            own = own + side_in[turn, d - 1].astype(F32)
+        return own
+
+    def mid_rows(chan):
+        return pl.ds(pl.multiple_of(MID_OWN * chan, MID_OWN), MID_OWN)
+
+    sent = sides(0, lambda c: dot_nt(g_expand, we[mid_rows(c)]))
+    own = dot_nt(g_expand, we[mid_rows(j)])
+    part = 16
+    for c in range(CHAN):
+        grads = dot_tn(act_d[c], g_expand).astype(BF16)
+        for n in range(8):
+            by_expand.parts[spot_of(8 * c + n)] = grads[part * n : part * (n + 1)]
+    by_expand.start()
+    grad_act = side_sum(0, own, sent)
+
+    unit = unit_d[...]
+    grad = grad_act * slope(unit * vec_mid[2:3] + vec_mid[3:4])
+    g_dilate, sums_d = norm_back(
+        grad, unit, near_m.at[0], across_m.at[0], vec_mid[2:3] * inv_mid[1:2]
+    )
+    own_rows = slice(section_rate, section_rate + OWN_ROWS)
+    halo[own_rows] = g_dilate.reshape(OWN_ROWS, TILE_W, MID_OWN)
+    low, high = slice(0, section_rate), slice(section_rate + OWN_ROWS, 2 * section_rate + OWN_ROWS)
+    first, last = slice(section_rate, 2 * section_rate), slice(OWN_ROWS, section_rate + OWN_ROWS)
+    to_before = links.send(halo.at[first], halo.at[high], pix=spot.before)
+    to_after = links.send(halo.at[last], halo.at[low], pix=spot.after)
+    by_expand.along_z()
+    for d in (1, 3, 2):
+        links.arrive(project_sent[d], project_in.at[d - 1])
+        project_wide[spot.chan(-d)] = project_in[d - 1].astype(F32)
+    project_wide[j] = projects[j].astype(F32)
+    links.arrive(to_before, halo.at[high])
+    links.arrive(to_after, halo.at[low])
+    for a in range(3):
+        rows = halo[section_rate * (2 - a) : section_rate * (2 - a) + OWN_ROWS]
+        rows = rows.reshape(OWN, MID_OWN).astype(F32)
+        if a != 1:
+            rows = rows * keep[1 - a // 2]
+        for b in range(3):
+            moved = rows if b == 1 else col_shift(rows, -section_rate * (b - 1))
+            tap = 3 * a + b
+            taps[:, MID_OWN * tap : MID_OWN * (tap + 1)] = moved.astype(BF16)
+    sent = sides(1, lambda c: dot_nt(taps[...], wd_cat[mid_rows(c)]))
+    own = dot_nt(taps[...], wd_cat[mid_rows(j)])
+    for c in range(CHAN):
+        act = act_r[c, own_rows].reshape(OWN, MID_OWN)
+        grads = dot_tn(act, taps[...]).astype(BF16)
+        for n in range(8):
+            for tap in range(9):
+                by_dilate.parts[(*spot_of(8 * c + n), tap)] = grads[
+                    part * n : part * (n + 1), MID_OWN * tap : MID_OWN * (tap + 1)
+                ]
+    by_dilate.start()
+    grad_act = side_sum(1, own, sent)
+    by_expand.along_x()
+
+    unit = unit_r[...]
+    grad = grad_act * slope(unit * vec_mid[0:1] + vec_mid[1:2])
+    g_reduce, sums_r = norm_back(
+        grad, unit, near_m.at[1], across_m.at[1], vec_mid[0:1] * inv_mid[0:1]
+    )
+    mid_grads[...] = jnp.concatenate([sums_r[0:2], sums_d[0:2], jnp.zeros((4, MID_OWN), F32)], axis=0)
+    full[j] = g_reduce
+    sent = {d: links.send(full.at[j], full.at[j], chan=spot.chan(d)) for d in (2, 1, 3)}
+    by_dilate.along_z()
+    for t in range(TASKS):
+        for device in range(PIX):
+            rows = []
+            for start in range(40 * device, 40 * device + 40, 8):
+                b, src, d = start // 256, start // HEAD % CHAN, start % HEAD
+                rows.append(project_wide[src, BRANCH_PLACE[b], t, d : d + 8])
+            rows.append(jnp.zeros((8, HEAD), F32))
+            by_project.parts[(*spot_of(device), t)] = jnp.concatenate(rows, axis=0).astype(BF16)
+    by_project.start()
+    grad_expand[...] = by_expand.finish()
+    for d in (1, 3, 2):
+        links.arrive(sent[d], full.at[spot.chan(-d)])
+    g_reduce = jnp.concatenate([full[c] for c in range(CHAN)], axis=1)
+    weight = jnp.concatenate([wr_all[c] for c in range(CHAN)], axis=1)
+    grads = dot_tn(pixels[...], g_reduce).astype(BF16)
+    for c in range(CHAN):
+        for n in range(8):
+            by_reduce.parts[spot_of(4 * n + c)] = grads[
+                HEAD * n : HEAD * (n + 1), MID_OWN * c : MID_OWN * (c + 1)
+            ]
+    by_reduce.start()
+    grad_pixels[...] = (grad_summed + dot_nt(g_reduce, weight)).astype(BF16)
+    by_project.along_z()
+    by_reduce.along_z()
+    by_dilate.along_x()
+    by_reduce.along_x()
+    by_project.along_x()
+    reduce_out[...] = by_reduce.finish()
+
+    def last_copies():
+        return (
+            lambda: remote(
+                reduce_out, grad_reduce, last_sems.at[0], last_sems.at[1], pix=owner_i, chan=owner_j
+            ),
+            lambda: pltpu.make_async_copy(reduce_out, grad_reduce, last_sems.at[1]),
         )
-        product = jnp.einsum(form, window, kernel[tap_index], preferred_element_type=jnp.float32)
-        product = product * seam_rows[row_step + 1][:, None, None]
-        result = product if result is None else result + product
-    return result
-
-
-def dilated_transpose(extended, kernel, dilation, reach_rows, seam_rows, row_count, form):
-    result = None
-    for tap_index, (row_step, col_step) in enumerate(tap_offsets):
-        window = tap_read(
-            extended, reach_rows - row_step * dilation, -col_step * dilation, row_count
-        )
-        product = jnp.einsum(form, window, kernel[tap_index], preferred_element_type=jnp.float32)
-        product = product * seam_rows[1 - row_step][:, None, None]
-        result = product if result is None else result + product
-    return result
-
-
-def dilated_weight_grad(extended, grad_pre, dilation, reach_rows, seam_rows, row_count):
-    products = []
-    for tap_index, (row_step, col_step) in enumerate(tap_offsets):
-        window = tap_read(
-            extended, reach_rows + row_step * dilation, col_step * dilation, row_count
-        )
-        masked = grad_pre * seam_rows[row_step + 1].astype(jnp.bfloat16)[:, None, None]
-        products.append(
-            jnp.einsum("rwc,rwd->cd", window, masked, preferred_element_type=jnp.float32)
-        )
-    return jnp.stack(products)
-
-
-def norm_forward(pre_act, scale_gain, shift_bias, pixel_total):
-    first_sum, second_sum = in_one(
-        (jnp.sum(pre_act, axis=(0, 1)), jnp.sum(pre_act * pre_act, axis=(0, 1))), "pix"
-    )
-    center = first_sum / pixel_total
-    variance = second_sum / pixel_total - center * center
-    inv_std = lax.rsqrt(variance + eps)
-    unit_act = (pre_act - center) * inv_std
-    return (unit_act * scale_gain + shift_bias, unit_act, inv_std)
-
-
-def norm_backward(grad_out, unit_act, inv_std, scale_gain, pixel_total):
-    grad_bias, grad_gain = in_one(
-        (jnp.sum(grad_out, axis=(0, 1)), jnp.sum(grad_out * unit_act, axis=(0, 1))), "pix"
-    )
-    grad_pre = (
-        scale_gain
-        * inv_std
-        * (grad_out - grad_bias / pixel_total - unit_act * grad_gain / pixel_total)
-    )
-    return (grad_pre, grad_gain, grad_bias)
-
-
-def silu_slope(pre_act):
-    logistic = jax.nn.sigmoid(pre_act)
-    return logistic * (1.0 + pre_act * (1.0 - logistic))
+
+    away, here = last_copies()
+    pl.when(jnp.logical_not(stays))(lambda: away().start())
+    pl.when(stays)(lambda: here().start())
+    grad_dilate[...] = by_dilate.finish()
+    grad_project[...] = by_project.finish()
+    pltpu.make_async_copy(reduce_out, grad_reduce, last_sems.at[1]).wait()
+    pl.when(jnp.logical_not(stays))(lambda: away().wait_send())
+    links.finish()
+
+
+def section_backward(*operands):
+    whole = pl.BlockSpec(memory_space=pltpu.VMEM)
+    shape = jax.ShapeDtypeStruct
+    dma = pltpu.SemaphoreType.DMA
+    mid, feat = (OWN, MID_OWN), (OWN, FEAT_OWN)
+    return pl.pallas_call(
+        section_backward_kernel,
+        in_specs=[whole] * len(operands),
+        out_specs=[whole] * 8,
+        out_shape=[
+            shape(feat, BF16),
+            shape((8, MID_OWN), F32),
+            shape((8, FEAT_OWN), F32),
+            shape((HEAD, MID_OWN), F32),
+            shape((9, 16, MID_OWN), F32),
+            shape((16, FEAT_OWN), F32),
+            shape((TASKS, 48, HEAD), F32),
+            shape((8, BRANCH), F32),
+        ],
+        scratch_shapes=[
+            pltpu.VMEM((2, 3, *mid), BF16),
+            pltpu.VMEM((2, 3, *mid), BF16),
+            pltpu.VMEM((OWN_ROWS + 2 * section_rate, TILE_W, MID_OWN), BF16),
+            pltpu.VMEM((OWN, 9 * MID_OWN), BF16),
+            pltpu.VMEM((CHAN, *mid), BF16),
+            pltpu.VMEM((CHAN, 16, FEAT_OWN), BF16),
+            pltpu.VMEM((3, 16, FEAT_OWN), BF16),
+            pltpu.VMEM((3, 5, TASKS, HEAD, HEAD), BF16),
+            pltpu.VMEM((CHAN, 5, TASKS, HEAD, HEAD), F32),
+            pltpu.VMEM((HEAD, MID_OWN), F32),
+            pltpu.VMEM((2, GROUP, 8, MID_OWN), F32),
+            pltpu.VMEM((2, 4, 8, MID_OWN), F32),
+            pltpu.VMEM((GROUP, 8, FEAT_OWN), F32),
+            pltpu.VMEM((4, 8, FEAT_OWN), F32),
+            pltpu.VMEM((GROUP, 8, 2 * MID_OWN), F32),
+            pltpu.VMEM((4, 8, 2 * MID_OWN), F32),
+            *scatter_scratch(16, FEAT_OWN),
+            *scatter_scratch(9, 16, MID_OWN),
+            *scatter_scratch(TASKS, 48, HEAD),
+            *scatter_scratch(HEAD, MID_OWN),
+            dma((96,)),
+            dma((96,)),
+            dma((2,)),
+        ],
+        compiler_params=pltpu.CompilerParams(
+            collective_id=6, has_side_effects=True, vmem_limit_bytes=VMEM_LIMIT
+        ),
+        cost_estimate=pl.CostEstimate(
+            flops=4_000_000_000, bytes_accessed=250_000_000, transcendentals=0
+        ),
+        name="section_backward",
+    )(*operands)
 
 
 def shards(
@@ -839,52 +1235,35 @@
     project_weight,
     cotangent,
 ):
-    highest = lax.Precision.HIGHEST
     pixel_count = pixels.shape[0]
-    row_count = pixel_count // TILE_W
-    pixel_total = pixel_count * lax.axis_size("pix")
-    tile_count = tile_number.shape[0] // 40 + 1
-    margin = section_rate
     device = lax.axis_index("pix")
-    first_row = lax.axis_index("pix") * row_count
-    tile_pad = jnp.pad(tile_number, (margin, margin), constant_values=-1)
-    own_tiles = lax.dynamic_slice_in_dim(tile_pad, first_row + margin, row_count)
-    row_onehot = (own_tiles[:, None] == jnp.arange(tile_count)[None, :]).astype(jnp.float32)
-    every_tile = (tile_number[:, None] == jnp.arange(tile_count)[None, :]).astype(jnp.float32)
-    tile_sizes = jnp.sum(every_tile, axis=0) * TILE_W
-    local_in = pixels.reshape(row_count, TILE_W, -1)
-    full_in = widen(local_in)
-    pre_reduce = jnp.einsum(
-        "rwc,cd->rwd", full_in, reduce_weight, preferred_element_type=jnp.float32
-    )
-    norm_reduce, unit_reduce, scale_reduce = norm_forward(
-        pre_reduce, reduce_gain, reduce_bias, pixel_total
-    )
-    act_reduce = jax.nn.silu(norm_reduce).astype(jnp.bfloat16)
-    section_seams = seam_masks(tile_pad, first_row, margin, section_rate, row_count)
-    reduce_ext = extend_rows(widen(act_reduce), section_rate, move_forward)
-    pre_dilate = dilated_apply(
-        reduce_ext,
-        dilate_weight,
-        section_rate,
-        section_rate,
-        section_seams,
-        row_count,
-        "rwc,cd->rwd",
-    )
-    norm_dilate, unit_dilate, scale_dilate = norm_forward(
-        pre_dilate, dilate_gain, dilate_bias, pixel_total
-    )
-    act_dilate = jax.nn.silu(norm_dilate).astype(jnp.bfloat16)
-    full_dilate = widen(act_dilate)
-    pre_expand = jnp.einsum(
-        "rwc,cd->rwd", full_dilate, expand_weight, preferred_element_type=jnp.float32
-    )
-    norm_expand, unit_expand, scale_expand = norm_forward(
-        pre_expand, expand_gain, expand_bias, pixel_total
-    )
-    summed = norm_expand + local_in.astype(jnp.float32)
-    trunk_out = jax.nn.silu(summed).astype(jnp.bfloat16)
+    first_row = device * OWN_ROWS
+    tile_count = 8
+    tiles = jnp.arange(tile_count)
+    tile_sizes = jnp.sum((tile_number[:, None] == tiles[None, :]).astype(F32), axis=0) * TILE_W
+    sizes = jnp.broadcast_to(jnp.maximum(tile_sizes, 1.0)[:, None], (tile_count, 128))
+    tile_pad = jnp.pad(tile_number, (section_rate, section_rate), constant_values=-1)
+    tiles_at = [
+        lax.dynamic_slice_in_dim(tile_pad, first_row + section_rate * (1 + step), OWN_ROWS)
+        for step in (-1, 0, 1)
+    ]
+    row_onehot = (tiles_at[1][:, None] == tiles[None, :]).astype(F32)
+    keep_rows = jnp.stack([tiles_at[0] == tiles_at[1], tiles_at[2] == tiles_at[1]]).astype(F32)
+    keep_section = jnp.broadcast_to(
+        keep_rows[:, :, None, None], (2, OWN_ROWS, TILE_W, MID_OWN)
+    ).reshape(2, OWN, MID_OWN)
+    vec_mid = jnp.pad(
+        jnp.stack([reduce_gain, reduce_bias, dilate_gain, dilate_bias]), ((0, 4), (0, 0))
+    )
+    vec_feat = jnp.pad(jnp.stack([expand_gain, expand_bias]), ((0, 6), (0, 0)))
+    (
+        trunk_out, unit_reduce, unit_dilate, unit_expand, act_reduce, act_dilate, reduce_all, inv_mid,
+        inv_feat, mean_all,
+    ) = section_forward(
+        pixels, reduce_weight, dilate_weight, expand_weight, vec_mid, vec_feat, keep_section,
+        row_onehot.T, sizes,
+    )
+    tile_mean = jnp.moveaxis(mean_all[:, :tile_count], 0, 1).reshape(tile_count, -1)
     group_x, group_z, core = device // GROUP, device % GROUP // 2, device % 2
     placed = jnp.array(PLACED_ROWS, jnp.int32)
     place_key = tile_number[placed] + 8 * (placed % 6)
@@ -899,15 +1278,8 @@
     keep_own = lax.dynamic_slice_in_dim(keep_all, device * OWN_ROWS, OWN_ROWS, axis=1)
     keep_group = lax.dynamic_slice_in_dim(keep_all, group_x * GROUP_ROWS, GROUP_ROWS, axis=1)
     place_tiles = lax.dynamic_slice_in_dim(tile_number[placed], device * OWN_ROWS, OWN_ROWS)
-    place_onehot = (place_tiles[:, None] == jnp.arange(tile_count)[None, :]).astype(jnp.float32)
+    place_onehot = (place_tiles[:, None] == tiles[None, :]).astype(F32)
     x_ext = gather_rows(trunk_out, REACH, 1, "gather_trunk")
-    row_sums = jnp.sum(trunk_out, axis=1, dtype=jnp.float32)
-    tile_sums = of_everyone_2(
-        jnp.dot(row_onehot.T, row_sums, precision=highest).astype(jnp.bfloat16), "pix"
-    )
-    tile_mean = lax.all_gather(
-        (tile_sums / tile_sizes[:, None]).astype(jnp.bfloat16), "chan", axis=1, tiled=True
-    )
     pre_pooled = jnp.einsum("kc,tdc->ktd", tile_mean, pooled_weight, preferred_element_type=F32)
     pooled_act = jax.nn.silu(pre_pooled).astype(jnp.bfloat16).reshape(tile_count, BRANCH)
     pooled_rows = jnp.dot(
@@ -969,9 +1341,7 @@
     trunk_parts = heads_input_grad(
         keep_own, g_own, g_low, g_high, atrous_weight.reshape(TASKS, 3, 3, 3, HEAD, -1), point_weight
     )
-    trunk_grad = return_rows(
-        trunk_parts.reshape(CHAN, OWN_ROWS, TILE_W, -1), 3, "return_trunk"
-    ).astype(jnp.float32)
+    trunk_grad = return_rows(trunk_parts.reshape(CHAN, OWN_ROWS, TILE_W, -1), 3, "return_trunk")
     maps_parts = jnp.moveaxis(
         head_part.reshape(OWN_ROWS, TILE_W, TASKS, CHAN, HEAD), 3, 0
     ).reshape(CHAN, OWN_ROWS, TILE_W, BRANCH)
@@ -994,118 +1364,37 @@
     grad_point_weight = jnp.transpose(
         sum_over_groups(point_parts).reshape(HEAD, TASKS, HEAD), (1, 0, 2)
     )
-    pooled_total = of_everyone(jnp.dot(place_onehot.T, pool_rows, precision=highest), "pix")
-    grad_pooled_pre = (
-        pooled_total.reshape(tile_count, TASKS, HEAD) * silu_slope(pre_pooled)
-    ).astype(jnp.bfloat16)
+    (
+        grad_pixels, mid_grads, feat_grads, grad_reduce, grad_dilate, grad_expand, grad_project,
+        grad_pooled,
+    ) = section_backward(
+        trunk_grad, pixels, unit_reduce, unit_dilate, unit_expand, act_reduce, act_dilate, reduce_all,
+        jnp.moveaxis(dilate_weight, 0, 1).reshape(-1, 9 * MID_OWN), expand_weight, vec_mid, vec_feat,
+        inv_mid, inv_feat, keep_section, pool_rows, place_onehot.T, row_onehot, sizes,
+        pre_pooled.reshape(tile_count, BRANCH), pooled_weight.reshape(BRANCH, -1), grad_project,
+    )
     grad_pooled_weight = jnp.einsum(
-        "kc,ktd->tcd", tile_mean, grad_pooled_pre, preferred_element_type=jnp.float32
-    )
-    mean_part = jnp.einsum(
-        "ktd,tdc->kc", grad_pooled_pre, pooled_weight, preferred_element_type=jnp.float32
-    )
-    (mean_grad,) = collect((mean_part.reshape(tile_count, 1, -1),))
-    mean_rows = jnp.dot(row_onehot, mean_grad[:, 0] / tile_sizes[:, None], precision=highest)
-    project_sides = lax.all_to_all(
-        jnp.moveaxis(
-            grad_project[jnp.array(BRANCH_PLACE)].reshape(5, TASKS, HEAD, CHAN, HEAD), 3, 0
-        ),
-        "chan",
-        0,
-        0,
-        tiled=True,
-    )
-    grad_project = jnp.transpose(project_sides, (2, 1, 0, 3, 4)).reshape(TASKS, -1, HEAD)
-    grad_trunk = trunk_grad + mean_rows[:, None, :]
-    grad_summed = grad_trunk * silu_slope(summed)
-    grad_expand_pre, grad_expand_gain, grad_expand_bias = norm_backward(
-        grad_summed, unit_expand, scale_expand, expand_gain, pixel_total
-    )
-    grad_expand_pre = grad_expand_pre.astype(jnp.bfloat16)
-    expand_grad = jnp.einsum(
-        "rwc,rwd->cd", full_dilate, grad_expand_pre, preferred_element_type=jnp.float32
-    )
-    (grad_dilate_act,) = collect(
-        (
-            jnp.einsum(
-                "rwd,cd->rwc", grad_expand_pre, expand_weight, preferred_element_type=jnp.float32
-            ),
-        )
-    )
-    grad_dilate_pre, grad_dilate_gain, grad_dilate_bias = norm_backward(
-        grad_dilate_act * silu_slope(norm_dilate),
-        unit_dilate,
-        scale_dilate,
-        dilate_gain,
-        pixel_total,
-    )
-    grad_dilate_pre = grad_dilate_pre.astype(jnp.bfloat16)
-    dilate_grad = dilated_weight_grad(
-        reduce_ext, grad_dilate_pre, section_rate, section_rate, section_seams, row_count
-    )
-    dilate_ext = extend_rows(grad_dilate_pre, section_rate, move_backward)
-    (grad_reduce_act,) = collect(
-        (
-            dilated_transpose(
-                dilate_ext,
-                dilate_weight,
-                section_rate,
-                section_rate,
-                section_seams,
-                row_count,
-                "rwd,cd->rwc",
-            ),
-        )
-    )
-    grad_reduce_pre, grad_reduce_gain, grad_reduce_bias = norm_backward(
-        grad_reduce_act * silu_slope(norm_reduce),
-        unit_reduce,
-        scale_reduce,
-        reduce_gain,
-        pixel_total,
-    )
-    grad_reduce_pre = grad_reduce_pre.astype(jnp.bfloat16)
-    reduce_grad = jnp.einsum(
-        "rwc,rwd->cd", full_in, grad_reduce_pre, preferred_element_type=jnp.float32
-    )
-    (grad_input,) = collect(
-        (
-            jnp.einsum(
-                "rwd,cd->rwc", grad_reduce_pre, reduce_weight, preferred_element_type=jnp.float32
-            ),
-        )
-    )
-    grad_pixels = (grad_input + grad_summed).astype(jnp.bfloat16).reshape(pixel_count, -1)
-    summed_grads = (
-        lax.psum_scatter(
-            reduce_grad[None].astype(jnp.bfloat16), "pix", scatter_dimension=1, tiled=True
-        ).astype(jnp.float32),
-        lax.psum_scatter(
-            dilate_grad.astype(jnp.bfloat16), "pix", scatter_dimension=1, tiled=True
-        ).astype(jnp.float32),
-        lax.psum_scatter(
-            expand_grad[None].astype(jnp.bfloat16), "pix", scatter_dimension=1, tiled=True
-        ).astype(jnp.float32),
-        lax.psum_scatter(
-            grad_project.astype(jnp.bfloat16), "pix", scatter_dimension=1, tiled=True
-        ).astype(jnp.float32),
+        "kc,ktd->tcd",
+        tile_mean,
+        grad_pooled.reshape(tile_count, TASKS, HEAD).astype(BF16),
+        preferred_element_type=F32,
     )
     return (
         task_maps,
         grad_pixels,
-        summed_grads[0][0],
-        grad_reduce_gain,
-        grad_reduce_bias,
-        summed_grads[1],
-        grad_dilate_gain,
-        grad_dilate_bias,
-        summed_grads[2][0],
-        grad_expand_gain,
-        grad_expand_bias,
+        grad_reduce,
+        mid_grads[1],
+        mid_grads[0],
+        grad_dilate,
+        mid_grads[3],
+        mid_grads[2],
+        grad_expand,
+        feat_grads[1],
+        feat_grads[0],
         grad_point_weight,
         grad_atrous_weight,
         grad_pooled_weight,
-        summed_grads[3],
+        grad_project[:, :40],
     )
 
 

time: 781 us -> 535 us (0.69)
  the two profiles are of different devices: /device:TPU:7 before, /device:TPU:1 now
where the time goes in v2:
time: 535 us; the launch traced here: 527 us
  Pallas kernels  374 us (70%)
  local copies, waits for them, and re-layouts  53.1 us (10%)
  starting transfers between devices  50.8 us (9%)
  waiting for transfers between devices  29.6 us (6%)
  other arithmetic  15 us (3%)
    pallas_call x1, Pallas kernels, section_backward(): pl.pallas_call(section_backward_kernel, in_specs=[whole] * len(operands),...  93.7 us
    pallas_call x1, Pallas kernels, section_forward(): pl.pallas_call(section_forward_kernel, in_specs=[whole] * 9, out_specs=[w...  83.7 us
    pallas_call x2, Pallas kernels, return_rows(): pl.pallas_call(return_rows_kernel, out_shape=jax.ShapeDtypeStruct(rows, B...  56.1 us
    pallas_call x2, Pallas kernels, gather_rows(): pl.pallas_call(functools.partial(gather_rows_kernel, reach), out_shape=ja...  47.7 us
    pallas_call x1, Pallas kernels, heads_weight_grad(): pl.pallas_call(heads_weight_grad_kernel, grid=(9,), in_specs=[smem] + [hb...  45.1 us
    ppermute x6, waiting for transfers between devices, sum_over_groups(): total = total + lax.ppermute(sent, 'pix', route).astype(jnp.float32)  29.6 us
    pallas_call x1, Pallas kernels, heads_forward(): pl.pallas_call(heads_forward_kernel, grid=(9,), in_specs=[pl.BlockSpec(me...  27.6 us
    pallas_call x1, Pallas kernels, heads_input_grad(): pl.pallas_call(heads_input_grad_kernel, grid=(2, 3), in_specs=[pl.BlockSp...  20.5 us
  transfers between devices with their start and end apart: 25, of which 2 were waited for; matrix products, arithmetic and copies ran while one was open for 10% of the time, Pallas kernels for 62%

profile of v2, /device:TPU:1, one launch (start us, length us, event | category | flops | bytes accessed | tf_op | source)
XLA Modules:
  0.0 527.0 jit_solution(4694722474910656718)
XLA Ops:
  0.6 2.0 reshape.142
  5.1 5.2 all-to-all-start
  10.4 1.9 gather_fusion
  16.3 83.7 %section_forward.1 = (bf16[8,64,512]{2,1,0:T(8,128)(2,1)}, f32[512,128]{1,0:T(8,128)}, f32[512,128]{1,0:T(8,128)}, f32[512,512]{1,0:T(8,128)}, bf16[4,16,64,128]...) custom-call(bf16[512,512]{1,0:T(8,128)(2,1)} %pixels.3, ...), custom_call_target="tpu_custom_call" | custom-call | flops 2000000000 | bytes 120000000 | tf_op jit(solution)/shard_map/section_forward/pallas_call | solution.py:872
  100.0 31.4 %gather_trunk.1.x_hbm = bf16[4,14,64,512]{3,2,1,0:T(8,128)(2,1)} custom-call(bf16[8,64,512]{2,1,0:T(8,128)(2,1)} %get-tuple-element.39.src), custom_call_target="tpu_custom_call" | custom-call | bytes 60000000 | tf_op jit(solution)/shard_map/gather_trunk/pallas_call | solution.py:211
  131.5 3.1 constant_dynamic-slice_fusion
  134.6 3.4 collective-permute-start.2
  138.0 3.9 collective-permute-start.3
  148.0 16.2 %gather_maps.1 = bf16[4,8,64,192]{3,2,1,0:T(8,128)(2,1)} custom-call(bf16[8,64,192]{2,1,0:T(8,128)(2,1)} %copy.113.src), custom_call_target="tpu_custom_call" | custom-call | bytes 60000000 | tf_op jit(solution)/shard_map/gather_maps/pallas_call | solution.py:211
  164.2 1.9 copy.114
  174.5 2.2 broadcast_multiply_fusion.spread
  177.5 27.6 %heads_forward.1 = (bf16[512,768]{1,0:T(8,128)(2,1)}, bf16[512,768]{1,0:T(8,128)(2,1)}, bf16[4,5,3,64,64]{4,3,2,1,0:T(8,128)(2,1)}, f32[8,256]{1,0:T(8,128)}) custom-call(s32[9,8]{1,0:T(8,128)} %constant_dynamic-slice_fusion.5.keep, bf16[4,14,64,512]{3,2,1,0:T(8,128)(2,1)} %gather_trunk.1.x_hbm, bf16[3,3,3,3,64,2048]{5,4,3,2,1,0:T(8,128)(2,1)} %bitcast.118, ...), custom_call_target="tpu_custom_call" | custom-call | flops 12000000000 | bytes 28000000 | tf_op jit(solution)/shard_map/heads_forward/pallas_call | solution.py:421
  205.0 3.8 collective-permute-start.9
  208.8 8.1 %collective-permute-start.10 = (bf16[8,64,768]{2,1,0:T(8,128)(2,1)}, bf16[8,64,768]{2,1,0:T(8,128)(2,1)}, u32[]{:S(2)}, u32[]{:S(2)}) collective-permute-start(bf16[8,64,768]{2,1,0:T(8,128)(2,1)} %bitcast.21.mid.refs_8_), channel_id=1, source_target_pairs={{0,4},{1,5},{2,6},{3,7},{4,0},{5,1},{6,2},{7,3},{8,12},{9,13},{10,... | collective-permute-start | bytes 2359304 | tf_op jit(solution)/shard_map/ppermute | solution.py:1321
  217.1 1.8 fusion.31
  219.0 4.4 collective-permute-start
  228.6 2.8 reshape.150
  234.6 23.8 %return_maps.1 = bf16[8,64,192]{2,1,0:T(8,128)(2,1)} custom-call(bf16[4,8,64,192]{3,2,1,0:T(8,128)(2,1)} %copy.119.src), custom_call_target="tpu_custom_call" | custom-call | bytes 60000000 | tf_op jit(solution)/shard_map/return_maps/pallas_call | solution.py:295
  260.5 3.1 collective-permute-start.4
  264.6 20.5 %heads_input_grad.1 = bf16[4,512,512]{2,1,0:T(8,128)(2,1)} custom-call(s32[9,8]{1,0:T(8,128)} %constant_dynamic-slice_fusion.5.keep, bf16[8,64,768]{2,1,0:T(8,128)(2,1)} %bitcast.21.mid.refs_8_, bf16[3,64,768]{2,1,0:T(8,128)(2,1)} %collective-permute-done.low, bf16[3,64,768]{2,1,0:T(8,128)(2,1)} %collective-permute-done.1.high, ...), custom_call_target="tpu_custom_call" | custom-call | flops 12000000000 | bytes 28000000 | tf_op jit(solution)/shard_map/heads_input_grad/pallas_call | solution.py:520
  285.2 32.4 %return_trunk.1.trunk_grad = bf16[8,64,512]{2,1,0:T(8,128)(2,1)} custom-call(bf16[4,8,64,512]{3,2,1,0:T(8,128)(2,1)} %bitcast.99), custom_call_target="tpu_custom_call" | custom-call | bytes 60000000 | tf_op jit(solution)/shard_map/return_trunk/pallas_call | solution.py:295
  320.2 3.8 collective-permute-start.16
  325.4 2.8 collective-permute-start.17
  328.2 93.7 %section_backward.1 = (bf16[512,512]{1,0:T(8,128)(2,1)}, f32[8,128]{1,0:T(8,128)}, f32[8,512]{1,0:T(8,128)}, f32[64,128]{1,0:T(8,128)}, f32[9,16,128]{2,1,0:T(8,...) custom-call(bf16[8,64,512]{2,1,0:T(8,128)(2,1)} %return_trunk.1.trunk_grad, ...), custom_call_target="tpu_custom_call" | custom-call | flops 4000000000 | bytes 250000000 | tf_op jit(solution)/shard_map/section_backward/pallas_call | solution.py:1170
  425.0 45.1 %heads_weight_grad.1 = (bf16[4,9,64,576]{3,2,1,0:T(8,128)(2,1)}, bf16[4,64,192]{2,1,0:T(8,128)(2,1)}) custom-call(s32[9,64]{1,0:T(8,128)} %constant_dynamic-slice_fusion.4.keep, bf16[4,8,64,128]{3,2,1,0:T(8,128)(2,1)} %get-tuple-element.143.refs_0_, bf16[4,8,64,128]{3,2,1,0:T(8,128)(2,1)} %collective-permute-done.2.refs_1_, ...), custom_call_target="tpu_custom_call" | custom-call | flops 12000000000 | bytes 28000000 | tf_op jit(solution)/shard_map/heads_weight_grad/pallas_call | solution.py:643
  470.9 3.4 collective-permute-start.20
  474.4 2.7 dynamic-slice_bitcast_fusion.2
  479.9 3.6 collective-permute-start.19
  484.6 28.3 %collective-permute-done.19 = bf16[64,192]{1,0:T(8,128)(2,1)S(1)} collective-permute-done((bf16[64,192]{1,0:T(8,128)(2,1)S(1)}, bf16[64,192]{1,0:T(8,128)(2,1)S(1)}, u32[]{:S(2)}, u32[]{:S(2)}) %collective-permute-start.19) | collective-permute-done | bytes 24608 | tf_op jit(solution)/shard_map/ppermute | solution.py:1358
  515.8 2.8 fusion.1
  518.6 2.6 copy.125
  521.3 2.6 copy.126
  (171 shorter events, 50.7 us)
Async XLA Ops:
  5.1 164.2 %all-to-all-start = ((bf16[4,2,30720]{2,1,0:T(2,128)(2,1)}), bf16[4,2,30720]{2,1,0:T(2,128)(2,1)S(1)}, u32[]{:S(2)}, u32[]{:S(2)}) async-start(bf16[4,2,30720]{2,1,0:T(2,128)(2,1)} %reshape.180), calls=%async_computation | async-start | bytes 983040 | tf_op jit(solution)/shard_map/all_to_all | solution.py:1299
  131.5 10.5 %copy-start.24 = (s32[3]{0:T(128)S(1)}, s32[3]{0:T(128)}, u32[]{:S(2)}) copy-start(s32[3]{0:T(128)} %param.21) | copy-start | bytes 40
  131.5 13.6 %copy-start.13 = (bf16[4,16,512]{2,1,0:T(8,128)(2,1)S(1)}, bf16[4,16,512]{2,1,0:T(8,128)(2,1)}, u32[]{:S(2)}) copy-start(bf16[4,16,512]{2,1,0:T(8,128)(2,1)} %get-tuple-element.40) | copy-start | bytes 196612
  131.5 13.6 %copy-start.8 = (bf16[3,512,64]{1,2,0:T(8,128)(2,1)S(1)}, bf16[3,512,64]{1,2,0:T(8,128)(2,1)}, u32[]{:S(2)}) copy-start(bf16[3,512,64]{1,2,0:T(8,128)(2,1)} %param.35) | copy-start | bytes 589828
  131.5 13.7 %copy-start.2 = (bf16[3,64,2048]{2,1,0:T(8,128)(2,1)S(1)}, bf16[3,64,2048]{2,1,0:T(8,128)(2,1)}, u32[]{:S(2)}) copy-start(bf16[3,64,2048]{2,1,0:T(8,128)(2,1)} %param.33) | copy-start | bytes 2359300
  134.6 84.4 %collective-permute-start.2 = (bf16[4,8,64,128]{3,2,1,0:T(8,128)(2,1)}, bf16[4,8,64,128]{3,2,1,0:T(8,128)(2,1)}, u32[]{:S(2)}, u32[]{:S(2)}) collective-permute-start(bf16[4,8,64,128]{3,2,1,0:T(8,128)(2,1)} %get-tuple-element.142), channel_id=1, source_target_pairs={{0,2},{1,3},{2,0},{3,1},{4,6},{5,7},{6,4},{7,5},{8,10},{9,11},{10,... | collective-permute-start | bytes 1572872 | tf_op jit(solution)/shard_map/ppermute | solution.py:1320
  138.0 85.4 %collective-permute-start.3 = (bf16[4,8,64,128]{3,2,1,0:T(8,128)(2,1)}, bf16[4,8,64,128]{3,2,1,0:T(8,128)(2,1)}, u32[]{:S(2)}, u32[]{:S(2)}) collective-permute-start(bf16[4,8,64,128]{3,2,1,0:T(8,128)(2,1)} %get-tuple-element.141), channel_id=1, source_target_pairs={{0,4},{1,5},{2,6},{3,7},{4,0},{5,1},{6,2},{7,3},{8,12},{9,13},{10,... | collective-permute-start | bytes 1572872 | tf_op jit(solution)/shard_map/ppermute | solution.py:1320
  205.0 20.1 %copy-start.1 = (bf16[9,512,128]{2,1,0:T(8,128)(2,1)S(1)}, bf16[9,512,128]{2,1,0:T(8,128)(2,1)}, u32[]{:S(2)}) copy-start(bf16[9,512,128]{2,1,0:T(8,128)(2,1)} %wd.1) | copy-start | bytes 3538948
  205.0 58.6 %collective-permute-start.9 = (bf16[8,64,768]{2,1,0:T(8,128)(2,1)}, bf16[8,64,768]{2,1,0:T(8,128)(2,1)}, u32[]{:S(2)}, u32[]{:S(2)}) collective-permute-start(bf16[8,64,768]{2,1,0:T(8,128)(2,1)} %bitcast.21.mid.refs_8_), channel_id=1, source_target_pairs={{0,2},{1,3},{2,0},{3,1},{4,6},{5,7},{6,4},{7,5},{8,10},{9,11},{10,... | collective-permute-start | bytes 2359304 | tf_op jit(solution)/shard_map/ppermute | solution.py:1321
  208.8 55.3 %collective-permute-start.10 = (bf16[8,64,768]{2,1,0:T(8,128)(2,1)}, bf16[8,64,768]{2,1,0:T(8,128)(2,1)}, u32[]{:S(2)}, u32[]{:S(2)}) collective-permute-start(bf16[8,64,768]{2,1,0:T(8,128)(2,1)} %bitcast.21.mid.refs_8_), channel_id=1, source_target_pairs={{0,4},{1,5},{2,6},{3,7},{4,0},{5,1},{6,2},{7,3},{8,12},{9,13},{10,... | collective-permute-start | bytes 2359304 | tf_op jit(solution)/shard_map/ppermute | solution.py:1321
  217.0 47.2 %collective-permute-start.11 = (bf16[8,64,768]{2,1,0:T(8,128)(2,1)}, bf16[8,64,768]{2,1,0:T(8,128)(2,1)}, u32[]{:S(2)}, u32[]{:S(2)}) collective-permute-start(bf16[8,64,768]{2,1,0:T(8,128)(2,1)} %bitcast.21.mid.refs_8_), channel_id=1, source_target_pairs={{0,6},{1,7},{2,4},{3,5},{4,2},{5,3},{6,0},{7,1},{8,14},{9,15},{10,... | collective-permute-start | bytes 2359304 | tf_op jit(solution)/shard_map/ppermute | solution.py:1321
  219.0 41.6 %collective-permute-start = (bf16[3,64,768]{2,1,0:T(8,128)(2,1)}, bf16[3,64,768]{2,1,0:T(8,128)(2,1)}, u32[]{:S(2)}, u32[]{:S(2)}) collective-permute-start(bf16[3,64,768]{2,1,0:T(8,128)(2,1)} %bitcast.22), channel_id=1, source_target_pairs={{0,1},{1,2},{2,3},{3,4},{4,5},{5,6},{6,7},{7,8},{8,9},{9,10},{10,1... | collective-permute-start | bytes 884744 | tf_op jit(solution)/shard_map/ppermute | solution.py:1311
  223.4 40.2 %collective-permute-start.1 = (bf16[3,64,768]{2,1,0:T(8,128)(2,1)S(1)}, bf16[3,64,768]{2,1,0:T(8,128)(2,1)}, u32[]{:S(2)}, u32[]{:S(2)}) collective-permute-start(bf16[3,64,768]{2,1,0:T(8,128)(2,1)S(1)} %bitcast.101), channel_id=1, source_target_pairs={{0,31},{1,0},{2,1},{3,2},{4,3},{5,4},{6,5},{7,6},{8,7},{9,8},{10,9... | collective-permute-start | bytes 884744 | tf_op jit(solution)/shard_map/ppermute | solution.py:1312
  234.6 25.9 %copy-start.5 = (bf16[4,8,64,128]{3,2,1,0:T(8,128)(2,1)S(1)}, bf16[4,8,64,128]{3,2,1,0:T(8,128)(2,1)}, u32[]{:S(2)}) copy-start(bf16[4,8,64,128]{3,2,1,0:T(8,128)(2,1)} %get-tuple-element.140) | copy-start | bytes 1572868
  260.5 57.0 %collective-permute-start.4 = (bf16[4,8,64,128]{3,2,1,0:T(8,128)(2,1)S(1)}, bf16[4,8,64,128]{3,2,1,0:T(8,128)(2,1)}, u32[]{:S(2)}, u32[]{:S(2)}) collective-permute-start(bf16[4,8,64,128]{3,2,1,0:T(8,128)(2,1)S(1)} %copy-done.5), channel_id=1, source_target_pairs={{0,6},{1,7},{2,4},{3,5},{4,2},{5,3},{6,0},{7,1},{8,14},{9,15},{10,... | collective-permute-start | bytes 1572872 | tf_op jit(solution)/shard_map/ppermute | solution.py:1320
  263.6 54.0 %collective-permute-start.12 = (bf16[8,64,768]{2,1,0:T(8,128)(2,1)}, bf16[8,64,768]{2,1,0:T(8,128)(2,1)S(1)}, u32[]{:S(2)}, u32[]{:S(2)}) collective-permute-start(bf16[8,64,768]{2,1,0:T(8,128)(2,1)} %bitcast.21.mid.refs_8_), channel_id=1, source_target_pairs={{0,1},{1,0},{2,3},{3,2},{4,5},{5,4},{6,7},{7,6},{8,9},{9,8},{10,11... | collective-permute-start | bytes 2359304 | tf_op jit(solution)/shard_map/ppermute | solution.py:1323
  263.6 54.5 %collective-permute-start.13 = (bf16[8,64,768]{2,1,0:T(8,128)(2,1)}, bf16[8,64,768]{2,1,0:T(8,128)(2,1)S(1)}, u32[]{:S(2)}, u32[]{:S(2)}) collective-permute-start(bf16[8,64,768]{2,1,0:T(8,128)(2,1)} %collective-permute-done.9.refs_9_), channel_id=1, source_target_pairs={{0,1},{1,0},{2,3},{3,2},{4,5},{5,4},{6,7},{7,6},{8,9},{9,8},{10,11... | collective-permute-start | bytes 2359304 | tf_op jit(solution)/shard_map/ppermute | solution.py:1323
  264.1 54.1 %collective-permute-start.14 = (bf16[8,64,768]{2,1,0:T(8,128)(2,1)}, bf16[8,64,768]{2,1,0:T(8,128)(2,1)}, u32[]{:S(2)}, u32[]{:S(2)}) collective-permute-start(bf16[8,64,768]{2,1,0:T(8,128)(2,1)} %collective-permute-done.10.refs_10_), channel_id=1, source_target_pairs={{0,1},{1,0},{2,3},{3,2},{4,5},{5,4},{6,7},{7,6},{8,9},{9,8},{10,11... | collective-permute-start | bytes 2359304 | tf_op jit(solution)/shard_map/ppermute | solution.py:1323
  264.2 54.5 %collective-permute-start.15 = (bf16[8,64,768]{2,1,0:T(8,128)(2,1)}, bf16[8,64,768]{2,1,0:T(8,128)(2,1)}, u32[]{:S(2)}, u32[]{:S(2)}) collective-permute-start(bf16[8,64,768]{2,1,0:T(8,128)(2,1)} %collective-permute-done.11.refs_11_), channel_id=1, source_target_pairs={{0,1},{1,0},{2,3},{3,2},{4,5},{5,4},{6,7},{7,6},{8,9},{9,8},{10,11... | collective-permute-start | bytes 2359304 | tf_op jit(solution)/shard_map/ppermute | solution.py:1323
  285.2 32.4 %copy-start.4 = (bf16[4,8,64,128]{3,2,1,0:T(8,128)(2,1)S(1)}, bf16[4,8,64,128]{3,2,1,0:T(8,128)(2,1)}, u32[]{:S(2)}) copy-start(bf16[4,8,64,128]{3,2,1,0:T(8,128)(2,1)} %get-tuple-element.143.refs_0_) | copy-start | bytes 1572868
  317.5 7.9 %collective-permute-start.5 = (bf16[4,8,64,128]{3,2,1,0:T(8,128)(2,1)S(1)}, bf16[4,8,64,128]{3,2,1,0:T(8,128)(2,1)S(1)}, u32[]{:S(2)}, u32[]{:S(2)}) collective-permute-start(bf16[4,8,64,128]{3,2,1,0:T(8,128)(2,1)S(1)} %copy-done.4), channel_id=1, source_target_pairs={{0,1},{1,0},{2,3},{3,2},{4,5},{5,4},{6,7},{7,6},{8,9},{9,8},{10,11... | collective-permute-start | bytes 1572872 | tf_op jit(solution)/shard_map/ppermute | solution.py:1322
  317.7 106.6 %collective-permute-start.6 = (bf16[4,8,64,128]{3,2,1,0:T(8,128)(2,1)}, bf16[4,8,64,128]{3,2,1,0:T(8,128)(2,1)}, u32[]{:S(2)}, u32[]{:S(2)}) collective-permute-start(bf16[4,8,64,128]{3,2,1,0:T(8,128)(2,1)} %collective-permute-done.2.refs_1_), channel_id=1, source_target_pairs={{0,1},{1,0},{2,3},{3,2},{4,5},{5,4},{6,7},{7,6},{8,9},{9,8},{10,11... | collective-permute-start | bytes 1572872 | tf_op jit(solution)/shard_map/ppermute | solution.py:1322
  318.2 106.1 %collective-permute-start.7 = (bf16[4,8,64,128]{3,2,1,0:T(8,128)(2,1)}, bf16[4,8,64,128]{3,2,1,0:T(8,128)(2,1)}, u32[]{:S(2)}, u32[]{:S(2)}) collective-permute-start(bf16[4,8,64,128]{3,2,1,0:T(8,128)(2,1)} %collective-permute-done.3.refs_2_), channel_id=1, source_target_pairs={{0,1},{1,0},{2,3},{3,2},{4,5},{5,4},{6,7},{7,6},{8,9},{9,8},{10,11... | collective-permute-start | bytes 1572872 | tf_op jit(solution)/shard_map/ppermute | solution.py:1322
  318.3 106.0 %collective-permute-start.8 = (bf16[4,8,64,128]{3,2,1,0:T(8,128)(2,1)}, bf16[4,8,64,128]{3,2,1,0:T(8,128)(2,1)}, u32[]{:S(2)}, u32[]{:S(2)}) collective-permute-start(bf16[4,8,64,128]{3,2,1,0:T(8,128)(2,1)} %collective-permute-done.4.refs_3_), channel_id=1, source_target_pairs={{0,1},{1,0},{2,3},{3,2},{4,5},{5,4},{6,7},{7,6},{8,9},{9,8},{10,11... | collective-permute-start | bytes 1572872 | tf_op jit(solution)/shard_map/ppermute | solution.py:1322
  320.2 104.1 %collective-permute-start.16 = (bf16[3,64,768]{2,1,0:T(8,128)(2,1)S(1)}, bf16[3,64,768]{2,1,0:T(8,128)(2,1)}, u32[]{:S(2)}, u32[]{:S(2)}) collective-permute-start(bf16[3,64,768]{2,1,0:T(8,128)(2,1)S(1)} %fusion.13), channel_id=1, source_target_pairs={{0,8},{1,9},{2,10},{3,11},{4,12},{5,13},{6,14},{7,15},{8,16},{9,17... | collective-permute-start | bytes 884744 | tf_op jit(solution)/shard_map/ppermute | solution.py:1333
  325.4 98.8 %collective-permute-start.17 = (bf16[3,64,768]{2,1,0:T(8,128)(2,1)S(1)}, bf16[3,64,768]{2,1,0:T(8,128)(2,1)S(1)}, u32[]{:S(2)}, u32[]{:S(2)}) collective-permute-start(bf16[3,64,768]{2,1,0:T(8,128)(2,1)S(1)} %fusion.7), channel_id=1, source_target_pairs={{0,24},{1,25},{2,26},{3,27},{4,28},{5,29},{6,30},{7,31},{8,0},{9,1... | collective-permute-start | bytes 884744 | tf_op jit(solution)/shard_map/ppermute | solution.py:1338
  470.9 12.5 %collective-permute-start.20 = (bf16[64,192]{1,0:T(8,128)(2,1)S(1)}, bf16[64,192]{1,0:T(8,128)(2,1)S(1)}, u32[]{:S(2)}, u32[]{:S(2)}) collective-permute-start(bf16[64,192]{1,0:T(8,128)(2,1)S(1)} %get-tuple-element.150), channel_id=1, source_target_pairs={{0,24},{1,25},{2,26},{3,27},{4,28},{5,29},{6,30},{7,31},{8,0},{9,1... | collective-permute-start | bytes 73736 | tf_op jit(solution)/shard_map/ppermute | solution.py:1358
  477.0 38.8 %collective-permute-start.23 = (bf16[9,64,576]{2,1,0:T(8,128)(2,1)}, bf16[9,64,576]{2,1,0:T(8,128)(2,1)S(1)}, u32[]{:S(2)}, u32[]{:S(2)}) collective-permute-start(bf16[9,64,576]{2,1,0:T(8,128)(2,1)} %get-tuple-element.145), channel_id=1, source_target_pairs={{0,24},{1,25},{2,26},{3,27},{4,28},{5,29},{6,30},{7,31},{8,0},{9,1... | collective-permute-start | bytes 1990664 | tf_op jit(solution)/shard_map/ppermute | solution.py:1358
  477.1 38.8 %collective-permute-start.22 = (bf16[9,64,576]{2,1,0:T(8,128)(2,1)S(1)}, bf16[9,64,576]{2,1,0:T(8,128)(2,1)S(1)}, u32[]{:S(2)}, u32[]{:S(2)}) collective-permute-start(bf16[9,64,576]{2,1,0:T(8,128)(2,1)S(1)} %get-tuple-element.146), channel_id=1, source_target_pairs={{0,16},{1,17},{2,18},{3,19},{4,20},{5,21},{6,22},{7,23},{8,24},{9,... | collective-permute-start | bytes 1990664 | tf_op jit(solution)/shard_map/ppermute | solution.py:1358
  477.1 38.8 %collective-permute-start.21 = (bf16[9,64,576]{2,1,0:T(8,128)(2,1)S(1)}, bf16[9,64,576]{2,1,0:T(8,128)(2,1)}, u32[]{:S(2)}, u32[]{:S(2)}) collective-permute-start(bf16[9,64,576]{2,1,0:T(8,128)(2,1)S(1)} %get-tuple-element.144), channel_id=1, source_target_pairs={{0,8},{1,9},{2,10},{3,11},{4,12},{5,13},{6,14},{7,15},{8,16},{9,17... | collective-permute-start | bytes 1990664 | tf_op jit(solution)/shard_map/ppermute | solution.py:1358
  479.9 33.0 %collective-permute-start.19 = (bf16[64,192]{1,0:T(8,128)(2,1)S(1)}, bf16[64,192]{1,0:T(8,128)(2,1)S(1)}, u32[]{:S(2)}, u32[]{:S(2)}) collective-permute-start(bf16[64,192]{1,0:T(8,128)(2,1)S(1)} %get-tuple-element.151), channel_id=1, source_target_pairs={{0,16},{1,17},{2,18},{3,19},{4,20},{5,21},{6,22},{7,23},{8,24},{9,... | collective-permute-start | bytes 73736 | tf_op jit(solution)/shard_map/ppermute | solution.py:1358
  483.5 30.8 %collective-permute-start.18 = (bf16[64,192]{1,0:T(8,128)(2,1)S(1)}, bf16[64,192]{1,0:T(8,128)(2,1)S(1)}, u32[]{:S(2)}, u32[]{:S(2)}) collective-permute-start(bf16[64,192]{1,0:T(8,128)(2,1)S(1)} %get-tuple-element.149), channel_id=1, source_target_pairs={{0,8},{1,9},{2,10},{3,11},{4,12},{5,13},{6,14},{7,15},{8,16},{9,17... | collective-permute-start | bytes 73736 | tf_op jit(solution)/shard_map/ppermute | solution.py:1358
  (20 other events, 141.7 us)

commit v3 on v2

--- a/solution.py
+++ b/solution.py
@@ -313,6 +313,75 @@
     )(parts)
 
 
+GROUP = 8
+GROUP_ROWS = GROUP * OWN_ROWS
+
+
+class Posts:
+    def __init__(self, send_sems, recv_sems):
+        self.send_sems, self.recv_sems, self.made = send_sems, recv_sems, []
+
+    def copy(self, n, make):
+        src, dst, where = make()
+        return remote(src, dst, self.send_sems.at[n], self.recv_sems.at[n], **where)
+
+    def post(self, make):
+        n = len(self.made)
+        self.made.append(make)
+        self.copy(n, make).start()
+        return n
+
+    def arrive(self, n, dst):
+        beside = {"chan": int_rem(lax.axis_index("chan") + 1, CHAN)}
+        remote(dst, dst, self.send_sems.at[n], self.recv_sems.at[n], **beside).wait_recv()
+
+    def finish(self):
+        for n, make in enumerate(self.made):
+            self.copy(n, make).wait_send()
+
+
+def greet(peers, more=0):
+    barrier = pltpu.get_barrier_semaphore()
+    for where in peers:
+        signal(barrier, **where)
+    pl.semaphore_wait(barrier, len(peers) + more)
+
+
+class Spot:
+    def __init__(self):
+        self.i, self.j = lax.axis_index("pix"), lax.axis_index("chan")
+        self.group, self.k = int_div(self.i, GROUP), int_rem(self.i, GROUP)
+        self.z, self.core = int_div(self.k, 2), int_rem(self.k, 2)
+        self.before, self.after = int_rem(self.i + PIX - 1, PIX), int_rem(self.i + 1, PIX)
+        self.mate = self.i + 1 - 2 * self.core
+
+    def chan(self, distance):
+        return int_rem(self.j + CHAN + distance, CHAN)
+
+    def in_group(self, distance):
+        return int_rem(self.k + GROUP + distance, GROUP)
+
+    def pix_in_group(self, distance):
+        return GROUP * self.group + self.in_group(distance)
+
+    def x_of(self, distance):
+        return int_rem(self.group + 4 + distance, 4)
+
+    def pix_in_x(self, distance):
+        return GROUP * self.x_of(distance) + self.k
+
+    def z_of(self, distance):
+        return int_rem(self.z + 4 + distance, 4)
+
+    def pix_in_z(self, distance):
+        return GROUP * self.group + 2 * self.z_of(distance) + self.core
+
+    def sum_peers(self):
+        return [{"pix": self.pix_in_group(d)} for d in range(1, GROUP)] + [
+            {"pix": self.pix_in_x(d)} for d in range(1, 4)
+        ]
+
+
 def dot_nt(a, b):
     return lax.dot_general(a, b, (((1,), (1,)), ((), ())), preferred_element_type=F32)
 
@@ -335,12 +404,41 @@
 
 
 def heads_forward_kernel(
-    keep, x_hbm, kernel, point, spread, maps, pooled, grad_pre, head_part, grad_project, pool_rows,
-    x, acc, pre, sems,
+    keep, x_hbm, maps_own, kernel, point, spread, pooled,
+    grad_pre, head_part, grad_project, pool_rows, x_group,
+    x, acc, pre, maps_in, relay, sems, ss_row, rs_row, send_sems, recv_sems, own_sem,
 ):
     step = pl.program_id(0)
     rate, row_tap = step // 3, step % 3
     first = REACH + (row_tap - 1) * (rate + 1)
+    spot = Spot()
+    posts = Posts(send_sems, recv_sems)
+    i, j = spot.i, spot.j
+    halves = (slice(0, OWN_ROWS // 2), slice(OWN_ROWS // 2, OWN_ROWS))
+    chans = (slice(0, 2), slice(2, 4))
+
+    def x_slice(distance, which=slice(0, CHAN)):
+        lanes = pl.ds(pl.multiple_of(128 * spot.z_of(distance), 128), 128)
+        return x_hbm.at[which, REACH : REACH + OWN_ROWS, :, lanes]
+
+    def x_rows(distance, core, which=slice(0, CHAN)):
+        return x_group.at[which, pl.ds(OWN_ROWS * (2 * spot.z_of(distance) + core), OWN_ROWS)]
+
+    def own_copy():
+        return pltpu.make_async_copy(x_slice(0), x_rows(0, spot.core), own_sem.at[0])
+
+    def row_send(s):
+        place = place_of(OWN_ROWS * i + s)
+        target, slot = int_div(place, OWN_ROWS), int_rem(place, OWN_ROWS)
+        return target, (
+            lambda: remote(
+                maps_own.at[s], maps_in.at[j, slot], ss_row.at[s], rs_row.at[slot], pix=target
+            ),
+            lambda: pltpu.make_async_copy(maps_own.at[s], maps_in.at[j, slot], rs_row.at[slot]),
+        )
+
+    ways = ((1, {"chan": spot.chan(1)}), (-1, {"chan": spot.chan(-1)}))
+    marks = {}
 
     @pl.when(step == 0)
     def _():
@@ -353,8 +451,90 @@
         ]
         for copy in copies:
             copy.start()
+        own_copy().start()
+        barrier = pltpu.get_barrier_semaphore()
+        expected = 0
+        for s in range(OWN_ROWS):
+            origin = int_div(row_of(OWN_ROWS * i + s), OWN_ROWS)
+
+            @pl.when(origin != i)
+            def _():
+                signal(barrier, pix=origin)
+
+            target = int_div(place_of(OWN_ROWS * i + s), OWN_ROWS)
+            expected = expected + (target != i).astype(jnp.int32)
+        greet(
+            [where for _, where in ways]
+            + [{"pix": spot.pix_in_z(d)} for d in (1, -1)]
+            + [{"pix": spot.mate}],
+            expected,
+        )
+        for s in range(OWN_ROWS):
+            target, (away, here) = row_send(s)
+            pl.when(target != i)(lambda: away().start())
+            pl.when(target == i)(lambda: here().start())
+        for way, d in enumerate((1, -1)):
+            marks["relay", way] = posts.post(
+                lambda way=way, d=d: (
+                    x_slice(2, chans[way]), relay.at[way], {"pix": spot.pix_in_z(d)}
+                )
+            )
+        for d in (1, -1):
+            marks["z", d] = posts.post(
+                lambda d=d: (x_slice(d), x_rows(0, spot.core), {"pix": spot.pix_in_z(d)})
+            )
+        marks["mate", 0] = posts.post(
+            lambda: (x_slice(0), x_rows(0, spot.core), {"pix": spot.mate})
+        )
         for copy in copies:
             copy.wait()
+
+    @pl.when(step == 1)
+    def _():
+        for s in range(OWN_ROWS):
+            pltpu.make_async_copy(maps_own.at[s], maps_in.at[j, s], rs_row.at[s]).wait()
+        for half in range(2):
+            for d, where in ways:
+                marks["maps", d, half] = posts.post(
+                    lambda half=half, where=where: (
+                        maps_in.at[j, halves[half]], maps_in.at[j, halves[half]], where
+                    )
+                )
+
+    @pl.when(step == 3)
+    def _():
+        for way, d in enumerate((1, -1)):
+            posts.arrive(marks["relay", way], relay.at[way])
+            marks["far", way] = posts.post(
+                lambda way=way, d=d: (
+                    relay.at[way],
+                    x_rows(-d, spot.core, chans[way]),
+                    {"pix": spot.pix_in_z(d)},
+                )
+            )
+
+    @pl.when(step == 4)
+    def _():
+        for d, _ in ways:
+            for half in range(2):
+                source = spot.chan(-d)
+                posts.arrive(marks["maps", d, half], maps_in.at[source, halves[half]])
+        for half, (d, where) in enumerate(ways):
+            marks["maps far", half] = posts.post(
+                lambda d=d, half=half, where=where: (
+                    maps_in.at[spot.chan(-d), halves[half]],
+                    maps_in.at[spot.chan(-d), halves[half]],
+                    where,
+                )
+            )
+
+    @pl.when(step == 6)
+    def _():
+        for d in (1, -1):
+            posts.arrive(marks["z", d], x_rows(-d, spot.core))
+            marks["mate", d] = posts.post(
+                lambda d=d: (x_rows(-d, spot.core), x_rows(-d, spot.core), {"pix": spot.mate})
+            )
 
     def rows_from(start):
         return x[pl.ds(start, OWN_ROWS)].reshape(OWN_ROWS * TILE_W, -1)
@@ -384,7 +564,14 @@
 
     @pl.when(step == 8)
     def _():
-        cot = maps[...]
+        for half in range(2):
+            posts.arrive(marks["maps far", half], maps_in.at[spot.chan(2), halves[half]])
+        for way in range(2):
+            posts.arrive(marks["far", way], x_rows(2, spot.core, chans[way]))
+        marks["mate", 2] = posts.post(
+            lambda: (x_rows(2, spot.core), x_rows(2, spot.core), {"pix": spot.mate})
+        )
+        cot = jnp.concatenate([maps_in[c].reshape(-1, BRANCH) for c in range(CHAN)], axis=1)
         head = None
         for which in range(5):
             if which < 4:
@@ -399,7 +586,7 @@
             grads = dot_tn(joined, cot)
             for t in range(TASKS):
                 for c in range(CHAN):
-                    lane = 256 * t + HEAD * c
+                    lane = BRANCH * c + HEAD * t
                     grad_project[c, which, t] = grads[
                         HEAD * t : HEAD * (t + 1), lane : lane + HEAD
                     ].astype(BF16)
@@ -411,56 +598,144 @@
                 sums = jnp.sum(back.reshape(OWN_ROWS, TILE_W, BRANCH), axis=1)
                 pool_rows[:, :BRANCH] = sums
                 pool_rows[:, BRANCH:] = jnp.zeros((OWN_ROWS, 256 - BRANCH), F32)
-        head_part[...] = head.astype(BF16)
-
-
-def heads_forward(keep, x_ext, kernels, point, spread, maps, pooled):
+        for c in range(CHAN):
+            head_part[c] = head[:, BRANCH * c : BRANCH * (c + 1)].astype(BF16)
+        for d in (0, 1, -1, 2):
+            other = 1 - spot.core
+            posts.arrive(marks["mate", d], x_rows(-d, other))
+        own_copy().wait()
+        for s in range(OWN_ROWS):
+            target, (away, here) = row_send(s)
+            pl.when(target != i)(lambda: away().wait_send())
+        posts.finish()
+
+
+def heads_forward(keep, x_ext, maps_own, kernels, point, spread, pooled):
     pixels = OWN_ROWS * TILE_W
     feat = point.shape[2]
     whole = pl.BlockSpec(memory_space=pltpu.VMEM)
+    hbm = pl.BlockSpec(memory_space=pl.ANY)
+    dma = pltpu.SemaphoreType.DMA
     return pl.pallas_call(
         heads_forward_kernel,
         grid=(9,),
         in_specs=[
             pl.BlockSpec(memory_space=pltpu.SMEM),
-            pl.BlockSpec(memory_space=pl.ANY),
+            hbm,
+            whole,
             pl.BlockSpec((TASKS, 1, 1, 3, HEAD, feat), lambda s: (0, s // 3, s % 3, 0, 0, 0)),
             whole,
             whole,
             whole,
-            whole,
         ],
-        out_specs=[whole] * 4,
+        out_specs=[whole] * 4 + [hbm],
         out_shape=[
             jax.ShapeDtypeStruct((pixels, 4 * BRANCH), BF16),
-            jax.ShapeDtypeStruct((pixels, 256 * TASKS), BF16),
+            jax.ShapeDtypeStruct((CHAN, pixels, BRANCH), BF16),
             jax.ShapeDtypeStruct((CHAN, 5, TASKS, HEAD, HEAD), BF16),
             jax.ShapeDtypeStruct((OWN_ROWS, 256), F32),
+            jax.ShapeDtypeStruct((CHAN, GROUP_ROWS, TILE_W, 128), BF16),
         ],
         scratch_shapes=[
             pltpu.VMEM((EXT_ROWS, TILE_W, feat), BF16),
             pltpu.VMEM((3, pixels, BRANCH), F32),
             pltpu.VMEM((4, pixels, BRANCH), F32),
-            pltpu.SemaphoreType.DMA((CHAN,)),
+            pltpu.VMEM((CHAN, OWN_ROWS, TILE_W, BRANCH), BF16),
+            pltpu.VMEM((2, 2, OWN_ROWS, TILE_W, 128), BF16),
+            dma((CHAN,)),
+            dma((OWN_ROWS,)),
+            dma((OWN_ROWS,)),
+            dma((16,)),
+            dma((16,)),
+            dma((1,)),
         ],
-        compiler_params=pltpu.CompilerParams(vmem_limit_bytes=VMEM_LIMIT),
+        compiler_params=pltpu.CompilerParams(
+            collective_id=2, has_side_effects=True, vmem_limit_bytes=VMEM_LIMIT
+        ),
         cost_estimate=pl.CostEstimate(
             flops=12_000_000_000, bytes_accessed=28_000_000, transcendentals=0
         ),
         name="heads_forward",
-    )(keep, x_ext, kernels, point, spread, maps, pooled)
+    )(keep, x_ext, maps_own, kernels, point, spread, pooled)
 
 
 PAD = 24
 PADDED = PAD + TILE_W + PAD
 
 
-def heads_input_grad_kernel(keep, mid, low, high, kernel, point, out, wide, taps, acc):
+def heads_input_grad_kernel(
+    keep, mid, parts, kernel, point, out, g_group, maps_out,
+    wide, taps, acc, edges, maps_in, maps_sum, ss_row, rs_row, send_sems, recv_sems, own_sem,
+):
     n, rate = pl.program_id(0), pl.program_id(1)
-
-    @pl.when((n == 0) & (rate == 0))
+    step = 3 * n + rate
+    spot = Spot()
+    posts = Posts(send_sems, recv_sems)
+    i, j = spot.i, spot.j
+    low, high = edges.at[0], edges.at[1]
+    half_rows = OWN_ROWS // 2
+    marks = {}
+
+    def g_rows(distance, core, half=None):
+        start = OWN_ROWS * (2 * spot.z_of(distance) + core)
+        if half is None:
+            return g_group.at[pl.ds(start, OWN_ROWS)]
+        return g_group.at[pl.ds(start + half_rows * half, half_rows)]
+
+    def own_copy():
+        return pltpu.make_async_copy(mid, g_rows(0, spot.core), own_sem.at[0])
+
+    def row_send(s):
+        row = row_of(OWN_ROWS * i + s)
+        target, slot = int_div(row, OWN_ROWS), int_rem(row, OWN_ROWS)
+        return target, (
+            lambda: remote(
+                maps_sum.at[s], maps_out.at[slot], ss_row.at[s], rs_row.at[slot], pix=target
+            ),
+            lambda: pltpu.make_async_copy(maps_sum.at[s], maps_out.at[slot], rs_row.at[slot]),
+        )
+
+    @pl.when(step == 0)
     def _():
+        own_copy().start()
+        barrier = pltpu.get_barrier_semaphore()
+        expected = 0
+        for s in range(OWN_ROWS):
+            origin = int_div(place_of(OWN_ROWS * i + s), OWN_ROWS)
+
+            @pl.when(origin != i)
+            def _():
+                signal(barrier, pix=origin)
+
+            target = int_div(row_of(OWN_ROWS * i + s), OWN_ROWS)
+            expected = expected + (target != i).astype(jnp.int32)
+        greet(
+            [{"chan": spot.chan(d)} for d in (1, 2, 3)]
+            + [{"pix": spot.pix_in_z(d)} for d in (1, -1)]
+            + [{"pix": p} for p in (spot.mate, spot.before, spot.after)],
+            expected,
+        )
+        marks["low"] = posts.post(
+            lambda: (mid.at[OWN_ROWS - REACH :], low, {"pix": spot.after})
+        )
+        marks["high"] = posts.post(lambda: (mid.at[:REACH], high, {"pix": spot.before}))
+        for d in (2, 1, 3):
+            marks["maps", d] = posts.post(
+                lambda d=d: (parts.at[spot.chan(d)], maps_in.at[d - 1], {"chan": spot.chan(d)})
+            )
+        for half in range(2):
+            for d in (1, -1):
+                marks["z", d, half] = posts.post(
+                    lambda half=half, d=d: (
+                        mid.at[half_rows * half : half_rows * (half + 1)],
+                        g_rows(0, spot.core, half),
+                        {"pix": spot.pix_in_z(d)},
+                    )
+                )
+        marks["mate", 0] = posts.post(lambda: (mid, g_rows(0, spot.core), {"pix": spot.mate}))
         wide[...] = jnp.zeros_like(wide)
+        posts.arrive(marks["low"], low)
+        posts.arrive(marks["high"], high)
         for start, part in ((0, low), (REACH, mid), (REACH + OWN_ROWS, high)):
             held = part[...].astype(F32)
             for which in range(3):
@@ -495,6 +770,37 @@
 
         lax.fori_loop(0, OWN_ROWS, one_row, 0)
 
+    @pl.when(step == 3)
+    def _():
+        for d in (1, 3, 2):
+            posts.arrive(marks["maps", d], maps_in.at[d - 1])
+        for s in range(OWN_ROWS):
+            held = parts[j, s].astype(F32)
+            for d in (1, 2, 3):
+                held = held + maps_in[d - 1, s].astype(F32)
+            maps_sum[s] = held.astype(BF16)
+            target, (away, here) = row_send(s)
+            pl.when(target != i)(lambda: away().start())
+            pl.when(target == i)(lambda: here().start())
+
+    @pl.when(step == 4)
+    def _():
+        for half, d in enumerate((1, -1)):
+            posts.arrive(marks["z", d, half], g_rows(-d, spot.core, half))
+            marks["far", half] = posts.post(
+                lambda half=half, d=d: (
+                    g_rows(-d, spot.core, half),
+                    g_rows(-d, spot.core, half),
+                    {"pix": spot.pix_in_z(d)},
+                )
+            )
+        for half, d in enumerate((-1, 1)):
+            posts.arrive(marks["z", d, half], g_rows(-d, spot.core, half))
+        for d in (1, -1):
+            marks["mate", d] = posts.post(
+                lambda d=d: (g_rows(-d, spot.core), g_rows(-d, spot.core), {"pix": spot.mate})
+            )
+
     product = dot_nn(taps[rate, :, : 27 * HEAD], kernel[...].reshape(27 * HEAD, -1))
 
     @pl.when(rate == 0)
@@ -512,11 +818,30 @@
         for c in range(out.shape[0]):
             out[c] = total[:, 512 * c : 512 * (c + 1)].astype(BF16)
 
-
-def heads_input_grad(keep, grad_mid, grad_low, grad_high, kernels, point):
+    @pl.when(step == 5)
+    def _():
+        for half in range(2):
+            posts.arrive(marks["far", half], g_rows(2, spot.core, half))
+        marks["mate", 2] = posts.post(
+            lambda: (g_rows(2, spot.core), g_rows(2, spot.core), {"pix": spot.mate})
+        )
+        for d in (0, 1, -1, 2):
+            posts.arrive(marks["mate", d], g_rows(-d, 1 - spot.core))
+        own_copy().wait()
+        for s in range(OWN_ROWS):
+            pltpu.make_async_copy(maps_sum.at[s], maps_out.at[s], rs_row.at[s]).wait()
+            target, (away, here) = row_send(s)
+            pl.when(target != i)(lambda: away().wait_send())
+        posts.finish()
+
+
+def heads_input_grad(keep, grad_mid, head_part, kernels, point):
     pixels = OWN_ROWS * TILE_W
     block = 1024
     whole = pl.BlockSpec(memory_space=pltpu.VMEM)
+    hbm = pl.BlockSpec(memory_space=pl.ANY)
+    dma = pltpu.SemaphoreType.DMA
+    maps = (OWN_ROWS, TILE_W, BRANCH)
     return pl.pallas_call(
         heads_input_grad_kernel,
         grid=(2, 3),
@@ -524,145 +849,77 @@
             pl.BlockSpec(memory_space=pltpu.SMEM),
             whole,
             whole,
-            whole,
             pl.BlockSpec((TASKS, 1, 3, 3, HEAD, block), lambda n, r: (0, r, 0, 0, 0, n)),
             pl.BlockSpec((TASKS, HEAD, block), lambda n, r: (0, 0, n)),
         ],
-        out_specs=pl.BlockSpec((block // 512, pixels, 512), lambda n, r: (n, 0, 0)),
-        out_shape=jax.ShapeDtypeStruct((CHAN, pixels, 512), BF16),
+        out_specs=[
+            pl.BlockSpec((block // 512, pixels, 512), lambda n, r: (n, 0, 0)),
+            hbm,
+            hbm,
+        ],
+        out_shape=[
+            jax.ShapeDtypeStruct((CHAN, pixels, 512), BF16),
+            jax.ShapeDtypeStruct((GROUP_ROWS, TILE_W, 4 * BRANCH), BF16),
+            jax.ShapeDtypeStruct(maps, BF16),
+        ],
         scratch_shapes=[
             pltpu.VMEM((9, EXT_ROWS, PADDED, 2 * HEAD), F32),
             pltpu.VMEM((3, pixels, 28 * HEAD), BF16),
             pltpu.VMEM((pixels, block), F32),
+            pltpu.VMEM((2, REACH, TILE_W, 4 * BRANCH), BF16),
+            pltpu.VMEM((CHAN - 1, *maps), BF16),
+            pltpu.VMEM(maps, BF16),
+            dma((OWN_ROWS,)),
+            dma((OWN_ROWS,)),
+            dma((16,)),
+            dma((16,)),
+            dma((1,)),
         ],
-        compiler_params=pltpu.CompilerParams(vmem_limit_bytes=VMEM_LIMIT),
+        compiler_params=pltpu.CompilerParams(
+            collective_id=3, has_side_effects=True, vmem_limit_bytes=VMEM_LIMIT
+        ),
         cost_estimate=pl.CostEstimate(
             flops=12_000_000_000, bytes_accessed=28_000_000, transcendentals=0
         ),
         name="heads_input_grad",
-    )(keep, grad_mid, grad_low, grad_high, kernels, point)
-
-
-GROUP = 8
-GROUP_ROWS = GROUP * OWN_ROWS
-
-
-def heads_weight_grad_kernel(keep, *refs):
-    x_parts, g_parts, (g_low, g_high) = refs[:8], refs[8:16], refs[16:18]
-    out, out_point, x_all, x_wide, x_now, g_all, g_now, sems = refs[18:]
-    step = pl.program_id(0)
-    device = lax.axis_index("pix")
-    spot, core = int_div(int_rem(device, GROUP), 2), int_rem(device, 2)
-
-    @pl.when(step == 0)
-    def _():
-        copies = []
-        rows = lambda z, c: pl.ds(OWN_ROWS * (2 * z + c), OWN_ROWS)
-        for m in range(4):
-            z = spot ^ m
-            for src, c in ((x_parts[m], core), (x_parts[4 + m], 1 - core)):
-                for chan in range(CHAN):
-                    copies.append((src.at[chan], x_all.at[chan, rows(z, c)]))
-            for src, c in ((g_parts[m], core), (g_parts[4 + m], 1 - core)):
-                copies.append((src, g_all.at[pl.ds(REACH + OWN_ROWS * (2 * z + c), OWN_ROWS)]))
-        copies.append((g_low, g_all.at[0:REACH]))
-        copies.append((g_high, g_all.at[REACH + GROUP_ROWS : 2 * REACH + GROUP_ROWS]))
-        started = [
-            pltpu.make_async_copy(src, dst, sems.at[n]) for n, (src, dst) in enumerate(copies)
-        ]
-        for copy in started:
-            copy.start()
-        x_wide[:, 0:PAD] = jnp.zeros((GROUP_ROWS, PAD, 256), F32)
-        x_wide[:, PAD + TILE_W :] = jnp.zeros((GROUP_ROWS, PAD, 256), F32)
-        for copy in started:
-            copy.wait()
-
-        def widen_row(r, carry):
-            is_low = lax.broadcasted_iota(jnp.int32, (TILE_W, 128), 1) < HEAD
-            for pair in range(2):
-                first = x_all[2 * pair, r].astype(F32)
-                second = x_all[2 * pair + 1, r].astype(F32)
-                lower = jnp.where(is_low, first, pltpu.roll(second, HEAD, 1))
-                upper = jnp.where(is_low, pltpu.roll(first, HEAD, 1), second)
-                x_wide[r, PAD : PAD + TILE_W, 128 * pair : 128 * (pair + 1)] = jnp.where(
-                    core == 0, lower, upper
-                )
-            return carry
-
-        lax.fori_loop(0, GROUP_ROWS, widen_row, 0)
-
-    for which in range(3):
-
-        @pl.when(step == 3 * which)
-        def _():
-            def pick(r, carry):
-                for a in range(3):
-                    piece = g_all[
-                        r + REACH - (a - 1) * (which + 1), :, BRANCH * which : BRANCH * (which + 1)
-                    ]
-                    g_now[a, pl.ds(pl.multiple_of(r * TILE_W, TILE_W), TILE_W)] = jnp.where(
-                        keep[3 * which + 2 - a, r] > 0, piece, jnp.zeros_like(piece)
-                    )
-                return carry
-
-            lax.fori_loop(0, GROUP_ROWS, pick, 0)
-
-    for which, dilation in enumerate(head_rates):
-        for b in range(3):
-
-            @pl.when(step == 3 * which + b)
-            def _():
-                start = PAD + (b - 1) * dilation
-
-                def move(r, carry):
-                    x_now[pl.ds(pl.multiple_of(r * TILE_W, TILE_W), TILE_W)] = x_wide[
-                        r, start : start + TILE_W
-                    ].astype(BF16)
-                    return carry
-
-                lax.fori_loop(0, GROUP_ROWS, move, 0)
-
-    for a in range(3):
-        product = dot_tn(x_now[...], g_now[a]).astype(BF16)
-        for c in range(CHAN):
-            out[c, 0, :, BRANCH * a : BRANCH * (a + 1)] = product[HEAD * c : HEAD * (c + 1)]
-
-    @pl.when(step == 1)
-    def _():
-        grads = g_all[REACH : REACH + GROUP_ROWS, :, 3 * BRANCH :].reshape(-1, BRANCH)
-        product = dot_tn(x_now[...], grads).astype(BF16)
-        for c in range(CHAN):
-            out_point[c] = product[HEAD * c : HEAD * (c + 1)]
-
-
-def heads_weight_grad(keep, x_parts, g_parts, g_low, g_high):
-    pixels = GROUP_ROWS * TILE_W
-    whole = pl.BlockSpec(memory_space=pltpu.VMEM)
-    smem = pl.BlockSpec(memory_space=pltpu.SMEM)
-    hbm = pl.BlockSpec(memory_space=pl.ANY)
-    return pl.pallas_call(
-        heads_weight_grad_kernel,
-        grid=(9,),
-        in_specs=[smem] + [hbm] * 18,
-        out_specs=[pl.BlockSpec((CHAN, 1, HEAD, 3 * BRANCH), lambda s: (0, s, 0, 0)), whole],
-        out_shape=[
-            jax.ShapeDtypeStruct((CHAN, 9, HEAD, 3 * BRANCH), BF16),
-            jax.ShapeDtypeStruct((CHAN, HEAD, BRANCH), BF16),
-        ],
-        scratch_shapes=[
-            pltpu.VMEM((CHAN, GROUP_ROWS, TILE_W, 128), BF16),
-            pltpu.VMEM((GROUP_ROWS, PADDED, 256), F32),
-            pltpu.VMEM((pixels, 256), BF16),
-            pltpu.VMEM((GROUP_ROWS + 2 * REACH, TILE_W, 4 * BRANCH), BF16),
-            pltpu.VMEM((3, pixels, BRANCH), BF16),
-            pltpu.SemaphoreType.DMA((42,)),
-        ],
-        compiler_params=pltpu.CompilerParams(vmem_limit_bytes=VMEM_LIMIT),
-        cost_estimate=pl.CostEstimate(
-            flops=12_000_000_000, bytes_accessed=28_000_000, transcendentals=0
-        ),
-        name="heads_weight_grad",
-    )(keep, *x_parts, *g_parts, g_low, g_high)
+    )(keep, grad_mid, head_part, kernels, point)
+
+
+class GroupSum:
+    def __init__(self, out, relay_in, side_in, spot, links):
+        self.out, self.relay_in, self.side_in, self.spot, self.links = out, relay_in, side_in, spot, links
+        self.open, self.arrivals = [], []
+
+    def send(self, n, way):
+        spot, links, out = self.spot, self.links, self.out
+        relay = links.send(out.at[n, spot.x_of(2)], self.relay_in.at[n], pix=spot.pix_in_x(way))
+        side = links.send(
+            out.at[n, spot.x_of(-way)], self.side_in.at[n, 0], pix=spot.pix_in_x(-way)
+        )
+        self.arrivals.append((side, n, 0))
+        self.open.append((n, way, relay))
+
+    def relay(self):
+        for n, way, relay in self.open:
+            self.links.arrive(relay, self.relay_in.at[n])
+            target = self.spot.x_of(way)
+            both = self.out[n, target].astype(F32) + self.relay_in[n].astype(F32)
+            self.out[n, target] = both.astype(BF16)
+            side = self.links.send(
+                self.out.at[n, target], self.side_in.at[n, 1], pix=self.spot.pix_in_x(way)
+            )
+            self.arrivals.append((side, n, 1))
+        self.open = []
+
+    def finish(self, total):
+        for side, n, which in self.arrivals:
+            self.links.arrive(side, self.side_in.at[n, which])
+        for n in range(self.out.shape[0]):
+            total[n] = (
+                self.out[n, self.spot.group].astype(F32)
+                + self.side_in[n, 0].astype(F32)
+                + self.side_in[n, 1].astype(F32)
+            )
 
 
 class Links:
@@ -686,54 +943,13 @@
             copy.wait_send()
 
 
-def greet(peers, more=0):
-    barrier = pltpu.get_barrier_semaphore()
-    for where in peers:
-        signal(barrier, **where)
-    pl.semaphore_wait(barrier, len(peers) + more)
-
-
-class Spot:
-    def __init__(self):
-        self.i, self.j = lax.axis_index("pix"), lax.axis_index("chan")
-        self.group, self.k = int_div(self.i, GROUP), int_rem(self.i, GROUP)
-        self.z, self.core = int_div(self.k, 2), int_rem(self.k, 2)
-        self.before, self.after = int_rem(self.i + PIX - 1, PIX), int_rem(self.i + 1, PIX)
-        self.mate = self.i + 1 - 2 * self.core
-
-    def chan(self, distance):
-        return int_rem(self.j + CHAN + distance, CHAN)
-
-    def in_group(self, distance):
-        return int_rem(self.k + GROUP + distance, GROUP)
-
-    def pix_in_group(self, distance):
-        return GROUP * self.group + self.in_group(distance)
-
-    def x_of(self, distance):
-        return int_rem(self.group + 4 + distance, 4)
-
-    def pix_in_x(self, distance):
-        return GROUP * self.x_of(distance) + self.k
-
-    def z_of(self, distance):
-        return int_rem(self.z + 4 + distance, 4)
-
-    def pix_in_z(self, distance):
-        return GROUP * self.group + 2 * self.z_of(distance) + self.core
-
-    def sum_peers(self):
-        return [{"pix": self.pix_in_group(d)} for d in range(1, GROUP)] + [
-            {"pix": self.pix_in_x(d)} for d in range(1, 4)
-        ]
-
-
-def sum_over_pix(value, near, across, spot, links):
+def sum_over_pix(value, near, across, spot, links, meanwhile=lambda: None):
     near[spot.k] = value
     sent = [
         links.send(near.at[spot.k], near.at[spot.k], pix=spot.pix_in_group(d))
         for d in range(1, GROUP)
     ]
+    meanwhile()
     for d, n in zip(range(1, GROUP), sent):
         links.arrive(n, near.at[spot.in_group(-d)])
     total = near[0]
@@ -744,6 +960,7 @@
         links.send(across.at[spot.group], across.at[spot.group], pix=spot.pix_in_x(d))
         for d in range(1, 4)
     ]
+    meanwhile()
     for d, n in zip(range(1, 4), sent):
         links.arrive(n, across.at[spot.x_of(-d)])
     return across[0] + across[1] + across[2] + across[3]
@@ -969,15 +1186,19 @@
 def section_backward_kernel(
     trunk_grad, pixels, unit_r, unit_d, unit_e, act_r, act_d, wr_all, wd_cat, we, vec_mid, vec_feat,
     inv_mid, inv_feat, keep, pool_rows, place_rows, tile_cols, sizes, pre_pooled, pooled, projects,
-    grad_pixels, mid_grads, feat_grads, grad_reduce, grad_dilate, grad_expand, grad_project, grad_pooled,
-    *scratch,
+    keep_group, x_group, g_group, *refs,
 ):
     (
+        grad_pixels, mid_grads, feat_grads, grad_reduce, grad_dilate, grad_expand, grad_project,
+        grad_pooled, grad_atrous, grad_point,
+    ) = refs[:10]
+    scratch = refs[10:]
+    (
         side_out, side_in, halo, taps, full, mean_out, mean_in, project_in, project_wide, reduce_out,
-        near_m, across_m, near_f, across_f, near_p, across_p,
-    ) = scratch[:16]
-    send_sems, recv_sems, last_sems = scratch[-3:]
-    buffers = scratch[16:-3]
+        near_m, across_m, near_f, across_f, near_p, across_p, x_all, x_base, x_now, g_all, g_now,
+    ) = scratch[:21]
+    send_sems, recv_sems, last_sems, load_sems = scratch[-4:]
+    buffers = scratch[21:-4]
     spot = Spot()
     links = Links(send_sems, recv_sems)
     i, j = spot.i, spot.j
@@ -997,6 +1218,96 @@
     peers += [{"pix": spot.before}, {"pix": spot.after}]
     greet(peers, 1 - stays.astype(jnp.int32))
 
+    atrous_sum = GroupSum(*buffers[24:27], spot, links)
+    point_sum = GroupSum(*buffers[27:30], spot, links)
+    loads = [
+        pltpu.make_async_copy(x_group, x_all, load_sems.at[0]),
+        pltpu.make_async_copy(g_group, g_all.at[REACH : REACH + GROUP_ROWS], load_sems.at[1]),
+    ]
+    for load in loads:
+        load.start()
+    edges = [
+        (g_group.at[GROUP_ROWS - REACH :], g_all.at[:REACH], 1),
+        (g_group.at[:REACH], g_all.at[REACH + GROUP_ROWS :], -1),
+    ]
+    edges = [(links.send(src, dst, pix=spot.pix_in_x(d)), dst) for src, dst, d in edges]
+
+    def row_block(r):
+        return pl.ds(pl.multiple_of(r * TILE_W, TILE_W), TILE_W)
+
+    def take():
+        for load in loads:
+            load.wait()
+        for n, dst in edges:
+            links.arrive(n, dst)
+
+        def one_row(r, carry):
+            is_low = lax.broadcasted_iota(jnp.int32, (TILE_W, 2 * HEAD), 1) < HEAD
+            for pair in range(2):
+                first = x_all[2 * pair, r].astype(F32)
+                second = x_all[2 * pair + 1, r].astype(F32)
+                lower = jnp.where(is_low, first, pltpu.roll(second, HEAD, 1))
+                upper = jnp.where(is_low, pltpu.roll(first, HEAD, 1), second)
+                x_base[row_block(r), 2 * HEAD * pair : 2 * HEAD * (pair + 1)] = jnp.where(
+                    spot.core == 0, lower, upper
+                ).astype(BF16)
+            return carry
+
+        lax.fori_loop(0, GROUP_ROWS, one_row, 0, unroll=4)
+
+    def pick(which):
+        def one_row(r, carry):
+            pieces = []
+            for a in range(3):
+                piece = g_all[
+                    r + REACH - (a - 1) * (which + 1), :, BRANCH * which : BRANCH * (which + 1)
+                ]
+                pieces.append(
+                    jnp.where(keep_group[3 * which + 2 - a, r] > 0, piece, jnp.zeros_like(piece))
+                )
+            g_now[row_block(r)] = jnp.concatenate(pieces, axis=1)
+            return carry
+
+        lax.fori_loop(0, GROUP_ROWS, one_row, 0, unroll=4)
+
+    def multiply(which, b):
+        held = x_base
+        if b != 1:
+            held = x_now
+
+            def one_row(r, carry):
+                row = x_base[row_block(r)].astype(F32)
+                x_now[row_block(r)] = col_shift(row, (b - 1) * head_rates[which]).astype(BF16)
+                return carry
+
+            lax.fori_loop(0, GROUP_ROWS, one_row, 0, unroll=4)
+        product = dot_tn(g_now[...], held[...]).T.astype(BF16)
+        n = 3 * which + b
+        for c in range(CHAN):
+            atrous_sum.out[n, c] = product[HEAD * c : HEAD * (c + 1)]
+        atrous_sum.relay()
+        atrous_sum.send(n, 1 if n % 2 else -1)
+
+    def multiply_point():
+        grads = g_all[REACH : REACH + GROUP_ROWS, :, 3 * BRANCH :].reshape(-1, BRANCH)
+        product = dot_tn(grads, x_base[...]).T.astype(BF16)
+        for c in range(CHAN):
+            point_sum.out[0, c] = product[HEAD * c : HEAD * (c + 1)]
+        point_sum.send(0, 1)
+
+    tasks = [take]
+    for which in range(3):
+        tasks.append(functools.partial(pick, which))
+        tasks += [functools.partial(multiply, which, b) for b in range(3)]
+    tasks += [multiply_point, point_sum.relay, atrous_sum.relay]
+    queue = iter(tasks)
+
+    def meanwhile(count=1):
+        for _ in range(count):
+            task = next(queue, None)
+            if task is not None:
+                task()
+
     project_sent = {
         d: links.send(projects.at[spot.chan(d)], project_in.at[d - 1], chan=spot.chan(d))
         for d in (2, 1, 3)
@@ -1005,7 +1316,7 @@
     sums = jnp.zeros((8, 2 * MID_OWN), F32)
     for r in range(OWN_ROWS):
         sums = sums + place_rows[:, r : r + 1] * pool_rows[r : r + 1]
-    sums = sum_over_pix(sums, near_p, across_p, spot, links)
+    sums = sum_over_pix(sums, near_p, across_p, spot, links, meanwhile)
     pooled_pre = (sums[:, :BRANCH] * slope(pre_pooled[...])).astype(BF16)
     grad_pooled[...] = pooled_pre.astype(F32)
     wide = jnp.concatenate([pooled_pre.astype(F32), jnp.zeros((8, BRANCH), F32)], axis=0).astype(BF16)
@@ -1015,6 +1326,7 @@
         d: links.send(mean_out.at[spot.chan(d)], mean_in.at[d - 1], chan=spot.chan(d))
         for d in (2, 1, 3)
     }
+    meanwhile()
     mean = mean_out[j].astype(F32)
     for d in (1, 3, 2):
         links.arrive(sent[d], mean_in.at[d - 1])
@@ -1025,7 +1337,7 @@
         mean_rows = mean_rows + tile_cols[:, k : k + 1] * mean[k : k + 1]
 
     def norm_back(grad, unit, near, across, scale):
-        sums = sum_over_pix(two_sums(grad, grad * unit), near, across, spot, links)
+        sums = sum_over_pix(two_sums(grad, grad * unit), near, across, spot, links, meanwhile)
         pre = scale * (grad - sums[0:1] / PIXELS - unit * (sums[1:2] / PIXELS))
         return pre.astype(BF16), sums
 
@@ -1063,6 +1375,7 @@
         for n in range(8):
             by_expand.parts[spot_of(8 * c + n)] = grads[part * n : part * (n + 1)]
     by_expand.start()
+    meanwhile()
     grad_act = side_sum(0, own, sent)
 
     unit = unit_d[...]
@@ -1077,6 +1390,7 @@
     to_before = links.send(halo.at[first], halo.at[high], pix=spot.before)
     to_after = links.send(halo.at[last], halo.at[low], pix=spot.after)
     by_expand.along_z()
+    meanwhile()
     for d in (1, 3, 2):
         links.arrive(project_sent[d], project_in.at[d - 1])
         project_wide[spot.chan(-d)] = project_in[d - 1].astype(F32)
@@ -1103,6 +1417,7 @@
                     part * n : part * (n + 1), MID_OWN * tap : MID_OWN * (tap + 1)
                 ]
     by_dilate.start()
+    meanwhile()
     grad_act = side_sum(1, own, sent)
     by_expand.along_x()
 
@@ -1125,6 +1440,7 @@
             by_project.parts[(*spot_of(device), t)] = jnp.concatenate(rows, axis=0).astype(BF16)
     by_project.start()
     grad_expand[...] = by_expand.finish()
+    meanwhile()
     for d in (1, 3, 2):
         links.arrive(sent[d], full.at[spot.chan(-d)])
     g_reduce = jnp.concatenate([full[c] for c in range(CHAN)], axis=1)
@@ -1138,10 +1454,13 @@
     by_reduce.start()
     grad_pixels[...] = (grad_summed + dot_nt(g_reduce, weight)).astype(BF16)
     by_project.along_z()
+    meanwhile(2)
     by_reduce.along_z()
+    meanwhile(2)
     by_dilate.along_x()
     by_reduce.along_x()
     by_project.along_x()
+    meanwhile(len(tasks))
     reduce_out[...] = by_reduce.finish()
 
     def last_copies():
@@ -1159,7 +1478,17 @@
     grad_project[...] = by_project.finish()
     pltpu.make_async_copy(reduce_out, grad_reduce, last_sems.at[1]).wait()
     pl.when(jnp.logical_not(stays))(lambda: away().wait_send())
+    atrous_sum.finish(grad_atrous)
+    point_sum.finish(grad_point)
     links.finish()
+
+
+def group_scratch(count, *shape):
+    return [
+        pltpu.VMEM((count, 4, *shape), BF16),
+        pltpu.VMEM((count, *shape), BF16),
+        pltpu.VMEM((count, 2, *shape), BF16),
+    ]
 
 
 def section_backward(*operands):
@@ -1169,8 +1498,10 @@
     mid, feat = (OWN, MID_OWN), (OWN, FEAT_OWN)
     return pl.pallas_call(
         section_backward_kernel,
-        in_specs=[whole] * len(operands),
-        out_specs=[whole] * 8,
+        in_specs=[whole] * 22
+        + [pl.BlockSpec(memory_space=pltpu.SMEM)]
+        + [pl.BlockSpec(memory_space=pl.ANY)] * 2,
+        out_specs=[whole] * 10,
         out_shape=[
             shape(feat, BF16),
             shape((8, MID_OWN), F32),
@@ -1180,6 +1511,8 @@
             shape((16, FEAT_OWN), F32),
             shape((TASKS, 48, HEAD), F32),
             shape((8, BRANCH), F32),
+            shape((9, HEAD, 3 * BRANCH), F32),
+            shape((1, HEAD, BRANCH), F32),
         ],
         scratch_shapes=[
             pltpu.VMEM((2, 3, *mid), BF16),
@@ -1198,19 +1531,27 @@
             pltpu.VMEM((4, 8, FEAT_OWN), F32),
             pltpu.VMEM((GROUP, 8, 2 * MID_OWN), F32),
             pltpu.VMEM((4, 8, 2 * MID_OWN), F32),
+            pltpu.VMEM((CHAN, GROUP_ROWS, TILE_W, 128), BF16),
+            pltpu.VMEM((GROUP_ROWS * TILE_W, 256), BF16),
+            pltpu.VMEM((GROUP_ROWS * TILE_W, 256), BF16),
+            pltpu.VMEM((GROUP_ROWS + 2 * REACH, TILE_W, 4 * BRANCH), BF16),
+            pltpu.VMEM((GROUP_ROWS * TILE_W, 3 * BRANCH), BF16),
             *scatter_scratch(16, FEAT_OWN),
             *scatter_scratch(9, 16, MID_OWN),
             *scatter_scratch(TASKS, 48, HEAD),
             *scatter_scratch(HEAD, MID_OWN),
-            dma((96,)),
-            dma((96,)),
+            *group_scratch(9, HEAD, 3 * BRANCH),
+            *group_scratch(1, HEAD, BRANCH),
+            dma((128,)),
+            dma((128,)),
+            dma((2,)),
             dma((2,)),
         ],
         compiler_params=pltpu.CompilerParams(
             collective_id=6, has_side_effects=True, vmem_limit_bytes=VMEM_LIMIT
         ),
         cost_estimate=pl.CostEstimate(
-            flops=4_000_000_000, bytes_accessed=250_000_000, transcendentals=0
+            flops=16_000_000_000, bytes_accessed=250_000_000, transcendentals=0
         ),
         name="section_backward",
     )(*operands)
@@ -1264,7 +1605,7 @@
         row_onehot.T, sizes,
     )
     tile_mean = jnp.moveaxis(mean_all[:, :tile_count], 0, 1).reshape(tile_count, -1)
-    group_x, group_z, core = device // GROUP, device % GROUP // 2, device % 2
+    group_x = device // GROUP
     placed = jnp.array(PLACED_ROWS, jnp.int32)
     place_key = tile_number[placed] + 8 * (placed % 6)
     key_pad = jnp.pad(place_key, (REACH, REACH), constant_values=-1)
@@ -1291,88 +1632,35 @@
     task_weight = jax.nn.softmax(task_draws.astype(jnp.float32) / 3.0)
     grad_maps = (task_weight[:, None, None] * cotangent.astype(jnp.float32)).astype(jnp.bfloat16)
     maps_own = jnp.moveaxis(grad_maps, 0, 1).reshape(OWN_ROWS, TILE_W, BRANCH)
-    maps_all = gather_rows(maps_own, 0, 2, "gather_maps")
-    maps_all = jnp.moveaxis(
-        maps_all.reshape(CHAN, pixel_count, TASKS, HEAD), 0, 2
-    ).reshape(pixel_count, 256 * TASKS)
     project_cut = jnp.moveaxis(project_weight.reshape(TASKS, HEAD, 5, CHAN, HEAD), 3, 0)
     project_own = lax.all_to_all(project_cut, "chan", 0, 0, tiled=True)
-    project_own = jnp.transpose(project_own, (3, 1, 4, 0, 2)).reshape(5, TASKS, HEAD, 256)
-    project_own = project_own[jnp.array(BRANCH_ORDER)]
-    spread = (
-        project_own[:, :, :, None, :] * jnp.eye(TASKS, dtype=jnp.bfloat16)[None, :, None, :, None]
-    ).reshape(5, BRANCH, 256 * TASKS)
-    grad_pre, head_part, grad_project, pool_rows = heads_forward(
-        keep_own, x_ext, atrous_weight.reshape(TASKS, 3, 3, 3, HEAD, -1), point_weight, spread,
-        maps_all, pooled_pixels,
+    project_own = jnp.transpose(project_own, (3, 1, 4, 0, 2))[jnp.array(BRANCH_ORDER)]
+    same = jnp.eye(TASKS, dtype=jnp.bfloat16)[None, :, None, None, :, None]
+    spread = (project_own[:, :, :, :, None, :] * same).reshape(5, BRANCH, 256 * TASKS)
+    kernels = atrous_weight.reshape(TASKS, 3, 3, 3, HEAD, -1)
+    grad_pre, head_part, grad_project, pool_rows, x_group = heads_forward(
+        keep_own, x_ext, maps_own, kernels, point_weight, spread, pooled_pixels
     )
-    g_own = grad_pre.reshape(OWN_ROWS, TILE_W, 4 * BRANCH)
-    ring = range(PIX)
-    g_low = lax.ppermute(g_own[OWN_ROWS - REACH :], "pix", [(p, (p + 1) % PIX) for p in ring])
-    g_high = lax.ppermute(g_own[:REACH], "pix", [(p, (p - 1) % PIX) for p in ring])
-    mate_route = [(p, p ^ 1) for p in ring]
-    x_parts, g_parts = [], []
-    for m in range(4):
-        block = lax.dynamic_slice(
-            x_ext, (0, REACH, 0, 128 * (group_z ^ m)), (CHAN, OWN_ROWS, TILE_W, 128)
-        )
-        route = [(p, p ^ (2 * m)) for p in ring]
-        x_parts.append(lax.ppermute(block, "pix", route) if m else block)
-        g_parts.append(lax.ppermute(g_own, "pix", route) if m else g_own)
-    x_parts = x_parts + [lax.ppermute(part, "pix", mate_route) for part in x_parts]
-    g_parts = g_parts + [lax.ppermute(part, "pix", mate_route) for part in g_parts]
-
-    def group_edge(spot, rows):
-        picked = g_parts[0][rows]
-        for m in range(4):
-            for other in range(2):
-                here = (group_z ^ m == spot // 2) & (core ^ other == spot % 2)
-                picked = jnp.where(here, g_parts[4 * other + m][rows], picked)
-        return picked
-
-    group_low = lax.ppermute(
-        group_edge(GROUP - 1, slice(OWN_ROWS - REACH, OWN_ROWS)),
-        "pix",
-        [(p, (p + GROUP) % PIX) for p in ring],
+    trunk_parts, g_group, task_maps = heads_input_grad(
+        keep_own, grad_pre.reshape(OWN_ROWS, TILE_W, 4 * BRANCH),
+        head_part.reshape(CHAN, OWN_ROWS, TILE_W, BRANCH), kernels, point_weight,
     )
-    group_high = lax.ppermute(
-        group_edge(0, slice(0, REACH)), "pix", [(p, (p - GROUP) % PIX) for p in ring]
-    )
-    trunk_parts = heads_input_grad(
-        keep_own, g_own, g_low, g_high, atrous_weight.reshape(TASKS, 3, 3, 3, HEAD, -1), point_weight
-    )
-    trunk_grad = return_rows(trunk_parts.reshape(CHAN, OWN_ROWS, TILE_W, -1), 3, "return_trunk")
-    maps_parts = jnp.moveaxis(
-        head_part.reshape(OWN_ROWS, TILE_W, TASKS, CHAN, HEAD), 3, 0
-    ).reshape(CHAN, OWN_ROWS, TILE_W, BRANCH)
-    task_maps = jnp.moveaxis(
-        return_rows(maps_parts, 4, "return_maps").reshape(pixel_count, TASKS, HEAD), 1, 0
-    )
-    weight_parts, point_parts = heads_weight_grad(keep_group, x_parts, g_parts, group_low, group_high)
-
-    def sum_over_groups(parts):
-        total = lax.dynamic_index_in_dim(parts, group_x, 0, False).astype(jnp.float32)
-        for step in range(1, 4):
-            sent = lax.dynamic_index_in_dim(parts, (group_x + step) % 4, 0, False)
-            route = [(p, (p + GROUP * step) % PIX) for p in ring]
-            total = total + lax.ppermute(sent, "pix", route).astype(jnp.float32)
-        return total
-
-    grad_atrous_weight = jnp.transpose(
-        sum_over_groups(weight_parts).reshape(3, 3, HEAD, 3, TASKS, HEAD), (4, 0, 3, 1, 2, 5)
-    ).reshape(TASKS, 3, 9, HEAD, HEAD)
-    grad_point_weight = jnp.transpose(
-        sum_over_groups(point_parts).reshape(HEAD, TASKS, HEAD), (1, 0, 2)
-    )
+    task_maps = jnp.moveaxis(task_maps.reshape(pixel_count, TASKS, HEAD), 1, 0)
+    trunk_grad = return_rows(trunk_parts.reshape(CHAN, OWN_ROWS, TILE_W, -1), 4, "return_trunk")
     (
         grad_pixels, mid_grads, feat_grads, grad_reduce, grad_dilate, grad_expand, grad_project,
-        grad_pooled,
+        grad_pooled, grad_atrous, grad_point,
     ) = section_backward(
         trunk_grad, pixels, unit_reduce, unit_dilate, unit_expand, act_reduce, act_dilate, reduce_all,
         jnp.moveaxis(dilate_weight, 0, 1).reshape(-1, 9 * MID_OWN), expand_weight, vec_mid, vec_feat,
         inv_mid, inv_feat, keep_section, pool_rows, place_onehot.T, row_onehot, sizes,
         pre_pooled.reshape(tile_count, BRANCH), pooled_weight.reshape(BRANCH, -1), grad_project,
+        keep_group, x_group, g_group,
     )
+    grad_atrous_weight = jnp.transpose(
+        grad_atrous.reshape(3, 3, HEAD, 3, TASKS, HEAD), (4, 0, 3, 1, 2, 5)
+    ).reshape(TASKS, 3, 9, HEAD, HEAD)
+    grad_point_weight = jnp.transpose(grad_point.reshape(HEAD, TASKS, HEAD), (1, 0, 2))
     grad_pooled_weight = jnp.einsum(
         "kc,ktd->tcd",
         tile_mean,

time: 535 us -> 420 us (0.79)
  the two profiles are of different devices: /device:TPU:1 before, /device:TPU:5 now
where the time goes in v3:
time: 420 us; the launch traced here: 412 us
  Pallas kernels  353 us (84%)
  local copies, waits for them, and re-layouts  44 us (10%)
  other arithmetic  6.79 us (2%)
    pallas_call x1, Pallas kernels, section_backward(): pl.pallas_call(section_backward_kernel, in_specs=[whole] * 22 + [pl.Block...  119 us
    pallas_call x1, Pallas kernels, section_forward(): pl.pallas_call(section_forward_kernel, in_specs=[whole] * 9, out_specs=[w...  82.5 us
    pallas_call x1, Pallas kernels, heads_input_grad(): pl.pallas_call(heads_input_grad_kernel, grid=(2, 3), in_specs=[pl.BlockSp...  44.8 us
    pallas_call x1, Pallas kernels, heads_forward(): pl.pallas_call(heads_forward_kernel, grid=(9,), in_specs=[pl.BlockSpec(me...  39.6 us
    pallas_call x1, Pallas kernels, gather_rows(): pl.pallas_call(functools.partial(gather_rows_kernel, reach), out_shape=ja...  34.8 us
    pallas_call x1, Pallas kernels, return_rows(): pl.pallas_call(return_rows_kernel, out_shape=jax.ShapeDtypeStruct(rows, B...  32.7 us
    mul x4, local copies, waits for them, and re-layouts, shards(): project_own[:, :, :, :, None, :] * same  11.2 us
  transfers between devices with their start and end apart: 1, of which 0 were waited for; matrix products, arithmetic and copies ran while one was open for 4% of the time, Pallas kernels for 28%

profile of v3, /device:TPU:5, one launch (start us, length us, event | category | flops | bytes accessed | tf_op | source)
XLA Modules:
  0.0 411.7 jit_solution(13499601738301044829)
XLA Ops:
  0.6 2.0 reshape.124
  3.0 1.5 reshape.155
  4.5 4.2 %all-to-all-start = ((bf16[4,2,30720]{2,1,0:T(2,128)(2,1)}), bf16[4,2,30720]{2,1,0:T(2,128)(2,1)S(1)}, u32[]{:S(2)}, u32[]{:S(2)}) async-start(bf16[4,2,30720]{2,1,0:T(2,128)(2,1)} %reshape.155), calls=%async_computation | async-start | bytes 983040 | tf_op jit(solution)/shard_map/all_to_all | solution.py:1636
  8.8 1.9 gather_fusion
  13.4 1.3 fusion.14
  14.6 1.3 broadcast_divide_fusion
  17.2 1.0 broadcast_in_dim.17.keep
  18.9 82.5 %section_forward.1 = (bf16[8,64,512]{2,1,0:T(8,128)(2,1)}, f32[512,128]{1,0:T(8,128)}, f32[512,128]{1,0:T(8,128)}, f32[512,512]{1,0:T(8,128)}, bf16[4,16,64,128]...) custom-call(bf16[512,512]{1,0:T(8,128)(2,1)} %pixels.3, ...), custom_call_target="tpu_custom_call" | custom-call | flops 2000000000 | bytes 120000000 | tf_op jit(solution)/shard_map/section_forward/pallas_call | solution.py:1089
  101.4 0.9 slice.51
  103.4 34.8 %gather_trunk.1.x_hbm = bf16[4,14,64,512]{3,2,1,0:T(8,128)(2,1)} custom-call(bf16[8,64,512]{2,1,0:T(8,128)(2,1)} %get-tuple-element.43.src), custom_call_target="tpu_custom_call" | custom-call | bytes 60000000 | tf_op jit(solution)/shard_map/gather_trunk/pallas_call | solution.py:211
  138.4 1.0 copy.109.maps_own
  140.3 1.6 copy.113.wd_cat
  144.8 0.7 gather_fusion.1
  145.5 0.8 copy.107
  146.4 3.5 mul.59
  149.9 6.9 %mul.60 = bf16[5,192,768]{2,1,0:T(8,128)(2,1)S(1)} reshape(bf16[5,3,64,4,3,64]{5,4,3,2,1,0:T(4,128)(2,1)} %mul.59) | data formatting | bytes 2949120 | tf_op jit(solution)/shard_map/mul | solution.py:1639
  156.8 1.3 broadcast_multiply_fusion.spread
  158.0 0.7 broadcast_in_dim.20
  158.8 39.6 %heads_forward.1 = (bf16[512,768]{1,0:T(8,128)(2,1)}, bf16[4,512,192]{2,1,0:T(8,128)(2,1)}, bf16[4,5,3,64,64]{4,3,2,1,0:T(8,128)(2,1)}, f32[8,256]{1,0:T(8,128)}, bf16[4,64,64,128]{3,2,1,0:T(8,128)(2,1)}) custom-call(s32[9,8]{1,0:T(8,128)} %constant_dynamic-slice_fusion.keep, bf16[4,14,64,512]{3,2,1,0:T(8,128)(2,1)} %gather_trunk.1.x_hbm, ...), custom_call_target="tpu_custom_call" | custom-call | flops 12000000000 | bytes 28000000 | tf_op jit(solution)/shard_map/heads_forward/pallas_call | solution.py:619
  198.3 44.8 %heads_input_grad.1 = (bf16[4,512,512]{2,1,0:T(8,128)(2,1)}, bf16[64,64,768]{2,1,0:T(8,128)(2,1)}, bf16[8,64,192]{2,1,0:T(8,128)(2,1)}) custom-call(s32[9,8]{1,0:T(8,128)} %constant_dynamic-slice_fusion.keep, bf16[8,64,768]{2,1,0:T(8,128)(2,1)} %bitcast.85, bf16[4,8,64,192]{3,2,1,0:T(8,128)(2,1)} %bitcast.84, bf16[3,3,3,3,64,2048]{5,4,3,2,1,0:T(8,128)(2,1)} %bitcast.83, ...), custom_call_target="tpu_custom_call" | custom-call | flops 12000000000 | bytes 28000000 | tf_op jit(solution)/shard_map/heads_input_grad/pallas_call | solution.py:845
  243.2 1.2 copy.110
  244.4 0.9 reshape.130
  245.3 32.7 %return_trunk.1.trunk_grad = bf16[8,64,512]{2,1,0:T(8,128)(2,1)} custom-call(bf16[4,8,64,512]{3,2,1,0:T(8,128)(2,1)} %bitcast.67), custom_call_target="tpu_custom_call" | custom-call | bytes 60000000 | tf_op jit(solution)/shard_map/return_trunk/pallas_call | solution.py:295
  278.0 118.6 %section_backward.1 = (bf16[512,512]{1,0:T(8,128)(2,1)}, f32[8,128]{1,0:T(8,128)}, f32[8,512]{1,0:T(8,128)}, f32[64,128]{1,0:T(8,128)}, f32[9,16,128]{2,1,0:T(8,...) custom-call(bf16[8,64,512]{2,1,0:T(8,128)(2,1)} %return_trunk.1.trun, ...), custom_call_target="tpu_custom_call" | custom-call | flops 16000000000 | bytes 250000000 | tf_op jit(solution)/shard_map/section_backward/pallas_call | solution.py:1499
  396.6 1.3 slice_bitcast_fusion
  398.0 1.4 fusion.15
  399.3 0.9 copy.114
  400.3 0.7 copy.118
  401.0 2.6 copy.115
  403.7 2.6 copy.116
  406.4 1.5 convolution_bitcast_fusion
  408.6 0.8 copy.127
  (90 shorter events, 12.4 us)
Async XLA Ops:
  2.9 5.8 %copy-start.12 = (s32[256]{0:T(256)S(1)}, s32[256]{0:T(256)}, u32[]{:S(2)}) copy-start(s32[256]{0:T(256)} %constant.97) | copy-start | bytes 3076
  2.9 5.8 %copy-start = (s32[256]{0:T(256)S(1)}, s32[256]{0:T(256)}, u32[]{:S(2)}) copy-start(s32[256]{0:T(256)} %param.20) | copy-start | bytes 3076
  2.9 7.9 %copy-start.13 = (s32[256]{0:T(256)S(1)}, s32[256]{0:T(256)}, u32[]{:S(2)}) copy-start(s32[256]{0:T(256)} %constant.92) | copy-start | bytes 3076
  2.9 9.8 %copy-start.19 = (s32[3]{0:T(128)S(1)}, s32[3]{0:T(128)}, u32[]{:S(2)}) copy-start(s32[3]{0:T(128)} %param.21) | copy-start | bytes 40
  2.9 13.0 %copy-start.18 = (s32[5]{0:T(128)S(1)}, s32[5]{0:T(128)}, u32[]{:S(2)}) copy-start(s32[5]{0:T(128)} %constant.98) | copy-start | bytes 64
  2.9 13.0 %copy-start.10 = (f32[512]{0:T(512)S(1)}, f32[512]{0:T(512)}, u32[]{:S(2)}) copy-start(f32[512]{0:T(512)} %param.30) | copy-start | bytes 6148
  2.9 13.0 %copy-start.11 = (f32[512]{0:T(512)S(1)}, f32[512]{0:T(512)}, u32[]{:S(2)}) copy-start(f32[512]{0:T(512)} %param.29) | copy-start | bytes 6148
  3.0 13.6 %copy-start.14 = (f32[128]{0:T(128)S(1)}, f32[128]{0:T(128)}, u32[]{:S(2)}) copy-start(f32[128]{0:T(128)} %param.27) | copy-start | bytes 1540
  3.0 13.6 %copy-start.15 = (f32[128]{0:T(128)S(1)}, f32[128]{0:T(128)}, u32[]{:S(2)}) copy-start(f32[128]{0:T(128)} %param.26) | copy-start | bytes 1540
  3.0 13.6 %copy-start.16 = (f32[128]{0:T(128)S(1)}, f32[128]{0:T(128)}, u32[]{:S(2)}) copy-start(f32[128]{0:T(128)} %param.24) | copy-start | bytes 1540
  3.0 13.6 %copy-start.17 = (f32[128]{0:T(128)S(1)}, f32[128]{0:T(128)}, u32[]{:S(2)}) copy-start(f32[128]{0:T(128)} %param.23) | copy-start | bytes 1540
  4.5 139.0 %all-to-all-start = ((bf16[4,2,30720]{2,1,0:T(2,128)(2,1)}), bf16[4,2,30720]{2,1,0:T(2,128)(2,1)S(1)}, u32[]{:S(2)}, u32[]{:S(2)}) async-start(bf16[4,2,30720]{2,1,0:T(2,128)(2,1)} %reshape.155), calls=%async_computation | async-start | bytes 983040 | tf_op jit(solution)/shard_map/all_to_all | solution.py:1636
  18.8 83.4 %copy-start.4 = (bf16[3,512,64]{1,2,0:T(8,128)(2,1)S(1)}, bf16[3,512,64]{1,2,0:T(8,128)(2,1)}, u32[]{:S(2)}) copy-start(bf16[3,512,64]{1,2,0:T(8,128)(2,1)} %param.35) | copy-start | bytes 589828
  18.8 83.5 %copy-start.2 = (bf16[3,64,2048]{2,1,0:T(8,128)(2,1)S(1)}, bf16[3,64,2048]{2,1,0:T(8,128)(2,1)}, u32[]{:S(2)}) copy-start(bf16[3,64,2048]{2,1,0:T(8,128)(2,1)} %param.33) | copy-start | bytes 2359300
  101.3 1.4 copy-start.1
  403.7 2.6 copy-start.9
  406.2 1.7 copy-start.6
  406.2 2.3 copy-start.3
  406.3 3.1 copy-start.8
  406.3 3.7 copy-start.5
  406.3 4.3 %copy-start.7 = (f32[16,512]{1,0:T(8,128)S(1)}, f32[16,512]{1,0:T(8,128)}, u32[]{:S(2)}) copy-start(f32[16,512]{1,0:T(8,128)} %get-tuple-element.203) | copy-start | bytes 98308

commit v4 on v3

--- a/solution.py
+++ b/solution.py
@@ -76,241 +76,138 @@
     )
 
 
-def gather_rows_kernel(
-    reach, src, out, ss_row, rs_row, ss_side, rs_side, ss_far, rs_far, ss_halo, rs_halo
-):
-    i, j = lax.axis_index("pix"), lax.axis_index("chan")
-    right, left = int_rem(j + 1, CHAN), int_rem(j + CHAN - 1, CHAN)
-    far = int_rem(j + 2, CHAN)
-    after, before = int_rem(i + 1, PIX), int_rem(i + PIX - 1, PIX)
-    barrier = pltpu.get_barrier_semaphore()
-    expected = 2 + (2 if reach else 0)
-    for s in range(OWN_ROWS):
-        origin = int_div(row_of(OWN_ROWS * i + s), OWN_ROWS)
-
-        @pl.when(origin != i)
-        def _():
-            signal(barrier, pix=origin)
-
-        target = int_div(place_of(OWN_ROWS * i + s), OWN_ROWS)
-        expected = expected + (target != i).astype(jnp.int32)
-    signal(barrier, chan=right)
-    signal(barrier, chan=left)
-    if reach:
-        signal(barrier, pix=after)
-        signal(barrier, pix=before)
-    pl.semaphore_wait(barrier, expected)
-
-    def row_send(s):
-        place = place_of(OWN_ROWS * i + s)
+class RowGather:
+    def __init__(self, reach, src, out, spot, sems):
+        self.reach, self.src, self.out, self.spot = reach, src, out, spot
+        (
+            self.ss_row, self.rs_row, self.ss_side, self.rs_side, self.ss_far, self.rs_far, self.ss_halo,
+            self.rs_halo,
+        ) = sems
+        self.order = (0, 7, 1, 6, 2, 5, 3, 4)
+        self.edge = [s for s in self.order if s < reach or s >= OWN_ROWS - reach]
+
+    def greet(self):
+        barrier = pltpu.get_barrier_semaphore()
+        i, expected = self.spot.i, 0
+        for s in range(OWN_ROWS):
+            origin = int_div(row_of(OWN_ROWS * i + s), OWN_ROWS)
+
+            @pl.when(origin != i)
+            def _():
+                signal(barrier, pix=origin)
+
+            target = int_div(place_of(OWN_ROWS * i + s), OWN_ROWS)
+            expected = expected + (target != i).astype(jnp.int32)
+        return expected
+
+    def row_send(self, s):
+        place = place_of(OWN_ROWS * self.spot.i + s)
         target, slot = int_div(place, OWN_ROWS), int_rem(place, OWN_ROWS)
-        landing = out.at[j, reach + slot]
+        src, landing = self.src.at[s], self.out.at[self.spot.j, self.reach + slot]
         return target, (
-            lambda: remote(src.at[s], landing, ss_row.at[s], rs_row.at[slot], pix=target),
-            lambda: pltpu.make_async_copy(src.at[s], landing, rs_row.at[slot]),
-        )
-
-    for s in range(OWN_ROWS):
-        target, (away, here) = row_send(s)
-        pl.when(target != i)(lambda: away().start())
-        pl.when(target == i)(lambda: here().start())
-
-    def block(chan, s):
-        return out.at[chan, reach + s]
-
-    def side_send(way, s):
+            lambda: remote(src, landing, self.ss_row.at[s], self.rs_row.at[slot], pix=target),
+            lambda: pltpu.make_async_copy(src, landing, self.rs_row.at[slot]),
+        )
+
+    def block(self, chan, s):
+        return self.out.at[chan, self.reach + s]
+
+    def side(self, way):
+        return self.spot.chan((1, -1)[way])
+
+    def side_copy(self, way, s, chan):
+        block = self.block(chan, s)
         return remote(
-            block(j, s),
-            block(j, s),
-            ss_side.at[way, s],
-            rs_side.at[way, s],
-            chan=(right, left)[way],
-        )
-
-    def side_arrival(way, s):
-        chan = (left, right)[way]
+            block, block, self.ss_side.at[way, s], self.rs_side.at[way, s], chan=self.side(way)
+        )
+
+    def far_way(self, s):
+        return 0 if s < OWN_ROWS // 2 else 1
+
+    def far_copy(self, s, chan):
+        block = self.block(chan, s)
         return remote(
-            block(chan, s), block(chan, s), ss_side.at[way, s], rs_side.at[way, s], chan=chan
-        )
-
-    def far_send(s):
-        way = 0 if s < OWN_ROWS // 2 else 1
-        chan = (left, right)[way]
+            block, block, self.ss_far.at[s], self.rs_far.at[s], chan=self.side(self.far_way(s))
+        )
+
+    def halo_copy(self, turn, chan, s):
+        reach = self.reach
+        if s < reach:
+            lane, slot, target = s, reach + OWN_ROWS + s, self.spot.before
+        else:
+            lane, slot, target = s - OWN_ROWS + 2 * reach, s - OWN_ROWS + reach, self.spot.after
         return remote(
-            block(chan, s), block(chan, s), ss_far.at[s], rs_far.at[s], chan=(right, left)[way]
-        )
-
-    def far_arrival(s):
-        return remote(block(far, s), block(far, s), ss_far.at[s], rs_far.at[s], chan=left)
-
-    def halo_send(turn, chan, s):
-        if s < reach:
-            return remote(
-                block(chan, s),
-                out.at[chan, reach + OWN_ROWS + s],
-                ss_halo.at[turn, s],
-                rs_halo.at[chan, s],
-                pix=before,
-            )
-        lane = s - OWN_ROWS + 2 * reach
+            self.block(chan, s),
+            self.out.at[chan, slot],
+            self.ss_halo.at[turn, lane],
+            self.rs_halo.at[chan, lane],
+            pix=target,
+        )
+
+    def halo_arrival(self, chan, lane):
+        slot = self.reach + OWN_ROWS + lane if lane < self.reach else lane - self.reach
+        dst = self.out.at[chan, slot]
         return remote(
-            block(chan, s),
-            out.at[chan, s - OWN_ROWS + reach],
-            ss_halo.at[turn, lane],
-            rs_halo.at[chan, lane],
-            pix=after,
-        )
-
-    def halo_arrival(chan, lane):
-        slot = reach + OWN_ROWS + lane if lane < reach else lane - reach
-        return remote(
-            out.at[chan, slot],
-            out.at[chan, slot],
-            ss_halo.at[0, lane],
-            rs_halo.at[chan, lane],
-            pix=after,
-        )
-
-    order = (0, 7, 1, 6, 2, 5, 3, 4)
-    edge = [s for s in order if s < reach or s >= OWN_ROWS - reach]
-    for s in order:
-        pltpu.make_async_copy(src.at[s], block(j, s), rs_row.at[s]).wait()
-        side_send(0, s).start()
-        side_send(1, s).start()
-        if s in edge:
-            halo_send(0, j, s).start()
-    for s in order:
-        for way in range(2):
-            side_arrival(way, s).wait_recv()
-            if way == (0 if s < OWN_ROWS // 2 else 1):
-                far_send(s).start()
-            if s in edge:
-                halo_send(1 + way, (left, right)[way], s).start()
-    for s in order:
-        far_arrival(s).wait_recv()
-        if s in edge:
-            halo_send(3, far, s).start()
-    if reach:
+            dst, dst, self.ss_halo.at[0, lane], self.rs_halo.at[chan, lane], pix=self.spot.after
+        )
+
+    def send_rows(self):
+        for s in range(OWN_ROWS):
+            target, (away, here) = self.row_send(s)
+            pl.when(target != self.spot.i)(lambda: away().start())
+            pl.when(target == self.spot.i)(lambda: here().start())
+
+    def pass_own(self):
+        j = self.spot.j
+        for s in self.order:
+            pltpu.make_async_copy(self.src.at[s], self.block(j, s), self.rs_row.at[s]).wait()
+            self.side_copy(0, s, j).start()
+            self.side_copy(1, s, j).start()
+            if s in self.edge:
+                self.halo_copy(0, j, s).start()
+
+    def pass_sides(self):
+        for s in self.order:
+            for way in range(2):
+                chan = self.side(1 - way)
+                self.side_copy(way, s, chan).wait_recv()
+                if way == self.far_way(s):
+                    self.far_copy(s, chan).start()
+                if s in self.edge:
+                    self.halo_copy(1 + way, chan, s).start()
+
+    def finish(self):
+        spot, far = self.spot, self.spot.chan(2)
+        for s in self.order:
+            self.far_copy(s, far).wait_recv()
+            if s in self.edge:
+                self.halo_copy(3, far, s).start()
         for chan in range(CHAN):
-            for lane in range(2 * reach):
-                halo_arrival(chan, lane).wait_recv()
-    for s in range(OWN_ROWS):
-        target, (away, here) = row_send(s)
-        pl.when(target != i)(lambda: away().wait_send())
-        side_send(0, s).wait_send()
-        side_send(1, s).wait_send()
-        far_send(s).wait_send()
-    for turn, chan in enumerate((j, left, right, far)):
-        for s in edge:
-            halo_send(turn, chan, s).wait_send()
-
-
-def gather_rows(rows, reach, collective_id, name):
-    width = rows.shape[2]
+            for lane in range(2 * self.reach):
+                self.halo_arrival(chan, lane).wait_recv()
+        for s in range(OWN_ROWS):
+            target, (away, here) = self.row_send(s)
+            pl.when(target != spot.i)(lambda: away().wait_send())
+            self.side_copy(0, s, spot.j).wait_send()
+            self.side_copy(1, s, spot.j).wait_send()
+            self.far_copy(s, self.side(1 - self.far_way(s))).wait_send()
+        for turn, chan in enumerate((spot.j, self.side(1), self.side(0), far)):
+            for s in self.edge:
+                self.halo_copy(turn, chan, s).wait_send()
+
+
+def gather_sems(reach):
     dma = pltpu.SemaphoreType.DMA
-    return pl.pallas_call(
-        functools.partial(gather_rows_kernel, reach),
-        out_shape=jax.ShapeDtypeStruct((CHAN, OWN_ROWS + 2 * reach, TILE_W, width), rows.dtype),
-        in_specs=[pl.BlockSpec(memory_space=pl.ANY)],
-        out_specs=pl.BlockSpec(memory_space=pl.ANY),
-        scratch_shapes=[
-            dma((OWN_ROWS,)),
-            dma((OWN_ROWS,)),
-            dma((2, OWN_ROWS)),
-            dma((2, OWN_ROWS)),
-            dma((OWN_ROWS,)),
-            dma((OWN_ROWS,)),
-            dma((CHAN, max(2 * reach, 1))),
-            dma((CHAN, max(2 * reach, 1))),
-        ],
-        compiler_params=pltpu.CompilerParams(collective_id=collective_id, has_side_effects=True),
-        cost_estimate=pl.CostEstimate(flops=0, bytes_accessed=60_000_000, transcendentals=0),
-        name=name,
-    )(rows)
-
-
-def return_rows_kernel(src, out, own, arrived, total, ls, ss_side, rs_side, ss_row, rs_row):
-    i, j = lax.axis_index("pix"), lax.axis_index("chan")
-    barrier = pltpu.get_barrier_semaphore()
-    expected = 3
-    for s in range(OWN_ROWS):
-        origin = int_div(place_of(OWN_ROWS * i + s), OWN_ROWS)
-
-        @pl.when(origin != i)
-        def _():
-            signal(barrier, pix=origin)
-
-        target = int_div(row_of(OWN_ROWS * i + s), OWN_ROWS)
-        expected = expected + (target != i).astype(jnp.int32)
-    for distance in (1, 2, 3):
-        signal(barrier, chan=int_rem(j + distance, CHAN))
-    pl.semaphore_wait(barrier, expected)
-
-    def side_send(distance, s):
-        chan = int_rem(j + distance, CHAN)
-        return remote(
-            src.at[chan, s],
-            arrived.at[distance - 1, s],
-            ss_side.at[distance - 1, s],
-            rs_side.at[distance - 1, s],
-            chan=chan,
-        )
-
-    for s in range(OWN_ROWS):
-        for distance in (2, 1, 3):
-            side_send(distance, s).start()
-    load = pltpu.make_async_copy(src.at[j], own, ls)
-    load.start()
-    load.wait()
-
-    def row_send(s):
-        row = row_of(OWN_ROWS * i + s)
-        target, slot = int_div(row, OWN_ROWS), int_rem(row, OWN_ROWS)
-        return target, (
-            lambda: remote(total.at[s], out.at[slot], ss_row.at[s], rs_row.at[slot], pix=target),
-            lambda: pltpu.make_async_copy(total.at[s], out.at[slot], rs_row.at[slot]),
-        )
-
-    for s in range(OWN_ROWS):
-        held = own[s].astype(F32)
-        for distance in (1, 3, 2):
-            side_send(distance, s).wait_recv()
-            held = held + arrived[distance - 1, s].astype(F32)
-        total[s] = held.astype(BF16)
-        target, (away, here) = row_send(s)
-        pl.when(target != i)(lambda: away().start())
-        pl.when(target == i)(lambda: here().start())
-    for s in range(OWN_ROWS):
-        pltpu.make_async_copy(total.at[s], out.at[s], rs_row.at[s]).wait()
-        target, (away, here) = row_send(s)
-        pl.when(target != i)(lambda: away().wait_send())
-        for distance in (1, 2, 3):
-            side_send(distance, s).wait_send()
-
-
-def return_rows(parts, collective_id, name):
-    width = parts.shape[3]
-    dma = pltpu.SemaphoreType.DMA
-    rows = (OWN_ROWS, TILE_W, width)
-    return pl.pallas_call(
-        return_rows_kernel,
-        out_shape=jax.ShapeDtypeStruct(rows, BF16),
-        in_specs=[pl.BlockSpec(memory_space=pl.ANY)],
-        out_specs=pl.BlockSpec(memory_space=pl.ANY),
-        scratch_shapes=[
-            pltpu.VMEM(rows, BF16),
-            pltpu.VMEM((CHAN - 1, *rows), BF16),
-            pltpu.VMEM(rows, BF16),
-            dma,
-            dma((CHAN - 1, OWN_ROWS)),
-            dma((CHAN - 1, OWN_ROWS)),
-            dma((OWN_ROWS,)),
-            dma((OWN_ROWS,)),
-        ],
-        compiler_params=pltpu.CompilerParams(collective_id=collective_id, has_side_effects=True),
-        cost_estimate=pl.CostEstimate(flops=0, bytes_accessed=60_000_000, transcendentals=0),
-        name=name,
-    )(parts)
+    return [
+        dma((OWN_ROWS,)),
+        dma((OWN_ROWS,)),
+        dma((2, OWN_ROWS)),
+        dma((2, OWN_ROWS)),
+        dma((OWN_ROWS,)),
+        dma((OWN_ROWS,)),
+        dma((CHAN, 2 * reach)),
+        dma((CHAN, 2 * reach)),
+    ]
 
 
 GROUP = 8
@@ -404,9 +301,9 @@
 
 
 def heads_forward_kernel(
-    keep, x_hbm, maps_own, kernel, point, spread, pooled,
+    keep, x_hbm, maps_own, kernel, point, project, pooled,
     grad_pre, head_part, grad_project, pool_rows, x_group,
-    x, acc, pre, maps_in, relay, sems, ss_row, rs_row, send_sems, recv_sems, own_sem,
+    x, acc, pre, maps_in, relay, spread, sems, ss_row, rs_row, send_sems, recv_sems, own_sem,
 ):
     step = pl.program_id(0)
     rate, row_tap = step // 3, step % 3
@@ -486,6 +383,14 @@
         marks["mate", 0] = posts.post(
             lambda: (x_slice(0), x_rows(0, spot.core), {"pix": spot.mate})
         )
+        spread[...] = jnp.zeros_like(spread)
+        for which, b in enumerate(BRANCH_ORDER):
+            for c in range(CHAN):
+                for t in range(TASKS):
+                    start = BRANCH * c + HEAD * t
+                    spread[which, start : start + HEAD, HEAD * t : HEAD * (t + 1)] = project[
+                        c, b // 2, t, :, HEAD * (b % 2) : HEAD * (b % 2 + 1)
+                    ]
         for copy in copies:
             copy.wait()
 
@@ -581,7 +486,7 @@
             else:
                 joined = pooled[...]
             weight = spread[which]
-            term = dot_nn(joined, weight)
+            term = dot_nt(joined, weight)
             head = term if head is None else head + term
             grads = dot_tn(joined, cot)
             for t in range(TASKS):
@@ -590,7 +495,7 @@
                     grad_project[c, which, t] = grads[
                         HEAD * t : HEAD * (t + 1), lane : lane + HEAD
                     ].astype(BF16)
-            back = dot_nt(cot, weight)
+            back = dot_nn(cot, weight)
             if which < 4:
                 grad = back * (logistic * (1.0 + before * (1.0 - logistic)))
                 grad_pre[:, BRANCH * which : BRANCH * (which + 1)] = grad.astype(BF16)
@@ -610,7 +515,7 @@
         posts.finish()
 
 
-def heads_forward(keep, x_ext, maps_own, kernels, point, spread, pooled):
+def heads_forward(keep, x_ext, maps_own, kernels, point, project, pooled):
     pixels = OWN_ROWS * TILE_W
     feat = point.shape[2]
     whole = pl.BlockSpec(memory_space=pltpu.VMEM)
@@ -642,6 +547,7 @@
             pltpu.VMEM((4, pixels, BRANCH), F32),
             pltpu.VMEM((CHAN, OWN_ROWS, TILE_W, BRANCH), BF16),
             pltpu.VMEM((2, 2, OWN_ROWS, TILE_W, 128), BF16),
+            pltpu.VMEM((5, 256 * TASKS, BRANCH), BF16),
             dma((CHAN,)),
             dma((OWN_ROWS,)),
             dma((OWN_ROWS,)),
@@ -656,7 +562,7 @@
             flops=12_000_000_000, bytes_accessed=28_000_000, transcendentals=0
         ),
         name="heads_forward",
-    )(keep, x_ext, maps_own, kernels, point, spread, pooled)
+    )(keep, x_ext, maps_own, kernels, point, project, pooled)
 
 
 PAD = 24
@@ -664,8 +570,10 @@
 
 
 def heads_input_grad_kernel(
-    keep, mid, parts, kernel, point, out, g_group, maps_out,
-    wide, taps, acc, edges, maps_in, maps_sum, ss_row, rs_row, send_sems, recv_sems, own_sem,
+    keep, mid, parts, kernel, point, pool_rows, place_rows, tile_cols, sizes, pre_pooled, pooled,
+    trunk_grad, g_group, maps_out, mean_rows, grad_pooled,
+    wide, taps, acc, edges, maps_in, maps_sum, out, out_in, out_sum, near, across, mean_out, mean_in,
+    ss_row, rs_row, send_sems, recv_sems, own_sem, ss_side, rs_side, ss_back, rs_back,
 ):
     n, rate = pl.program_id(0), pl.program_id(1)
     step = 3 * n + rate
@@ -712,6 +620,7 @@
         greet(
             [{"chan": spot.chan(d)} for d in (1, 2, 3)]
             + [{"pix": spot.pix_in_z(d)} for d in (1, -1)]
+            + spot.sum_peers()
             + [{"pix": p} for p in (spot.mate, spot.before, spot.after)],
             expected,
         )
@@ -733,6 +642,14 @@
                     )
                 )
         marks["mate", 0] = posts.post(lambda: (mid, g_rows(0, spot.core), {"pix": spot.mate}))
+        sums = jnp.zeros((8, 256), F32)
+        for r in range(OWN_ROWS):
+            sums = sums + place_rows[:, r : r + 1] * pool_rows[r : r + 1]
+        near[spot.k] = sums
+        for d in range(1, GROUP):
+            marks["near", d] = posts.post(
+                lambda d=d: (near.at[spot.k], near.at[spot.k], {"pix": spot.pix_in_group(d)})
+            )
         wide[...] = jnp.zeros_like(wide)
         posts.arrive(marks["low"], low)
         posts.arrive(marks["high"], high)
@@ -770,8 +687,47 @@
 
         lax.fori_loop(0, OWN_ROWS, one_row, 0)
 
+    @pl.when(step == 1)
+    def _():
+        for d in range(1, GROUP):
+            posts.arrive(marks["near", d], near.at[spot.in_group(-d)])
+        total = near[0]
+        for k in range(1, GROUP):
+            total = total + near[k]
+        across[spot.group] = total
+        for d in range(1, 4):
+            marks["across", d] = posts.post(
+                lambda d=d: (
+                    across.at[spot.group], across.at[spot.group], {"pix": spot.pix_in_x(d)}
+                )
+            )
+
+    @pl.when(step == 2)
+    def _():
+        for d in range(1, 4):
+            posts.arrive(marks["across", d], across.at[spot.x_of(-d)])
+        sums = across[0] + across[1] + across[2] + across[3]
+        pooled_pre = (sums[:, :BRANCH] * slope(pre_pooled[...])).astype(BF16).astype(F32)
+        grad_pooled[...] = pooled_pre
+        tall = jnp.concatenate([pooled_pre, jnp.zeros((8, BRANCH), F32)], axis=0).astype(BF16)
+        for c in range(CHAN):
+            mean_out[c] = dot_nn(tall, pooled[:, 512 * c : 512 * (c + 1)]).astype(BF16)
+        for d in (2, 1, 3):
+            marks["mean", d] = posts.post(
+                lambda d=d: (mean_out.at[spot.chan(d)], mean_in.at[d - 1], {"chan": spot.chan(d)})
+            )
+
     @pl.when(step == 3)
     def _():
+        mean = mean_out[j].astype(F32)
+        for d in (1, 3, 2):
+            posts.arrive(marks["mean", d], mean_in.at[d - 1])
+            mean = mean + mean_in[d - 1].astype(F32)
+        mean = mean[0:8] / sizes[:, 0:1]
+        rows = jnp.zeros((OWN_ROWS, 512), F32)
+        for k in range(8):
+            rows = rows + tile_cols[:, k : k + 1] * mean[k : k + 1]
+        mean_rows[...] = rows
         for d in (1, 3, 2):
             posts.arrive(marks["maps", d], maps_in.at[d - 1])
         for s in range(OWN_ROWS):
@@ -815,33 +771,86 @@
     @pl.when(rate == 2)
     def _():
         total = acc[...] + product
-        for c in range(out.shape[0]):
-            out[c] = total[:, 512 * c : 512 * (c + 1)].astype(BF16)
+        for c in range(2):
+            chan = 2 * pair_at(n, j) + c
+            out[chan] = total[:, 512 * c : 512 * (c + 1)].astype(BF16).reshape(
+                OWN_ROWS, TILE_W, 512
+            )
+
+    def side_send(chan, s):
+        turn = int_rem(chan + CHAN - j, CHAN) - 1
+        return remote(
+            out.at[chan, s], out_in.at[turn, s], ss_side.at[turn, s], rs_side.at[turn, s], chan=chan
+        )
+
+    away_pair = 2 * pair_at(0, j)
+    beside = j + 1 - 2 * int_rem(j, 2)
+
+    @pl.when(step == 2)
+    def _():
+        for s in range(OWN_ROWS):
+            for c in range(2):
+                side_send(away_pair + c, s).start()
+
+    def back_send(s):
+        row = row_of(OWN_ROWS * i + s)
+        target, slot = int_div(row, OWN_ROWS), int_rem(row, OWN_ROWS)
+        return target, (
+            lambda: remote(
+                out_sum.at[s], trunk_grad.at[slot], ss_back.at[s], rs_back.at[slot], pix=target
+            ),
+            lambda: pltpu.make_async_copy(out_sum.at[s], trunk_grad.at[slot], rs_back.at[slot]),
+        )
+
+    def side_arrival(turn, s):
+        dst = out_in.at[turn, s]
+        return remote(dst, dst, ss_side.at[turn, s], rs_side.at[turn, s], chan=beside)
 
     @pl.when(step == 5)
     def _():
+        for s in range(OWN_ROWS):
+            side_send(beside, s).start()
         for half in range(2):
             posts.arrive(marks["far", half], g_rows(2, spot.core, half))
         marks["mate", 2] = posts.post(
             lambda: (g_rows(2, spot.core), g_rows(2, spot.core), {"pix": spot.mate})
         )
+        for s in range(OWN_ROWS):
+            held = out[j, s].astype(F32)
+            for turn in range(3):
+                side_arrival(turn, s).wait_recv()
+                held = held + out_in[turn, s].astype(F32)
+            out_sum[s] = held.astype(BF16)
+            target, (away, here) = back_send(s)
+            pl.when(target != i)(lambda: away().start())
+            pl.when(target == i)(lambda: here().start())
         for d in (0, 1, -1, 2):
             posts.arrive(marks["mate", d], g_rows(-d, 1 - spot.core))
         own_copy().wait()
         for s in range(OWN_ROWS):
+            pltpu.make_async_copy(out_sum.at[s], trunk_grad.at[s], rs_back.at[s]).wait()
+            target, (away, here) = back_send(s)
+            pl.when(target != i)(lambda: away().wait_send())
+            for c in range(2):
+                side_send(away_pair + c, s).wait_send()
+            side_send(beside, s).wait_send()
             pltpu.make_async_copy(maps_sum.at[s], maps_out.at[s], rs_row.at[s]).wait()
             target, (away, here) = row_send(s)
             pl.when(target != i)(lambda: away().wait_send())
         posts.finish()
 
 
-def heads_input_grad(keep, grad_mid, head_part, kernels, point):
+def pair_at(n, chan):
+    return int_rem(1 + n - int_div(chan, 2) + 2, 2)
+
+
+def heads_input_grad(keep, grad_mid, head_part, kernels, point, *pool_operands):
     pixels = OWN_ROWS * TILE_W
     block = 1024
     whole = pl.BlockSpec(memory_space=pltpu.VMEM)
     hbm = pl.BlockSpec(memory_space=pl.ANY)
     dma = pltpu.SemaphoreType.DMA
-    maps = (OWN_ROWS, TILE_W, BRANCH)
+    maps, trunk = (OWN_ROWS, TILE_W, BRANCH), (OWN_ROWS, TILE_W, 512)
     return pl.pallas_call(
         heads_input_grad_kernel,
         grid=(2, 3),
@@ -849,18 +858,19 @@
             pl.BlockSpec(memory_space=pltpu.SMEM),
             whole,
             whole,
-            pl.BlockSpec((TASKS, 1, 3, 3, HEAD, block), lambda n, r: (0, r, 0, 0, 0, n)),
-            pl.BlockSpec((TASKS, HEAD, block), lambda n, r: (0, 0, n)),
-        ],
-        out_specs=[
-            pl.BlockSpec((block // 512, pixels, 512), lambda n, r: (n, 0, 0)),
-            hbm,
-            hbm,
-        ],
+            pl.BlockSpec((TASKS, 1, 3, 3, HEAD, block), lambda n, r: (0, r, 0, 0, 0, pair_at(n, lax.axis_index("chan")))),
+            pl.BlockSpec(
+                (TASKS, HEAD, block), lambda n, r: (0, 0, pair_at(n, lax.axis_index("chan")))
+            ),
+        ]
+        + [whole] * 6,
+        out_specs=[hbm, hbm, hbm, whole, whole],
         out_shape=[
-            jax.ShapeDtypeStruct((CHAN, pixels, 512), BF16),
+            jax.ShapeDtypeStruct(trunk, BF16),
             jax.ShapeDtypeStruct((GROUP_ROWS, TILE_W, 4 * BRANCH), BF16),
             jax.ShapeDtypeStruct(maps, BF16),
+            jax.ShapeDtypeStruct((OWN_ROWS, 512), F32),
+            jax.ShapeDtypeStruct((8, BRANCH), F32),
         ],
         scratch_shapes=[
             pltpu.VMEM((9, EXT_ROWS, PADDED, 2 * HEAD), F32),
@@ -869,11 +879,22 @@
             pltpu.VMEM((2, REACH, TILE_W, 4 * BRANCH), BF16),
             pltpu.VMEM((CHAN - 1, *maps), BF16),
             pltpu.VMEM(maps, BF16),
+            pltpu.VMEM((CHAN, *trunk), BF16),
+            pltpu.VMEM((CHAN - 1, *trunk), BF16),
+            pltpu.VMEM(trunk, BF16),
+            pltpu.VMEM((GROUP, 8, 256), F32),
+            pltpu.VMEM((4, 8, 256), F32),
+            pltpu.VMEM((CHAN, 16, 512), BF16),
+            pltpu.VMEM((CHAN - 1, 16, 512), BF16),
             dma((OWN_ROWS,)),
             dma((OWN_ROWS,)),
-            dma((16,)),
-            dma((16,)),
+            dma((32,)),
+            dma((32,)),
             dma((1,)),
+            dma((CHAN - 1, OWN_ROWS)),
+            dma((CHAN - 1, OWN_ROWS)),
+            dma((OWN_ROWS,)),
+            dma((OWN_ROWS,)),
         ],
         compiler_params=pltpu.CompilerParams(
             collective_id=3, has_side_effects=True, vmem_limit_bytes=VMEM_LIMIT
@@ -882,7 +903,7 @@
             flops=12_000_000_000, bytes_accessed=28_000_000, transcendentals=0
         ),
         name="heads_input_grad",
-    )(keep, grad_mid, head_part, kernels, point)
+    )(keep, grad_mid, head_part, kernels, point, *pool_operands)
 
 
 class GroupSum:
@@ -988,38 +1009,88 @@
 
 
 def section_forward_kernel(
-    pixels, wr, wd, we, vec_mid, vec_feat, keep, tile_rows, sizes,
-    trunk, unit_r, unit_d, unit_e, act_r, act_d, wr_all, inv_mid, inv_feat, mean_all,
-    part_out, part_in, near_m, across_m, near_f, across_f, near_t, across_t, send_sems, recv_sems,
+    pixels, wr, wd, we, vec_mid, vec_feat, keep, tile_rows, sizes, project,
+    x_ext, unit_r, unit_d, unit_e, act_r, act_d, wr_all, inv_mid, inv_feat, mean_all, project_all,
+    trunk, project_out, part_out, part_in, near_m, across_m, near_f, across_f, near_t, across_t,
+    *sems,
 ):
+    send_sems, recv_sems, sems = sems[0], sems[1], sems[2:]
     spot = Spot()
     links = Links(send_sems, recv_sems)
+    rows_out = RowGather(REACH, trunk, x_ext, spot, sems)
     j = spot.j
-    peers = [{"chan": spot.chan(d)} for d in (1, 2, 3)] + spot.sum_peers()
-    for d in range(CHAN):
-        peers += [{"pix": p, "chan": spot.chan(d)} for p in (spot.before, spot.after)]
-    greet(peers)
-
-    def block(chan):
-        return pl.ds(pl.multiple_of(FEAT_OWN * chan, FEAT_OWN), FEAT_OWN)
-
+    expected = rows_out.greet()
+    greet(
+        [{"chan": spot.chan(d)} for d in (1, 2, 3)]
+        + spot.sum_peers()
+        + [{"pix": p} for p in (spot.before, spot.after, spot.mate)],
+        expected,
+    )
+    half = FEAT_OWN // 2
+
+    def half_of(chan, core):
+        return pl.ds(pl.multiple_of(FEAT_OWN * chan + half * core, half), half)
+
+    own_half = half_of(0, spot.core)
+    other_half = half_of(0, 1 - spot.core)
     sent = {
-        d: links.send(wr.at[block(spot.chan(d))], wr_all.at[j], chan=spot.chan(d)) for d in (2, 1, 3)
+        d: links.send(
+            wr.at[half_of(spot.chan(d), spot.core)], wr_all.at[j, own_half], chan=spot.chan(d)
+        )
+        for d in (2, 1, 3)
     }
-    wr_all[j] = wr[block(j)]
+    wr_all[j] = wr[pl.ds(pl.multiple_of(FEAT_OWN * j, FEAT_OWN), FEAT_OWN)]
     pre = dot_nn(pixels[...], wr_all[j])
+    for c in range(CHAN):
+        for b in range(5):
+            lane = HEAD * (b % 2)
+            project_out[c, b // 2, :, :, lane : lane + HEAD] = project[
+                :, :, 256 * b + HEAD * c : 256 * b + HEAD * (c + 1)
+            ]
+        project_out[c, 2, :, :, HEAD:] = jnp.zeros((TASKS, HEAD, HEAD), BF16)
+    mates = {}
+    for d in (1, 3, 2):
+        source = spot.chan(-d)
+        links.arrive(sent[d], wr_all.at[source, own_half])
+        mates[d] = links.send(
+            wr_all.at[source, own_half], wr_all.at[source, own_half], pix=spot.mate
+        )
     back = {}
     for d in (1, 3, 2):
         source = spot.chan(-d)
-        links.arrive(sent[d], wr_all.at[source])
+        links.arrive(mates[d], wr_all.at[source, other_half])
         part_out[d - 1] = dot_nn(pixels[...], wr_all[source]).astype(BF16)
         back[d] = links.send(part_out.at[d - 1], part_in.at[d - 1], chan=source)
     for d in (1, 3, 2):
         links.arrive(back[d], part_in.at[d - 1])
         pre = pre + part_in[d - 1].astype(F32)
 
+    project_sent = {}
+
+    def send_project():
+        for d in (2, 1, 3):
+            for last, part in ((False, spot.core), (True, 2)):
+                project_sent[d, last] = links.send(
+                    project_out.at[spot.chan(d), part], project_all.at[j, part], chan=spot.chan(d)
+                )
+
+    def swap_project():
+        for d in (1, 3, 2):
+            source = spot.chan(-d)
+            links.arrive(project_sent[d, False], project_all.at[source, spot.core])
+            links.arrive(project_sent[d, True], project_all.at[source, 2])
+            project_sent[d] = links.send(
+                project_all.at[source, spot.core], project_all.at[source, spot.core], pix=spot.mate
+            )
+
+    todo = [send_project, lambda: None, swap_project]
+
+    def meanwhile():
+        if todo:
+            todo.pop(0)()
+
     def norm(value, near, across, gain, bias):
-        sums = sum_over_pix(two_sums(value, value * value), near, across, spot, links)
+        sums = sum_over_pix(two_sums(value, value * value), near, across, spot, links, meanwhile)
         center = sums[0:1] / PIXELS
         inv = lax.rsqrt(sums[1:2] / PIXELS - center * center + eps)
         unit = (value - center) * inv
@@ -1031,15 +1102,17 @@
     act_r[j, own] = silu(normed).astype(BF16).reshape(OWN_ROWS, TILE_W, MID_OWN)
     low, high = slice(0, section_rate), slice(section_rate + OWN_ROWS, 2 * section_rate + OWN_ROWS)
     first, last = slice(section_rate, 2 * section_rate), slice(OWN_ROWS, section_rate + OWN_ROWS)
+    sent = {
+        d: links.send(act_r.at[j, own], act_r.at[j, own], chan=spot.chan(d)) for d in (2, 1, 3)
+    }
     arrivals = []
-    for d in (2, 1, 3, 0):
-        to, source = spot.chan(d), spot.chan(-d)
+    for d in (0, 1, 3, 2):
+        source = spot.chan(-d)
         if d:
-            n = links.send(act_r.at[j, own], act_r.at[j, own], chan=to)
-            arrivals.append((n, act_r.at[source, own]))
-        n = links.send(act_r.at[j, first], act_r.at[j, high], pix=spot.before, chan=to)
+            links.arrive(sent[d], act_r.at[source, own])
+        n = links.send(act_r.at[source, first], act_r.at[source, high], pix=spot.before)
         arrivals.append((n, act_r.at[source, high]))
-        n = links.send(act_r.at[j, last], act_r.at[j, low], pix=spot.after, chan=to)
+        n = links.send(act_r.at[source, last], act_r.at[source, low], pix=spot.after)
         arrivals.append((n, act_r.at[source, low]))
     for n, dst in arrivals:
         links.arrive(n, dst)
@@ -1068,30 +1141,36 @@
     inv_feat[...] = jnp.concatenate([inv_e, jnp.zeros((7, FEAT_OWN), F32)], axis=0)
     out = silu(normed + pixels[...].astype(F32)).astype(BF16)
     trunk[...] = out.reshape(OWN_ROWS, TILE_W, FEAT_OWN)
+    rows_out.send_rows()
     row_sums = jnp.sum(out.astype(F32).reshape(OWN_ROWS, TILE_W, FEAT_OWN), axis=1)
     sums = jnp.zeros((8, FEAT_OWN), F32)
     for r in range(OWN_ROWS):
         sums = sums + tile_rows[:, r : r + 1] * row_sums[r : r + 1]
-    sums = sum_over_pix(sums, near_t, across_t, spot, links)
+    todo[:] = [rows_out.pass_own]
+    sums = sum_over_pix(sums, near_t, across_t, spot, links, meanwhile)
     mean = jnp.concatenate([sums / sizes[:, 0:1], jnp.zeros((8, FEAT_OWN), F32)], axis=0)
     mean_all[j] = mean.astype(BF16)
     sent = {d: links.send(mean_all.at[j], mean_all.at[j], chan=spot.chan(d)) for d in (2, 1, 3)}
+    rows_out.pass_sides()
     for d in (1, 3, 2):
         links.arrive(sent[d], mean_all.at[spot.chan(-d)])
+        links.arrive(project_sent[d], project_all.at[spot.chan(-d), 1 - spot.core])
+    project_all[j] = project_out[j]
+    rows_out.finish()
     links.finish()
 
 
-def section_forward(pixels, wr, wd, we, vec_mid, vec_feat, keep, tile_rows, sizes):
+def section_forward(*operands):
     whole = pl.BlockSpec(memory_space=pltpu.VMEM)
     shape = jax.ShapeDtypeStruct
     mid, feat = (OWN, MID_OWN), (OWN, FEAT_OWN)
     dma = pltpu.SemaphoreType.DMA
     return pl.pallas_call(
         section_forward_kernel,
-        in_specs=[whole] * 9,
-        out_specs=[whole] * 10,
+        in_specs=[whole] * 10,
+        out_specs=[pl.BlockSpec(memory_space=pl.ANY)] + [whole] * 10,
         out_shape=[
-            shape((OWN_ROWS, TILE_W, FEAT_OWN), BF16),
+            shape((CHAN, EXT_ROWS, TILE_W, FEAT_OWN), BF16),
             shape(mid, F32),
             shape(mid, F32),
             shape(feat, F32),
@@ -1101,8 +1180,11 @@
             shape((8, MID_OWN), F32),
             shape((8, FEAT_OWN), F32),
             shape((CHAN, 16, FEAT_OWN), BF16),
+            shape((CHAN, 3, TASKS, HEAD, 2 * HEAD), BF16),
         ],
         scratch_shapes=[
+            pltpu.VMEM((OWN_ROWS, TILE_W, FEAT_OWN), BF16),
+            pltpu.VMEM((CHAN, 3, TASKS, HEAD, 2 * HEAD), BF16),
             pltpu.VMEM((3, *mid), BF16),
             pltpu.VMEM((3, *mid), BF16),
             pltpu.VMEM((2, GROUP, 8, MID_OWN), F32),
@@ -1111,8 +1193,9 @@
             pltpu.VMEM((4, 8, FEAT_OWN), F32),
             pltpu.VMEM((GROUP, 8, FEAT_OWN), F32),
             pltpu.VMEM((4, 8, FEAT_OWN), F32),
-            dma((64,)),
-            dma((64,)),
+            dma((80,)),
+            dma((80,)),
+            *gather_sems(REACH),
         ],
         compiler_params=pltpu.CompilerParams(
             collective_id=5, has_side_effects=True, vmem_limit_bytes=VMEM_LIMIT
@@ -1121,7 +1204,7 @@
             flops=2_000_000_000, bytes_accessed=120_000_000, transcendentals=0
         ),
         name="section_forward",
-    )(pixels, wr, wd, we, vec_mid, vec_feat, keep, tile_rows, sizes)
+    )(*operands)
 
 
 class Scatter:
@@ -1185,20 +1268,19 @@
 
 def section_backward_kernel(
     trunk_grad, pixels, unit_r, unit_d, unit_e, act_r, act_d, wr_all, wd_cat, we, vec_mid, vec_feat,
-    inv_mid, inv_feat, keep, pool_rows, place_rows, tile_cols, sizes, pre_pooled, pooled, projects,
-    keep_group, x_group, g_group, *refs,
+    inv_mid, inv_feat, keep, mean_rows, projects, keep_group, x_group, g_group, *refs,
 ):
     (
         grad_pixels, mid_grads, feat_grads, grad_reduce, grad_dilate, grad_expand, grad_project,
-        grad_pooled, grad_atrous, grad_point,
-    ) = refs[:10]
-    scratch = refs[10:]
+        grad_atrous, grad_point,
+    ) = refs[:9]
+    scratch = refs[9:]
     (
-        side_out, side_in, halo, taps, full, mean_out, mean_in, project_in, project_wide, reduce_out,
-        near_m, across_m, near_f, across_f, near_p, across_p, x_all, x_base, x_now, g_all, g_now,
-    ) = scratch[:21]
+        side_out, side_in, halo, taps, full, project_in, project_wide, reduce_out,
+        near_m, across_m, near_f, across_f, x_all, x_base, x_now, g_all, g_now,
+    ) = scratch[:17]
     send_sems, recv_sems, last_sems, load_sems = scratch[-4:]
-    buffers = scratch[21:-4]
+    buffers = scratch[17:-4]
     spot = Spot()
     links = Links(send_sems, recv_sems)
     i, j = spot.i, spot.j
@@ -1313,35 +1395,12 @@
         for d in (2, 1, 3)
     }
 
-    sums = jnp.zeros((8, 2 * MID_OWN), F32)
-    for r in range(OWN_ROWS):
-        sums = sums + place_rows[:, r : r + 1] * pool_rows[r : r + 1]
-    sums = sum_over_pix(sums, near_p, across_p, spot, links, meanwhile)
-    pooled_pre = (sums[:, :BRANCH] * slope(pre_pooled[...])).astype(BF16)
-    grad_pooled[...] = pooled_pre.astype(F32)
-    wide = jnp.concatenate([pooled_pre.astype(F32), jnp.zeros((8, BRANCH), F32)], axis=0).astype(BF16)
-    for c in range(CHAN):
-        mean_out[c] = dot_nn(wide, pooled[:, FEAT_OWN * c : FEAT_OWN * (c + 1)]).astype(BF16)
-    sent = {
-        d: links.send(mean_out.at[spot.chan(d)], mean_in.at[d - 1], chan=spot.chan(d))
-        for d in (2, 1, 3)
-    }
-    meanwhile()
-    mean = mean_out[j].astype(F32)
-    for d in (1, 3, 2):
-        links.arrive(sent[d], mean_in.at[d - 1])
-        mean = mean + mean_in[d - 1].astype(F32)
-    mean = mean[0:8] / sizes[:, 0:1]
-    mean_rows = jnp.zeros((OWN_ROWS, FEAT_OWN), F32)
-    for k in range(8):
-        mean_rows = mean_rows + tile_cols[:, k : k + 1] * mean[k : k + 1]
-
     def norm_back(grad, unit, near, across, scale):
         sums = sum_over_pix(two_sums(grad, grad * unit), near, across, spot, links, meanwhile)
         pre = scale * (grad - sums[0:1] / PIXELS - unit * (sums[1:2] / PIXELS))
         return pre.astype(BF16), sums
 
-    grad_trunk = trunk_grad[...].astype(F32) + mean_rows[:, None, :]
+    grad_trunk = trunk_grad[...].astype(F32) + mean_rows[...][:, None, :]
     grad_trunk = grad_trunk.reshape(OWN, FEAT_OWN)
     unit = unit_e[...]
     summed = unit * vec_feat[0:1] + vec_feat[1:2] + pixels[...].astype(F32)
@@ -1498,10 +1557,10 @@
     mid, feat = (OWN, MID_OWN), (OWN, FEAT_OWN)
     return pl.pallas_call(
         section_backward_kernel,
-        in_specs=[whole] * 22
+        in_specs=[whole] * 17
         + [pl.BlockSpec(memory_space=pltpu.SMEM)]
         + [pl.BlockSpec(memory_space=pl.ANY)] * 2,
-        out_specs=[whole] * 10,
+        out_specs=[whole] * 9,
         out_shape=[
             shape(feat, BF16),
             shape((8, MID_OWN), F32),
@@ -1510,7 +1569,6 @@
             shape((9, 16, MID_OWN), F32),
             shape((16, FEAT_OWN), F32),
             shape((TASKS, 48, HEAD), F32),
-            shape((8, BRANCH), F32),
             shape((9, HEAD, 3 * BRANCH), F32),
             shape((1, HEAD, BRANCH), F32),
         ],
@@ -1520,8 +1578,6 @@
             pltpu.VMEM((OWN_ROWS + 2 * section_rate, TILE_W, MID_OWN), BF16),
             pltpu.VMEM((OWN, 9 * MID_OWN), BF16),
             pltpu.VMEM((CHAN, *mid), BF16),
-            pltpu.VMEM((CHAN, 16, FEAT_OWN), BF16),
-            pltpu.VMEM((3, 16, FEAT_OWN), BF16),
             pltpu.VMEM((3, 5, TASKS, HEAD, HEAD), BF16),
             pltpu.VMEM((CHAN, 5, TASKS, HEAD, HEAD), F32),
             pltpu.VMEM((HEAD, MID_OWN), F32),
@@ -1529,8 +1585,6 @@
             pltpu.VMEM((2, 4, 8, MID_OWN), F32),
             pltpu.VMEM((GROUP, 8, FEAT_OWN), F32),
             pltpu.VMEM((4, 8, FEAT_OWN), F32),
-            pltpu.VMEM((GROUP, 8, 2 * MID_OWN), F32),
-            pltpu.VMEM((4, 8, 2 * MID_OWN), F32),
             pltpu.VMEM((CHAN, GROUP_ROWS, TILE_W, 128), BF16),
             pltpu.VMEM((GROUP_ROWS * TILE_W, 256), BF16),
             pltpu.VMEM((GROUP_ROWS * TILE_W, 256), BF16),
@@ -1598,11 +1652,11 @@
     )
     vec_feat = jnp.pad(jnp.stack([expand_gain, expand_bias]), ((0, 6), (0, 0)))
     (
-        trunk_out, unit_reduce, unit_dilate, unit_expand, act_reduce, act_dilate, reduce_all, inv_mid,
-        inv_feat, mean_all,
+        x_ext, unit_reduce, unit_dilate, unit_expand, act_reduce, act_dilate, reduce_all, inv_mid,
+        inv_feat, mean_all, project_all,
     ) = section_forward(
         pixels, reduce_weight, dilate_weight, expand_weight, vec_mid, vec_feat, keep_section,
-        row_onehot.T, sizes,
+        row_onehot.T, sizes, project_weight,
     )
     tile_mean = jnp.moveaxis(mean_all[:, :tile_count], 0, 1).reshape(tile_count, -1)
     group_x = device // GROUP
@@ -1620,7 +1674,6 @@
     keep_group = lax.dynamic_slice_in_dim(keep_all, group_x * GROUP_ROWS, GROUP_ROWS, axis=1)
     place_tiles = lax.dynamic_slice_in_dim(tile_number[placed], device * OWN_ROWS, OWN_ROWS)
     place_onehot = (place_tiles[:, None] == tiles[None, :]).astype(F32)
-    x_ext = gather_rows(trunk_out, REACH, 1, "gather_trunk")
     pre_pooled = jnp.einsum("kc,tdc->ktd", tile_mean, pooled_weight, preferred_element_type=F32)
     pooled_act = jax.nn.silu(pre_pooled).astype(jnp.bfloat16).reshape(tile_count, BRANCH)
     pooled_rows = jnp.dot(
@@ -1632,30 +1685,24 @@
     task_weight = jax.nn.softmax(task_draws.astype(jnp.float32) / 3.0)
     grad_maps = (task_weight[:, None, None] * cotangent.astype(jnp.float32)).astype(jnp.bfloat16)
     maps_own = jnp.moveaxis(grad_maps, 0, 1).reshape(OWN_ROWS, TILE_W, BRANCH)
-    project_cut = jnp.moveaxis(project_weight.reshape(TASKS, HEAD, 5, CHAN, HEAD), 3, 0)
-    project_own = lax.all_to_all(project_cut, "chan", 0, 0, tiled=True)
-    project_own = jnp.transpose(project_own, (3, 1, 4, 0, 2))[jnp.array(BRANCH_ORDER)]
-    same = jnp.eye(TASKS, dtype=jnp.bfloat16)[None, :, None, None, :, None]
-    spread = (project_own[:, :, :, :, None, :] * same).reshape(5, BRANCH, 256 * TASKS)
     kernels = atrous_weight.reshape(TASKS, 3, 3, 3, HEAD, -1)
     grad_pre, head_part, grad_project, pool_rows, x_group = heads_forward(
-        keep_own, x_ext, maps_own, kernels, point_weight, spread, pooled_pixels
+        keep_own, x_ext, maps_own, kernels, point_weight, project_all, pooled_pixels
     )
-    trunk_parts, g_group, task_maps = heads_input_grad(
+    trunk_grad, g_group, task_maps, mean_rows, grad_pooled = heads_input_grad(
         keep_own, grad_pre.reshape(OWN_ROWS, TILE_W, 4 * BRANCH),
-        head_part.reshape(CHAN, OWN_ROWS, TILE_W, BRANCH), kernels, point_weight,
+        head_part.reshape(CHAN, OWN_ROWS, TILE_W, BRANCH), kernels, point_weight, pool_rows,
+        place_onehot.T, row_onehot, sizes, pre_pooled.reshape(tile_count, BRANCH),
+        pooled_weight.reshape(BRANCH, -1),
     )
     task_maps = jnp.moveaxis(task_maps.reshape(pixel_count, TASKS, HEAD), 1, 0)
-    trunk_grad = return_rows(trunk_parts.reshape(CHAN, OWN_ROWS, TILE_W, -1), 4, "return_trunk")
     (
         grad_pixels, mid_grads, feat_grads, grad_reduce, grad_dilate, grad_expand, grad_project,
-        grad_pooled, grad_atrous, grad_point,
+        grad_atrous, grad_point,
     ) = section_backward(
         trunk_grad, pixels, unit_reduce, unit_dilate, unit_expand, act_reduce, act_dilate, reduce_all,
         jnp.moveaxis(dilate_weight, 0, 1).reshape(-1, 9 * MID_OWN), expand_weight, vec_mid, vec_feat,
-        inv_mid, inv_feat, keep_section, pool_rows, place_onehot.T, row_onehot, sizes,
-        pre_pooled.reshape(tile_count, BRANCH), pooled_weight.reshape(BRANCH, -1), grad_project,
-        keep_group, x_group, g_group,
+        inv_mid, inv_feat, keep_section, mean_rows, grad_project, keep_group, x_group, g_group,
     )
     grad_atrous_weight = jnp.transpose(
         grad_atrous.reshape(3, 3, HEAD, 3, TASKS, HEAD), (4, 0, 3, 1, 2, 5)

time: 420 us -> 356 us (0.85)
  the two profiles are of different devices: /device:TPU:5 before, /device:TPU:7 now
where the time goes in v4:
time: 356 us; the launch traced here: 350 us
  Pallas kernels  310 us (87%)
  local copies, waits for them, and re-layouts  25.9 us (7%)
  other arithmetic  10.4 us (3%)
    pallas_call x1, Pallas kernels, section_backward(): pl.pallas_call(section_backward_kernel, in_specs=[whole] * 17 + [pl.Block...  102 us
    pallas_call x1, Pallas kernels, section_forward(): pl.pallas_call(section_forward_kernel, in_specs=[whole] * 10, out_specs=[...  98.2 us
    pallas_call x1, Pallas kernels, heads_input_grad(): pl.pallas_call(heads_input_grad_kernel, grid=(2, 3), in_specs=[pl.BlockSp...  67.2 us
    pallas_call x1, Pallas kernels, heads_forward(): pl.pallas_call(heads_forward_kernel, grid=(9,), in_specs=[pl.BlockSpec(me...  42.9 us

profile of v4, /device:TPU:7, one launch (start us, length us, event | category | flops | bytes accessed | tf_op | source)
XLA Modules:
  0.0 349.8 jit_solution(1671601934598269688)
XLA Ops:
  0.6 0.7 pad_clamp_fusion
  1.3 2.0 gather_fusion
  3.3 0.7 add.54
  4.2 0.7 constant_dynamic-slice_fusion.keep
  4.9 1.3 select_maximum_fusion.1.vec_mid
  6.2 1.3 select_maximum_fusion.vec_feat
  7.5 0.8 compare_bitcast_fusion.1
  8.4 0.8 compare_bitcast_fusion
  9.3 1.0 broadcast_in_dim.15.keep
  11.0 0.8 convert_reduce_fusion
  12.5 98.2 %section_forward.1 = (bf16[4,14,64,512]{3,2,1,0:T(8,128)(2,1)}, f32[512,128]{1,0:T(8,128)}, f32[512,128]{1,0:T(8,128)}, f32[512,512]{1,0:T(8,128)}, bf16[4,16,64...) custom-call(bf16[512,512]{1,0:T(8,128)(2,1)} %pixels.3, ...), custom_call_target="tpu_custom_call" | custom-call | flops 2000000000 | bytes 120000000 | tf_op jit(solution)/shard_map/section_forward/pallas_call | solution.py:1168
  111.3 1.3 fusion.13
  112.5 1.3 broadcast_divide_fusion
  114.2 1.0 copy.62.maps_own
  115.2 0.8 slice.51
  116.6 0.7 broadcast_in_dim.17
  117.3 42.9 %heads_forward.1 = (bf16[512,768]{1,0:T(8,128)(2,1)}, bf16[4,512,192]{2,1,0:T(8,128)(2,1)}, bf16[4,5,3,64,64]{4,3,2,1,0:T(8,128)(2,1)}, f32[8,256]{1,0:T(8,128)}, bf16[4,64,64,128]{3,2,1,0:T(8,128)(2,1)}) custom-call(s32[9,8]{1,0:T(8,128)} %constant_dynamic-slice_fusion.keep, bf16[4,14,64,512]{3,2,1,0:T(8,128)(2,1)} %get-tuple-element.45.x_hbm, ...), custom_call_target="tpu_custom_call" | custom-call | flops 12000000000 | bytes 28000000 | tf_op jit(solution)/shard_map/heads_forward/pallas_call | solution.py:524
  160.3 0.7 reshape.111.pre_pooled
  161.0 67.2 %heads_input_grad.1 = (bf16[8,64,512]{2,1,0:T(8,128)(2,1)}, bf16[64,64,768]{2,1,0:T(8,128)(2,1)}, bf16[8,64,192]{2,1,0:T(8,128)(2,1)}, f32[8,512]{1,0:T(8,128)}, f32[8,192]{1,0:T(8,128)}) custom-call(s32[9,8]{1,0:T(8,128)} %constant_dynamic-slice_fusion.keep, bf16[8,64,768]{2,1,0:T(8,128)(2,1)} %bitcast.73, bf16[4,8,64,192]{3,2,1,0:T(8,128)(2,1)} %bitcast.72, ...), custom_call_target="tpu_custom_call" | custom-call | flops 12000000000 | bytes 28000000 | tf_op jit(solution)/shard_map/heads_input_grad/pallas_call | solution.py:854
  228.2 1.2 copy.64
  229.4 0.9 reshape.113
  230.9 1.4 copy.66.wd_cat
  232.3 0.7 constant_dynamic-slice_fusion.1.keep_group
  233.0 101.7 %section_backward.1 = (bf16[512,512]{1,0:T(8,128)(2,1)}, f32[8,128]{1,0:T(8,128)}, f32[8,512]{1,0:T(8,128)}, f32[64,128]{1,0:T(8,128)}, f32[9,16,128]{2,1,0:T(8,...) custom-call(bf16[8,64,512]{2,1,0:T(8,128)(2,1)} %get-tuple-element.52.trunk_grad, ...), custom_call_target="tpu_custom_call" | custom-call | flops 16000000000 | bytes 250000000 | tf_op jit(solution)/shard_map/section_backward/pallas_call | solution.py:1558
  334.7 1.3 slice_bitcast_fusion
  336.1 1.4 fusion.14
  337.4 0.9 copy.67
  338.4 0.7 copy.71
  339.1 2.6 copy.68
  341.8 2.6 copy.69
  344.5 1.5 convolution_bitcast_fusion
  346.7 0.8 copy.78
  (52 shorter events, 6.6 us)
Async XLA Ops:
  12.5 98.2 %copy-start.9 = (s32[3]{0:T(128)S(1)}, s32[3]{0:T(128)}, u32[]{:S(2)}) copy-start(s32[3]{0:T(128)} %param.20) | copy-start | bytes 40
  12.5 101.3 %copy-start.3 = (bf16[3,512,64]{1,2,0:T(8,128)(2,1)S(1)}, bf16[3,512,64]{1,2,0:T(8,128)(2,1)}, u32[]{:S(2)}) copy-start(bf16[3,512,64]{1,2,0:T(8,128)(2,1)} %param.34) | copy-start | bytes 589828
  12.5 103.4 %copy-start.1 = (bf16[3,64,2048]{2,1,0:T(8,128)(2,1)S(1)}, bf16[3,64,2048]{2,1,0:T(8,128)(2,1)}, u32[]{:S(2)}) copy-start(bf16[3,64,2048]{2,1,0:T(8,128)(2,1)} %param.32) | copy-start | bytes 2359300
  161.0 69.3 %copy-start = (bf16[9,512,128]{2,1,0:T(8,128)(2,1)S(1)}, bf16[9,512,128]{2,1,0:T(8,128)(2,1)}, u32[]{:S(2)}) copy-start(bf16[9,512,128]{2,1,0:T(8,128)(2,1)} %wd.1) | copy-start | bytes 3538948
  341.8 2.6 copy-start.8
  341.8 4.2 %copy-start.5 = (f32[3,48,64]{2,1,0:T(8,128)S(1)}, f32[3,48,64]{2,1,0:T(8,128)}, u32[]{:S(2)}) copy-start(f32[3,48,64]{2,1,0:T(8,128)} %get-tuple-element.74) | copy-start | bytes 110596
  341.8 4.9 %copy-start.2 = (bf16[512,512]{1,0:T(8,128)(2,1)S(1)}, bf16[512,512]{1,0:T(8,128)(2,1)}, u32[]{:S(2)}) copy-start(bf16[512,512]{1,0:T(8,128)(2,1)} %get-tuple-element.155) | copy-start | bytes 1572868
  344.4 3.1 copy-start.7
  344.4 3.7 %copy-start.4 = (f32[9,16,128]{2,1,0:T(8,128)S(1)}, f32[9,16,128]{2,1,0:T(8,128)}, u32[]{:S(2)}) copy-start(f32[9,16,128]{2,1,0:T(8,128)} %get-tuple-element.159) | copy-start | bytes 221188
  344.4 4.3 %copy-start.6 = (f32[16,512]{1,0:T(8,128)S(1)}, f32[16,512]{1,0:T(8,128)}, u32[]{:S(2)}) copy-start(f32[16,512]{1,0:T(8,128)} %get-tuple-element.162) | copy-start | bytes 98308

commit v5 on v4

--- a/solution.py
+++ b/solution.py
@@ -17,7 +17,6 @@
 EXT_ROWS = OWN_ROWS + 2 * REACH
 HEAD = 64
 BRANCH = TASKS * HEAD
-TILES = 7
 BRANCH_ORDER = (1, 2, 3, 0, 4)
 BRANCH_PLACE = (3, 0, 1, 2, 4)
 
@@ -30,25 +29,14 @@
 VMEM_LIMIT = 60 * 2**20
 
 
-def place_of_row(row):
-    kind = row % 6
-    return 43 * kind - kind // 5 + row // 6
-
-
-def row_at_place(place):
-    kind = (place + place // 214) // 43
-    return 6 * (place - 43 * kind + kind // 5) + kind
-
-
-PLACED_ROWS = tuple(row_at_place(place) for place in range(NROWS))
-
-
 def int_div(a, b):
-    return lax.div(a, jnp.int32(b))
+    if b & (b - 1) == 0:
+        return lax.shift_right_logical(a, jnp.int32(b.bit_length() - 1))
+    return lax.shift_right_logical(a * (2**16 // b + 1), jnp.int32(16))
 
 
 def int_rem(a, b):
-    return lax.rem(a, jnp.int32(b))
+    return a - b * int_div(a, b)
 
 
 def place_of(row):
@@ -59,6 +47,50 @@
 def row_of(place):
     kind = int_div(place + int_div(place, 214), 43)
     return 6 * (place - 43 * kind + int_div(kind, 5)) + kind
+
+
+def tile_at(tiles, row):
+    return jnp.where((row >= 0) & (row < NROWS), tiles[jnp.clip(row, 0, NROWS - 1)], -1)
+
+
+def fill_keys(tiles, keys, first, count):
+    start = row_of(jnp.maximum(first, 0))
+
+    def one(n, carry):
+        row, kind = carry
+        inside = (first + n >= 0) & (first + n < NROWS)
+        keys[n] = jnp.where(inside, tiles[row] + 8 * kind, -1)
+        end = row + 6 >= NROWS
+        next_kind = jnp.where(end, jnp.minimum(kind + 1, 5), kind)
+        next_row = jnp.where(end, next_kind, row + 6)
+        return jnp.where(inside, next_row, row), jnp.where(inside, next_kind, kind)
+
+    lax.fori_loop(0, count, one, (start, int_rem(start, 6)))
+
+
+def fill_keep(tiles, keep, i):
+    for r in range(OWN_ROWS):
+        here = tile_at(tiles, OWN_ROWS * i + r)
+        for side, step in enumerate((-section_rate, section_rate)):
+            same = jnp.where(tile_at(tiles, OWN_ROWS * i + r + step) == here, 1.0, 0.0)
+            keep[side, TILE_W * r : TILE_W * (r + 1)] = jnp.full((TILE_W, 128), same, F32)
+
+
+def rows_at(value, tile):
+    row = lax.broadcasted_iota(jnp.int32, value.shape, 0)
+    return jnp.sum(jnp.where(row == tile, value, 0.0), axis=0, keepdims=True)
+
+
+def add_at(sums, row, tile):
+    return sums + jnp.where(lax.broadcasted_iota(jnp.int32, sums.shape, 0) == tile, row, 0.0)
+
+
+def tile_sizes(grid):
+    sizes = jnp.zeros((8, 128), F32)
+    for tile in range(8):
+        here = jnp.sum(jnp.where(grid == tile, 1.0, 0.0), axis=1, keepdims=True)
+        sizes = add_at(sizes, TILE_W * jnp.sum(here, axis=0, keepdims=True), tile)
+    return jnp.maximum(sizes, 1.0)
 
 
 def signal(sem, **where):
@@ -237,10 +269,11 @@
             self.copy(n, make).wait_send()
 
 
-def greet(peers, more=0):
+def greet(peers, more=0, meanwhile=lambda: None):
     barrier = pltpu.get_barrier_semaphore()
     for where in peers:
         signal(barrier, **where)
+    meanwhile()
     pl.semaphore_wait(barrier, len(peers) + more)
 
 
@@ -301,9 +334,9 @@
 
 
 def heads_forward_kernel(
-    keep, x_hbm, maps_own, kernel, point, project, pooled,
-    grad_pre, head_part, grad_project, pool_rows, x_group,
-    x, acc, pre, maps_in, relay, spread, sems, ss_row, rs_row, send_sems, recv_sems, own_sem,
+    tiles, draws, x_hbm, cotangent, kernel, point, project, mean_all, pooled_weight,
+    grad_pre, head_part, grad_project, pool_rows, x_group, pre_pooled,
+    keys, maps_own, pooled, x, acc, pre, maps_in, relay, spread, sems, ss_row, rs_row, send_sems, recv_sems, own_sem,
 ):
     step = pl.program_id(0)
     rate, row_tap = step // 3, step % 3
@@ -360,11 +393,45 @@
 
             target = int_div(place_of(OWN_ROWS * i + s), OWN_ROWS)
             expected = expected + (target != i).astype(jnp.int32)
+
+        def prepare():
+            lane = lax.broadcasted_iota(jnp.int32, (8, 128), 1)
+            drawn = jnp.full((8, 128), -1e30, F32)
+            for t in range(TASKS):
+                drawn = jnp.where(lane == t, draws[t].astype(F32) / 3.0, drawn)
+            grown = jnp.where(lane < TASKS, jnp.exp(drawn - jnp.max(drawn, axis=1, keepdims=True)), 0.0)
+            grown = grown / jnp.sum(grown, axis=1, keepdims=True)
+            for t in range(TASKS):
+                weight = jnp.sum(jnp.where(lane == t, grown, 0.0), axis=1, keepdims=True)[0:1]
+                scaled = (cotangent[t].astype(F32).T * weight).astype(BF16)
+                maps_own[:, :, HEAD * t : HEAD * (t + 1)] = scaled.reshape(OWN_ROWS, TILE_W, HEAD)
+            fill_keys(tiles, keys, OWN_ROWS * i - REACH, EXT_ROWS)
+            act = None
+            for c in range(CHAN):
+                term = dot_nt(mean_all[c], pooled_weight[:, 512 * c : 512 * (c + 1)])
+                act = term if act is None else act + term
+            pre_pooled[...] = act
+            act = silu(act).astype(BF16).astype(F32)
+            for r in range(OWN_ROWS):
+                row = rows_at(act, tiles[row_of(OWN_ROWS * i + r)])
+                pooled[TILE_W * r : TILE_W * (r + 1)] = jnp.broadcast_to(row, (TILE_W, BRANCH)).astype(
+                    BF16
+                )
+            spread[...] = jnp.zeros_like(spread)
+            for which, b in enumerate(BRANCH_ORDER):
+                for c in range(CHAN):
+                    for t in range(TASKS):
+                        start = BRANCH * c + HEAD * t
+                        spread[which, start : start + HEAD, HEAD * t : HEAD * (t + 1)] = project[
+                            c, b // 2, t, :, HEAD * (b % 2) : HEAD * (b % 2 + 1)
+                        ]
+
         greet(
             [where for _, where in ways]
             + [{"pix": spot.pix_in_z(d)} for d in (1, -1)]
             + [{"pix": spot.mate}],
             expected,
+            prepare,
         )
         for s in range(OWN_ROWS):
             target, (away, here) = row_send(s)
@@ -383,14 +450,6 @@
         marks["mate", 0] = posts.post(
             lambda: (x_slice(0), x_rows(0, spot.core), {"pix": spot.mate})
         )
-        spread[...] = jnp.zeros_like(spread)
-        for which, b in enumerate(BRANCH_ORDER):
-            for c in range(CHAN):
-                for t in range(TASKS):
-                    start = BRANCH * c + HEAD * t
-                    spread[which, start : start + HEAD, HEAD * t : HEAD * (t + 1)] = project[
-                        c, b // 2, t, :, HEAD * (b % 2) : HEAD * (b % 2 + 1)
-                    ]
         for copy in copies:
             copy.wait()
 
@@ -449,7 +508,8 @@
         product = dot_nt(window, kernel[:, 0, 0, b].reshape(BRANCH, -1))
         for r in range(OWN_ROWS):
             part = slice(TILE_W * r, TILE_W * (r + 1))
-            term = jnp.where(keep[step, r] > 0, product[part], 0.0)
+            same = keys[REACH + r] == keys[first + r]
+            term = jnp.where(same, product[part], 0.0)
             acc[b, part] = jnp.where(row_tap > 0, acc[b, part], 0.0) + term
 
     for which, dilation in enumerate(head_rates):
@@ -515,7 +575,7 @@
         posts.finish()
 
 
-def heads_forward(keep, x_ext, maps_own, kernels, point, project, pooled):
+def heads_forward(tiles, draws, x_ext, cotangent, kernels, point, project, mean_all, pooled_weight):
     pixels = OWN_ROWS * TILE_W
     feat = point.shape[2]
     whole = pl.BlockSpec(memory_space=pltpu.VMEM)
@@ -526,22 +586,28 @@
         grid=(9,),
         in_specs=[
             pl.BlockSpec(memory_space=pltpu.SMEM),
+            pl.BlockSpec(memory_space=pltpu.SMEM),
             hbm,
             whole,
             pl.BlockSpec((TASKS, 1, 1, 3, HEAD, feat), lambda s: (0, s // 3, s % 3, 0, 0, 0)),
             whole,
             whole,
             whole,
+            whole,
         ],
-        out_specs=[whole] * 4 + [hbm],
+        out_specs=[whole] * 4 + [hbm, whole],
         out_shape=[
             jax.ShapeDtypeStruct((pixels, 4 * BRANCH), BF16),
             jax.ShapeDtypeStruct((CHAN, pixels, BRANCH), BF16),
             jax.ShapeDtypeStruct((CHAN, 5, TASKS, HEAD, HEAD), BF16),
             jax.ShapeDtypeStruct((OWN_ROWS, 256), F32),
             jax.ShapeDtypeStruct((CHAN, GROUP_ROWS, TILE_W, 128), BF16),
+            jax.ShapeDtypeStruct((16, BRANCH), F32),
         ],
         scratch_shapes=[
+            pltpu.SMEM((EXT_ROWS,), jnp.int32),
+            pltpu.VMEM((OWN_ROWS, TILE_W, BRANCH), BF16),
+            pltpu.VMEM((pixels, BRANCH), BF16),
             pltpu.VMEM((EXT_ROWS, TILE_W, feat), BF16),
             pltpu.VMEM((3, pixels, BRANCH), F32),
             pltpu.VMEM((4, pixels, BRANCH), F32),
@@ -562,7 +628,7 @@
             flops=12_000_000_000, bytes_accessed=28_000_000, transcendentals=0
         ),
         name="heads_forward",
-    )(keep, x_ext, maps_own, kernels, point, project, pooled)
+    )(tiles, draws, x_ext, cotangent, kernels, point, project, mean_all, pooled_weight)
 
 
 PAD = 24
@@ -570,9 +636,9 @@
 
 
 def heads_input_grad_kernel(
-    keep, mid, parts, kernel, point, pool_rows, place_rows, tile_cols, sizes, pre_pooled, pooled,
-    trunk_grad, g_group, maps_out, mean_rows, grad_pooled,
-    wide, taps, acc, edges, maps_in, maps_sum, out, out_in, out_sum, near, across, mean_out, mean_in,
+    tiles, tile_grid, mid, parts, kernel, point, pool_rows, pre_pooled, pooled,
+    trunk_grad, g_group, maps_out, mean_rows, tall,
+    keys, wide, taps, acc, edges, maps_in, maps_sum, out, out_in, out_sum, near, across, mean_out, mean_in,
     ss_row, rs_row, send_sems, recv_sems, own_sem, ss_side, rs_side, ss_back, rs_back,
 ):
     n, rate = pl.program_id(0), pl.program_id(1)
@@ -598,10 +664,27 @@
         target, slot = int_div(row, OWN_ROWS), int_rem(row, OWN_ROWS)
         return target, (
             lambda: remote(
-                maps_sum.at[s], maps_out.at[slot], ss_row.at[s], rs_row.at[slot], pix=target
+                maps_sum.at[s], maps_out.at[:, slot], ss_row.at[s], rs_row.at[slot], pix=target
             ),
-            lambda: pltpu.make_async_copy(maps_sum.at[s], maps_out.at[slot], rs_row.at[slot]),
-        )
+            lambda: pltpu.make_async_copy(
+                maps_sum.at[s], maps_out.at[:, slot], rs_row.at[slot]
+            ),
+        )
+
+    def widen(start, part):
+        held = part[...].astype(F32)
+        for which in range(3):
+            for t in range(TASKS):
+                lane = BRANCH * which + HEAD * t
+                one = held[:, :, lane : lane + HEAD]
+                wide[3 * t + which, start : start + held.shape[0], PAD : PAD + TILE_W] = (
+                    jnp.concatenate([one, one], axis=2)
+                )
+
+    def prepare():
+        fill_keys(tiles, keys, OWN_ROWS * i - REACH, EXT_ROWS)
+        wide[...] = jnp.zeros_like(wide)
+        widen(REACH, mid)
 
     @pl.when(step == 0)
     def _():
@@ -623,6 +706,7 @@
             + spot.sum_peers()
             + [{"pix": p} for p in (spot.mate, spot.before, spot.after)],
             expected,
+            prepare,
         )
         marks["low"] = posts.post(
             lambda: (mid.at[OWN_ROWS - REACH :], low, {"pix": spot.after})
@@ -632,8 +716,9 @@
             marks["maps", d] = posts.post(
                 lambda d=d: (parts.at[spot.chan(d)], maps_in.at[d - 1], {"chan": spot.chan(d)})
             )
-        for half in range(2):
+        for turn in range(2):
             for d in (1, -1):
+                half = turn if d == 1 else 1 - turn
                 marks["z", d, half] = posts.post(
                     lambda half=half, d=d: (
                         mid.at[half_rows * half : half_rows * (half + 1)],
@@ -644,24 +729,16 @@
         marks["mate", 0] = posts.post(lambda: (mid, g_rows(0, spot.core), {"pix": spot.mate}))
         sums = jnp.zeros((8, 256), F32)
         for r in range(OWN_ROWS):
-            sums = sums + place_rows[:, r : r + 1] * pool_rows[r : r + 1]
+            sums = add_at(sums, pool_rows[r : r + 1], tiles[row_of(OWN_ROWS * i + r)])
         near[spot.k] = sums
         for d in range(1, GROUP):
             marks["near", d] = posts.post(
                 lambda d=d: (near.at[spot.k], near.at[spot.k], {"pix": spot.pix_in_group(d)})
             )
-        wide[...] = jnp.zeros_like(wide)
         posts.arrive(marks["low"], low)
         posts.arrive(marks["high"], high)
-        for start, part in ((0, low), (REACH, mid), (REACH + OWN_ROWS, high)):
-            held = part[...].astype(F32)
-            for which in range(3):
-                for t in range(TASKS):
-                    lane = BRANCH * which + HEAD * t
-                    one = held[:, :, lane : lane + HEAD]
-                    wide[3 * t + which, start : start + held.shape[0], PAD : PAD + TILE_W] = (
-                        jnp.concatenate([one, one], axis=2)
-                    )
+        widen(0, low)
+        widen(REACH + OWN_ROWS, high)
 
         def one_row(r, carry):
             is_low = lax.broadcasted_iota(jnp.int32, (TILE_W, 2 * HEAD), 1) < HEAD
@@ -675,7 +752,8 @@
                         r + REACH - a * (which + 1),
                         PAD - b * dilation : PAD - b * dilation + TILE_W,
                     ]
-                    return jnp.where(keep[3 * which + 1 - a, r] > 0, piece, 0.0)
+                    same = keys[REACH + r] == keys[REACH + r - a * (which + 1)]
+                    return jnp.where(same, piece, 0.0)
 
                 for pair in range(14):
                     first = shifted(2 * pair)
@@ -687,7 +765,7 @@
 
         lax.fori_loop(0, OWN_ROWS, one_row, 0)
 
-    @pl.when(step == 1)
+    @pl.when(step == 2)
     def _():
         for d in range(1, GROUP):
             posts.arrive(marks["near", d], near.at[spot.in_group(-d)])
@@ -702,44 +780,42 @@
                 )
             )
 
-    @pl.when(step == 2)
+    @pl.when(step == 4)
     def _():
         for d in range(1, 4):
             posts.arrive(marks["across", d], across.at[spot.x_of(-d)])
         sums = across[0] + across[1] + across[2] + across[3]
-        pooled_pre = (sums[:, :BRANCH] * slope(pre_pooled[...])).astype(BF16).astype(F32)
-        grad_pooled[...] = pooled_pre
-        tall = jnp.concatenate([pooled_pre, jnp.zeros((8, BRANCH), F32)], axis=0).astype(BF16)
+        pooled_pre = sums[:, :BRANCH] * slope(pre_pooled[0:8])
+        tall[...] = jnp.concatenate([pooled_pre, jnp.zeros((8, BRANCH), F32)], axis=0).astype(BF16)
         for c in range(CHAN):
-            mean_out[c] = dot_nn(tall, pooled[:, 512 * c : 512 * (c + 1)]).astype(BF16)
+            mean_out[c] = dot_nn(tall[...], pooled[:, 512 * c : 512 * (c + 1)]).astype(BF16)
         for d in (2, 1, 3):
             marks["mean", d] = posts.post(
                 lambda d=d: (mean_out.at[spot.chan(d)], mean_in.at[d - 1], {"chan": spot.chan(d)})
             )
 
-    @pl.when(step == 3)
+    @pl.when(step == 8)
     def _():
         mean = mean_out[j].astype(F32)
         for d in (1, 3, 2):
             posts.arrive(marks["mean", d], mean_in.at[d - 1])
             mean = mean + mean_in[d - 1].astype(F32)
-        mean = mean[0:8] / sizes[:, 0:1]
-        rows = jnp.zeros((OWN_ROWS, 512), F32)
-        for k in range(8):
-            rows = rows + tile_cols[:, k : k + 1] * mean[k : k + 1]
-        mean_rows[...] = rows
+        mean = mean[0:8] / tile_sizes(tile_grid[...])[:, 0:1]
+        for r in range(OWN_ROWS):
+            mean_rows[r : r + 1] = rows_at(mean, tiles[OWN_ROWS * i + r])
         for d in (1, 3, 2):
             posts.arrive(marks["maps", d], maps_in.at[d - 1])
         for s in range(OWN_ROWS):
             held = parts[j, s].astype(F32)
             for d in (1, 2, 3):
                 held = held + maps_in[d - 1, s].astype(F32)
-            maps_sum[s] = held.astype(BF16)
+            for t in range(TASKS):
+                maps_sum[s, t] = held[:, HEAD * t : HEAD * (t + 1)].astype(BF16)
             target, (away, here) = row_send(s)
             pl.when(target != i)(lambda: away().start())
             pl.when(target == i)(lambda: here().start())
 
-    @pl.when(step == 4)
+    @pl.when(step == 5)
     def _():
         for half, d in enumerate((1, -1)):
             posts.arrive(marks["z", d, half], g_rows(-d, spot.core, half))
@@ -750,6 +826,9 @@
                     {"pix": spot.pix_in_z(d)},
                 )
             )
+
+    @pl.when(step == 10)
+    def _():
         for half, d in enumerate((-1, 1)):
             posts.arrive(marks["z", d, half], g_rows(-d, spot.core, half))
         for d in (1, -1):
@@ -771,11 +850,7 @@
     @pl.when(rate == 2)
     def _():
         total = acc[...] + product
-        for c in range(2):
-            chan = 2 * pair_at(n, j) + c
-            out[chan] = total[:, 512 * c : 512 * (c + 1)].astype(BF16).reshape(
-                OWN_ROWS, TILE_W, 512
-            )
+        out[block_at(n, j)] = total.astype(BF16).reshape(OWN_ROWS, TILE_W, 512)
 
     def side_send(chan, s):
         turn = int_rem(chan + CHAN - j, CHAN) - 1
@@ -783,14 +858,10 @@
             out.at[chan, s], out_in.at[turn, s], ss_side.at[turn, s], rs_side.at[turn, s], chan=chan
         )
 
-    away_pair = 2 * pair_at(0, j)
-    beside = j + 1 - 2 * int_rem(j, 2)
-
-    @pl.when(step == 2)
+    @pl.when((rate == 2) & (n < 3))
     def _():
         for s in range(OWN_ROWS):
-            for c in range(2):
-                side_send(away_pair + c, s).start()
+            side_send(block_at(n, j), s).start()
 
     def back_send(s):
         row = row_of(OWN_ROWS * i + s)
@@ -804,17 +875,10 @@
 
     def side_arrival(turn, s):
         dst = out_in.at[turn, s]
-        return remote(dst, dst, ss_side.at[turn, s], rs_side.at[turn, s], chan=beside)
-
-    @pl.when(step == 5)
+        return remote(dst, dst, ss_side.at[turn, s], rs_side.at[turn, s], chan=spot.chan(1))
+
+    @pl.when(step == 11)
     def _():
-        for s in range(OWN_ROWS):
-            side_send(beside, s).start()
-        for half in range(2):
-            posts.arrive(marks["far", half], g_rows(2, spot.core, half))
-        marks["mate", 2] = posts.post(
-            lambda: (g_rows(2, spot.core), g_rows(2, spot.core), {"pix": spot.mate})
-        )
         for s in range(OWN_ROWS):
             held = out[j, s].astype(F32)
             for turn in range(3):
@@ -824,6 +888,11 @@
             target, (away, here) = back_send(s)
             pl.when(target != i)(lambda: away().start())
             pl.when(target == i)(lambda: here().start())
+        for half in range(2):
+            posts.arrive(marks["far", half], g_rows(2, spot.core, half))
+        marks["mate", 2] = posts.post(
+            lambda: (g_rows(2, spot.core), g_rows(2, spot.core), {"pix": spot.mate})
+        )
         for d in (0, 1, -1, 2):
             posts.arrive(marks["mate", d], g_rows(-d, 1 - spot.core))
         own_copy().wait()
@@ -831,54 +900,59 @@
             pltpu.make_async_copy(out_sum.at[s], trunk_grad.at[s], rs_back.at[s]).wait()
             target, (away, here) = back_send(s)
             pl.when(target != i)(lambda: away().wait_send())
-            for c in range(2):
-                side_send(away_pair + c, s).wait_send()
-            side_send(beside, s).wait_send()
-            pltpu.make_async_copy(maps_sum.at[s], maps_out.at[s], rs_row.at[s]).wait()
+            for d in (1, 2, 3):
+                side_send(spot.chan(d), s).wait_send()
+            pltpu.make_async_copy(maps_sum.at[s], maps_out.at[:, s], rs_row.at[s]).wait()
             target, (away, here) = row_send(s)
             pl.when(target != i)(lambda: away().wait_send())
         posts.finish()
 
 
-def pair_at(n, chan):
-    return int_rem(1 + n - int_div(chan, 2) + 2, 2)
-
-
-def heads_input_grad(keep, grad_mid, head_part, kernels, point, *pool_operands):
+def block_at(n, chan):
+    ahead = jnp.where(n == 0, 2, jnp.where(n == 1, 1, jnp.where(n == 2, 3, 0)))
+    return int_rem(chan + ahead, CHAN)
+
+
+def heads_input_grad(tiles, tile_grid, grad_mid, head_part, kernels, point, *pool_operands):
     pixels = OWN_ROWS * TILE_W
-    block = 1024
+    block = 512
     whole = pl.BlockSpec(memory_space=pltpu.VMEM)
     hbm = pl.BlockSpec(memory_space=pl.ANY)
     dma = pltpu.SemaphoreType.DMA
     maps, trunk = (OWN_ROWS, TILE_W, BRANCH), (OWN_ROWS, TILE_W, 512)
     return pl.pallas_call(
         heads_input_grad_kernel,
-        grid=(2, 3),
+        grid=(4, 3),
         in_specs=[
             pl.BlockSpec(memory_space=pltpu.SMEM),
             whole,
             whole,
-            pl.BlockSpec((TASKS, 1, 3, 3, HEAD, block), lambda n, r: (0, r, 0, 0, 0, pair_at(n, lax.axis_index("chan")))),
+            whole,
             pl.BlockSpec(
-                (TASKS, HEAD, block), lambda n, r: (0, 0, pair_at(n, lax.axis_index("chan")))
+                (TASKS, 1, 3, 3, HEAD, block),
+                lambda n, r: (0, r, 0, 0, 0, block_at(n, lax.axis_index("chan"))),
+            ),
+            pl.BlockSpec(
+                (TASKS, HEAD, block), lambda n, r: (0, 0, block_at(n, lax.axis_index("chan")))
             ),
         ]
-        + [whole] * 6,
+        + [whole] * 3,
         out_specs=[hbm, hbm, hbm, whole, whole],
         out_shape=[
             jax.ShapeDtypeStruct(trunk, BF16),
             jax.ShapeDtypeStruct((GROUP_ROWS, TILE_W, 4 * BRANCH), BF16),
-            jax.ShapeDtypeStruct(maps, BF16),
+            jax.ShapeDtypeStruct((TASKS, OWN_ROWS, TILE_W, HEAD), BF16),
             jax.ShapeDtypeStruct((OWN_ROWS, 512), F32),
-            jax.ShapeDtypeStruct((8, BRANCH), F32),
+            jax.ShapeDtypeStruct((16, BRANCH), BF16),
         ],
         scratch_shapes=[
+            pltpu.SMEM((EXT_ROWS,), jnp.int32),
             pltpu.VMEM((9, EXT_ROWS, PADDED, 2 * HEAD), F32),
             pltpu.VMEM((3, pixels, 28 * HEAD), BF16),
             pltpu.VMEM((pixels, block), F32),
             pltpu.VMEM((2, REACH, TILE_W, 4 * BRANCH), BF16),
             pltpu.VMEM((CHAN - 1, *maps), BF16),
-            pltpu.VMEM(maps, BF16),
+            pltpu.VMEM((OWN_ROWS, TASKS, TILE_W, HEAD), BF16),
             pltpu.VMEM((CHAN, *trunk), BF16),
             pltpu.VMEM((CHAN - 1, *trunk), BF16),
             pltpu.VMEM(trunk, BF16),
@@ -903,13 +977,19 @@
             flops=12_000_000_000, bytes_accessed=28_000_000, transcendentals=0
         ),
         name="heads_input_grad",
-    )(keep, grad_mid, head_part, kernels, point, *pool_operands)
+    )(tiles, tile_grid, grad_mid, head_part, kernels, point, *pool_operands)
 
 
 class GroupSum:
     def __init__(self, out, relay_in, side_in, spot, links):
         self.out, self.relay_in, self.side_in, self.spot, self.links = out, relay_in, side_in, spot, links
-        self.open, self.arrivals = [], []
+        self.ready, self.open, self.arrivals = [], [], []
+
+    def flush(self):
+        self.relay()
+        for n, way in self.ready:
+            self.send(n, way)
+        self.ready = []
 
     def send(self, n, way):
         spot, links, out = self.spot, self.links, self.out
@@ -932,15 +1012,12 @@
             self.arrivals.append((side, n, 1))
         self.open = []
 
-    def finish(self, total):
+    def finish(self, place):
         for side, n, which in self.arrivals:
             self.links.arrive(side, self.side_in.at[n, which])
         for n in range(self.out.shape[0]):
-            total[n] = (
-                self.out[n, self.spot.group].astype(F32)
-                + self.side_in[n, 0].astype(F32)
-                + self.side_in[n, 1].astype(F32)
-            )
+            total = self.out[n, self.spot.group].astype(F32)
+            place(n, total + self.side_in[n, 0].astype(F32) + self.side_in[n, 1].astype(F32))
 
 
 class Links:
@@ -997,7 +1074,6 @@
 OWN = OWN_ROWS * TILE_W
 MID_OWN = 128
 FEAT_OWN = 512
-ROW_COLS = OWN_ROWS * TILE_W
 
 
 def col_shift(value, distance):
@@ -1009,9 +1085,9 @@
 
 
 def section_forward_kernel(
-    pixels, wr, wd, we, vec_mid, vec_feat, keep, tile_rows, sizes, project,
+    tiles, tile_grid, pixels, wr, wd, we, gain_r, bias_r, gain_d, bias_d, gain_e, bias_e, project,
     x_ext, unit_r, unit_d, unit_e, act_r, act_d, wr_all, inv_mid, inv_feat, mean_all, project_all,
-    trunk, project_out, part_out, part_in, near_m, across_m, near_f, across_f, near_t, across_t,
+    keep, trunk, project_out, part_out, part_in, near_m, across_m, near_f, across_f, near_t, across_t,
     *sems,
 ):
     send_sems, recv_sems, sems = sems[0], sems[1], sems[2:]
@@ -1020,11 +1096,23 @@
     rows_out = RowGather(REACH, trunk, x_ext, spot, sems)
     j = spot.j
     expected = rows_out.greet()
+
+    def prepare():
+        fill_keep(tiles, keep, spot.i)
+        for c in range(CHAN):
+            for b in range(5):
+                lane = HEAD * (b % 2)
+                project_out[c, b // 2, :, :, lane : lane + HEAD] = project[
+                    :, :, 256 * b + HEAD * c : 256 * b + HEAD * (c + 1)
+                ]
+            project_out[c, 2, :, :, HEAD:] = jnp.zeros((TASKS, HEAD, HEAD), BF16)
+
     greet(
         [{"chan": spot.chan(d)} for d in (1, 2, 3)]
         + spot.sum_peers()
         + [{"pix": p} for p in (spot.before, spot.after, spot.mate)],
         expected,
+        prepare,
     )
     half = FEAT_OWN // 2
 
@@ -1041,13 +1129,6 @@
     }
     wr_all[j] = wr[pl.ds(pl.multiple_of(FEAT_OWN * j, FEAT_OWN), FEAT_OWN)]
     pre = dot_nn(pixels[...], wr_all[j])
-    for c in range(CHAN):
-        for b in range(5):
-            lane = HEAD * (b % 2)
-            project_out[c, b // 2, :, :, lane : lane + HEAD] = project[
-                :, :, 256 * b + HEAD * c : 256 * b + HEAD * (c + 1)
-            ]
-        project_out[c, 2, :, :, HEAD:] = jnp.zeros((TASKS, HEAD, HEAD), BF16)
     mates = {}
     for d in (1, 3, 2):
         source = spot.chan(-d)
@@ -1096,7 +1177,7 @@
         unit = (value - center) * inv
         return unit, unit * gain + bias, inv
 
-    unit, normed, inv_r = norm(pre, near_m.at[0], across_m.at[0], vec_mid[0:1], vec_mid[1:2])
+    unit, normed, inv_r = norm(pre, near_m.at[0], across_m.at[0], gain_r[...], bias_r[...])
     unit_r[...] = unit
     own = slice(section_rate, section_rate + OWN_ROWS)
     act_r[j, own] = silu(normed).astype(BF16).reshape(OWN_ROWS, TILE_W, MID_OWN)
@@ -1126,7 +1207,7 @@
         term = terms[1] + col_shift(terms[0], -section_rate) + col_shift(terms[2], section_rate)
         pre = pre + (term if a == 1 else term * keep[a // 2])
 
-    unit, normed, inv_d = norm(pre, near_m.at[1], across_m.at[1], vec_mid[2:3], vec_mid[3:4])
+    unit, normed, inv_d = norm(pre, near_m.at[1], across_m.at[1], gain_d[...], bias_d[...])
     unit_d[...] = unit
     inv_mid[...] = jnp.concatenate([inv_r, inv_d, jnp.zeros((6, MID_OWN), F32)], axis=0)
     act_d[j] = silu(normed).astype(BF16)
@@ -1135,7 +1216,7 @@
         links.arrive(sent[d], act_d.at[spot.chan(-d)])
     full = jnp.concatenate([act_d[c] for c in range(CHAN)], axis=1)
     unit, normed, inv_e = norm(
-        dot_nn(full, we[...]), near_f, across_f, vec_feat[0:1], vec_feat[1:2]
+        dot_nn(full, we[...]), near_f, across_f, gain_e[...], bias_e[...]
     )
     unit_e[...] = unit
     inv_feat[...] = jnp.concatenate([inv_e, jnp.zeros((7, FEAT_OWN), F32)], axis=0)
@@ -1145,10 +1226,10 @@
     row_sums = jnp.sum(out.astype(F32).reshape(OWN_ROWS, TILE_W, FEAT_OWN), axis=1)
     sums = jnp.zeros((8, FEAT_OWN), F32)
     for r in range(OWN_ROWS):
-        sums = sums + tile_rows[:, r : r + 1] * row_sums[r : r + 1]
+        sums = add_at(sums, row_sums[r : r + 1], tile_at(tiles, OWN_ROWS * spot.i + r))
     todo[:] = [rows_out.pass_own]
     sums = sum_over_pix(sums, near_t, across_t, spot, links, meanwhile)
-    mean = jnp.concatenate([sums / sizes[:, 0:1], jnp.zeros((8, FEAT_OWN), F32)], axis=0)
+    mean = jnp.concatenate([sums / tile_sizes(tile_grid[...])[:, 0:1], jnp.zeros((8, FEAT_OWN), F32)], axis=0)
     mean_all[j] = mean.astype(BF16)
     sent = {d: links.send(mean_all.at[j], mean_all.at[j], chan=spot.chan(d)) for d in (2, 1, 3)}
     rows_out.pass_sides()
@@ -1167,7 +1248,7 @@
     dma = pltpu.SemaphoreType.DMA
     return pl.pallas_call(
         section_forward_kernel,
-        in_specs=[whole] * 10,
+        in_specs=[pl.BlockSpec(memory_space=pltpu.SMEM)] + [whole] * 12,
         out_specs=[pl.BlockSpec(memory_space=pl.ANY)] + [whole] * 10,
         out_shape=[
             shape((CHAN, EXT_ROWS, TILE_W, FEAT_OWN), BF16),
@@ -1183,6 +1264,7 @@
             shape((CHAN, 3, TASKS, HEAD, 2 * HEAD), BF16),
         ],
         scratch_shapes=[
+            pltpu.VMEM((2, OWN, MID_OWN), F32),
             pltpu.VMEM((OWN_ROWS, TILE_W, FEAT_OWN), BF16),
             pltpu.VMEM((CHAN, 3, TASKS, HEAD, 2 * HEAD), BF16),
             pltpu.VMEM((3, *mid), BF16),
@@ -1267,20 +1349,21 @@
 
 
 def section_backward_kernel(
-    trunk_grad, pixels, unit_r, unit_d, unit_e, act_r, act_d, wr_all, wd_cat, we, vec_mid, vec_feat,
-    inv_mid, inv_feat, keep, mean_rows, projects, keep_group, x_group, g_group, *refs,
+    tiles, trunk_grad, pixels, unit_r, unit_d, unit_e, act_r, act_d, wr_all, wd, we,
+    gain_r, bias_r, gain_d, bias_d, gain_e, bias_e, inv_mid, inv_feat, mean_rows, projects, x_group,
+    g_group, *refs,
 ):
     (
-        grad_pixels, mid_grads, feat_grads, grad_reduce, grad_dilate, grad_expand, grad_project,
-        grad_atrous, grad_point,
-    ) = refs[:9]
-    scratch = refs[9:]
+        grad_pixels, grad_reduce, grad_gain_r, grad_bias_r, grad_dilate, grad_gain_d, grad_bias_d,
+        grad_expand, grad_gain_e, grad_bias_e, grad_point, grad_atrous, grad_project,
+    ) = refs[:13]
+    scratch = refs[13:]
     (
-        side_out, side_in, halo, taps, full, project_in, project_wide, reduce_out,
+        keys, keep, wd_cat, side_out, side_in, halo, taps, full, project_in, project_wide, reduce_out,
         near_m, across_m, near_f, across_f, x_all, x_base, x_now, g_all, g_now,
-    ) = scratch[:17]
-    send_sems, recv_sems, last_sems, load_sems = scratch[-4:]
-    buffers = scratch[17:-4]
+    ) = scratch[:20]
+    send_sems, recv_sems, ss_reduce, rs_reduce, load_sems = scratch[-5:]
+    buffers = scratch[20:-5]
     spot = Spot()
     links = Links(send_sems, recv_sems)
     i, j = spot.i, spot.j
@@ -1298,16 +1381,24 @@
 
     peers = [{"chan": spot.chan(d)} for d in (1, 2, 3)] + spot.sum_peers()
     peers += [{"pix": spot.before}, {"pix": spot.after}]
-    greet(peers, 1 - stays.astype(jnp.int32))
-
-    atrous_sum = GroupSum(*buffers[24:27], spot, links)
-    point_sum = GroupSum(*buffers[27:30], spot, links)
+
     loads = [
         pltpu.make_async_copy(x_group, x_all, load_sems.at[0]),
         pltpu.make_async_copy(g_group, g_all.at[REACH : REACH + GROUP_ROWS], load_sems.at[1]),
     ]
-    for load in loads:
-        load.start()
+
+    def prepare():
+        for load in loads:
+            load.start()
+        fill_keep(tiles, keep, i)
+        fill_keys(tiles, keys, GROUP_ROWS * spot.group - REACH, GROUP_ROWS + 2 * REACH)
+        for tap in range(9):
+            wd_cat[:, MID_OWN * tap : MID_OWN * (tap + 1)] = wd[tap]
+
+    greet(peers, 1 - stays.astype(jnp.int32), prepare)
+
+    atrous_sum = GroupSum(*buffers[24:27], spot, links)
+    point_sum = GroupSum(*buffers[27:30], spot, links)
     edges = [
         (g_group.at[GROUP_ROWS - REACH :], g_all.at[:REACH], 1),
         (g_group.at[:REACH], g_all.at[REACH + GROUP_ROWS :], -1),
@@ -1344,9 +1435,8 @@
                 piece = g_all[
                     r + REACH - (a - 1) * (which + 1), :, BRANCH * which : BRANCH * (which + 1)
                 ]
-                pieces.append(
-                    jnp.where(keep_group[3 * which + 2 - a, r] > 0, piece, jnp.zeros_like(piece))
-                )
+                same = keys[r + REACH] == keys[r + REACH - (a - 1) * (which + 1)]
+                pieces.append(jnp.where(same, piece, jnp.zeros_like(piece)))
             g_now[row_block(r)] = jnp.concatenate(pieces, axis=1)
             return carry
 
@@ -1367,22 +1457,25 @@
         n = 3 * which + b
         for c in range(CHAN):
             atrous_sum.out[n, c] = product[HEAD * c : HEAD * (c + 1)]
-        atrous_sum.relay()
-        atrous_sum.send(n, 1 if n % 2 else -1)
+        atrous_sum.ready.append((n, 1 if n % 2 else -1))
 
     def multiply_point():
         grads = g_all[REACH : REACH + GROUP_ROWS, :, 3 * BRANCH :].reshape(-1, BRANCH)
         product = dot_tn(grads, x_base[...]).T.astype(BF16)
         for c in range(CHAN):
             point_sum.out[0, c] = product[HEAD * c : HEAD * (c + 1)]
-        point_sum.send(0, 1)
+        point_sum.ready.append((0, 1))
 
     tasks = [take]
     for which in range(3):
         tasks.append(functools.partial(pick, which))
         tasks += [functools.partial(multiply, which, b) for b in range(3)]
-    tasks += [multiply_point, point_sum.relay, atrous_sum.relay]
+    tasks += [multiply_point]
     queue = iter(tasks)
+
+    def flush():
+        atrous_sum.flush()
+        point_sum.flush()
 
     def meanwhile(count=1):
         for _ in range(count):
@@ -1403,10 +1496,11 @@
     grad_trunk = trunk_grad[...].astype(F32) + mean_rows[...][:, None, :]
     grad_trunk = grad_trunk.reshape(OWN, FEAT_OWN)
     unit = unit_e[...]
-    summed = unit * vec_feat[0:1] + vec_feat[1:2] + pixels[...].astype(F32)
+    summed = unit * gain_e[...] + bias_e[...] + pixels[...].astype(F32)
     grad_summed = grad_trunk * slope(summed)
-    g_expand, sums = norm_back(grad_summed, unit, near_f, across_f, vec_feat[0:1] * inv_feat[0:1])
-    feat_grads[...] = sums
+    g_expand, sums = norm_back(grad_summed, unit, near_f, across_f, gain_e[...] * inv_feat[0:1])
+    grad_bias_e[...] = sums[0:1]
+    grad_gain_e[...] = sums[1:2]
 
     def sides(turn, make):
         sent = {}
@@ -1434,14 +1528,17 @@
         for n in range(8):
             by_expand.parts[spot_of(8 * c + n)] = grads[part * n : part * (n + 1)]
     by_expand.start()
-    meanwhile()
+    flush()
+    meanwhile(2)
     grad_act = side_sum(0, own, sent)
 
     unit = unit_d[...]
-    grad = grad_act * slope(unit * vec_mid[2:3] + vec_mid[3:4])
-    g_dilate, sums_d = norm_back(
-        grad, unit, near_m.at[0], across_m.at[0], vec_mid[2:3] * inv_mid[1:2]
+    grad = grad_act * slope(unit * gain_d[...] + bias_d[...])
+    g_dilate, sums = norm_back(
+        grad, unit, near_m.at[0], across_m.at[0], gain_d[...] * inv_mid[1:2]
     )
+    grad_bias_d[...] = sums[0:1]
+    grad_gain_d[...] = sums[1:2]
     own_rows = slice(section_rate, section_rate + OWN_ROWS)
     halo[own_rows] = g_dilate.reshape(OWN_ROWS, TILE_W, MID_OWN)
     low, high = slice(0, section_rate), slice(section_rate + OWN_ROWS, 2 * section_rate + OWN_ROWS)
@@ -1449,6 +1546,7 @@
     to_before = links.send(halo.at[first], halo.at[high], pix=spot.before)
     to_after = links.send(halo.at[last], halo.at[low], pix=spot.after)
     by_expand.along_z()
+    flush()
     meanwhile()
     for d in (1, 3, 2):
         links.arrive(project_sent[d], project_in.at[d - 1])
@@ -1476,19 +1574,22 @@
                     part * n : part * (n + 1), MID_OWN * tap : MID_OWN * (tap + 1)
                 ]
     by_dilate.start()
-    meanwhile()
+    flush()
+    meanwhile(2)
     grad_act = side_sum(1, own, sent)
     by_expand.along_x()
 
     unit = unit_r[...]
-    grad = grad_act * slope(unit * vec_mid[0:1] + vec_mid[1:2])
-    g_reduce, sums_r = norm_back(
-        grad, unit, near_m.at[1], across_m.at[1], vec_mid[0:1] * inv_mid[0:1]
+    grad = grad_act * slope(unit * gain_r[...] + bias_r[...])
+    g_reduce, sums = norm_back(
+        grad, unit, near_m.at[1], across_m.at[1], gain_r[...] * inv_mid[0:1]
     )
-    mid_grads[...] = jnp.concatenate([sums_r[0:2], sums_d[0:2], jnp.zeros((4, MID_OWN), F32)], axis=0)
+    grad_bias_r[...] = sums[0:1]
+    grad_gain_r[...] = sums[1:2]
     full[j] = g_reduce
     sent = {d: links.send(full.at[j], full.at[j], chan=spot.chan(d)) for d in (2, 1, 3)}
     by_dilate.along_z()
+    flush()
     for t in range(TASKS):
         for device in range(PIX):
             rows = []
@@ -1499,7 +1600,7 @@
             by_project.parts[(*spot_of(device), t)] = jnp.concatenate(rows, axis=0).astype(BF16)
     by_project.start()
     grad_expand[...] = by_expand.finish()
-    meanwhile()
+    meanwhile(2)
     for d in (1, 3, 2):
         links.arrive(sent[d], full.at[spot.chan(-d)])
     g_reduce = jnp.concatenate([full[c] for c in range(CHAN)], axis=1)
@@ -1512,33 +1613,48 @@
             ]
     by_reduce.start()
     grad_pixels[...] = (grad_summed + dot_nt(g_reduce, weight)).astype(BF16)
+    by_reduce.along_z()
     by_project.along_z()
     meanwhile(2)
-    by_reduce.along_z()
-    meanwhile(2)
+    by_reduce.along_x()
+    flush()
     by_dilate.along_x()
-    by_reduce.along_x()
+    meanwhile(len(tasks))
     by_project.along_x()
-    meanwhile(len(tasks))
+    flush()
     reduce_out[...] = by_reduce.finish()
 
-    def last_copies():
+    def reduce_copies():
         return (
             lambda: remote(
-                reduce_out, grad_reduce, last_sems.at[0], last_sems.at[1], pix=owner_i, chan=owner_j
+                reduce_out, grad_reduce, ss_reduce.at[0], rs_reduce.at[0], pix=owner_i, chan=owner_j
             ),
-            lambda: pltpu.make_async_copy(reduce_out, grad_reduce, last_sems.at[1]),
-        )
-
-    away, here = last_copies()
+            lambda: pltpu.make_async_copy(reduce_out, grad_reduce, rs_reduce.at[0]),
+        )
+
+    away, here = reduce_copies()
     pl.when(jnp.logical_not(stays))(lambda: away().start())
     pl.when(stays)(lambda: here().start())
+    flush()
     grad_dilate[...] = by_dilate.finish()
-    grad_project[...] = by_project.finish()
-    pltpu.make_async_copy(reduce_out, grad_reduce, last_sems.at[1]).wait()
+    grad_project[...] = by_project.finish()[:, :40]
+
+    def place(n, total):
+        which, b = n // 3, n % 3
+        for a in range(3):
+            for t in range(TASKS):
+                lane = BRANCH * a + HEAD * t
+                grad_atrous[t, which, 3 * a + b] = total[:, lane : lane + HEAD]
+
+    def place_point(n, total):
+        for t in range(TASKS):
+            grad_point[t] = total[:, HEAD * t : HEAD * (t + 1)]
+
+    atrous_sum.finish(place)
+    point_sum.finish(place_point)
+
+    pltpu.make_async_copy(reduce_out, grad_reduce, rs_reduce.at[0]).wait()
     pl.when(jnp.logical_not(stays))(lambda: away().wait_send())
-    atrous_sum.finish(grad_atrous)
-    point_sum.finish(grad_point)
     links.finish()
 
 
@@ -1557,22 +1673,29 @@
     mid, feat = (OWN, MID_OWN), (OWN, FEAT_OWN)
     return pl.pallas_call(
         section_backward_kernel,
-        in_specs=[whole] * 17
-        + [pl.BlockSpec(memory_space=pltpu.SMEM)]
+        in_specs=[pl.BlockSpec(memory_space=pltpu.SMEM)]
+        + [whole] * 20
         + [pl.BlockSpec(memory_space=pl.ANY)] * 2,
-        out_specs=[whole] * 9,
+        out_specs=[whole] * 13,
         out_shape=[
             shape(feat, BF16),
-            shape((8, MID_OWN), F32),
-            shape((8, FEAT_OWN), F32),
             shape((HEAD, MID_OWN), F32),
+            shape((1, MID_OWN), F32),
+            shape((1, MID_OWN), F32),
             shape((9, 16, MID_OWN), F32),
+            shape((1, MID_OWN), F32),
+            shape((1, MID_OWN), F32),
             shape((16, FEAT_OWN), F32),
-            shape((TASKS, 48, HEAD), F32),
-            shape((9, HEAD, 3 * BRANCH), F32),
-            shape((1, HEAD, BRANCH), F32),
+            shape((1, FEAT_OWN), F32),
+            shape((1, FEAT_OWN), F32),
+            shape((TASKS, HEAD, HEAD), F32),
+            shape((TASKS, 3, 9, HEAD, HEAD), F32),
+            shape((TASKS, 40, HEAD), F32),
         ],
         scratch_shapes=[
+            pltpu.SMEM((GROUP_ROWS + 2 * REACH,), jnp.int32),
+            pltpu.VMEM((2, OWN, MID_OWN), F32),
+            pltpu.VMEM((FEAT_OWN, 9 * MID_OWN), BF16),
             pltpu.VMEM((2, 3, *mid), BF16),
             pltpu.VMEM((2, 3, *mid), BF16),
             pltpu.VMEM((OWN_ROWS + 2 * section_rate, TILE_W, MID_OWN), BF16),
@@ -1596,9 +1719,10 @@
             *scatter_scratch(HEAD, MID_OWN),
             *group_scratch(9, HEAD, 3 * BRANCH),
             *group_scratch(1, HEAD, BRANCH),
-            dma((128,)),
-            dma((128,)),
-            dma((2,)),
+            dma((112,)),
+            dma((112,)),
+            dma((1,)),
+            dma((1,)),
             dma((2,)),
         ],
         compiler_params=pltpu.CompilerParams(
@@ -1609,6 +1733,40 @@
         ),
         name="section_backward",
     )(*operands)
+
+
+def hand_out_kernel(maps, tall, mean_all, *refs):
+    count = (len(refs) - 3) // 2
+    grads, (task_maps, grad_pooled), outs, sems = (
+        refs[:count], refs[count : count + 2], refs[count + 2 : -1], refs[-1],
+    )
+    copies = [pltpu.make_async_copy(src, dst, sems.at[n]) for n, (src, dst) in enumerate(zip(grads, outs))]
+    for copy in copies:
+        copy.start()
+    for c in range(CHAN):
+        part = dot_tn(tall[...], mean_all[c])
+        for t in range(TASKS):
+            grad_pooled[t, :, 512 * c : 512 * (c + 1)] = part[HEAD * t : HEAD * (t + 1)]
+    for t in range(TASKS):
+        task_maps[t] = maps[t].reshape(OWN, HEAD).astype(F32).T.astype(BF16)
+    for copy in copies:
+        copy.wait()
+
+
+def hand_out(maps, pooled_grad, mean_all, *grads):
+    whole = pl.BlockSpec(memory_space=pltpu.VMEM)
+    shape = jax.ShapeDtypeStruct
+    return pl.pallas_call(
+        hand_out_kernel,
+        in_specs=[whole] * (3 + len(grads)),
+        out_specs=[whole] * 2 + [pl.BlockSpec(memory_space=pl.ANY)] * len(grads),
+        out_shape=[shape((TASKS, HEAD, OWN), BF16), shape((TASKS, HEAD, CHAN * 512), F32)]
+        + [shape(grad.shape, grad.dtype) for grad in grads],
+        scratch_shapes=[pltpu.SemaphoreType.DMA((len(grads),))],
+        compiler_params=pltpu.CompilerParams(vmem_limit_bytes=VMEM_LIMIT),
+        cost_estimate=pl.CostEstimate(flops=0, bytes_accessed=10_000_000, transcendentals=0),
+        name="hand_out",
+    )(maps, pooled_grad, mean_all, *grads)
 
 
 def shards(
@@ -1630,106 +1788,55 @@
     project_weight,
     cotangent,
 ):
-    pixel_count = pixels.shape[0]
-    device = lax.axis_index("pix")
-    first_row = device * OWN_ROWS
-    tile_count = 8
-    tiles = jnp.arange(tile_count)
-    tile_sizes = jnp.sum((tile_number[:, None] == tiles[None, :]).astype(F32), axis=0) * TILE_W
-    sizes = jnp.broadcast_to(jnp.maximum(tile_sizes, 1.0)[:, None], (tile_count, 128))
-    tile_pad = jnp.pad(tile_number, (section_rate, section_rate), constant_values=-1)
-    tiles_at = [
-        lax.dynamic_slice_in_dim(tile_pad, first_row + section_rate * (1 + step), OWN_ROWS)
-        for step in (-1, 0, 1)
+    tile_grid = tile_number.reshape(2, 128)
+    norms = [
+        v.reshape(1, -1)
+        for v in (reduce_gain, reduce_bias, dilate_gain, dilate_bias, expand_gain, expand_bias)
     ]
-    row_onehot = (tiles_at[1][:, None] == tiles[None, :]).astype(F32)
-    keep_rows = jnp.stack([tiles_at[0] == tiles_at[1], tiles_at[2] == tiles_at[1]]).astype(F32)
-    keep_section = jnp.broadcast_to(
-        keep_rows[:, :, None, None], (2, OWN_ROWS, TILE_W, MID_OWN)
-    ).reshape(2, OWN, MID_OWN)
-    vec_mid = jnp.pad(
-        jnp.stack([reduce_gain, reduce_bias, dilate_gain, dilate_bias]), ((0, 4), (0, 0))
-    )
-    vec_feat = jnp.pad(jnp.stack([expand_gain, expand_bias]), ((0, 6), (0, 0)))
+    pooled_rows = pooled_weight.reshape(BRANCH, -1)
     (
         x_ext, unit_reduce, unit_dilate, unit_expand, act_reduce, act_dilate, reduce_all, inv_mid,
         inv_feat, mean_all, project_all,
     ) = section_forward(
-        pixels, reduce_weight, dilate_weight, expand_weight, vec_mid, vec_feat, keep_section,
-        row_onehot.T, sizes, project_weight,
+        tile_number, tile_grid, pixels, reduce_weight, dilate_weight, expand_weight, *norms,
+        project_weight,
     )
-    tile_mean = jnp.moveaxis(mean_all[:, :tile_count], 0, 1).reshape(tile_count, -1)
-    group_x = device // GROUP
-    placed = jnp.array(PLACED_ROWS, jnp.int32)
-    place_key = tile_number[placed] + 8 * (placed % 6)
-    key_pad = jnp.pad(place_key, (REACH, REACH), constant_values=-1)
-    keep_all = jnp.stack(
-        [
-            key_pad[REACH + a * k : REACH + a * k + NROWS] == place_key
-            for k in (1, 2, 3)
-            for a in (-1, 0, 1)
-        ]
-    ).astype(jnp.int32)
-    keep_own = lax.dynamic_slice_in_dim(keep_all, device * OWN_ROWS, OWN_ROWS, axis=1)
-    keep_group = lax.dynamic_slice_in_dim(keep_all, group_x * GROUP_ROWS, GROUP_ROWS, axis=1)
-    place_tiles = lax.dynamic_slice_in_dim(tile_number[placed], device * OWN_ROWS, OWN_ROWS)
-    place_onehot = (place_tiles[:, None] == tiles[None, :]).astype(F32)
-    pre_pooled = jnp.einsum("kc,tdc->ktd", tile_mean, pooled_weight, preferred_element_type=F32)
-    pooled_act = jax.nn.silu(pre_pooled).astype(jnp.bfloat16).reshape(tile_count, BRANCH)
-    pooled_rows = jnp.dot(
-        place_onehot.astype(jnp.bfloat16), pooled_act, preferred_element_type=F32
-    ).astype(jnp.bfloat16)
-    pooled_pixels = jnp.broadcast_to(
-        pooled_rows[:, None, :], (OWN_ROWS, TILE_W, BRANCH)
-    ).reshape(pixel_count, BRANCH)
-    task_weight = jax.nn.softmax(task_draws.astype(jnp.float32) / 3.0)
-    grad_maps = (task_weight[:, None, None] * cotangent.astype(jnp.float32)).astype(jnp.bfloat16)
-    maps_own = jnp.moveaxis(grad_maps, 0, 1).reshape(OWN_ROWS, TILE_W, BRANCH)
     kernels = atrous_weight.reshape(TASKS, 3, 3, 3, HEAD, -1)
-    grad_pre, head_part, grad_project, pool_rows, x_group = heads_forward(
-        keep_own, x_ext, maps_own, kernels, point_weight, project_all, pooled_pixels
+    grad_pre, head_part, grad_project, pool_rows, x_group, pre_pooled = heads_forward(
+        tile_number, task_draws, x_ext, jnp.swapaxes(cotangent, 1, 2), kernels, point_weight, project_all, mean_all,
+        pooled_rows,
     )
-    trunk_grad, g_group, task_maps, mean_rows, grad_pooled = heads_input_grad(
-        keep_own, grad_pre.reshape(OWN_ROWS, TILE_W, 4 * BRANCH),
+    trunk_grad, g_group, maps, mean_rows, pooled_grad = heads_input_grad(
+        tile_number, tile_grid, grad_pre.reshape(OWN_ROWS, TILE_W, 4 * BRANCH),
         head_part.reshape(CHAN, OWN_ROWS, TILE_W, BRANCH), kernels, point_weight, pool_rows,
-        place_onehot.T, row_onehot, sizes, pre_pooled.reshape(tile_count, BRANCH),
-        pooled_weight.reshape(BRANCH, -1),
+        pre_pooled, pooled_rows,
     )
-    task_maps = jnp.moveaxis(task_maps.reshape(pixel_count, TASKS, HEAD), 1, 0)
+    grads = section_backward(
+        tile_number, trunk_grad, pixels, unit_reduce, unit_dilate, unit_expand, act_reduce, act_dilate,
+        reduce_all, dilate_weight, expand_weight, *norms, inv_mid, inv_feat, mean_rows, grad_project,
+        x_group, g_group,
+    )
     (
-        grad_pixels, mid_grads, feat_grads, grad_reduce, grad_dilate, grad_expand, grad_project,
-        grad_atrous, grad_point,
-    ) = section_backward(
-        trunk_grad, pixels, unit_reduce, unit_dilate, unit_expand, act_reduce, act_dilate, reduce_all,
-        jnp.moveaxis(dilate_weight, 0, 1).reshape(-1, 9 * MID_OWN), expand_weight, vec_mid, vec_feat,
-        inv_mid, inv_feat, keep_section, mean_rows, grad_project, keep_group, x_group, g_group,
-    )
-    grad_atrous_weight = jnp.transpose(
-        grad_atrous.reshape(3, 3, HEAD, 3, TASKS, HEAD), (4, 0, 3, 1, 2, 5)
-    ).reshape(TASKS, 3, 9, HEAD, HEAD)
-    grad_point_weight = jnp.transpose(grad_point.reshape(HEAD, TASKS, HEAD), (1, 0, 2))
-    grad_pooled_weight = jnp.einsum(
-        "kc,ktd->tcd",
-        tile_mean,
-        grad_pooled.reshape(tile_count, TASKS, HEAD).astype(BF16),
-        preferred_element_type=F32,
-    )
+        task_maps, grad_pooled, grad_pixels, grad_reduce, grad_gain_r, grad_bias_r, grad_dilate,
+        grad_gain_d, grad_bias_d, grad_expand, grad_gain_e, grad_bias_e, grad_point, grad_atrous,
+        grad_project,
+    ) = hand_out(maps, pooled_grad, mean_all, *grads)
     return (
-        task_maps,
+        jnp.swapaxes(task_maps, 1, 2),
         grad_pixels,
         grad_reduce,
-        mid_grads[1],
-        mid_grads[0],
+        grad_gain_r[0],
+        grad_bias_r[0],
         grad_dilate,
-        mid_grads[3],
-        mid_grads[2],
+        grad_gain_d[0],
+        grad_bias_d[0],
         grad_expand,
-        feat_grads[1],
-        feat_grads[0],
-        grad_point_weight,
-        grad_atrous_weight,
-        grad_pooled_weight,
-        grad_project[:, :40],
+        grad_gain_e[0],
+        grad_bias_e[0],
+        grad_point,
+        grad_atrous,
+        jnp.swapaxes(grad_pooled, 1, 2),
+        grad_project,
     )
 
 

time: 356 us -> 317 us (0.89)
  local copies, waits for them, and re-layouts: 25.9 us -> 0 us
  other arithmetic: 10.4 us -> 0 us
    pallas_call x3 -> x0, local copies, waits for them, and re-layouts: 4.77 us -> none  [the longest x2 3.58 us: section_backward(): pl.pallas_call(section_backward_kernel, in_specs=[whole] * 17 + [pl.Block...]
    reshape x6 -> x0, local copies, waits for them, and re-layouts: 4.31 us -> none  [the longest x1 1.41 us: shards(): jnp.moveaxis(dilate_weight, 0, 1).reshape(-1, 9 * MID_OWN)]
    another operation x4 -> x0, other arithmetic: 4.21 us -> none  [the longest x2 1.59 us: shards(): jnp.stack([tiles_at[0] == tiles_at[1], tiles_at[2] == tiles_at[1]])]
    unnamed x26 -> x0, local copies, waits for them, and re-layouts: 4.03 us -> none
    pallas_call x3 -> x4, Pallas kernels: 267 us -> 269 us  [the longest x1 98 us: section_backward(): pl.pallas_call(section_backward_kernel, in_specs=[pl.BlockSpec(memory_spa...]
where the time goes in v5:
time: 317 us; the launch traced here: 312 us
  Pallas kernels  312 us (98%)
    pallas_call x1, Pallas kernels, section_backward(): pl.pallas_call(section_backward_kernel, in_specs=[pl.BlockSpec(memory_spa...  98 us
    pallas_call x1, Pallas kernels, section_forward(): pl.pallas_call(section_forward_kernel, in_specs=[pl.BlockSpec(memory_spac...  97.7 us
    pallas_call x1, Pallas kernels, heads_input_grad(): pl.pallas_call(heads_input_grad_kernel, grid=(4, 3), in_specs=[pl.BlockSp...  67.5 us
    pallas_call x1, Pallas kernels, heads_forward(): pl.pallas_call(heads_forward_kernel, grid=(9,), in_specs=[pl.BlockSpec(me...  43 us

profile of v5, /device:TPU:7, one launch (start us, length us, event | category | flops | bytes accessed | tf_op | source)
XLA Modules:
  0.0 312.4 jit_solution(12283361291768599270)
XLA Ops:
  0.6 97.7 %section_forward.1 = (bf16[4,14,64,512]{3,2,1,0:T(8,128)(2,1)}, f32[512,128]{1,0:T(8,128)}, f32[512,128]{1,0:T(8,128)}, f32[512,512]{1,0:T(8,128)}, bf16[4,16,64...) custom-call(s32[256]{0:T(256)} %tiles.7, ...), custom_call_target="tpu_custom_call" | custom-call | flops 2000000000 | bytes 120000000 | tf_op jit(solution)/shard_map/section_forward/pallas_call | solution.py:1249
  98.3 43.0 %heads_forward.1 = (bf16[512,768]{1,0:T(8,128)(2,1)}, bf16[4,512,192]{2,1,0:T(8,128)(2,1)}, bf16[4,5,3,64,64]{4,3,2,1,0:T(8,128)(2,1)}, f32[8,256]{1,0:T(8,128)}...) custom-call(s32[256]{0:T(256)} %tiles.7, s32[3]{0:T(128)} %draws.1, ...), custom_call_target="tpu_custom_call" | custom-call | flops 12000000000 | bytes 28000000 | tf_op jit(solution)/shard_map/heads_forward/pallas_call | solution.py:584
  141.3 67.5 %heads_input_grad.1 = (bf16[8,64,512]{2,1,0:T(8,128)(2,1)}, bf16[64,64,768]{2,1,0:T(8,128)(2,1)}, bf16[3,8,64,64]{3,2,1,0:T(8,128)(2,1)}, f32[8,512]{1,0:T(8,128)}, bf16[16,192]{1,0:T(8,128)(2,1)}) custom-call(s32[256]{0:T(256)} %tiles.7, s32[2,128]{1,0:T(2,128)} %bitcast.34, bf16[8,64,768]{2,1,0:T(8,128)(2,1)} %bitcast.48, ...), custom_call_target="tpu_custom_call" | custom-call | flops 12000000000 | bytes 28000000 | tf_op jit(solution)/shard_map/heads_input_grad/pallas_call | solution.py:923
  208.8 98.0 %section_backward.1 = (bf16[512,512]{1,0:T(8,128)(2,1)}, f32[64,128]{1,0:T(8,128)}, f32[1,128]{1,0:T(1,128)}, f32[1,128]{1,0:T(1,128)}, f32[9,16,128]{2,1,0:T(8,...) custom-call(s32[256]{0:T(256)} %tiles.7, ...), custom_call_target="tpu_custom_call" | custom-call | flops 16000000000 | bytes 250000000 | tf_op jit(solution)/shard_map/section_backward/pallas_call | solution.py:1674
  306.9 5.3 %hand_out.1 = (bf16[3,64,512]{2,1,0:T(8,128)(2,1)}, f32[3,64,2048]{2,1,0:T(8,128)}, bf16[512,512]{1,0:T(8,128)(2,1)}, f32[64,128]{1,0:T(8,128)}, f32[1,128]{1,0:...) custom-call(bf16[3,8,64,64]{3,2,1,0:T(8,128)(2,1)} %get-tuple-elemen, ...), custom_call_target="tpu_custom_call" | custom-call | bytes 10000000 | tf_op jit(solution)/shard_map/hand_out/pallas_call | solution.py:1759

commit v6 on v5

--- a/solution.py
+++ b/solution.py
@@ -108,6 +108,20 @@
     )
 
 
+def greet_origins(i):
+    barrier, expected = pltpu.get_barrier_semaphore(), 0
+    for s in range(OWN_ROWS):
+        origin = int_div(row_of(OWN_ROWS * i + s), OWN_ROWS)
+
+        @pl.when(origin != i)
+        def _():
+            signal(barrier, pix=origin)
+
+        target = int_div(place_of(OWN_ROWS * i + s), OWN_ROWS)
+        expected = expected + (target != i).astype(jnp.int32)
+    return expected
+
+
 class RowGather:
     def __init__(self, reach, src, out, spot, sems):
         self.reach, self.src, self.out, self.spot = reach, src, out, spot
@@ -117,20 +131,6 @@
         ) = sems
         self.order = (0, 7, 1, 6, 2, 5, 3, 4)
         self.edge = [s for s in self.order if s < reach or s >= OWN_ROWS - reach]
-
-    def greet(self):
-        barrier = pltpu.get_barrier_semaphore()
-        i, expected = self.spot.i, 0
-        for s in range(OWN_ROWS):
-            origin = int_div(row_of(OWN_ROWS * i + s), OWN_ROWS)
-
-            @pl.when(origin != i)
-            def _():
-                signal(barrier, pix=origin)
-
-            target = int_div(place_of(OWN_ROWS * i + s), OWN_ROWS)
-            expected = expected + (target != i).astype(jnp.int32)
-        return expected
 
     def row_send(self, s):
         place = place_of(OWN_ROWS * self.spot.i + s)
@@ -208,15 +208,19 @@
                 if s in self.edge:
                     self.halo_copy(1 + way, chan, s).start()
 
-    def finish(self):
-        spot, far = self.spot, self.spot.chan(2)
+    def pass_far(self):
+        far = self.spot.chan(2)
         for s in self.order:
             self.far_copy(s, far).wait_recv()
             if s in self.edge:
                 self.halo_copy(3, far, s).start()
-        for chan in range(CHAN):
-            for lane in range(2 * self.reach):
-                self.halo_arrival(chan, lane).wait_recv()
+
+    def await_halo(self, chan):
+        for lane in range(2 * self.reach):
+            self.halo_arrival(chan, lane).wait_recv()
+
+    def drain(self):
+        spot, far = self.spot, self.spot.chan(2)
         for s in range(OWN_ROWS):
             target, (away, here) = self.row_send(s)
             pl.when(target != spot.i)(lambda: away().wait_send())
@@ -333,90 +337,153 @@
     return v * jax.nn.sigmoid(v)
 
 
-def heads_forward_kernel(
-    tiles, draws, x_hbm, cotangent, kernel, point, project, mean_all, pooled_weight,
-    grad_pre, head_part, grad_project, pool_rows, x_group, pre_pooled,
-    keys, maps_own, pooled, x, acc, pre, maps_in, relay, spread, sems, ss_row, rs_row, send_sems, recv_sems, own_sem,
+def order_at(turn, chan):
+    ahead = jnp.where(turn == 0, 0, jnp.where(turn == 1, 3, jnp.where(turn == 2, 1, 2)))
+    return int_rem(chan + ahead, CHAN)
+
+
+def greet_returns(i):
+    barrier, expected = pltpu.get_barrier_semaphore(), 0
+    for s in range(OWN_ROWS):
+        origin = int_div(place_of(OWN_ROWS * i + s), OWN_ROWS)
+
+        @pl.when(origin != i)
+        def _():
+            signal(barrier, pix=origin)
+
+        target = int_div(row_of(OWN_ROWS * i + s), OWN_ROWS)
+        expected = expected + (target != i).astype(jnp.int32)
+    return expected
+
+
+PAD = 24
+PADDED = PAD + TILE_W + PAD
+
+
+def block_at(n, chan):
+    ahead = jnp.where(n == 0, 2, jnp.where(n == 1, 1, jnp.where(n == 2, 3, 0)))
+    return int_rem(chan + ahead, CHAN)
+
+
+def heads_kernel(
+    tiles, tile_grid, trunk, maps_in, kernel, point, project, pooled_weight, kernel_b,
+    grad_project, x_group, mean_kept, trunk_grad, g_group, maps_out, mean_rows, tall,
+    keys, mean_all, pooled, x, lhs, acc, pre, relay, spread, near, across, mid, parts, pool_rows, pre_pooled,
+    wide, taps, acc_b, edges, head_in, maps_sum, out, out_in, out_sum, near_b, across_b, mean_out, mean_in,
+    send_sems, recv_sems, own_sem, ss_row, rs_row, ss_side, rs_side, ss_back, rs_back, *gather,
 ):
-    step = pl.program_id(0)
-    rate, row_tap = step // 3, step % 3
-    first = REACH + (row_tap - 1) * (rate + 1)
+    turn, rate = pl.program_id(0), pl.program_id(1)
+    step = 3 * turn + rate
+    n, grad_step = turn - 4, step - 12
     spot = Spot()
     posts = Posts(send_sems, recv_sems)
+    rows = RowGather(REACH, trunk, x, spot, gather)
     i, j = spot.i, spot.j
-    halves = (slice(0, OWN_ROWS // 2), slice(OWN_ROWS // 2, OWN_ROWS))
-    chans = (slice(0, 2), slice(2, 4))
-
-    def x_slice(distance, which=slice(0, CHAN)):
+    grad_pre, head_part = mid, parts
+    blocks = (j, spot.chan(-1), spot.chan(1), spot.chan(2))
+    relay_way = (1, 1, -1, -1)
+    half_rows = OWN_ROWS // 2
+    marks = {}
+
+    low, high = edges.at[0], edges.at[1]
+
+    def g_rows(distance, core, half=None):
+        start = OWN_ROWS * (2 * spot.z_of(distance) + core)
+        if half is None:
+            return g_group.at[pl.ds(start, OWN_ROWS)]
+        return g_group.at[pl.ds(start + half_rows * half, half_rows)]
+
+    def g_copy():
+        return pltpu.make_async_copy(mid, g_rows(0, spot.core), own_sem.at[1])
+
+    def row_send(s):
+        row = row_of(OWN_ROWS * i + s)
+        target, slot = int_div(row, OWN_ROWS), int_rem(row, OWN_ROWS)
+        return target, (
+            lambda: remote(
+                maps_sum.at[s], maps_out.at[:, slot], ss_row.at[s], rs_row.at[slot], pix=target
+            ),
+            lambda: pltpu.make_async_copy(
+                maps_sum.at[s], maps_out.at[:, slot], rs_row.at[slot]
+            ),
+        )
+
+    def widen(start, part):
+        held = part[...].astype(F32)
+        for which in range(3):
+            for t in range(TASKS):
+                lane = BRANCH * which + HEAD * t
+                one = held[:, :, lane : lane + HEAD]
+                wide[3 * t + which, start : start + held.shape[0], PAD : PAD + TILE_W] = (
+                    jnp.concatenate([one, one], axis=2)
+                )
+
+    def start_grads():
+        g_copy().start()
+        marks["low"] = posts.post(
+            lambda: (mid.at[OWN_ROWS - REACH :], low, {"pix": spot.after})
+        )
+        marks["high"] = posts.post(lambda: (mid.at[:REACH], high, {"pix": spot.before}))
+        for d in (2, 1, 3):
+            marks["head", d] = posts.post(
+                lambda d=d: (parts.at[spot.chan(d)], head_in.at[d - 1], {"chan": spot.chan(d)})
+            )
+        for turn in range(2):
+            for d in (1, -1):
+                half = turn if d == 1 else 1 - turn
+                marks["z", d, half] = posts.post(
+                    lambda half=half, d=d: (
+                        mid.at[half_rows * half : half_rows * (half + 1)],
+                        g_rows(0, spot.core, half),
+                        {"pix": spot.pix_in_z(d)},
+                    )
+                )
+        sums = jnp.zeros((8, 256), F32)
+        for r in range(OWN_ROWS):
+            sums = add_at(sums, pool_rows[r : r + 1], tiles[row_of(OWN_ROWS * i + r)])
+        near_b[spot.k] = sums
+        for d in range(1, GROUP):
+            marks["near b", d] = posts.post(
+                lambda d=d: (near_b.at[spot.k], near_b.at[spot.k], {"pix": spot.pix_in_group(d)})
+            )
+        wide[...] = jnp.zeros_like(wide)
+        widen(REACH, mid)
+
+    def x_slice(distance, chan=slice(0, CHAN)):
         lanes = pl.ds(pl.multiple_of(128 * spot.z_of(distance), 128), 128)
-        return x_hbm.at[which, REACH : REACH + OWN_ROWS, :, lanes]
-
-    def x_rows(distance, core, which=slice(0, CHAN)):
-        return x_group.at[which, pl.ds(OWN_ROWS * (2 * spot.z_of(distance) + core), OWN_ROWS)]
+        return x.at[chan, REACH : REACH + OWN_ROWS, :, lanes]
+
+    def x_rows(distance, core, chan=slice(0, CHAN)):
+        return x_group.at[chan, pl.ds(OWN_ROWS * (2 * spot.z_of(distance) + core), OWN_ROWS)]
 
     def own_copy():
         return pltpu.make_async_copy(x_slice(0), x_rows(0, spot.core), own_sem.at[0])
 
-    def row_send(s):
-        place = place_of(OWN_ROWS * i + s)
-        target, slot = int_div(place, OWN_ROWS), int_rem(place, OWN_ROWS)
-        return target, (
-            lambda: remote(
-                maps_own.at[s], maps_in.at[j, slot], ss_row.at[s], rs_row.at[slot], pix=target
-            ),
-            lambda: pltpu.make_async_copy(maps_own.at[s], maps_in.at[j, slot], rs_row.at[slot]),
+    def post_x(q):
+        way = relay_way[q]
+        marks["relay", q] = posts.post(
+            lambda: (x_slice(2, blocks[q]), relay.at[q], {"pix": spot.pix_in_z(way)})
         )
-
-    ways = ((1, {"chan": spot.chan(1)}), (-1, {"chan": spot.chan(-1)}))
-    marks = {}
+        for d in (1, -1):
+            marks["x", d, q] = posts.post(
+                lambda d=d: (
+                    x_slice(d, blocks[q]), x_rows(0, spot.core, blocks[q]), {"pix": spot.pix_in_z(d)}
+                )
+            )
+
+    def pass_x(q):
+        way = relay_way[q]
+        posts.arrive(marks["relay", q], relay.at[q])
+        marks["far", q] = posts.post(
+            lambda: (relay.at[q], x_rows(-way, spot.core, blocks[q]), {"pix": spot.pix_in_z(way)})
+        )
 
     @pl.when(step == 0)
     def _():
-        width = x_hbm.shape[3]
-        copies = [
-            pltpu.make_async_copy(
-                x_hbm.at[chan], x.at[:, :, width * chan : width * (chan + 1)], sems.at[chan]
-            )
-            for chan in range(CHAN)
-        ]
-        for copy in copies:
-            copy.start()
-        own_copy().start()
-        barrier = pltpu.get_barrier_semaphore()
-        expected = 0
-        for s in range(OWN_ROWS):
-            origin = int_div(row_of(OWN_ROWS * i + s), OWN_ROWS)
-
-            @pl.when(origin != i)
-            def _():
-                signal(barrier, pix=origin)
-
-            target = int_div(place_of(OWN_ROWS * i + s), OWN_ROWS)
-            expected = expected + (target != i).astype(jnp.int32)
+        expected = greet_origins(i) + greet_returns(i)
 
         def prepare():
-            lane = lax.broadcasted_iota(jnp.int32, (8, 128), 1)
-            drawn = jnp.full((8, 128), -1e30, F32)
-            for t in range(TASKS):
-                drawn = jnp.where(lane == t, draws[t].astype(F32) / 3.0, drawn)
-            grown = jnp.where(lane < TASKS, jnp.exp(drawn - jnp.max(drawn, axis=1, keepdims=True)), 0.0)
-            grown = grown / jnp.sum(grown, axis=1, keepdims=True)
-            for t in range(TASKS):
-                weight = jnp.sum(jnp.where(lane == t, grown, 0.0), axis=1, keepdims=True)[0:1]
-                scaled = (cotangent[t].astype(F32).T * weight).astype(BF16)
-                maps_own[:, :, HEAD * t : HEAD * (t + 1)] = scaled.reshape(OWN_ROWS, TILE_W, HEAD)
             fill_keys(tiles, keys, OWN_ROWS * i - REACH, EXT_ROWS)
-            act = None
-            for c in range(CHAN):
-                term = dot_nt(mean_all[c], pooled_weight[:, 512 * c : 512 * (c + 1)])
-                act = term if act is None else act + term
-            pre_pooled[...] = act
-            act = silu(act).astype(BF16).astype(F32)
-            for r in range(OWN_ROWS):
-                row = rows_at(act, tiles[row_of(OWN_ROWS * i + r)])
-                pooled[TILE_W * r : TILE_W * (r + 1)] = jnp.broadcast_to(row, (TILE_W, BRANCH)).astype(
-                    BF16
-                )
             spread[...] = jnp.zeros_like(spread)
             for which, b in enumerate(BRANCH_ORDER):
                 for c in range(CHAN):
@@ -427,115 +494,129 @@
                         ]
 
         greet(
-            [where for _, where in ways]
+            [{"chan": spot.chan(d)} for d in (1, 2, 3)]
             + [{"pix": spot.pix_in_z(d)} for d in (1, -1)]
-            + [{"pix": spot.mate}],
+            + spot.sum_peers()
+            + [{"pix": p} for p in (spot.before, spot.after)],
             expected,
             prepare,
         )
-        for s in range(OWN_ROWS):
-            target, (away, here) = row_send(s)
-            pl.when(target != i)(lambda: away().start())
-            pl.when(target == i)(lambda: here().start())
-        for way, d in enumerate((1, -1)):
-            marks["relay", way] = posts.post(
-                lambda way=way, d=d: (
-                    x_slice(2, chans[way]), relay.at[way], {"pix": spot.pix_in_z(d)}
+        rows.send_rows()
+        row_sums = jnp.sum(trunk[...].astype(F32), axis=1)
+        sums = jnp.zeros((8, 512), F32)
+        for r in range(OWN_ROWS):
+            sums = add_at(sums, row_sums[r : r + 1], tile_at(tiles, OWN_ROWS * i + r))
+        near[spot.k] = sums
+        for d in range(1, GROUP):
+            marks["near", d] = posts.post(
+                lambda d=d: (near.at[spot.k], near.at[spot.k], {"pix": spot.pix_in_group(d)})
+            )
+        rows.pass_own()
+        post_x(0)
+        rows.await_halo(j)
+
+    @pl.when(step == 1)
+    def _():
+        for d in range(1, GROUP):
+            posts.arrive(marks["near", d], near.at[spot.in_group(-d)])
+        total = near[0]
+        for k in range(1, GROUP):
+            total = total + near[k]
+        across[spot.group] = total
+        for d in range(1, 4):
+            marks["across", d] = posts.post(
+                lambda d=d: (
+                    across.at[spot.group], across.at[spot.group], {"pix": spot.pix_in_x(d)}
                 )
             )
-        for d in (1, -1):
-            marks["z", d] = posts.post(
-                lambda d=d: (x_slice(d), x_rows(0, spot.core), {"pix": spot.pix_in_z(d)})
-            )
-        marks["mate", 0] = posts.post(
-            lambda: (x_slice(0), x_rows(0, spot.core), {"pix": spot.mate})
-        )
-        for copy in copies:
-            copy.wait()
-
-    @pl.when(step == 1)
-    def _():
-        for s in range(OWN_ROWS):
-            pltpu.make_async_copy(maps_own.at[s], maps_in.at[j, s], rs_row.at[s]).wait()
-        for half in range(2):
-            for d, where in ways:
-                marks["maps", d, half] = posts.post(
-                    lambda half=half, where=where: (
-                        maps_in.at[j, halves[half]], maps_in.at[j, halves[half]], where
-                    )
-                )
 
     @pl.when(step == 3)
     def _():
-        for way, d in enumerate((1, -1)):
-            posts.arrive(marks["relay", way], relay.at[way])
-            marks["far", way] = posts.post(
-                lambda way=way, d=d: (
-                    relay.at[way],
-                    x_rows(-d, spot.core, chans[way]),
-                    {"pix": spot.pix_in_z(d)},
-                )
+        rows.pass_sides()
+        post_x(1)
+        post_x(2)
+        pass_x(0)
+        for d in range(1, 4):
+            posts.arrive(marks["across", d], across.at[spot.x_of(-d)])
+        sums = across[0] + across[1] + across[2] + across[3]
+        mean = sums / tile_sizes(tile_grid[...])[:, 0:1]
+        mean_all[j] = jnp.concatenate([mean, jnp.zeros((8, 512), F32)], axis=0).astype(BF16)
+        for d in (2, 1, 3):
+            marks["mean", d] = posts.post(
+                lambda d=d: (mean_all.at[j], mean_all.at[j], {"chan": spot.chan(d)})
             )
-
-    @pl.when(step == 4)
-    def _():
-        for d, _ in ways:
-            for half in range(2):
-                source = spot.chan(-d)
-                posts.arrive(marks["maps", d, half], maps_in.at[source, halves[half]])
-        for half, (d, where) in enumerate(ways):
-            marks["maps far", half] = posts.post(
-                lambda d=d, half=half, where=where: (
-                    maps_in.at[spot.chan(-d), halves[half]],
-                    maps_in.at[spot.chan(-d), halves[half]],
-                    where,
-                )
-            )
+        rows.await_halo(blocks[1])
 
     @pl.when(step == 6)
     def _():
-        for d in (1, -1):
-            posts.arrive(marks["z", d], x_rows(-d, spot.core))
-            marks["mate", d] = posts.post(
-                lambda d=d: (x_rows(-d, spot.core), x_rows(-d, spot.core), {"pix": spot.mate})
+        rows.await_halo(blocks[2])
+        for d in (1, 2, 3):
+            posts.arrive(marks["mean", d], mean_all.at[spot.chan(-d)])
+        mean_kept[...] = mean_all[...]
+        act = None
+        for c in range(CHAN):
+            term = dot_nt(mean_all[c], pooled_weight[:, 512 * c : 512 * (c + 1)])
+            act = term if act is None else act + term
+        pre_pooled[...] = act
+        act = silu(act).astype(BF16).astype(F32)
+        for r in range(OWN_ROWS):
+            row = rows_at(act, tiles[row_of(OWN_ROWS * i + r)])
+            pooled[TILE_W * r : TILE_W * (r + 1)] = jnp.broadcast_to(row, (TILE_W, BRANCH)).astype(
+                BF16
             )
-
-    def rows_from(start):
-        return x[pl.ds(start, OWN_ROWS)].reshape(OWN_ROWS * TILE_W, -1)
-
-    window = rows_from(first)
-    for b in range(3):
-        product = dot_nt(window, kernel[:, 0, 0, b].reshape(BRANCH, -1))
-        for r in range(OWN_ROWS):
-            part = slice(TILE_W * r, TILE_W * (r + 1))
-            same = keys[REACH + r] == keys[first + r]
-            term = jnp.where(same, product[part], 0.0)
-            acc[b, part] = jnp.where(row_tap > 0, acc[b, part], 0.0) + term
-
-    for which, dilation in enumerate(head_rates):
-
-        @pl.when(step == 3 * which + 2)
+        rows.pass_far()
+        post_x(3)
+        own_copy().start()
+        pass_x(1)
+        pass_x(2)
+
+    @pl.when(step == 9)
+    def _():
+        rows.await_halo(blocks[3])
+        pass_x(3)
+
+    @pl.when(turn < 4)
+    def _():
+        chan = order_at(turn, j)
+        for a in range(3):
+            for r in range(OWN_ROWS):
+                slot = REACH + r + (a - 1) * (rate + 1)
+                row = x[chan, slot]
+                if a != 1:
+                    row = jnp.where(keys[REACH + r] == keys[slot], row, jnp.zeros_like(row))
+                lhs[TILE_W * r : TILE_W * (r + 1), 512 * a : 512 * (a + 1)] = row
+        taps = jnp.concatenate([kernel[:, 0, a].reshape(3 * BRANCH, 512) for a in range(3)], axis=1)
+        product = dot_nt(lhs[...], taps)
+
+        @pl.when(turn == 0)
         def _():
-            col = lax.broadcasted_iota(jnp.int32, (OWN_ROWS * TILE_W, BRANCH), 0) % TILE_W
-            total = acc[1]
-            behind = pltpu.roll(acc[0], dilation, 0)
-            ahead = pltpu.roll(acc[2], OWN_ROWS * TILE_W - dilation, 0)
-            total = total + jnp.where(col >= dilation, behind, 0.0)
-            pre[which] = total + jnp.where(col < TILE_W - dilation, ahead, 0.0)
-
-    @pl.when(step == 0)
+            acc[rate] = product
+
+        @pl.when(turn > 0)
+        def _():
+            acc[rate] += product
+
+        @pl.when(rate == 0)
+        def _():
+            lanes = pl.ds(pl.multiple_of(512 * chan, 512), 512)
+            own = x[chan, REACH : REACH + OWN_ROWS].reshape(OWN_ROWS * TILE_W, 512)
+            term = dot_nt(own, point[:, :, lanes].reshape(BRANCH, 512))
+            pre[3] = jnp.where(turn > 0, pre[3], 0.0) + term
+
+    @pl.when(step == 11)
     def _():
-        pre[3] = dot_nt(rows_from(REACH), point[...].reshape(BRANCH, -1))
-
-    @pl.when(step == 8)
-    def _():
-        for half in range(2):
-            posts.arrive(marks["maps far", half], maps_in.at[spot.chan(2), halves[half]])
-        for way in range(2):
-            posts.arrive(marks["far", way], x_rows(2, spot.core, chans[way]))
-        marks["mate", 2] = posts.post(
-            lambda: (x_rows(2, spot.core), x_rows(2, spot.core), {"pix": spot.mate})
-        )
+        col = lax.broadcasted_iota(jnp.int32, (OWN_ROWS * TILE_W, HEAD), 0) % TILE_W
+        for which, dilation in enumerate(head_rates):
+            for t in range(TASKS):
+                behind, total, ahead = (
+                    acc[which, :, BRANCH * t + HEAD * b : BRANCH * t + HEAD * (b + 1)]
+                    for b in range(3)
+                )
+                behind = pltpu.roll(behind, dilation, 0)
+                ahead = pltpu.roll(ahead, OWN_ROWS * TILE_W - dilation, 0)
+                total = total + jnp.where(col >= dilation, behind, 0.0)
+                total = total + jnp.where(col < TILE_W - dilation, ahead, 0.0)
+                pre[which, :, HEAD * t : HEAD * (t + 1)] = total
         cot = jnp.concatenate([maps_in[c].reshape(-1, BRANCH) for c in range(CHAN)], axis=1)
         head = None
         for which in range(5):
@@ -558,183 +639,20 @@
             back = dot_nn(cot, weight)
             if which < 4:
                 grad = back * (logistic * (1.0 + before * (1.0 - logistic)))
-                grad_pre[:, BRANCH * which : BRANCH * (which + 1)] = grad.astype(BF16)
+                grad_pre[:, :, BRANCH * which : BRANCH * (which + 1)] = grad.astype(BF16).reshape(
+                    OWN_ROWS, TILE_W, BRANCH
+                )
             else:
                 sums = jnp.sum(back.reshape(OWN_ROWS, TILE_W, BRANCH), axis=1)
                 pool_rows[:, :BRANCH] = sums
                 pool_rows[:, BRANCH:] = jnp.zeros((OWN_ROWS, 256 - BRANCH), F32)
         for c in range(CHAN):
-            head_part[c] = head[:, BRANCH * c : BRANCH * (c + 1)].astype(BF16)
-        for d in (0, 1, -1, 2):
-            other = 1 - spot.core
-            posts.arrive(marks["mate", d], x_rows(-d, other))
-        own_copy().wait()
-        for s in range(OWN_ROWS):
-            target, (away, here) = row_send(s)
-            pl.when(target != i)(lambda: away().wait_send())
-        posts.finish()
-
-
-def heads_forward(tiles, draws, x_ext, cotangent, kernels, point, project, mean_all, pooled_weight):
-    pixels = OWN_ROWS * TILE_W
-    feat = point.shape[2]
-    whole = pl.BlockSpec(memory_space=pltpu.VMEM)
-    hbm = pl.BlockSpec(memory_space=pl.ANY)
-    dma = pltpu.SemaphoreType.DMA
-    return pl.pallas_call(
-        heads_forward_kernel,
-        grid=(9,),
-        in_specs=[
-            pl.BlockSpec(memory_space=pltpu.SMEM),
-            pl.BlockSpec(memory_space=pltpu.SMEM),
-            hbm,
-            whole,
-            pl.BlockSpec((TASKS, 1, 1, 3, HEAD, feat), lambda s: (0, s // 3, s % 3, 0, 0, 0)),
-            whole,
-            whole,
-            whole,
-            whole,
-        ],
-        out_specs=[whole] * 4 + [hbm, whole],
-        out_shape=[
-            jax.ShapeDtypeStruct((pixels, 4 * BRANCH), BF16),
-            jax.ShapeDtypeStruct((CHAN, pixels, BRANCH), BF16),
-            jax.ShapeDtypeStruct((CHAN, 5, TASKS, HEAD, HEAD), BF16),
-            jax.ShapeDtypeStruct((OWN_ROWS, 256), F32),
-            jax.ShapeDtypeStruct((CHAN, GROUP_ROWS, TILE_W, 128), BF16),
-            jax.ShapeDtypeStruct((16, BRANCH), F32),
-        ],
-        scratch_shapes=[
-            pltpu.SMEM((EXT_ROWS,), jnp.int32),
-            pltpu.VMEM((OWN_ROWS, TILE_W, BRANCH), BF16),
-            pltpu.VMEM((pixels, BRANCH), BF16),
-            pltpu.VMEM((EXT_ROWS, TILE_W, feat), BF16),
-            pltpu.VMEM((3, pixels, BRANCH), F32),
-            pltpu.VMEM((4, pixels, BRANCH), F32),
-            pltpu.VMEM((CHAN, OWN_ROWS, TILE_W, BRANCH), BF16),
-            pltpu.VMEM((2, 2, OWN_ROWS, TILE_W, 128), BF16),
-            pltpu.VMEM((5, 256 * TASKS, BRANCH), BF16),
-            dma((CHAN,)),
-            dma((OWN_ROWS,)),
-            dma((OWN_ROWS,)),
-            dma((16,)),
-            dma((16,)),
-            dma((1,)),
-        ],
-        compiler_params=pltpu.CompilerParams(
-            collective_id=2, has_side_effects=True, vmem_limit_bytes=VMEM_LIMIT
-        ),
-        cost_estimate=pl.CostEstimate(
-            flops=12_000_000_000, bytes_accessed=28_000_000, transcendentals=0
-        ),
-        name="heads_forward",
-    )(tiles, draws, x_ext, cotangent, kernels, point, project, mean_all, pooled_weight)
-
-
-PAD = 24
-PADDED = PAD + TILE_W + PAD
-
-
-def heads_input_grad_kernel(
-    tiles, tile_grid, mid, parts, kernel, point, pool_rows, pre_pooled, pooled,
-    trunk_grad, g_group, maps_out, mean_rows, tall,
-    keys, wide, taps, acc, edges, maps_in, maps_sum, out, out_in, out_sum, near, across, mean_out, mean_in,
-    ss_row, rs_row, send_sems, recv_sems, own_sem, ss_side, rs_side, ss_back, rs_back,
-):
-    n, rate = pl.program_id(0), pl.program_id(1)
-    step = 3 * n + rate
-    spot = Spot()
-    posts = Posts(send_sems, recv_sems)
-    i, j = spot.i, spot.j
-    low, high = edges.at[0], edges.at[1]
-    half_rows = OWN_ROWS // 2
-    marks = {}
-
-    def g_rows(distance, core, half=None):
-        start = OWN_ROWS * (2 * spot.z_of(distance) + core)
-        if half is None:
-            return g_group.at[pl.ds(start, OWN_ROWS)]
-        return g_group.at[pl.ds(start + half_rows * half, half_rows)]
-
-    def own_copy():
-        return pltpu.make_async_copy(mid, g_rows(0, spot.core), own_sem.at[0])
-
-    def row_send(s):
-        row = row_of(OWN_ROWS * i + s)
-        target, slot = int_div(row, OWN_ROWS), int_rem(row, OWN_ROWS)
-        return target, (
-            lambda: remote(
-                maps_sum.at[s], maps_out.at[:, slot], ss_row.at[s], rs_row.at[slot], pix=target
-            ),
-            lambda: pltpu.make_async_copy(
-                maps_sum.at[s], maps_out.at[:, slot], rs_row.at[slot]
-            ),
-        )
-
-    def widen(start, part):
-        held = part[...].astype(F32)
-        for which in range(3):
-            for t in range(TASKS):
-                lane = BRANCH * which + HEAD * t
-                one = held[:, :, lane : lane + HEAD]
-                wide[3 * t + which, start : start + held.shape[0], PAD : PAD + TILE_W] = (
-                    jnp.concatenate([one, one], axis=2)
-                )
-
-    def prepare():
-        fill_keys(tiles, keys, OWN_ROWS * i - REACH, EXT_ROWS)
-        wide[...] = jnp.zeros_like(wide)
-        widen(REACH, mid)
-
-    @pl.when(step == 0)
+            part = head[:, BRANCH * c : BRANCH * (c + 1)].astype(BF16)
+            head_part[c] = part.reshape(OWN_ROWS, TILE_W, BRANCH)
+        start_grads()
+
+    @pl.when(grad_step == 0)
     def _():
-        own_copy().start()
-        barrier = pltpu.get_barrier_semaphore()
-        expected = 0
-        for s in range(OWN_ROWS):
-            origin = int_div(place_of(OWN_ROWS * i + s), OWN_ROWS)
-
-            @pl.when(origin != i)
-            def _():
-                signal(barrier, pix=origin)
-
-            target = int_div(row_of(OWN_ROWS * i + s), OWN_ROWS)
-            expected = expected + (target != i).astype(jnp.int32)
-        greet(
-            [{"chan": spot.chan(d)} for d in (1, 2, 3)]
-            + [{"pix": spot.pix_in_z(d)} for d in (1, -1)]
-            + spot.sum_peers()
-            + [{"pix": p} for p in (spot.mate, spot.before, spot.after)],
-            expected,
-            prepare,
-        )
-        marks["low"] = posts.post(
-            lambda: (mid.at[OWN_ROWS - REACH :], low, {"pix": spot.after})
-        )
-        marks["high"] = posts.post(lambda: (mid.at[:REACH], high, {"pix": spot.before}))
-        for d in (2, 1, 3):
-            marks["maps", d] = posts.post(
-                lambda d=d: (parts.at[spot.chan(d)], maps_in.at[d - 1], {"chan": spot.chan(d)})
-            )
-        for turn in range(2):
-            for d in (1, -1):
-                half = turn if d == 1 else 1 - turn
-                marks["z", d, half] = posts.post(
-                    lambda half=half, d=d: (
-                        mid.at[half_rows * half : half_rows * (half + 1)],
-                        g_rows(0, spot.core, half),
-                        {"pix": spot.pix_in_z(d)},
-                    )
-                )
-        marks["mate", 0] = posts.post(lambda: (mid, g_rows(0, spot.core), {"pix": spot.mate}))
-        sums = jnp.zeros((8, 256), F32)
-        for r in range(OWN_ROWS):
-            sums = add_at(sums, pool_rows[r : r + 1], tiles[row_of(OWN_ROWS * i + r)])
-        near[spot.k] = sums
-        for d in range(1, GROUP):
-            marks["near", d] = posts.post(
-                lambda d=d: (near.at[spot.k], near.at[spot.k], {"pix": spot.pix_in_group(d)})
-            )
         posts.arrive(marks["low"], low)
         posts.arrive(marks["high"], high)
         widen(0, low)
@@ -765,61 +683,61 @@
 
         lax.fori_loop(0, OWN_ROWS, one_row, 0)
 
-    @pl.when(step == 2)
+    @pl.when(grad_step == 2)
     def _():
         for d in range(1, GROUP):
-            posts.arrive(marks["near", d], near.at[spot.in_group(-d)])
-        total = near[0]
+            posts.arrive(marks["near b", d], near_b.at[spot.in_group(-d)])
+        total = near_b[0]
         for k in range(1, GROUP):
-            total = total + near[k]
-        across[spot.group] = total
+            total = total + near_b[k]
+        across_b[spot.group] = total
         for d in range(1, 4):
-            marks["across", d] = posts.post(
+            marks["across b", d] = posts.post(
                 lambda d=d: (
-                    across.at[spot.group], across.at[spot.group], {"pix": spot.pix_in_x(d)}
+                    across_b.at[spot.group], across_b.at[spot.group], {"pix": spot.pix_in_x(d)}
                 )
             )
 
-    @pl.when(step == 4)
+    @pl.when(grad_step == 4)
     def _():
         for d in range(1, 4):
-            posts.arrive(marks["across", d], across.at[spot.x_of(-d)])
-        sums = across[0] + across[1] + across[2] + across[3]
+            posts.arrive(marks["across b", d], across_b.at[spot.x_of(-d)])
+        sums = across_b[0] + across_b[1] + across_b[2] + across_b[3]
         pooled_pre = sums[:, :BRANCH] * slope(pre_pooled[0:8])
         tall[...] = jnp.concatenate([pooled_pre, jnp.zeros((8, BRANCH), F32)], axis=0).astype(BF16)
         for c in range(CHAN):
-            mean_out[c] = dot_nn(tall[...], pooled[:, 512 * c : 512 * (c + 1)]).astype(BF16)
+            mean_out[c] = dot_nn(tall[...], pooled_weight[:, 512 * c : 512 * (c + 1)]).astype(BF16)
         for d in (2, 1, 3):
-            marks["mean", d] = posts.post(
+            marks["mean b", d] = posts.post(
                 lambda d=d: (mean_out.at[spot.chan(d)], mean_in.at[d - 1], {"chan": spot.chan(d)})
             )
 
-    @pl.when(step == 8)
+    @pl.when(grad_step == 8)
     def _():
         mean = mean_out[j].astype(F32)
         for d in (1, 3, 2):
-            posts.arrive(marks["mean", d], mean_in.at[d - 1])
+            posts.arrive(marks["mean b", d], mean_in.at[d - 1])
             mean = mean + mean_in[d - 1].astype(F32)
         mean = mean[0:8] / tile_sizes(tile_grid[...])[:, 0:1]
         for r in range(OWN_ROWS):
             mean_rows[r : r + 1] = rows_at(mean, tiles[OWN_ROWS * i + r])
         for d in (1, 3, 2):
-            posts.arrive(marks["maps", d], maps_in.at[d - 1])
+            posts.arrive(marks["head", d], head_in.at[d - 1])
         for s in range(OWN_ROWS):
             held = parts[j, s].astype(F32)
             for d in (1, 2, 3):
-                held = held + maps_in[d - 1, s].astype(F32)
+                held = held + head_in[d - 1, s].astype(F32)
             for t in range(TASKS):
                 maps_sum[s, t] = held[:, HEAD * t : HEAD * (t + 1)].astype(BF16)
             target, (away, here) = row_send(s)
             pl.when(target != i)(lambda: away().start())
             pl.when(target == i)(lambda: here().start())
 
-    @pl.when(step == 5)
+    @pl.when(grad_step == 5)
     def _():
         for half, d in enumerate((1, -1)):
             posts.arrive(marks["z", d, half], g_rows(-d, spot.core, half))
-            marks["far", half] = posts.post(
+            marks["far g", half] = posts.post(
                 lambda half=half, d=d: (
                     g_rows(-d, spot.core, half),
                     g_rows(-d, spot.core, half),
@@ -827,30 +745,29 @@
                 )
             )
 
-    @pl.when(step == 10)
+    @pl.when(grad_step == 10)
     def _():
         for half, d in enumerate((-1, 1)):
             posts.arrive(marks["z", d, half], g_rows(-d, spot.core, half))
-        for d in (1, -1):
-            marks["mate", d] = posts.post(
-                lambda d=d: (g_rows(-d, spot.core), g_rows(-d, spot.core), {"pix": spot.mate})
-            )
-
-    product = dot_nn(taps[rate, :, : 27 * HEAD], kernel[...].reshape(27 * HEAD, -1))
-
-    @pl.when(rate == 0)
+
+    @pl.when(turn >= 4)
     def _():
-        grads = mid[...].reshape(OWN_ROWS * TILE_W, -1)[:, 3 * BRANCH :]
-        acc[...] = product + dot_nn(grads, point[...].reshape(BRANCH, -1))
-
-    @pl.when(rate == 1)
-    def _():
-        acc[...] += product
-
-    @pl.when(rate == 2)
-    def _():
-        total = acc[...] + product
-        out[block_at(n, j)] = total.astype(BF16).reshape(OWN_ROWS, TILE_W, 512)
+        product = dot_nn(taps[rate, :, : 27 * HEAD], kernel_b[...].reshape(27 * HEAD, -1))
+
+        @pl.when(rate == 0)
+        def _():
+            lanes = pl.ds(pl.multiple_of(512 * block_at(n, j), 512), 512)
+            grads = mid[...].reshape(OWN_ROWS * TILE_W, -1)[:, 3 * BRANCH :]
+            acc_b[...] = product + dot_nn(grads, point[:, :, lanes].reshape(BRANCH, 512))
+
+        @pl.when(rate == 1)
+        def _():
+            acc_b[...] += product
+
+        @pl.when(rate == 2)
+        def _():
+            total = acc_b[...] + product
+            out[block_at(n, j)] = total.astype(BF16).reshape(OWN_ROWS, TILE_W, 512)
 
     def side_send(chan, s):
         turn = int_rem(chan + CHAN - j, CHAN) - 1
@@ -858,7 +775,7 @@
             out.at[chan, s], out_in.at[turn, s], ss_side.at[turn, s], rs_side.at[turn, s], chan=chan
         )
 
-    @pl.when((rate == 2) & (n < 3))
+    @pl.when((turn >= 4) & (rate == 2) & (n < 3))
     def _():
         for s in range(OWN_ROWS):
             side_send(block_at(n, j), s).start()
@@ -877,7 +794,7 @@
         dst = out_in.at[turn, s]
         return remote(dst, dst, ss_side.at[turn, s], rs_side.at[turn, s], chan=spot.chan(1))
 
-    @pl.when(step == 11)
+    @pl.when(grad_step == 11)
     def _():
         for s in range(OWN_ROWS):
             held = out[j, s].astype(F32)
@@ -889,13 +806,8 @@
             pl.when(target != i)(lambda: away().start())
             pl.when(target == i)(lambda: here().start())
         for half in range(2):
-            posts.arrive(marks["far", half], g_rows(2, spot.core, half))
-        marks["mate", 2] = posts.post(
-            lambda: (g_rows(2, spot.core), g_rows(2, spot.core), {"pix": spot.mate})
-        )
-        for d in (0, 1, -1, 2):
-            posts.arrive(marks["mate", d], g_rows(-d, 1 - spot.core))
-        own_copy().wait()
+            posts.arrive(marks["far g", half], g_rows(2, spot.core, half))
+        g_copy().wait()
         for s in range(OWN_ROWS):
             pltpu.make_async_copy(out_sum.at[s], trunk_grad.at[s], rs_back.at[s]).wait()
             target, (away, here) = back_send(s)
@@ -905,79 +817,98 @@
             pltpu.make_async_copy(maps_sum.at[s], maps_out.at[:, s], rs_row.at[s]).wait()
             target, (away, here) = row_send(s)
             pl.when(target != i)(lambda: away().wait_send())
+        for q in range(4):
+            for d in (1, -1):
+                posts.arrive(marks["x", d, q], x_rows(-d, spot.core, blocks[q]))
+            posts.arrive(marks["far", q], x_rows(2, spot.core, blocks[q]))
+        own_copy().wait()
+        rows.drain()
         posts.finish()
 
 
-def block_at(n, chan):
-    ahead = jnp.where(n == 0, 2, jnp.where(n == 1, 1, jnp.where(n == 2, 3, 0)))
-    return int_rem(chan + ahead, CHAN)
-
-
-def heads_input_grad(tiles, tile_grid, grad_mid, head_part, kernels, point, *pool_operands):
+def heads(*operands):
     pixels = OWN_ROWS * TILE_W
-    block = 512
     whole = pl.BlockSpec(memory_space=pltpu.VMEM)
     hbm = pl.BlockSpec(memory_space=pl.ANY)
     dma = pltpu.SemaphoreType.DMA
-    maps, trunk = (OWN_ROWS, TILE_W, BRANCH), (OWN_ROWS, TILE_W, 512)
+    shape = jax.ShapeDtypeStruct
+    maps, rows = (OWN_ROWS, TILE_W, BRANCH), (OWN_ROWS, TILE_W, 512)
+
+    def forward_block(q, r):
+        chan = order_at(jnp.minimum(q, 3), lax.axis_index("chan"))
+        return (0, jnp.where(q < 4, r, 2), 0, 0, 0, chan)
+
+    def grad_block(q, r):
+        chan = block_at(jnp.maximum(q - 4, 0), lax.axis_index("chan"))
+        return (0, jnp.where(q < 4, 0, r), 0, 0, 0, chan)
+
     return pl.pallas_call(
-        heads_input_grad_kernel,
-        grid=(4, 3),
-        in_specs=[
-            pl.BlockSpec(memory_space=pltpu.SMEM),
-            whole,
-            whole,
-            whole,
-            pl.BlockSpec(
-                (TASKS, 1, 3, 3, HEAD, block),
-                lambda n, r: (0, r, 0, 0, 0, block_at(n, lax.axis_index("chan"))),
-            ),
-            pl.BlockSpec(
-                (TASKS, HEAD, block), lambda n, r: (0, 0, block_at(n, lax.axis_index("chan")))
-            ),
-        ]
-        + [whole] * 3,
-        out_specs=[hbm, hbm, hbm, whole, whole],
+        heads_kernel,
+        grid=(8, 3),
+        in_specs=[pl.BlockSpec(memory_space=pltpu.SMEM)]
+        + [whole] * 3
+        + [pl.BlockSpec((TASKS, 1, 3, 3, HEAD, 512), forward_block)]
+        + [whole] * 3
+        + [pl.BlockSpec((TASKS, 1, 3, 3, HEAD, 512), grad_block)],
+        out_specs=[whole, hbm, whole, hbm, hbm, hbm, whole, whole],
         out_shape=[
-            jax.ShapeDtypeStruct(trunk, BF16),
-            jax.ShapeDtypeStruct((GROUP_ROWS, TILE_W, 4 * BRANCH), BF16),
-            jax.ShapeDtypeStruct((TASKS, OWN_ROWS, TILE_W, HEAD), BF16),
-            jax.ShapeDtypeStruct((OWN_ROWS, 512), F32),
-            jax.ShapeDtypeStruct((16, BRANCH), BF16),
+            shape((CHAN, 5, TASKS, HEAD, HEAD), BF16),
+            shape((CHAN, GROUP_ROWS, TILE_W, 128), BF16),
+            shape((CHAN, 16, 512), BF16),
+            shape(rows, BF16),
+            shape((GROUP_ROWS, TILE_W, 4 * BRANCH), BF16),
+            shape((TASKS, OWN_ROWS, TILE_W, HEAD), BF16),
+            shape((OWN_ROWS, 512), F32),
+            shape((16, BRANCH), BF16),
         ],
         scratch_shapes=[
             pltpu.SMEM((EXT_ROWS,), jnp.int32),
+            pltpu.VMEM((CHAN, 16, 512), BF16),
+            pltpu.VMEM((pixels, BRANCH), BF16),
+            pltpu.VMEM((CHAN, EXT_ROWS, TILE_W, 512), BF16),
+            pltpu.VMEM((pixels, 3 * 512), BF16),
+            pltpu.VMEM((3, pixels, 3 * BRANCH), F32),
+            pltpu.VMEM((4, pixels, BRANCH), F32),
+            pltpu.VMEM((4, OWN_ROWS, TILE_W, 128), BF16),
+            pltpu.VMEM((5, 256 * TASKS, BRANCH), BF16),
+            pltpu.VMEM((GROUP, 8, 512), F32),
+            pltpu.VMEM((4, 8, 512), F32),
+            pltpu.VMEM((OWN_ROWS, TILE_W, 4 * BRANCH), BF16),
+            pltpu.VMEM((CHAN, *maps), BF16),
+            pltpu.VMEM((OWN_ROWS, 256), F32),
+            pltpu.VMEM((16, BRANCH), F32),
             pltpu.VMEM((9, EXT_ROWS, PADDED, 2 * HEAD), F32),
             pltpu.VMEM((3, pixels, 28 * HEAD), BF16),
-            pltpu.VMEM((pixels, block), F32),
+            pltpu.VMEM((pixels, 512), F32),
             pltpu.VMEM((2, REACH, TILE_W, 4 * BRANCH), BF16),
             pltpu.VMEM((CHAN - 1, *maps), BF16),
             pltpu.VMEM((OWN_ROWS, TASKS, TILE_W, HEAD), BF16),
-            pltpu.VMEM((CHAN, *trunk), BF16),
-            pltpu.VMEM((CHAN - 1, *trunk), BF16),
-            pltpu.VMEM(trunk, BF16),
+            pltpu.VMEM((CHAN, *rows), BF16),
+            pltpu.VMEM((CHAN - 1, *rows), BF16),
+            pltpu.VMEM(rows, BF16),
             pltpu.VMEM((GROUP, 8, 256), F32),
             pltpu.VMEM((4, 8, 256), F32),
             pltpu.VMEM((CHAN, 16, 512), BF16),
             pltpu.VMEM((CHAN - 1, 16, 512), BF16),
+            dma((64,)),
+            dma((64,)),
+            dma((2,)),
             dma((OWN_ROWS,)),
             dma((OWN_ROWS,)),
-            dma((32,)),
-            dma((32,)),
-            dma((1,)),
             dma((CHAN - 1, OWN_ROWS)),
             dma((CHAN - 1, OWN_ROWS)),
             dma((OWN_ROWS,)),
             dma((OWN_ROWS,)),
+            *gather_sems(REACH),
         ],
         compiler_params=pltpu.CompilerParams(
-            collective_id=3, has_side_effects=True, vmem_limit_bytes=VMEM_LIMIT
+            collective_id=2, has_side_effects=True, vmem_limit_bytes=VMEM_LIMIT
         ),
         cost_estimate=pl.CostEstimate(
-            flops=12_000_000_000, bytes_accessed=28_000_000, transcendentals=0
+            flops=24_000_000_000, bytes_accessed=56_000_000, transcendentals=0
         ),
-        name="heads_input_grad",
-    )(tiles, tile_grid, grad_mid, head_part, kernels, point, *pool_operands)
+        name="heads",
+    )(*operands)
 
 
 class GroupSum:
@@ -1085,20 +1016,38 @@
 
 
 def section_forward_kernel(
-    tiles, tile_grid, pixels, wr, wd, we, gain_r, bias_r, gain_d, bias_d, gain_e, bias_e, project,
-    x_ext, unit_r, unit_d, unit_e, act_r, act_d, wr_all, inv_mid, inv_feat, mean_all, project_all,
-    keep, trunk, project_out, part_out, part_in, near_m, across_m, near_f, across_f, near_t, across_t,
-    *sems,
+    tiles, draws, pixels, wr, wd, we, gain_r, bias_r, gain_d, bias_d, gain_e, bias_e, project, cotangent,
+    trunk, unit_r, unit_d, unit_e, act_r, act_d, wr_all, inv_mid, inv_feat, project_all, maps_in,
+    keep, project_out, part_out, part_in, near_m, across_m, near_f, across_f, maps_own,
+    send_sems, recv_sems, ss_map, rs_map,
 ):
-    send_sems, recv_sems, sems = sems[0], sems[1], sems[2:]
     spot = Spot()
     links = Links(send_sems, recv_sems)
-    rows_out = RowGather(REACH, trunk, x_ext, spot, sems)
-    j = spot.j
-    expected = rows_out.greet()
+    i, j = spot.i, spot.j
+    expected = greet_origins(i)
+
+    def map_send(s):
+        place = place_of(OWN_ROWS * i + s)
+        target, slot = int_div(place, OWN_ROWS), int_rem(place, OWN_ROWS)
+        return target, (
+            lambda: remote(
+                maps_own.at[s], maps_in.at[j, slot], ss_map.at[s], rs_map.at[slot], pix=target
+            ),
+            lambda: pltpu.make_async_copy(maps_own.at[s], maps_in.at[j, slot], rs_map.at[slot]),
+        )
 
     def prepare():
         fill_keep(tiles, keep, spot.i)
+        lane = lax.broadcasted_iota(jnp.int32, (8, 128), 1)
+        drawn = jnp.full((8, 128), -1e30, F32)
+        for t in range(TASKS):
+            drawn = jnp.where(lane == t, draws[t].astype(F32) / 3.0, drawn)
+        grown = jnp.where(lane < TASKS, jnp.exp(drawn - jnp.max(drawn, axis=1, keepdims=True)), 0.0)
+        grown = grown / jnp.sum(grown, axis=1, keepdims=True)
+        for t in range(TASKS):
+            weight = jnp.sum(jnp.where(lane == t, grown, 0.0), axis=1, keepdims=True)[0:1]
+            scaled = (cotangent[t].astype(F32).T * weight).astype(BF16)
+            maps_own[:, :, HEAD * t : HEAD * (t + 1)] = scaled.reshape(OWN_ROWS, TILE_W, HEAD)
         for c in range(CHAN):
             for b in range(5):
                 lane = HEAD * (b % 2)
@@ -1127,6 +1076,10 @@
         )
         for d in (2, 1, 3)
     }
+    for s in range(OWN_ROWS):
+        target, (away, here) = map_send(s)
+        pl.when(target != i)(lambda: away().start())
+        pl.when(target == i)(lambda: here().start())
     wr_all[j] = wr[pl.ds(pl.multiple_of(FEAT_OWN * j, FEAT_OWN), FEAT_OWN)]
     pre = dot_nn(pixels[...], wr_all[j])
     mates = {}
@@ -1164,7 +1117,26 @@
                 project_all.at[source, spot.core], project_all.at[source, spot.core], pix=spot.mate
             )
 
-    todo = [send_project, lambda: None, swap_project]
+    halves = (slice(0, OWN_ROWS // 2), slice(OWN_ROWS // 2, OWN_ROWS))
+    maps_sent = {}
+
+    def send_maps():
+        for s in range(OWN_ROWS):
+            pltpu.make_async_copy(maps_own.at[s], maps_in.at[j, s], rs_map.at[s]).wait()
+        for part in halves:
+            for d in (1, -1):
+                block = maps_in.at[j, part]
+                maps_sent[d, part.start] = links.send(block, block, chan=spot.chan(d))
+
+    def pass_maps():
+        for d in (1, -1):
+            for part in halves:
+                links.arrive(maps_sent[d, part.start], maps_in.at[spot.chan(-d), part])
+        for d, part in zip((1, -1), halves):
+            block = maps_in.at[spot.chan(-d), part]
+            maps_sent[part.start] = links.send(block, block, chan=spot.chan(d))
+
+    todo = [send_project, send_maps, swap_project, pass_maps]
 
     def meanwhile():
         if todo:
@@ -1222,22 +1194,14 @@
     inv_feat[...] = jnp.concatenate([inv_e, jnp.zeros((7, FEAT_OWN), F32)], axis=0)
     out = silu(normed + pixels[...].astype(F32)).astype(BF16)
     trunk[...] = out.reshape(OWN_ROWS, TILE_W, FEAT_OWN)
-    rows_out.send_rows()
-    row_sums = jnp.sum(out.astype(F32).reshape(OWN_ROWS, TILE_W, FEAT_OWN), axis=1)
-    sums = jnp.zeros((8, FEAT_OWN), F32)
-    for r in range(OWN_ROWS):
-        sums = add_at(sums, row_sums[r : r + 1], tile_at(tiles, OWN_ROWS * spot.i + r))
-    todo[:] = [rows_out.pass_own]
-    sums = sum_over_pix(sums, near_t, across_t, spot, links, meanwhile)
-    mean = jnp.concatenate([sums / tile_sizes(tile_grid[...])[:, 0:1], jnp.zeros((8, FEAT_OWN), F32)], axis=0)
-    mean_all[j] = mean.astype(BF16)
-    sent = {d: links.send(mean_all.at[j], mean_all.at[j], chan=spot.chan(d)) for d in (2, 1, 3)}
-    rows_out.pass_sides()
     for d in (1, 3, 2):
-        links.arrive(sent[d], mean_all.at[spot.chan(-d)])
         links.arrive(project_sent[d], project_all.at[spot.chan(-d), 1 - spot.core])
     project_all[j] = project_out[j]
-    rows_out.finish()
+    for part in halves:
+        links.arrive(maps_sent[part.start], maps_in.at[spot.chan(2), part])
+    for s in range(OWN_ROWS):
+        target, (away, here) = map_send(s)
+        pl.when(target != i)(lambda: away().wait_send())
     links.finish()
 
 
@@ -1248,10 +1212,10 @@
     dma = pltpu.SemaphoreType.DMA
     return pl.pallas_call(
         section_forward_kernel,
-        in_specs=[pl.BlockSpec(memory_space=pltpu.SMEM)] + [whole] * 12,
-        out_specs=[pl.BlockSpec(memory_space=pl.ANY)] + [whole] * 10,
+        in_specs=[pl.BlockSpec(memory_space=pltpu.SMEM)] * 2 + [whole] * 12,
+        out_specs=[whole] * 11,
         out_shape=[
-            shape((CHAN, EXT_ROWS, TILE_W, FEAT_OWN), BF16),
+            shape((OWN_ROWS, TILE_W, FEAT_OWN), BF16),
             shape(mid, F32),
             shape(mid, F32),
             shape(feat, F32),
@@ -1260,12 +1224,11 @@
             shape((CHAN, FEAT_OWN, MID_OWN), BF16),
             shape((8, MID_OWN), F32),
             shape((8, FEAT_OWN), F32),
-            shape((CHAN, 16, FEAT_OWN), BF16),
             shape((CHAN, 3, TASKS, HEAD, 2 * HEAD), BF16),
+            shape((CHAN, OWN_ROWS, TILE_W, BRANCH), BF16),
         ],
         scratch_shapes=[
             pltpu.VMEM((2, OWN, MID_OWN), F32),
-            pltpu.VMEM((OWN_ROWS, TILE_W, FEAT_OWN), BF16),
             pltpu.VMEM((CHAN, 3, TASKS, HEAD, 2 * HEAD), BF16),
             pltpu.VMEM((3, *mid), BF16),
             pltpu.VMEM((3, *mid), BF16),
@@ -1273,11 +1236,11 @@
             pltpu.VMEM((2, 4, 8, MID_OWN), F32),
             pltpu.VMEM((GROUP, 8, FEAT_OWN), F32),
             pltpu.VMEM((4, 8, FEAT_OWN), F32),
-            pltpu.VMEM((GROUP, 8, FEAT_OWN), F32),
-            pltpu.VMEM((4, 8, FEAT_OWN), F32),
-            dma((80,)),
-            dma((80,)),
-            *gather_sems(REACH),
+            pltpu.VMEM((OWN_ROWS, TILE_W, BRANCH), BF16),
+            dma((72,)),
+            dma((72,)),
+            dma((OWN_ROWS,)),
+            dma((OWN_ROWS,)),
         ],
         compiler_params=pltpu.CompilerParams(
             collective_id=5, has_side_effects=True, vmem_limit_bytes=VMEM_LIMIT
@@ -1362,8 +1325,8 @@
         keys, keep, wd_cat, side_out, side_in, halo, taps, full, project_in, project_wide, reduce_out,
         near_m, across_m, near_f, across_f, x_all, x_base, x_now, g_all, g_now,
     ) = scratch[:20]
-    send_sems, recv_sems, ss_reduce, rs_reduce, load_sems = scratch[-5:]
-    buffers = scratch[20:-5]
+    send_sems, recv_sems, ss_reduce, rs_reduce, load_sems, edge_sems = scratch[-6:]
+    buffers = scratch[20:-6]
     spot = Spot()
     links = Links(send_sems, recv_sems)
     i, j = spot.i, spot.j
@@ -1382,9 +1345,20 @@
     peers = [{"chan": spot.chan(d)} for d in (1, 2, 3)] + spot.sum_peers()
     peers += [{"pix": spot.before}, {"pix": spot.after}]
 
+    def core_rows(z, core, first=0):
+        return pl.ds(first + OWN_ROWS * (2 * z + core), OWN_ROWS)
+
+    def shares(core):
+        pairs = []
+        for z in range(4):
+            rows, moved = core_rows(z, core), core_rows(z, core, REACH)
+            pairs.append((x_group.at[:, rows], x_all.at[:, rows]))
+            pairs.append((g_group.at[rows], g_all.at[moved]))
+        return pairs
+
     loads = [
-        pltpu.make_async_copy(x_group, x_all, load_sems.at[0]),
-        pltpu.make_async_copy(g_group, g_all.at[REACH : REACH + GROUP_ROWS], load_sems.at[1]),
+        pltpu.make_async_copy(src, dst, load_sems.at[n])
+        for n, (src, dst) in enumerate(shares(spot.core))
     ]
 
     def prepare():
@@ -1395,15 +1369,33 @@
         for tap in range(9):
             wd_cat[:, MID_OWN * tap : MID_OWN * (tap + 1)] = wd[tap]
 
+    for step in (1, -1):
+        x_maker = int_rem(spot.group + 4 - step, 4)
+        maker_core = (1 + step) // 2
+        peers.append({"pix": GROUP * x_maker + 2 * spot.z + maker_core})
+    peers.append({"pix": spot.mate})
     greet(peers, 1 - stays.astype(jnp.int32), prepare)
 
     atrous_sum = GroupSum(*buffers[24:27], spot, links)
     point_sum = GroupSum(*buffers[27:30], spot, links)
-    edges = [
-        (g_group.at[GROUP_ROWS - REACH :], g_all.at[:REACH], 1),
-        (g_group.at[:REACH], g_all.at[REACH + GROUP_ROWS :], -1),
-    ]
-    edges = [(links.send(src, dst, pix=spot.pix_in_x(d)), dst) for src, dst, d in edges]
+    x_target = int_rem(spot.group + 3 + 2 * spot.core, 4)
+
+    def edge_copy(core):
+        return remote(
+            g_group.at[pl.ds(spot.core * (GROUP_ROWS - REACH), REACH)],
+            g_all.at[pl.ds((1 - spot.core) * (GROUP_ROWS + REACH), REACH)],
+            edge_sems.at[core],
+            edge_sems.at[2 + 1 - spot.core],
+            pix=GROUP * x_target + 2 * spot.z + core,
+        )
+
+    def edge_arrival(high):
+        dst = g_all.at[pl.ds(high * (GROUP_ROWS + REACH), REACH)]
+        return remote(dst, dst, edge_sems.at[0], edge_sems.at[2 + high], chan=spot.chan(1))
+
+    for core in range(2):
+        edge_copy(core).start()
+    mates = [links.send(src, dst, pix=spot.mate) for src, dst in shares(spot.core)]
 
     def row_block(r):
         return pl.ds(pl.multiple_of(r * TILE_W, TILE_W), TILE_W)
@@ -1411,8 +1403,10 @@
     def take():
         for load in loads:
             load.wait()
-        for n, dst in edges:
+        for n, (_, dst) in zip(mates, shares(1 - spot.core)):
             links.arrive(n, dst)
+        for high in range(2):
+            edge_arrival(high).wait_recv()
 
         def one_row(r, carry):
             is_low = lax.broadcasted_iota(jnp.int32, (TILE_W, 2 * HEAD), 1) < HEAD
@@ -1466,7 +1460,7 @@
             point_sum.out[0, c] = product[HEAD * c : HEAD * (c + 1)]
         point_sum.ready.append((0, 1))
 
-    tasks = [take]
+    tasks = [lambda: None, lambda: None, take]
     for which in range(3):
         tasks.append(functools.partial(pick, which))
         tasks += [functools.partial(multiply, which, b) for b in range(3)]
@@ -1529,7 +1523,7 @@
             by_expand.parts[spot_of(8 * c + n)] = grads[part * n : part * (n + 1)]
     by_expand.start()
     flush()
-    meanwhile(2)
+    meanwhile(3)
     grad_act = side_sum(0, own, sent)
 
     unit = unit_d[...]
@@ -1652,6 +1646,8 @@
 
     atrous_sum.finish(place)
     point_sum.finish(place_point)
+    for core in range(2):
+        edge_copy(core).wait_send()
 
     pltpu.make_async_copy(reduce_out, grad_reduce, rs_reduce.at[0]).wait()
     pl.when(jnp.logical_not(stays))(lambda: away().wait_send())
@@ -1723,7 +1719,8 @@
             dma((112,)),
             dma((1,)),
             dma((1,)),
-            dma((2,)),
+            dma((8,)),
+            dma((4,)),
         ],
         compiler_params=pltpu.CompilerParams(
             collective_id=6, has_side_effects=True, vmem_limit_bytes=VMEM_LIMIT
@@ -1758,7 +1755,7 @@
     shape = jax.ShapeDtypeStruct
     return pl.pallas_call(
         hand_out_kernel,
-        in_specs=[whole] * (3 + len(grads)),
+        in_specs=[whole] * 3 + [pl.BlockSpec(memory_space=pl.ANY)] * len(grads),
         out_specs=[whole] * 2 + [pl.BlockSpec(memory_space=pl.ANY)] * len(grads),
         out_shape=[shape((TASKS, HEAD, OWN), BF16), shape((TASKS, HEAD, CHAN * 512), F32)]
         + [shape(grad.shape, grad.dtype) for grad in grads],
@@ -1795,21 +1792,15 @@
     ]
     pooled_rows = pooled_weight.reshape(BRANCH, -1)
     (
-        x_ext, unit_reduce, unit_dilate, unit_expand, act_reduce, act_dilate, reduce_all, inv_mid,
-        inv_feat, mean_all, project_all,
+        trunk, unit_reduce, unit_dilate, unit_expand, act_reduce, act_dilate, reduce_all, inv_mid,
+        inv_feat, project_all, maps_all,
     ) = section_forward(
-        tile_number, tile_grid, pixels, reduce_weight, dilate_weight, expand_weight, *norms,
-        project_weight,
+        tile_number, task_draws, pixels, reduce_weight, dilate_weight, expand_weight, *norms,
+        project_weight, jnp.swapaxes(cotangent, 1, 2),
     )
     kernels = atrous_weight.reshape(TASKS, 3, 3, 3, HEAD, -1)
-    grad_pre, head_part, grad_project, pool_rows, x_group, pre_pooled = heads_forward(
-        tile_number, task_draws, x_ext, jnp.swapaxes(cotangent, 1, 2), kernels, point_weight, project_all, mean_all,
-        pooled_rows,
-    )
-    trunk_grad, g_group, maps, mean_rows, pooled_grad = heads_input_grad(
-        tile_number, tile_grid, grad_pre.reshape(OWN_ROWS, TILE_W, 4 * BRANCH),
-        head_part.reshape(CHAN, OWN_ROWS, TILE_W, BRANCH), kernels, point_weight, pool_rows,
-        pre_pooled, pooled_rows,
+    grad_project, x_group, mean_all, trunk_grad, g_group, maps, mean_rows, pooled_grad = heads(
+        tile_number, tile_grid, trunk, maps_all, kernels, point_weight, project_all, pooled_rows, kernels
     )
     grads = section_backward(
         tile_number, trunk_grad, pixels, unit_reduce, unit_dilate, unit_expand, act_reduce, act_dilate,

time: 317 us -> 408 us (1.29)
  Pallas kernels: 312 us -> 402 us
    pallas_call x3 -> x2, Pallas kernels: 116 us -> 233 us  [the longest x1 124 us: heads(): pl.pallas_call(heads_kernel, grid=(8, 3), in_specs=[pl.BlockSpec(memory_s...]
    pallas_call x1, Pallas kernels: 97.7 us -> 73.5 us  [section_forward(): pl.pallas_call(section_forward_kernel, in_specs=[pl.BlockSpec(memory_spac...]
where the time goes in v6:
time: 408 us; the launch traced here: 403 us
  Pallas kernels  402 us (99%)
    pallas_call x1, Pallas kernels, heads(): pl.pallas_call(heads_kernel, grid=(8, 3), in_specs=[pl.BlockSpec(memory_s...  124 us
    pallas_call x1, Pallas kernels, hand_out(): pl.pallas_call(hand_out_kernel, in_specs=[whole] * 3 + [pl.BlockSpec(memo...  109 us
    pallas_call x1, Pallas kernels, section_backward(): pl.pallas_call(section_backward_kernel, in_specs=[pl.BlockSpec(memory_spa...  96.5 us
    pallas_call x1, Pallas kernels, section_forward(): pl.pallas_call(section_forward_kernel, in_specs=[pl.BlockSpec(memory_spac...  73.5 us

profile of v6, /device:TPU:7, one launch (start us, length us, event | category | flops | bytes accessed | tf_op | source)
XLA Modules:
  0.0 403.4 jit_solution(146601960682443583)
XLA Ops:
  0.6 73.5 %section_forward.1 = (bf16[8,64,512]{2,1,0:T(8,128)(2,1)}, f32[512,128]{1,0:T(8,128)}, f32[512,128]{1,0:T(8,128)}, f32[512,512]{1,0:T(8,128)}, bf16[4,16,64,128]...) custom-call(s32[256]{0:T(256)} %tiles.5, s32[3]{0:T(128)} %draws.1, ...), custom_call_target="tpu_custom_call" | custom-call | flops 2000000000 | bytes 120000000 | tf_op jit(solution)/shard_map/section_forward/pallas_call | solution.py:1213
  74.1 123.5 %heads.1 = (bf16[4,5,3,64,64]{4,3,2,1,0:T(8,128)(2,1)}, bf16[4,64,64,128]{3,2,1,0:T(8,128)(2,1)}, bf16[4,16,512]{2,1,0:T(8,128)(2,1)}, bf16[8,64,512]{2,1,0:T(8,...) custom-call(s32[256]{0:T(256)} %tiles.5, ...), custom_call_target="tpu_custom_call" | custom-call | flops 24000000000 | bytes 56000000 | tf_op jit(solution)/shard_map/heads/pallas_call | solution.py:845
  197.7 96.5 %section_backward.1 = (bf16[512,512]{1,0:T(8,128)(2,1)}, f32[64,128]{1,0:T(8,128)}, f32[1,128]{1,0:T(1,128)}, f32[1,128]{1,0:T(1,128)}, f32[9,16,128]{2,1,0:T(8,...) custom-call(s32[256]{0:T(256)} %tiles.5, ...), custom_call_target="tpu_custom_call" | custom-call | flops 16000000000 | bytes 250000000 | tf_op jit(solution)/shard_map/section_backward/pallas_call | solution.py:1670
  294.1 109.0 %hand_out.1 = (bf16[3,64,512]{2,1,0:T(8,128)(2,1)}, f32[3,64,2048]{2,1,0:T(8,128)}, bf16[512,512]{1,0:T(8,128)(2,1)}, f32[64,128]{1,0:T(8,128)}, f32[1,128]{1,0:...) custom-call(bf16[3,8,64,64]{3,2,1,0:T(8,128)(2,1)} %get-tuple-elemen, ...), custom_call_target="tpu_custom_call" | custom-call | bytes 10000000 | tf_op jit(solution)/shard_map/hand_out/pallas_call | solution.py:1756

commit v7 on v6

--- a/solution.py
+++ b/solution.py
@@ -1755,7 +1755,7 @@
     shape = jax.ShapeDtypeStruct
     return pl.pallas_call(
         hand_out_kernel,
-        in_specs=[whole] * 3 + [pl.BlockSpec(memory_space=pl.ANY)] * len(grads),
+        in_specs=[whole] * (3 + len(grads)),
         out_specs=[whole] * 2 + [pl.BlockSpec(memory_space=pl.ANY)] * len(grads),
         out_shape=[shape((TASKS, HEAD, OWN), BF16), shape((TASKS, HEAD, CHAN * 512), F32)]
         + [shape(grad.shape, grad.dtype) for grad in grads],

time: 408 us -> 304 us (0.75)
  Pallas kernels: 402 us -> 299 us
    pallas_call x1, Pallas kernels: 109 us -> 5.33 us  [hand_out(): pl.pallas_call(hand_out_kernel, in_specs=[whole] * (3 + len(grads)), out_...]
where the time goes in v7:
time: 304 us; the launch traced here: 300 us
  Pallas kernels  299 us (98%)
    pallas_call x1, Pallas kernels, heads(): pl.pallas_call(heads_kernel, grid=(8, 3), in_specs=[pl.BlockSpec(memory_s...  124 us
    pallas_call x1, Pallas kernels, section_backward(): pl.pallas_call(section_backward_kernel, in_specs=[pl.BlockSpec(memory_spa...  96.5 us
    pallas_call x1, Pallas kernels, section_forward(): pl.pallas_call(section_forward_kernel, in_specs=[pl.BlockSpec(memory_spac...  73.5 us

profile of v7, /device:TPU:7, one launch (start us, length us, event | category | flops | bytes accessed | tf_op | source)
XLA Modules:
  0.0 299.7 jit_solution(17903651556071550909)
XLA Ops:
  0.6 73.5 %section_forward.1 = (bf16[8,64,512]{2,1,0:T(8,128)(2,1)}, f32[512,128]{1,0:T(8,128)}, f32[512,128]{1,0:T(8,128)}, f32[512,512]{1,0:T(8,128)}, bf16[4,16,64,128]...) custom-call(s32[256]{0:T(256)} %tiles.5, s32[3]{0:T(128)} %draws.1, ...), custom_call_target="tpu_custom_call" | custom-call | flops 2000000000 | bytes 120000000 | tf_op jit(solution)/shard_map/section_forward/pallas_call | solution.py:1213
  74.1 123.5 %heads.1 = (bf16[4,5,3,64,64]{4,3,2,1,0:T(8,128)(2,1)}, bf16[4,64,64,128]{3,2,1,0:T(8,128)(2,1)}, bf16[4,16,512]{2,1,0:T(8,128)(2,1)}, bf16[8,64,512]{2,1,0:T(8,...) custom-call(s32[256]{0:T(256)} %tiles.5, ...), custom_call_target="tpu_custom_call" | custom-call | flops 24000000000 | bytes 56000000 | tf_op jit(solution)/shard_map/heads/pallas_call | solution.py:845
  197.7 96.5 %section_backward.1 = (bf16[512,512]{1,0:T(8,128)(2,1)}, f32[64,128]{1,0:T(8,128)}, f32[1,128]{1,0:T(1,128)}, f32[1,128]{1,0:T(1,128)}, f32[9,16,128]{2,1,0:T(8,...) custom-call(s32[256]{0:T(256)} %tiles.5, ...), custom_call_target="tpu_custom_call" | custom-call | flops 16000000000 | bytes 250000000 | tf_op jit(solution)/shard_map/section_backward/pallas_call | solution.py:1670
  294.1 5.3 %hand_out.1 = (bf16[3,64,512]{2,1,0:T(8,128)(2,1)}, f32[3,64,2048]{2,1,0:T(8,128)}, bf16[512,512]{1,0:T(8,128)(2,1)}, f32[64,128]{1,0:T(8,128)}, f32[1,128]{1,0:...) custom-call(bf16[3,8,64,64]{3,2,1,0:T(8,128)(2,1)} %get-tuple-elemen, ...), custom_call_target="tpu_custom_call" | custom-call | bytes 10000000 | tf_op jit(solution)/shard_map/hand_out/pallas_call | solution.py:1756

commit v8 on v7

--- a/solution.py
+++ b/solution.py
@@ -1136,7 +1136,7 @@
             block = maps_in.at[spot.chan(-d), part]
             maps_sent[part.start] = links.send(block, block, chan=spot.chan(d))
 
-    todo = [send_project, send_maps, swap_project, pass_maps]
+    todo = [send_project, lambda: None, swap_project]
 
     def meanwhile():
         if todo:
@@ -1158,6 +1158,7 @@
     sent = {
         d: links.send(act_r.at[j, own], act_r.at[j, own], chan=spot.chan(d)) for d in (2, 1, 3)
     }
+    send_maps()
     arrivals = []
     for d in (0, 1, 3, 2):
         source = spot.chan(-d)
@@ -1184,6 +1185,7 @@
     inv_mid[...] = jnp.concatenate([inv_r, inv_d, jnp.zeros((6, MID_OWN), F32)], axis=0)
     act_d[j] = silu(normed).astype(BF16)
     sent = {d: links.send(act_d.at[j], act_d.at[j], chan=spot.chan(d)) for d in (2, 1, 3)}
+    pass_maps()
     for d in (1, 3, 2):
         links.arrive(sent[d], act_d.at[spot.chan(-d)])
     full = jnp.concatenate([act_d[c] for c in range(CHAN)], axis=1)

time: 304 us -> 302 us (level)
  no operation moved by 1% of the time
where the time goes in v8:
time: 302 us; the launch traced here: 298 us
  Pallas kernels  297 us (98%)
    pallas_call x1, Pallas kernels, heads(): pl.pallas_call(heads_kernel, grid=(8, 3), in_specs=[pl.BlockSpec(memory_s...  123 us
    pallas_call x1, Pallas kernels, section_backward(): pl.pallas_call(section_backward_kernel, in_specs=[pl.BlockSpec(memory_spa...  96.4 us
    pallas_call x1, Pallas kernels, section_forward(): pl.pallas_call(section_forward_kernel, in_specs=[pl.BlockSpec(memory_spac...  71.4 us

profile of v8, /device:TPU:7, one launch (start us, length us, event | category | flops | bytes accessed | tf_op | source)
XLA Modules:
  0.0 297.5 jit_solution(17268651259748476466)
XLA Ops:
  0.6 71.4 %section_forward.1 = (bf16[8,64,512]{2,1,0:T(8,128)(2,1)}, f32[512,128]{1,0:T(8,128)}, f32[512,128]{1,0:T(8,128)}, f32[512,512]{1,0:T(8,128)}, bf16[4,16,64,128]...) custom-call(s32[256]{0:T(256)} %tiles.5, s32[3]{0:T(128)} %draws.1, ...), custom_call_target="tpu_custom_call" | custom-call | flops 2000000000 | bytes 120000000 | tf_op jit(solution)/shard_map/section_forward/pallas_call | solution.py:1215
  72.1 123.5 %heads.1 = (bf16[4,5,3,64,64]{4,3,2,1,0:T(8,128)(2,1)}, bf16[4,64,64,128]{3,2,1,0:T(8,128)(2,1)}, bf16[4,16,512]{2,1,0:T(8,128)(2,1)}, bf16[8,64,512]{2,1,0:T(8,...) custom-call(s32[256]{0:T(256)} %tiles.5, ...), custom_call_target="tpu_custom_call" | custom-call | flops 24000000000 | bytes 56000000 | tf_op jit(solution)/shard_map/heads/pallas_call | solution.py:845
  195.5 96.4 %section_backward.1 = (bf16[512,512]{1,0:T(8,128)(2,1)}, f32[64,128]{1,0:T(8,128)}, f32[1,128]{1,0:T(1,128)}, f32[1,128]{1,0:T(1,128)}, f32[9,16,128]{2,1,0:T(8,...) custom-call(s32[256]{0:T(256)} %tiles.5, ...), custom_call_target="tpu_custom_call" | custom-call | flops 16000000000 | bytes 250000000 | tf_op jit(solution)/shard_map/section_backward/pallas_call | solution.py:1672
  292.0 5.3 %hand_out.1 = (bf16[3,64,512]{2,1,0:T(8,128)(2,1)}, f32[3,64,2048]{2,1,0:T(8,128)}, bf16[512,512]{1,0:T(8,128)(2,1)}, f32[64,128]{1,0:T(8,128)}, f32[1,128]{1,0:...) custom-call(bf16[3,8,64,64]{3,2,1,0:T(8,128)(2,1)} %get-tuple-elemen, ...), custom_call_target="tpu_custom_call" | custom-call | bytes 10000000 | tf_op jit(solution)/shard_map/hand_out/pallas_call | solution.py:1758
